TPU v7x, 32 devices: a whole 2x2x4 slice. The times are simulated.
32 devices in a mesh: fsdp: 2 (over y), heads: 4 (over x, core), tensor: 4 (over z).
Axes of the slice: x: 2, y: 2, z: 4, core: 2. Of those that a mesh axis runs over, the one named last changes fastest.
Arguments:
- inputs: bfloat16 [32, 729, 1152], P(('fsdp', 'heads', 'tensor')), may hold values from -6 to 6
- slot_mask: int32 [32], P(('fsdp', 'heads', 'tensor')), may hold values from 0 to 1, as said below
- ln1_gain: float32 [1152], replicated, may hold values from 0.5 to 1.5
- ln1_bias: float32 [1152], replicated, may hold values from -0.625 to 0.625
- qkv_weight: float32 [1152, 3, 1152], P(('fsdp', 'tensor'), None, 'heads'), may hold values from -0.1875 to 0.1875
- qv_bias: float32 [2, 1152], replicated, may hold values from -0.625 to 0.625
- out_weight: float32 [1152, 1152], P('heads', ('fsdp', 'tensor')), may hold values from -3 to 3
- out_bias: float32 [1152], replicated, may hold values from -1.25 to 1.25
- ln2_gain: float32 [1152], replicated, may hold values from 0.5 to 1.5
- ln2_bias: float32 [1152], replicated, may hold values from -0.625 to 0.625
- up_weight: float32 [1152, 4304], P(('fsdp', 'heads'), 'tensor'), may hold values from -0.1875 to 0.1875
- up_bias: float32 [4304], replicated, may hold values from -1.25 to 1.25
- down_weight: float32 [4304, 1152], P('tensor', ('fsdp', 'heads')), may hold values from -0.09375 to 0.09375
- down_bias: float32 [1152], replicated, may hold values from -1.25 to 1.25
- out_grad: bfloat16 [32, 729, 1152], P(('fsdp', 'heads', 'tensor')), may hold values from -12 to 12
Outputs:
- output: bfloat16 [32, 729, 1152], P(('fsdp', 'heads', 'tensor'))
- input_grad: float32 [32, 729, 1152], P(('fsdp', 'heads', 'tensor'))
- ln1_gain_grad: float32 [1152], replicated
- ln1_bias_grad: float32 [1152], replicated
- qkv_weight_grad: float32 [1152, 3, 1152], P(('fsdp', 'tensor'), None, 'heads')
- qv_bias_grad: float32 [2, 1152], replicated
- out_weight_grad: float32 [1152, 1152], P('heads', ('fsdp', 'tensor'))
- out_bias_grad: float32 [1152], replicated
- ln2_gain_grad: float32 [1152], replicated
- ln2_bias_grad: float32 [1152], replicated
- up_weight_grad: float32 [1152, 4304], P(('fsdp', 'heads'), 'tensor')
- up_bias_grad: float32 [4304], replicated
- down_weight_grad: float32 [4304, 1152], P('tensor', ('fsdp', 'heads'))
- down_bias_grad: float32 [1152], replicated
Inputs may be any that keep to these rules, and one draw needn't show every extreme that they name: slot_mask is 0 or 1; the 16 slots of some index of fsdp are all 1.
All inputs are finite; a program needn't handle non-finite values.
Results may differ from a plain program's by a relative error of at most 0.014.
Values may be sent and summed in bfloat16 or wider, within the bound.
No kernel may reach another device: no remote copies, remote signals or barrier semaphores. Data moves between devices by JAX's collectives and lax.ppermute only.
A program may use at most 256 MiB of HBM per device.

v0:
```python
import jax
import jax.numpy as jnp
from jax import lax
from jax.sharding import PartitionSpec as P

HEAD_DIM = 72


epsilon = 1e-06


def layer_norm(values, scaling, offset):
    center = values - jnp.mean(values, axis=-1, keepdims=True)
    spread = jnp.mean(center * center, axis=-1, keepdims=True)
    return center * lax.rsqrt(spread + epsilon) * scaling + offset


def gelu_tanh(values):
    return jax.nn.gelu(values, approximate=True)


def attend_image(query_rows, key_rows, value_rows, score_scale):
    scores = (
        jnp.einsum("shd,thd->hst", query_rows, key_rows, preferred_element_type=jnp.float32)
        * score_scale
    )
    row_top = jnp.max(scores, axis=-1, keepdims=True)
    weights = jnp.exp(scores - row_top)
    weight_total = jnp.sum(weights, axis=-1, keepdims=True)
    probabilities = (weights / weight_total).astype(jnp.bfloat16)
    mixed_rows = jnp.einsum(
        "hst,thd->shd", probabilities, value_rows, preferred_element_type=jnp.float32
    )
    return (mixed_rows, (row_top + jnp.log(weight_total))[..., 0])


def attend_back(query_rows, key_rows, value_rows, logsums, grad_mixed, score_scale):
    scores = (
        jnp.einsum("shd,thd->hst", query_rows, key_rows, preferred_element_type=jnp.float32)
        * score_scale
    )
    probabilities = jnp.exp(scores - logsums[..., None])
    grad_probs = jnp.einsum(
        "shd,thd->hst", grad_mixed, value_rows, preferred_element_type=jnp.float32
    )
    grad_values = jnp.einsum(
        "hst,shd->thd",
        probabilities.astype(jnp.bfloat16),
        grad_mixed,
        preferred_element_type=jnp.float32,
    )
    inner_sum = jnp.sum(probabilities * grad_probs, axis=-1, keepdims=True)
    grad_scores = (probabilities * (grad_probs - inner_sum)).astype(jnp.bfloat16)
    grad_queries = (
        jnp.einsum("hst,thd->shd", grad_scores, key_rows, preferred_element_type=jnp.float32)
        * score_scale
    )
    grad_keys = (
        jnp.einsum("hst,shd->thd", grad_scores, query_rows, preferred_element_type=jnp.float32)
        * score_scale
    )
    return jnp.stack([grad_queries, grad_keys, grad_values], axis=1).astype(jnp.bfloat16)


def attention_forward(normed, qkv_rows, qkv_shift, out_cols, score_scale):
    image_total, length = (normed.shape[0], normed.shape[1])
    projected = (
        jnp.einsum("bsd,dch->bsch", normed, qkv_rows, preferred_element_type=jnp.float32)
        + qkv_shift
    )
    projected = projected.astype(jnp.bfloat16)
    split_rows = projected.reshape(image_total, length, 3, -1, HEAD_DIM)

    def one_image(element):
        return attend_image(element[:, 0], element[:, 1], element[:, 2], score_scale)

    mixed_rows, logsums = lax.map(one_image, split_rows)
    mixed_low = mixed_rows.reshape(image_total, length, -1).astype(jnp.bfloat16)
    partial_value = jnp.einsum(
        "bsh,hd->bsd", mixed_low, out_cols, preferred_element_type=jnp.float32
    )
    return (projected, mixed_low, logsums, partial_value)


def attention_backward(
    normed, projected, mixed_low, logsums, grad_low, qkv_rows, out_cols, score_scale
):
    image_total, length = (normed.shape[0], normed.shape[1])
    grad_mixed = jnp.einsum(
        "bsd,hd->bsh", grad_low, out_cols, preferred_element_type=jnp.float32
    ).astype(jnp.bfloat16)
    cols_grad = jnp.einsum("bsh,bsd->hd", mixed_low, grad_low, preferred_element_type=jnp.float32)
    split_rows = projected.reshape(image_total, length, 3, -1, HEAD_DIM)
    grad_split = grad_mixed.reshape(image_total, length, -1, HEAD_DIM)

    def one_image(element):
        pieces, gradients, image_sums = element
        return attend_back(
            pieces[:, 0], pieces[:, 1], pieces[:, 2], image_sums, gradients, score_scale
        )

    grad_proj = lax.map(one_image, (split_rows, grad_split, logsums)).reshape(
        image_total, length, 3, -1
    )
    rows_grad = jnp.einsum("bsd,bsch->dch", normed, grad_proj, preferred_element_type=jnp.float32)
    shift_grads = jnp.sum(grad_proj, axis=(0, 1), dtype=jnp.float32)
    grad_normed = jnp.einsum(
        "bsch,dch->bsd", grad_proj, qkv_rows, preferred_element_type=jnp.float32
    )
    return (rows_grad, cols_grad, shift_grads, grad_normed)


def mlp_forward(normed, up_matrix, up_shift, down_matrix):
    upper_pre = (
        jnp.einsum("bsd,df->bsf", normed, up_matrix, preferred_element_type=jnp.float32) + up_shift
    )
    active_low = gelu_tanh(upper_pre).astype(jnp.bfloat16)
    partial_value = jnp.einsum(
        "bsf,fd->bsd", active_low, down_matrix, preferred_element_type=jnp.float32
    )
    return (upper_pre, active_low, partial_value)


def mlp_backward(normed, upper_pre, active_low, grad_low, up_matrix, down_matrix):
    down_grad = jnp.einsum("bsf,bsd->fd", active_low, grad_low, preferred_element_type=jnp.float32)
    grad_active = jnp.einsum(
        "bsd,fd->bsf", grad_low, down_matrix, preferred_element_type=jnp.float32
    )
    grad_upper = jax.vjp(gelu_tanh, upper_pre)[1](grad_active)[0].astype(jnp.bfloat16)
    up_grad = jnp.einsum("bsd,bsf->df", normed, grad_upper, preferred_element_type=jnp.float32)
    shift_grad = jnp.sum(grad_upper, axis=(0, 1), dtype=jnp.float32)
    grad_normed = jnp.einsum(
        "bsf,df->bsd", grad_upper, up_matrix, preferred_element_type=jnp.float32
    )
    return (up_grad, down_grad, shift_grad, grad_normed)


def on_device(
    inputs,
    slot_mask,
    ln1_gain,
    ln1_bias,
    qkv_weight,
    qv_bias,
    out_weight,
    out_bias,
    ln2_gain,
    ln2_bias,
    up_weight,
    up_bias,
    down_weight,
    down_bias,
    out_grad,
):
    score_scale = HEAD_DIM ** (-0.5)
    valid_slot = slot_mask[0].astype(jnp.float32)
    residual = inputs.astype(jnp.float32)
    qkv_rows, out_cols = (
        lax.all_gather(qkv_weight.astype(jnp.bfloat16), ("fsdp", "tensor"), axis=0, tiled=True),
        lax.all_gather(out_weight.astype(jnp.bfloat16), ("fsdp", "tensor"), axis=1, tiled=True),
    )
    up_rows, down_cols = (
        lax.all_gather(up_weight.astype(jnp.bfloat16), ("fsdp", "heads"), axis=0, tiled=True),
        lax.all_gather(down_weight.astype(jnp.bfloat16), ("fsdp", "heads"), axis=1, tiled=True),
    )
    head_width = qkv_rows.shape[2]
    head_start = lax.axis_index("heads") * head_width
    bias_cols = lax.dynamic_slice_in_dim(qv_bias, head_start, head_width, 1)
    qkv_shift = jnp.stack([bias_cols[0], jnp.zeros_like(bias_cols[0]), bias_cols[1]])
    normed_one, ln_one_back = jax.vjp(layer_norm, residual, ln1_gain, ln1_bias)
    normed_low = normed_one.astype(jnp.bfloat16)
    head_inputs = lax.all_gather(normed_low, "heads", axis=0, tiled=True)
    projected, mixed_low, logsums, attn_partial = attention_forward(
        head_inputs, qkv_rows, qkv_shift, out_cols, score_scale
    )
    attn_sum = lax.psum_scatter(attn_partial, "heads", scatter_dimension=0, tiled=True)
    hidden = residual + (attn_sum + out_bias)
    normed_two, ln_two_back = jax.vjp(layer_norm, hidden, ln2_gain, ln2_bias)
    normed_two_low = normed_two.astype(jnp.bfloat16)
    direct_grad = valid_slot * out_grad.astype(jnp.float32)
    branch_grad = direct_grad.astype(jnp.bfloat16)
    unit_width = up_rows.shape[1]
    unit_start = lax.axis_index("tensor") * unit_width
    mlp_inputs, mlp_grad_in = (
        lax.all_gather(normed_two_low, "tensor", axis=0, tiled=True),
        lax.all_gather(branch_grad, "tensor", axis=0, tiled=True),
    )
    up_matrix, down_matrix = (up_rows, down_cols)
    up_shift = lax.dynamic_slice_in_dim(up_bias, unit_start, unit_width)
    upper_pre, active_low, mlp_partial = mlp_forward(mlp_inputs, up_matrix, up_shift, down_matrix)
    mlp_sum = lax.psum_scatter(
        mlp_partial.astype(jnp.bfloat16), "tensor", scatter_dimension=0, tiled=True
    ).astype(jnp.float32)
    output = (valid_slot * (hidden + (mlp_sum + down_bias))).astype(jnp.bfloat16)
    up_grad, down_grad, shift_grad, grad_normed_part = mlp_backward(
        mlp_inputs, upper_pre, active_low, mlp_grad_in, up_matrix, down_matrix
    )
    grad_normed_two = lax.psum_scatter(grad_normed_part, "tensor", scatter_dimension=0, tiled=True)
    up_part, down_part = (up_grad, down_grad)
    up_bias_grad = lax.dynamic_update_slice_in_dim(
        jnp.zeros_like(up_bias), shift_grad, unit_start, 0
    )
    up_weight_grad, down_weight_grad = (
        lax.psum_scatter(
            up_part.astype(jnp.bfloat16), ("fsdp", "heads"), scatter_dimension=0, tiled=True
        ).astype(jnp.float32),
        lax.psum_scatter(
            down_part.astype(jnp.bfloat16), ("fsdp", "heads"), scatter_dimension=1, tiled=True
        ).astype(jnp.float32),
    )
    hidden_back, ln2_gain_grad, ln2_bias_grad = ln_two_back(grad_normed_two)
    grad_hidden = direct_grad + hidden_back
    grad_attn_low = grad_hidden.astype(jnp.bfloat16)
    head_gradients = lax.all_gather(grad_attn_low, "heads", axis=0, tiled=True)
    rows_grad, cols_grad, shift_grads, grad_normed_heads = attention_backward(
        head_inputs, projected, mixed_low, logsums, head_gradients, qkv_rows, out_cols, score_scale
    )
    grad_normed_one = lax.psum_scatter(
        grad_normed_heads.astype(jnp.bfloat16), "heads", scatter_dimension=0, tiled=True
    ).astype(jnp.float32)
    input_back, ln1_gain_grad, ln1_bias_grad = ln_one_back(grad_normed_one)
    input_grad = grad_hidden + input_back
    qkv_weight_grad, out_weight_grad = (
        lax.psum_scatter(rows_grad, ("fsdp", "tensor"), scatter_dimension=0, tiled=True),
        lax.psum_scatter(cols_grad, ("fsdp", "tensor"), scatter_dimension=1, tiled=True),
    )
    bias_piece = jnp.stack([shift_grads[0], shift_grads[2]])
    bias_full = lax.dynamic_update_slice_in_dim(jnp.zeros_like(qv_bias), bias_piece, head_start, 1)
    out_bias_grad = jnp.sum(grad_attn_low, axis=(0, 1), dtype=jnp.float32)
    down_bias_grad = jnp.sum(branch_grad, axis=(0, 1), dtype=jnp.float32)
    vector_sums = lax.psum(
        (
            ln1_gain_grad,
            ln1_bias_grad,
            bias_full,
            out_bias_grad,
            ln2_gain_grad,
            ln2_bias_grad,
            up_bias_grad,
            down_bias_grad,
        ),
        ("fsdp", "heads", "tensor"),
    )
    return (
        output,
        input_grad,
        vector_sums[0],
        vector_sums[1],
        qkv_weight_grad,
        vector_sums[2],
        out_weight_grad,
        vector_sums[3],
        vector_sums[4],
        vector_sums[5],
        up_weight_grad,
        vector_sums[6],
        down_weight_grad,
        vector_sums[7],
    )


def solution(mesh):
    in_specs = (
        P(("fsdp", "heads", "tensor"), None, None),
        P(("fsdp", "heads", "tensor")),
        P(),
        P(),
        P(("fsdp", "tensor"), None, "heads"),
        P(),
        P("heads", ("fsdp", "tensor")),
        P(),
        P(),
        P(),
        P(("fsdp", "heads"), "tensor"),
        P(),
        P("tensor", ("fsdp", "heads")),
        P(),
        P(("fsdp", "heads", "tensor"), None, None),
    )
    out_specs = (
        P(("fsdp", "heads", "tensor"), None, None),
        P(("fsdp", "heads", "tensor"), None, None),
        P(),
        P(),
        P(("fsdp", "tensor"), None, "heads"),
        P(),
        P("heads", ("fsdp", "tensor")),
        P(),
        P(),
        P(),
        P(("fsdp", "heads"), "tensor"),
        P(),
        P("tensor", ("fsdp", "heads")),
        P(),
    )
    return jax.shard_map(
        on_device, mesh=mesh, in_specs=in_specs, out_specs=out_specs, check_vma=False
    )
```

profile of v0, /device:TPU:0, one launch (start us, length us, event | category | flops | bytes accessed | tf_op | source)
XLA Modules:
  0.0 1399.6 jit_solution(17066862210791716632)
XLA Ops:
  8.1 2.0 convert_element_type.115
  12.6 1.9 fusion.53
  15.6 41.7 %all_gather.26 = bf16[288,1152]{0,1:T(8,128)(2,1)S(1)} all-gather(bf16[288,144]{0,1:T(8,128)(2,1)S(1)} %convert_element_type.119), channel_id=1, replica_groups=mesh['fsdp'=2,'heads'=4,'tensor'=4] {'fsdp','tensor'}, dimensions={1}, use_global_device_ids=true | all-gather | bytes 746496 | tf_op jit(solution)/shard_map/all_gather | solution.py:160
  57.3 21.4 %all-gather.10.cloned.1.call-done = bf16[1152,3,288]{2,0,1:T(8,128)(2,1)} async-done(((bf16[144,3,288]{2,0,1:T(8,128)(2,1)}), bf16[1152,3,288]{2,0,1:T(8,128)(2,1)}) %all-gather.10.cloned.1.call-update) | async-done | bytes 1990672 | tf_op jit(solution)/shard_map/all_gather | solution.py:159
  78.7 50.4 %all-gather.8.cloned.1.call-done = bf16[4,729,1152]{2,1,0:T(8,128)(2,1)} async-done(((bf16[1,729,1152]{2,1,0:T(8,128)(2,1)}), bf16[4,729,1152]{2,1,0:T(8,128)(2,1)}) %all-gather.8.cloned.1.call-update) | async-done | bytes 6718480 | tf_op jit(solution)/shard_map/all_gather | solution.py:172
  129.2 11.7 add_convert_fusion
  140.8 31.1 %while.22 = (s32[]{:T(128)}, bf16[4,729,4,72]{1,3,2,0:T(8,128)(2,1)}, f32[4,4,729]{2,1,0:T(4,128)S(1)}, bf16[4,729,3,4,72]{1,4,3,2,0:T(8,128)(2,1)}, s32[]{:T(128)}) while((s32[]{:T(128)}, bf16[4,729,4,72]{1,3,2,0:T(8,128)(2,1)}, f32[4,4,729]{2,1,0:T(4,128)S(1)}, bf16[4,729,3,4,72]{1,4,3,2,0:T(8,128)(2,1)}, s32[]{:T(128)}) %tuple.92), condition=%wide.region_5.6_spmd, body=%wide.region_2.5_spmd.sunk | while | flops 631348992 | bytes 44314840 | solution.py:77
  145.2 2.2 fusion.107
  153.0 2.2 fusion.107
  160.8 2.2 fusion.107
  168.5 2.2 fusion.107
  171.9 10.3 fusion.71
  184.2 104.0 %reduce-scatter.9.cloned.1.call-done = f32[1,729,1152]{2,1,0:T(8,128)} async-done(((f32[4,729,1152]{2,1,0:T(8,128)}), f32[1,729,1152]{2,1,0:T(8,128)}) %reduce-scatter.9.cloned.1.call-update) | async-done | bytes 3359248 | tf_op jit(solution)/shard_map/reduce_scatter | solution.py:176
  288.2 3.0 fusion.78
  291.9 1.8 add_convert_fusion.1
  293.8 1.9 convert_element_type.123
  296.3 3.6 convert_reduce_fusion.4
  300.8 116.2 %all-gather.12.cloned.1.call-done = bf16[4,729,1152]{2,1,0:T(8,128)(2,1)} async-done(((bf16[1,729,1152]{2,1,0:T(8,128)(2,1)}), bf16[4,729,1152]{2,1,0:T(8,128)(2,1)}) %all-gather.12.cloned.1.call-update) | async-done | bytes 6718480 | tf_op jit(solution)/shard_map/all_gather | solution.py:185
  417.0 19.0 %multiply_convert_fusion.1 = (bf16[4,729,1076]{1,2,0:T(8,128)(2,1)}, f32[4,729,1076]{1,2,0:T(8,128)}) fusion(f32[1076]{0:T(1024)S(1)} %dynamic_slice.22, bf16[4,729,1152]{2,1,0:T(8,128)(2,1)} %all-gather.12.cloned.1.call-done, bf16[1152,1076]{1,0:T(8,128)(2,1)} %all-gather.14.cloned.1.call-done), kind=kOutput, calls=%fused_computation.55 | convolution fusion | flops 7260442624 | bytes 28027568 | tf_op jit(solution)/shard_map/bsd,df->bsf/dot_general | solution.py:115
  436.1 11.6 all-gather.16.cloned.1.call-done
  447.7 125.4 %all-gather.18.cloned.1.call-done = bf16[4,729,1152]{2,1,0:T(8,128)(2,1)} async-done(((bf16[1,729,1152]{2,1,0:T(8,128)(2,1)}), bf16[4,729,1152]{2,1,0:T(8,128)(2,1)}) %all-gather.18.cloned.1.call-update) | async-done | bytes 6718480 | tf_op jit(solution)/shard_map/all_gather | solution.py:186
  573.1 25.4 %convert_reduce_fusion = (f32[1076]{0:T(1024)}, bf16[4,729,1076]{1,2,0:T(8,128)(2,1)}) fusion(f32[4,729,1076]{1,2,0:T(8,128)} %get-tuple-element.146, f32[1076]{0:T(1024)S(1)} %dynamic_slice.22, bf16[4,729,1152]{2,1,0:T(8,128)(2,1)} %all-gather.18.cloned.1.call-done, bf16[1076,1152]{0,1:T(8,128)(2,1)} %all-gather.16.cloned.1.call-done), kind=kOutput, calls=%fused_computation.54 | convolution fusion | flops 7301229568 | bytes 28031872 | tf_op jit(solution)/shard_map/bsd,fd->bsf/dot_general | solution.py:126
  598.5 15.3 %fusion.62 = f32[4,729,1152]{2,1,0:T(8,128)} fusion(bf16[4,729,1076]{1,2,0:T(8,128)(2,1)} %get-tuple-element.148, bf16[1152,1076]{1,0:T(8,128)(2,1)S(1)} %copy-done.37), kind=kOutput, calls=%fused_computation.101 | convolution fusion | flops 7229067264 | bytes 22191264 | tf_op jit(solution)/shard_map/bsf,df->bsd/dot_general | solution.py:132
  613.9 14.8 %convolution_convert_fusion = bf16[4,729,1152]{2,1,0:T(8,128)(2,1)} fusion(bf16[4,729,1076]{1,2,0:T(8,128)(2,1)} %get-tuple-element.145, bf16[1076,1152]{0,1:T(8,128)(2,1)} %all-gather.16.cloned.1.call-done), kind=kOutput, calls=%fused_computation.66 | convolution fusion | flops 7232426496 | bytes 15472800 | tf_op jit(solution)/shard_map/bsf,fd->bsd/dot_general | solution.py:118
  628.8 211.0 %reduce-scatter.13.cloned.1.call-done = f32[1,729,1152]{2,1,0:T(8,128)} async-done(((f32[4,729,1152]{2,1,0:T(8,128)}), f32[1,729,1152]{2,1,0:T(8,128)}) %reduce-scatter.13.cloned.1.call-update) | async-done | bytes 3359248 | tf_op jit(solution)/shard_map/reduce_scatter | solution.py:198
  839.8 3.7 multiply_reduce_fusion.2
  843.5 118.5 %reduce-scatter.11.cloned.1.call-done = bf16[1,729,1152]{2,1,0:T(8,128)(2,1)} async-done(((bf16[4,729,1152]{2,1,0:T(8,128)(2,1)}), bf16[1,729,1152]{2,1,0:T(8,128)(2,1)}) %reduce-scatter.11.cloned.1.call-update) | async-done | bytes 1679632 | tf_op jit(solution)/shard_map/reduce_scatter | solution.py:191
  962.0 5.0 fusion.77
  967.0 2.8 convert_reduce_fusion.5
  969.9 14.4 %fusion.38 = bf16[1076,1152]{0,1:T(8,128)(2,1)} fusion(bf16[4,729,1076]{1,2,0:T(8,128)(2,1)} %get-tuple-element.145, bf16[4,729,1152]{2,1,0:T(8,128)(2,1)} %all-gather.18.cloned.1.call-done), kind=kOutput, calls=%fused_computation.61 | convolution fusion | flops 7230306816 | bytes 15472800 | tf_op jit(solution)/shard_map/bsf,bsd->fd/dot_general | solution.py:125
  984.4 14.6 %fusion.37 = bf16[1152,1076]{1,0:T(8,128)(2,1)} fusion(bf16[4,729,1152]{2,1,0:T(8,128)(2,1)} %all-gather.12.cloned.1.call-done, bf16[4,729,1076]{1,2,0:T(8,128)(2,1)} %get-tuple-element.148), kind=kOutput, calls=%fused_computation.60 | convolution fusion | flops 7230306816 | bytes 15472800 | tf_op jit(solution)/shard_map/bsd,bsf->df/dot_general | solution.py:130
  999.0 20.9 %all-gather.20.cloned.1.call-done = bf16[4,729,1152]{2,1,0:T(8,128)(2,1)} async-done(((bf16[1,729,1152]{2,1,0:T(8,128)(2,1)}), bf16[4,729,1152]{2,1,0:T(8,128)(2,1)}) %all-gather.20.cloned.1.call-update) | async-done | bytes 6718480 | tf_op jit(solution)/shard_map/all_gather | solution.py:214
  1019.9 6.8 convolution_convert_fusion.1
  1026.7 111.1 %while.23 = (s32[]{:T(128)}, bf16[4,729,3,4,72]{1,4,3,2,0:T(8,128)(2,1)}, bf16[4,729,3,4,72]{1,4,3,2,0:T(8,128)(2,1)}, f32[4,4,729]{2,1,0:T(4,128)S(1)}, bf16[4,729,4,72]{1,3,2,0:T(8,128)(2,1)}, /*index=5*/s32[]{:T(128)}) while((s32[]{:T(128)}, bf16[4,729,3,4,72]{1,4,3,2,0:T(8,128)(2,1)}, bf16[4,729,3,4,72]{1,4,3,2,0:T(8,128)(2,1)}, ...), condition=%wide.region_15.16_spmd, body=%wide.region_13.15_spmd.sunk | while | flops 1560885248 | bytes 132407608 | solution.py:102
  1031.4 1.8 copy-done
  1033.3 4.7 multiply_reduce_fusion.8
  1038.0 10.2 multiply_convert_fusion.4
  1048.2 3.6 fusion.115
  1059.5 1.8 copy-done
  1061.4 4.7 multiply_reduce_fusion.8
  1066.1 10.2 multiply_convert_fusion.4
  1076.3 3.3 fusion.115
  1087.3 1.8 copy-done
  1089.2 4.7 multiply_reduce_fusion.8
  1093.8 10.2 multiply_convert_fusion.4
  1104.0 3.3 fusion.115
  1114.8 1.8 copy-done
  1116.7 4.7 multiply_reduce_fusion.8
  1121.3 10.2 multiply_convert_fusion.4
  1131.5 3.3 fusion.115
  1137.8 14.6 %bitcast_convert_fusion = bf16[4,729,1152]{2,1,0:T(8,128)(2,1)} fusion(bf16[4,729,3,288]{1,3,2,0:T(8,128)(2,1)} %bitcast.178, bf16[1152,3,288]{2,0,1:T(8,128)(2,1)} %all-gather.10.cloned.1.call-done), kind=kOutput, calls=%fused_computation.46 | convolution fusion | flops 5808112128 | bytes 13747968 | tf_op jit(solution)/shard_map/bsch,dch->bsd/dot_general | solution.py:107
  1153.9 7.4 convolution_bitcast_fusion.2
  1161.4 15.7 %fusion.47 = f32[1152,3,288]{2,0,1:T(8,128)} fusion(bf16[4,729,3,288]{1,3,2,0:T(8,128)(2,1)} %bitcast.179, bf16[4,729,1152]{2,1,0:T(8,128)(2,1)} %all-gather.8.cloned.1.call-done), kind=kOutput, calls=%fused_computation.79 | convolution fusion | flops 5804752896 | bytes 15738624 | tf_op jit(solution)/shard_map/bsd,bsch->dch/dot_general | solution.py:105
  1177.9 1.9 convert_element_type.140
  1179.8 2.0 convert_element_type.137
  1181.8 3.4 convert_reduce_fusion.1
  1185.6 28.5 %reduce-scatter.15.cloned.1.call-done = bf16[1,729,1152]{2,1,0:T(8,128)(2,1)} async-done(((bf16[4,729,1152]{2,1,0:T(8,128)(2,1)}), bf16[1,729,1152]{2,1,0:T(8,128)(2,1)}) %reduce-scatter.15.cloned.1.call-update) | async-done | bytes 1679632 | tf_op jit(solution)/shard_map/reduce_scatter | solution.py:218
  1214.2 2.7 convert_reduce_fusion.2
  1216.9 3.3 fusion.56
  1220.2 1.9 add_add_fusion.2
  1222.1 5.2 copy.40
  1227.3 41.9 %all-reduce = (f32[1152]{0:T(1024)}, f32[1152]{0:T(1024)}, f32[2,1152]{1,0:T(2,128)}, f32[1152]{0:T(1024)}, f32[1152]{0:T(1024)}, /*index=5*/f32[1152]{0:T(1024)}, f32[4304]{0:T(1024)}, f32[1152]{0:T(1024)}) all-reduce(f32[1152]{0:T(1024)S(1)} %get-tuple-element.97, ...), channel_id=1, replica_groups=mesh['fsdp'=2,'heads'=4,'tensor'=4] {'fsdp','heads','tensor'}, use_global_device_ids=true, to_apply=%region_20.21 | all-reduce | flops 13520 | bytes 108160 | tf_op jit(solution)/shard_map/psum | solution.py:231
  1269.2 15.7 %reduce-scatter.19.cloned.1.call-done = f32[288,144]{0,1:T(8,128)} async-done(((f32[288,1152]{0,1:T(8,128)}), f32[288,144]{0,1:T(8,128)}) %reduce-scatter.19.cloned.1.call-update) | async-done | bytes 165904 | tf_op jit(solution)/shard_map/reduce_scatter | solution.py:225
  1284.9 107.0 %reduce-scatter.17.cloned.1.call-done = f32[144,3,288]{2,0,1:T(8,128)} async-done(((f32[1152,3,288]{2,0,1:T(8,128)}), f32[144,3,288]{2,0,1:T(8,128)}) %reduce-scatter.17.cloned.1.call-update) | async-done | bytes 497680 | tf_op jit(solution)/shard_map/reduce_scatter | solution.py:224
  (203 shorter events, 63.0 us)
Async XLA Ops:
  8.0 3.9 copy-start.2
  8.0 4.5 copy-start.19
  8.0 4.5 copy-start.32
  8.0 70.7 %all-gather.10.cloned.1.call-start = ((), (), s32[]{:S(2)}) async-start(), calls=%async_computation.9 | async-start | bytes 2985984 | tf_op jit(solution)/shard_map/all_gather | solution.py:159
  10.1 119.1 %all-gather.8.cloned.1.call-start = ((), (), s32[]{:S(2)}) async-start(), calls=%async_computation.8 | async-start | bytes 8478720 | tf_op jit(solution)/shard_map/all_gather | solution.py:172
  11.9 2.6 copy-start.17
  11.9 2.6 copy-start.16
  12.5 3.0 copy-start.26
  12.6 2.9 copy-start.22
  14.5 273.7 %reduce-scatter.9.cloned.1.call-start = ((), (), s32[]{:S(2)}) async-start(), calls=%async_computation.10 | async-start | bytes 16957440 | tf_op jit(solution)/shard_map/reduce_scatter | solution.py:176
  57.3 114.6 %copy-start.10 = (bf16[288,1152]{0,1:T(8,128)(2,1)}, bf16[288,1152]{0,1:T(8,128)(2,1)S(1)}, u32[]{:S(2)}) copy-start(bf16[288,1152]{0,1:T(8,128)(2,1)S(1)} %all_gather.26) | copy-start | bytes 1990660
  143.6 1.6 copy-start.12
  147.4 1.2 copy-start.13
  151.4 1.6 copy-start.12
  155.2 1.2 copy-start.13
  159.2 1.6 copy-start.12
  162.9 1.2 copy-start.13
  167.0 1.6 copy-start.12
  170.7 1.2 copy-start.13
  182.3 105.9 %copy-start.35 = (f32[1152]{0:T(1024)S(1)}, f32[1152]{0:T(1024)}, u32[]{:S(2)}) copy-start(f32[1152]{0:T(1024)} %param.26) | copy-start | bytes 13828
  182.3 118.6 %all-gather.14.cloned.1.call-start = ((), (), s32[]{:S(2)}) async-start(), calls=%async_computation.12 | async-start | bytes 2985984 | tf_op jit(solution)/shard_map/all_gather | solution.py:163
  184.1 232.9 %all-gather.12.cloned.1.call-start = ((), (), s32[]{:S(2)}) async-start(), calls=%async_computation.11 | async-start | bytes 8478720 | tf_op jit(solution)/shard_map/all_gather | solution.py:185
  293.7 154.0 %all-gather.16.cloned.1.call-start = ((), (), s32[]{:S(2)}) async-start(), calls=%async_computation.13 | async-start | bytes 2985984 | tf_op jit(solution)/shard_map/all_gather | solution.py:164
  295.6 277.5 %all-gather.18.cloned.1.call-start = ((), (), s32[]{:S(2)}) async-start(), calls=%async_computation.15 | async-start | bytes 8478720 | tf_op jit(solution)/shard_map/all_gather | solution.py:186
  300.0 539.8 %reduce-scatter.13.cloned.1.call-start = ((), (), s32[]{:S(2)}) async-start(), calls=%async_computation.16 | async-start | bytes 16957440 | tf_op jit(solution)/shard_map/reduce_scatter | solution.py:198
  573.1 25.4 %copy-start.37 = (bf16[1152,1076]{1,0:T(8,128)(2,1)S(1)}, bf16[1152,1076]{1,0:T(8,128)(2,1)}, u32[]{:S(2)}) copy-start(bf16[1152,1076]{1,0:T(8,128)(2,1)} %all-gather.14.cloned.1.call-done) | copy-start | bytes 7437316
  613.9 348.1 %reduce-scatter.11.cloned.1.call-start = ((), (), s32[]{:S(2)}) async-start(), calls=%async_computation.14 | async-start | bytes 8478720 | tf_op jit(solution)/shard_map/reduce_scatter | solution.py:191
  628.8 333.2 %copy-start.36 = (f32[1152]{0:T(1024)S(1)}, f32[1152]{0:T(1024)}, u32[]{:S(2)}) copy-start(f32[1152]{0:T(1024)} %param.32) | copy-start | bytes 13828
  628.8 391.1 %all-gather.20.cloned.1.call-start = ((), (), s32[]{:S(2)}) async-start(), calls=%async_computation.17 | async-start | bytes 8478720 | tf_op jit(solution)/shard_map/all_gather | solution.py:214
  962.0 5.0 copy-start.6
  967.0 2.8 copy-start.4
  967.0 2.8 copy-start.24
  969.9 208.1 %reduce-scatter.23.cloned.1.call-start = ((), (), s32[]{:S(2)}) async-start(), calls=%async_computation.22 | async-start | bytes 2985984 | tf_op jit(solution)/shard_map/reduce_scatter | solution.py:207
  984.3 195.5 %reduce-scatter.21.cloned.1.call-start = ((), (), s32[]{:S(2)}) async-start(), calls=%async_computation.21 | async-start | bytes 2985984 | tf_op jit(solution)/shard_map/reduce_scatter | solution.py:204
  984.4 35.5 %copy-start.11 = (bf16[288,1152]{0,1:T(8,128)(2,1)S(1)}, bf16[288,1152]{0,1:T(8,128)(2,1)}, u32[]{:S(2)}) copy-start(bf16[288,1152]{0,1:T(8,128)(2,1)} %copy-done.10) | copy-start | bytes 1990660
  999.0 215.2 %reduce-scatter.15.cloned.1.call-start = ((), (), s32[]{:S(2)}) async-start(), calls=%async_computation.18 | async-start | bytes 8478720 | tf_op jit(solution)/shard_map/reduce_scatter | solution.py:218
  1028.3 1.5 copy-start.9
  1029.8 3.5 copy-start
  1048.2 4.1 copy-start.1
  1056.4 1.5 copy-start.9
  1057.8 3.5 copy-start
  1076.3 3.8 copy-start.1
  1084.2 1.5 copy-start.9
  1085.7 3.5 copy-start
  1104.0 3.6 copy-start.1
  1111.7 1.5 copy-start.9
  1113.2 3.5 copy-start
  1131.5 3.6 copy-start.1
  1152.5 1.5 copy-start.14
  1152.5 132.4 %reduce-scatter.19.cloned.1.call-start = ((), (), s32[]{:S(2)}) async-start(), calls=%async_computation.20 | async-start | bytes 1990656 | tf_op jit(solution)/shard_map/reduce_scatter | solution.py:225
  1161.3 230.6 %reduce-scatter.17.cloned.1.call-start = ((), (), s32[]{:S(2)}) async-start(), calls=%async_computation.19 | async-start | bytes 5971968 | tf_op jit(solution)/shard_map/reduce_scatter | solution.py:224
  1179.8 34.3 %copy-start.3 = (bf16[1,729,1152]{2,1,0:T(8,128)(2,1)S(1)}, bf16[1,729,1152]{2,1,0:T(8,128)(2,1)}, u32[]{:S(2)}) copy-start(bf16[1,729,1152]{2,1,0:T(8,128)(2,1)} %param.19) | copy-start | bytes 5038852
  1179.8 34.3 %copy-start.18 = (f32[729]{0:T(1024)S(1)}, f32[729]{0:T(1024)}, u32[]{:S(2)}) copy-start(f32[729]{0:T(1024)} %copy-done.17) | copy-start | bytes 8752
  1179.8 34.3 %copy-start.20 = (f32[1152]{0:T(1024)S(1)}, f32[1152]{0:T(1024)}, u32[]{:S(2)}) copy-start(f32[1152]{0:T(1024)} %param.21) | copy-start | bytes 13828
  1181.8 35.0 %copy-start.27 = (f32[729]{0:T(1024)S(1)}, f32[729]{0:T(1024)}, u32[]{:S(2)}) copy-start(f32[729]{0:T(1024)} %copy-done.26) | copy-start | bytes 8752
  1181.8 35.1 %copy-start.23 = (f32[729]{0:T(1024)S(1)}, f32[729]{0:T(1024)}, u32[]{:S(2)}) copy-start(f32[729]{0:T(1024)} %copy-done.22) | copy-start | bytes 8752
  1185.6 34.6 %copy-start.7 = (bf16[1,729,1152]{2,1,0:T(8,128)(2,1)S(1)}, bf16[1,729,1152]{2,1,0:T(8,128)(2,1)}, u32[]{:S(2)}) copy-start(bf16[1,729,1152]{2,1,0:T(8,128)(2,1)} %param.33) | copy-start | bytes 5038852
  1185.6 34.6 %copy-start.25 = (f32[729]{0:T(1024)S(1)}, f32[729]{0:T(1024)}, u32[]{:S(2)}) copy-start(f32[729]{0:T(1024)} %copy-done.24) | copy-start | bytes 8752
  1214.1 6.1 copy-start.5
  1214.2 6.1 copy-start.8
  1222.1 5.2 copy-start.28
  1222.1 5.2 copy-start.29
  1222.1 5.2 copy-start.30
  1222.1 5.2 copy-start.31
  (4 other events, 3.2 us)
Sparse Core Ops, SparseCore 0:
  11.7 67.0 all-gather.9
  80.9 48.2 all-gather.7
  182.4 105.7 reduce-scatter.8
  970.0 49.8 all-gather.19
Sparse Core Ops, SparseCore 1:
  185.2 30.2 all-gather.13
  293.8 123.2 all-gather.11
  419.4 28.3 all-gather.15
  449.9 123.2 all-gather.17
  614.0 225.8 reduce-scatter.12
  842.3 119.6 reduce-scatter.10
  984.4 54.0 reduce-scatter.22
  1042.7 43.6 reduce-scatter.20
  1152.6 61.5 reduce-scatter.14
  1218.6 66.2 reduce-scatter.18
  1288.9 102.9 reduce-scatter.16
where the time goes:
time: 1410 us; the launch traced here: 1400 us
  waiting for transfers between devices  931 us (66%)
  matrix products  234 us (17%)
  other arithmetic  96.3 us (7%)
  blocking collectives  83.6 us (6%)
  local copies, waits for them, and re-layouts  36.1 us (3%)
  between operations  17.1 us (1%)
    reduce_scatter x1, waiting for transfers between devices, on_device(): lax.psum_scatter(grad_normed_part, 'tensor', scatter_dimension=0, tiled=T...  211 us
    all_gather x1, waiting for transfers between devices, on_device(): lax.all_gather(branch_grad, 'tensor', axis=0, tiled=True)  125 us
    reduce_scatter x1, waiting for transfers between devices, on_device(): lax.psum_scatter(mlp_partial.astype(jnp.bfloat16), 'tensor', scatter_dime...  118 us
    all_gather x1, waiting for transfers between devices, on_device(): lax.all_gather(normed_two_low, 'tensor', axis=0, tiled=True)  116 us
    reduce_scatter x1, waiting for transfers between devices, on_device(): lax.psum_scatter(rows_grad, ('fsdp', 'tensor'), scatter_dimension=0, tile...  107 us
    reduce_scatter x1, waiting for transfers between devices, on_device(): lax.psum_scatter(attn_partial, 'heads', scatter_dimension=0, tiled=True)  104 us
    all_gather x1, waiting for transfers between devices, on_device(): head_inputs = lax.all_gather(normed_low, 'heads', axis=0, tiled=True)  50.4 us
    psum x1, blocking collectives, on_device(): lax.psum((ln1_gain_grad, ln1_bias_grad, bias_full, out_bias_grad, ln2_gai...  41.9 us
  transfers between devices with their start and end apart: 15, of which 12 were waited for; matrix products, arithmetic and copies ran while one was open for 18% of the time, Pallas kernels for 0%

commit v1 on v0

v1 whole, which is shorter than its diff:
```python
import functools
import math

import jax
import jax.numpy as jnp
from jax import lax
from jax.experimental import pallas as pl
from jax.experimental.pallas import tpu as pltpu
from jax.sharding import PartitionSpec as P

HEAD_DIM = 72
GROUP_HEADS = 4
PAD = 768
EPS = 1e-06
VMEM_BYTES = 60 * 1024 * 1024
BF16 = jnp.bfloat16
F32 = jnp.float32
LOG2E = math.log2(math.e)


def nn(a, b):
    return lax.dot_general(a, b, (((1,), (0,)), ((), ())), preferred_element_type=F32)


def nt(a, b):
    return lax.dot_general(a, b, (((1,), (1,)), ((), ())), preferred_element_type=F32)


def tn(a, b):
    return lax.dot_general(a, b, (((0,), (0,)), ((), ())), preferred_element_type=F32)


def params(**kw):
    return pltpu.CompilerParams(vmem_limit_bytes=VMEM_BYTES, **kw)


def cost(flops, bytes_):
    return pl.CostEstimate(flops=int(flops), bytes_accessed=int(bytes_), transcendentals=0)


def whole(shape):
    zeros = (0,) * len(shape)
    return pl.BlockSpec(shape, lambda *_: zeros)


class Plan:
    def __init__(self, entries, columns):
        self.entries = entries
        self.columns = columns

    def copies(self, slot, pieces, table, dst, sems):
        for number, (piece, src, rows, to, entry, column) in enumerate(self.entries):
            if to != slot:
                continue
            row = pl.multiple_of(table[entry], 16)
            yield pltpu.make_async_copy(
                pieces[piece].at[pl.ds(src, rows), :],
                dst.at[pl.ds(row, rows), pl.ds(column, self.columns)],
                sems.at[number],
            )


def attn_fwd_kernel(plan, pieces_total, has_acc, seq, groups, *refs):
    table, x, bias = refs[:3]
    pieces = refs[3 : 3 + pieces_total]
    rest = refs[3 + pieces_total :]
    if has_acc:
        acc_in, rest = rest[0], rest[1:]
    proj, mixed, lse, acc, w_out, w, mixed_t, sems, out_sems = rest
    g = pl.program_id(0)
    width = GROUP_HEADS * HEAD_DIM
    keys = -(-seq // 16) * 16
    low = seq // 8 * 8
    scale = HEAD_DIM**-0.5 * LOG2E

    @pl.when(g == 0)
    def _():
        for slot in range(groups):
            for c in plan.copies(slot, pieces, table, w.at[slot], sems):
                c.start()

    for slot in range(groups):

        @pl.when(g == slot)
        def _(slot=slot):
            for c in plan.copies(slot, pieces, table, w.at[slot], sems):
                c.wait()
            pltpu.make_async_copy(w.at[slot], w_out.at[slot], out_sems.at[slot]).start()

    proj[0] = (nn(x[...], w[g, :, 0 : 3 * width]) + bias[0]).astype(BF16)
    for h in range(GROUP_HEADS):
        q = proj[0, :, h * HEAD_DIM : (h + 1) * HEAD_DIM]
        k = proj[0, 0:keys, width + h * HEAD_DIM : width + (h + 1) * HEAD_DIM]
        v = proj[0, 0:keys, 2 * width + h * HEAD_DIM : 2 * width + (h + 1) * HEAD_DIM]
        for c in range(0, PAD, QCHUNK):
            s = nt(k, q[c : c + QCHUNK])
            tail_rows = lax.broadcasted_iota(jnp.int32, (keys - low, QCHUNK), 0)
            tail = jnp.where(tail_rows < seq - low, s[low:keys], -1e30)
            top = jnp.maximum(
                jnp.max(s[0:low], axis=0, keepdims=True), jnp.max(tail, axis=0, keepdims=True)
            )
            shift = top * scale
            p = jnp.exp2(jnp.concatenate([s[0:low], tail], axis=0) * scale - shift)
            total = jnp.sum(p, axis=0, keepdims=True)
            o = tn(v, p.astype(BF16)) / total
            mixed_t[h * HEAD_DIM : (h + 1) * HEAD_DIM, c : c + QCHUNK] = o
            lse[0, h : h + 1, c : c + QCHUNK] = shift + jnp.log2(total)
    mixed[0] = mixed_t[...].T.astype(BF16)
    part = nt(mixed[0], w[g, :, 3 * width : 4 * width])

    @pl.when(g == 0)
    def _():
        acc[...] = part + acc_in[...] if has_acc else part

    @pl.when(g > 0)
    def _():
        acc[...] += part

    @pl.when(g == groups - 1)
    def _():
        for slot in range(groups):
            pltpu.make_async_copy(w.at[slot], w_out.at[slot], out_sems.at[slot]).wait()


QCHUNK = 768


def attn_fwd(table, x, bias, pieces, plan, acc_in, seq, groups):
    d = x.shape[1]
    gw = plan.columns
    width = GROUP_HEADS * HEAD_DIM
    has_acc = acc_in is not None
    args = [table, x, bias, *pieces] + ([acc_in] if has_acc else [])
    return pl.pallas_call(
        functools.partial(attn_fwd_kernel, plan, len(pieces), has_acc, seq, groups),
        grid=(groups,),
        in_specs=[
            pl.BlockSpec(memory_space=pltpu.SMEM),
            whole((PAD, d)),
            pl.BlockSpec((1, 1, 3 * width), lambda g: (g, 0, 0)),
            *[pl.BlockSpec(memory_space=pl.ANY) for _ in pieces],
            *([whole((PAD, d))] if has_acc else []),
        ],
        out_specs=[
            pl.BlockSpec((1, PAD, 3 * width), lambda g: (g, 0, 0)),
            pl.BlockSpec((1, PAD, width), lambda g: (g, 0, 0)),
            pl.BlockSpec((1, 8, PAD), lambda g: (g, 0, 0)),
            whole((PAD, d)),
            pl.BlockSpec(memory_space=pl.ANY),
        ],
        out_shape=[
            jax.ShapeDtypeStruct((groups, PAD, 3 * width), BF16),
            jax.ShapeDtypeStruct((groups, PAD, width), BF16),
            jax.ShapeDtypeStruct((groups, 8, PAD), F32),
            jax.ShapeDtypeStruct((PAD, d), F32),
            jax.ShapeDtypeStruct((groups, d, gw), BF16),
        ],
        scratch_shapes=[
            pltpu.VMEM((groups, d, gw), BF16),
            pltpu.VMEM((width, PAD), F32),
            pltpu.SemaphoreType.DMA((len(plan.entries),)),
            pltpu.SemaphoreType.DMA((groups,)),
        ],
        compiler_params=params(),
        cost_estimate=cost(
            groups * 2 * PAD * (d * 4 * width + 8 * PAD * 256), groups * (d * gw * 4 + PAD * d * 4)
        ),
        name="attn_fwd",
    )(*args)


def attn_bwd_kernel(has_acc, seq, groups, *refs):
    proj, lse, ga, w = refs[:4]
    rest = refs[4:]
    if has_acc:
        acc_in, rest = rest[0], rest[1:]
    dproj, acc, sums, gm, dq_t = rest
    g = pl.program_id(0)
    width = GROUP_HEADS * HEAD_DIM
    keys = -(-seq // 16) * 16
    low = seq // 8 * 8
    factor = HEAD_DIM**-0.5
    scale = factor * LOG2E
    gm[...] = nn(ga[...], w[0, :, 3 * width : 4 * width]).astype(BF16)
    for h in range(GROUP_HEADS):
        sl = slice(h * HEAD_DIM, (h + 1) * HEAD_DIM)
        q = proj[0, :, h * HEAD_DIM : (h + 1) * HEAD_DIM]
        k = proj[0, 0:keys, width + h * HEAD_DIM : width + (h + 1) * HEAD_DIM]
        v = proj[0, 0:keys, 2 * width + h * HEAD_DIM : 2 * width + (h + 1) * HEAD_DIM]
        do = gm[:, sl]
        dk = jnp.zeros((keys, HEAD_DIM), F32)
        dv = jnp.zeros((keys, HEAD_DIM), F32)
        for c in range(0, PAD, QCHUNK):
            qc, doc = q[c : c + QCHUNK], do[c : c + QCHUNK]
            s = nt(k, qc)
            e = s * scale - lse[0, h : h + 1, c : c + QCHUNK]
            tail_rows = lax.broadcasted_iota(jnp.int32, (keys - low, QCHUNK), 0)
            tail = jnp.where(tail_rows < seq - low, e[low:keys], -1e30)
            p = jnp.exp2(jnp.concatenate([e[0:low], tail], axis=0))
            dp = nt(v, doc)
            delta = jnp.sum(p * dp, axis=0, keepdims=True)
            ds = (p * (dp - delta)).astype(BF16)
            dv += nn(p.astype(BF16), doc)
            dk += nn(ds, qc)
            dq_t[sl, c : c + QCHUNK] = tn(k, ds)
        dproj[0, 0:keys, width + h * HEAD_DIM : width + (h + 1) * HEAD_DIM] = (dk * factor).astype(BF16)
        dproj[0, 0:keys, 2 * width + h * HEAD_DIM : 2 * width + (h + 1) * HEAD_DIM] = dv.astype(BF16)
    dproj[0, keys:PAD, width : 3 * width] = jnp.zeros((PAD - keys, 2 * width), BF16)
    dproj[0, :, 0:width] = (dq_t[...] * factor).T.astype(BF16)
    sums[0] = jnp.sum(dproj[0].astype(F32), axis=0, keepdims=True)
    part = nt(dproj[0], w[0, :, 0 : 3 * width])

    @pl.when(g == 0)
    def _():
        acc[...] = part + acc_in[...] if has_acc else part

    @pl.when(g > 0)
    def _():
        acc[...] += part


def attn_bwd(proj, lse, ga, w, acc_in, seq):
    groups, _, gw = w.shape
    d = ga.shape[1]
    width = GROUP_HEADS * HEAD_DIM
    has_acc = acc_in is not None
    args = [proj, lse, ga, w] + ([acc_in] if has_acc else [])
    return pl.pallas_call(
        functools.partial(attn_bwd_kernel, has_acc, seq, groups),
        grid=(groups,),
        in_specs=[
            pl.BlockSpec((1, PAD, 3 * width), lambda g: (g, 0, 0)),
            pl.BlockSpec((1, 8, PAD), lambda g: (g, 0, 0)),
            whole((PAD, d)),
            pl.BlockSpec((1, d, gw), lambda g: (g, 0, 0)),
            *([whole((PAD, d))] if has_acc else []),
        ],
        out_specs=[
            pl.BlockSpec((1, PAD, 3 * width), lambda g: (g, 0, 0)),
            whole((PAD, d)),
            pl.BlockSpec((1, 1, 3 * width), lambda g: (g, 0, 0)),
        ],
        out_shape=[
            jax.ShapeDtypeStruct((groups, PAD, 3 * width), BF16),
            jax.ShapeDtypeStruct((PAD, d), F32),
            jax.ShapeDtypeStruct((groups, 1, 3 * width), F32),
        ],
        scratch_shapes=[pltpu.VMEM((PAD, width), BF16), pltpu.VMEM((width, PAD), F32)],
        compiler_params=params(),
        cost_estimate=cost(
            groups * 2 * PAD * (d * 4 * width + 20 * PAD * 256), groups * (d * gw * 2 + PAD * d * 4)
        ),
        name="attn_bwd",
    )(*args)


def tile_of(units):
    return next(t for t in (1024, 768, 512, 256, 128) if units % t == 0)


def first_need(tile, columns, slots):
    return [slot * columns // tile for slot in range(slots)]


def ff_up_kernel(plan, pieces_total, slots, tile, *refs):
    table, x, bias = refs[:3]
    pieces = refs[3 : 3 + pieces_total]
    active, slope, w_out, w, sems, out_sems = refs[3 + pieces_total :]
    n = pl.program_id(0)
    cols = plan.columns

    @pl.when(n == 0)
    def _():
        for slot in range(slots):
            for c in plan.copies(slot, pieces, table, w, sems):
                c.start()

    def out_copy(slot):
        part = pl.ds(slot * cols, cols)
        return pltpu.make_async_copy(w.at[:, part], w_out.at[:, part], out_sems.at[slot])

    for slot, step in enumerate(first_need(tile, cols, slots)):

        @pl.when(n == step)
        def _(slot=slot):
            for c in plan.copies(slot, pieces, table, w, sems):
                c.wait()
            out_copy(slot).start()

    u = nn(x[...], w[:, pl.ds(pl.multiple_of(n * tile, tile), tile)]) + bias[...]
    root = math.sqrt(2.0 / math.pi)
    square = u * u
    t = jnp.tanh(u * (root + (root * 0.044715) * square))
    half = 0.5 * (1.0 + t)
    active[...] = (u * half).astype(BF16)
    slope[...] = (
        half + (0.5 * u) * (1.0 - t * t) * (root + (3.0 * root * 0.044715) * square)
    ).astype(BF16)

    @pl.when(n == pl.num_programs(0) - 1)
    def _():
        for slot in range(slots):
            out_copy(slot).wait()


def ff_up(table, x, bias, pieces, plan, slots):
    d = x.shape[1]
    units = slots * plan.columns
    tile = tile_of(units)
    return pl.pallas_call(
        functools.partial(ff_up_kernel, plan, len(pieces), slots, tile),
        grid=(units // tile,),
        in_specs=[
            pl.BlockSpec(memory_space=pltpu.SMEM),
            whole((PAD, d)),
            pl.BlockSpec((1, tile), lambda n: (0, n)),
            *[pl.BlockSpec(memory_space=pl.ANY) for _ in pieces],
        ],
        out_specs=[
            pl.BlockSpec((PAD, tile), lambda n: (0, n)),
            pl.BlockSpec((PAD, tile), lambda n: (0, n)),
            pl.BlockSpec(memory_space=pl.ANY),
        ],
        out_shape=[
            jax.ShapeDtypeStruct((PAD, units), BF16),
            jax.ShapeDtypeStruct((PAD, units), BF16),
            jax.ShapeDtypeStruct((d, units), BF16),
        ],
        scratch_shapes=[
            pltpu.VMEM((d, units), BF16),
            pltpu.SemaphoreType.DMA((len(plan.entries),)),
            pltpu.SemaphoreType.DMA((slots,)),
        ],
        compiler_params=params(),
        cost_estimate=cost(2 * PAD * d * units, 4 * d * units + 4 * PAD * units),
        name="ff_up",
    )(table, x, bias, *pieces)


def ff_down_kernel(plan, pieces_total, slots, tile, *refs):
    table, gl, active, slope = refs[:4]
    pieces = refs[4 : 4 + pieces_total]
    acc, gu, sums, w, sems = refs[4 + pieces_total :]
    n = pl.program_id(0)
    cols = plan.columns

    @pl.when(n == 0)
    def _():
        for slot in range(slots):
            for c in plan.copies(slot, pieces, table, w, sems):
                c.start()

    for slot, step in enumerate(first_need(tile, cols, slots)):

        @pl.when(n == step)
        def _(slot=slot):
            for c in plan.copies(slot, pieces, table, w, sems):
                c.wait()

    wt = w[:, pl.ds(pl.multiple_of(n * tile, tile), tile)]
    grad = (nn(gl[...], wt) * slope[...].astype(F32)).astype(BF16)
    gu[...] = grad
    sums[...] = jnp.sum(grad.astype(F32), axis=0, keepdims=True)
    part = nt(active[...], wt)

    @pl.when(n == 0)
    def _():
        acc[...] = part

    @pl.when(n > 0)
    def _():
        acc[...] += part


def ff_down(table, gl, active, slope, pieces, plan, slots):
    d = gl.shape[1]
    units = slots * plan.columns
    tile = tile_of(units)
    return pl.pallas_call(
        functools.partial(ff_down_kernel, plan, len(pieces), slots, tile),
        grid=(units // tile,),
        in_specs=[
            pl.BlockSpec(memory_space=pltpu.SMEM),
            whole((PAD, d)),
            pl.BlockSpec((PAD, tile), lambda n: (0, n)),
            pl.BlockSpec((PAD, tile), lambda n: (0, n)),
            *[pl.BlockSpec(memory_space=pl.ANY) for _ in pieces],
        ],
        out_specs=[
            whole((PAD, d)),
            pl.BlockSpec((PAD, tile), lambda n: (0, n)),
            pl.BlockSpec((1, tile), lambda n: (0, n)),
        ],
        out_shape=[
            jax.ShapeDtypeStruct((PAD, d), F32),
            jax.ShapeDtypeStruct((PAD, units), BF16),
            jax.ShapeDtypeStruct((1, units), F32),
        ],
        scratch_shapes=[
            pltpu.VMEM((d, units), BF16),
            pltpu.SemaphoreType.DMA((len(plan.entries),)),
        ],
        compiler_params=params(),
        cost_estimate=cost(4 * PAD * d * units, 2 * d * units + 6 * PAD * units),
        name="ff_down",
    )(table, gl, active, slope, *pieces)


def ff_back_kernel(gu, w, acc):
    part = nt(gu[...], w[...])

    @pl.when(pl.program_id(0) == 0)
    def _():
        acc[...] = part

    @pl.when(pl.program_id(0) > 0)
    def _():
        acc[...] += part


def ff_back(gu, w):
    d, units = w.shape
    tile = tile_of(units)
    return pl.pallas_call(
        ff_back_kernel,
        grid=(units // tile,),
        in_specs=[
            pl.BlockSpec((PAD, tile), lambda n: (0, n)),
            pl.BlockSpec((d, tile), lambda n: (0, n)),
        ],
        out_specs=whole((PAD, d)),
        out_shape=jax.ShapeDtypeStruct((PAD, d), F32),
        compiler_params=params(),
        cost_estimate=cost(2 * PAD * d * units, 2 * d * units + 2 * PAD * units),
        name="ff_back",
    )(gu, w)


def turn_kernel(blocks, table, x, out):
    rows = x.shape[1] // blocks
    t = x[...].T
    for b in range(blocks):
        out[pl.ds(pl.multiple_of(table[b], 16), rows), :] = t[b * rows : (b + 1) * rows, :]


def turn(table, x):
    blocks = table.shape[0]
    d = x.shape[1]
    return pl.pallas_call(
        functools.partial(turn_kernel, blocks),
        in_specs=[pl.BlockSpec(memory_space=pltpu.SMEM), pl.BlockSpec(memory_space=pltpu.VMEM)],
        out_specs=pl.BlockSpec(memory_space=pltpu.VMEM),
        out_shape=jax.ShapeDtypeStruct((d, PAD), BF16),
        compiler_params=params(),
        cost_estimate=cost(PAD * d * 8, PAD * d * 4),
        name="turn",
    )(table, x)


def ff_grad_kernel(total, parts, rows, *refs):
    lhs, rhs, outs = refs[:total], refs[total : 2 * total], refs[2 * total :]
    value = nn(lhs[0][...], rhs[0][...])
    for a, b in zip(lhs[1:], rhs[1:]):
        value += nn(a[...], b[...])
    for number in range(parts):
        outs[number][0] = value[number * rows : (number + 1) * rows].astype(BF16)


def ff_grad(lhs, rhs, slots, parts):
    total = len(lhs)
    height = lhs[0].shape[0]
    rows = height // parts
    cols = rhs[0].shape[1] // slots
    return pl.pallas_call(
        functools.partial(ff_grad_kernel, total, parts, rows),
        grid=(slots,),
        in_specs=[
            *[whole((height, PAD)) for _ in lhs],
            *[pl.BlockSpec((PAD, cols), lambda n: (0, n)) for _ in rhs],
        ],
        out_specs=[pl.BlockSpec((1, rows, cols), lambda n: (n, 0, 0)) for _ in range(parts)],
        out_shape=[jax.ShapeDtypeStruct((slots, rows, cols), BF16) for _ in range(parts)],
        compiler_params=params(),
        cost_estimate=cost(
            2 * total * PAD * height * slots * cols, 2 * slots * cols * (total * PAD + height)
        ),
        name="ff_grad",
    )(*lhs, *rhs)


def attn_grad_kernel(total, parts, slots, rows, *refs):
    na, dp = refs[:total], refs[total : 2 * total]
    ga, mx = refs[2 * total : 3 * total], refs[3 * total : 4 * total]
    outs = refs[4 * total :]
    left = nn(na[0][...], dp[0][0])
    right = nn(ga[0][...], mx[0][0])
    for i in range(1, total):
        left += nn(na[i][...], dp[i][0])
        right += nn(ga[i][...], mx[i][0])
    cut = left.shape[1]
    for part in range(parts):
        for slot in range(slots):
            block = slice((part * slots + slot) * rows, (part * slots + slot + 1) * rows)
            outs[part][slot, 0, :, 0:cut] = left[block].astype(BF16)
            outs[part][slot, 0, :, cut:] = right[block].astype(BF16)


def attn_grad(na, dp, ga, mx, parts, slots):
    total = len(na)
    height = na[0].shape[0]
    rows = height // (parts * slots)
    groups, _, cut = dp[0].shape
    cols = cut + mx[0].shape[2]
    return pl.pallas_call(
        functools.partial(attn_grad_kernel, total, parts, slots, rows),
        grid=(groups,),
        in_specs=[
            *[whole((height, PAD)) for _ in na],
            *[pl.BlockSpec((1, PAD, cut), lambda g: (g, 0, 0)) for _ in dp],
            *[whole((height, PAD)) for _ in ga],
            *[pl.BlockSpec((1, PAD, cols - cut), lambda g: (g, 0, 0)) for _ in mx],
        ],
        out_specs=[
            pl.BlockSpec((slots, 1, rows, cols), lambda g: (0, g, 0, 0)) for _ in range(parts)
        ],
        out_shape=[jax.ShapeDtypeStruct((slots, groups, rows, cols), BF16) for _ in range(parts)],
        compiler_params=params(),
        cost_estimate=cost(
            2 * total * PAD * height * groups * cols, 2 * groups * cols * (total * PAD + height)
        ),
        name="attn_grad",
    )(*na, *dp, *ga, *mx)


def layer_norm(values, scaling, offset):
    center = values - jnp.mean(values, axis=-1, keepdims=True)
    spread = jnp.mean(center * center, axis=-1, keepdims=True)
    return center * lax.rsqrt(spread + EPS) * scaling + offset


def hop(x, axis, n, step):
    return lax.ppermute(x, axis, [(i, (i + step) % n) for i in range(n)])


def cat(*arrays):
    return jnp.concatenate(arrays, axis=0)


def total_sum(value, sizes):
    for axis, n in sizes.items():
        step = 1
        while step < n:
            value = value + lax.ppermute(value, axis, [(i, i ^ step) for i in range(n)])
            step *= 2
    return value


class Links:
    def __init__(self, sizes, rows):
        self.nz = sizes["z"]
        nz = self.nz
        self.rows = rows
        blocks = [(dy, dz) for dy in range(2) for dz in range(nz)]
        self.attn_plans = []
        for dc in range(2):
            entries = []
            for dx in range(2):
                for dy, dz in blocks:
                    if dc == 1:
                        piece, at = dy, dz * 2 + dx
                    elif dy == 0:
                        piece, at = dz, dx
                    else:
                        piece, at = nz + dz // 2, dz % 2 * 2 + dx
                    entries.append((piece, at * rows, rows, dx, dy * nz + dz, 0))
            self.attn_plans.append(entries)
        self.ff_entries = []
        for dz in range(nz):
            for dc in range(2):
                for dy in range(2):
                    for dx in range(2):
                        if dc == 0:
                            piece, at = dx * 2 + dy, dz
                        else:
                            piece, at = 4 + dx, dy * nz + dz
                        self.ff_entries.append((piece, at * rows, rows, dz, dc * 4 + dy * 2 + dx))

    def gather_attn(self, own):
        s = [cat(own, hop(own, "x", 2, 1))]
        for _ in range(self.nz - 1):
            s.append(hop(s[-1], "z", self.nz, 1))
        y = [hop(cat(*s[i : i + 2]), "y", 2, 1) for i in range(0, self.nz, 2)]
        far = [hop(cat(*s), "c", 2, 1), hop(cat(*y), "c", 2, 1)]
        return [s + y, far]

    def gather_ff(self, own):
        u = [own]
        for _ in range(self.nz - 1):
            u.append(hop(u[-1], "z", self.nz, 1))
        y = [hop(cat(*u[i : i + 2]), "y", 2, 1) for i in range(0, self.nz, 2)]
        a, b = cat(*u), cat(*y)
        xa, xb = hop(a, "x", 2, 1), hop(b, "x", 2, 1)
        return [a, b, xa, xb, hop(cat(a, b), "c", 2, 1), hop(cat(xa, xb), "c", 2, 1)]

    def line(self, part):
        value = part[self.nz - 1]
        for k in range(self.nz - 2, -1, -1):
            value = hop(value, "z", self.nz, -1) + part[k]
        return value

    def scatter_ff(self, parts):
        p00, p01, p10, p11 = parts
        far = p10 + hop(p11, "x", 2, 1)
        near = p00 + hop(p01, "x", 2, 1) + hop(far, "y", 2, 1)
        return self.line(near)

    def scatter_attn(self, parts):
        pair = self.line(parts[0] + hop(parts[1], "y", 2, 1))
        return pair[0] + hop(pair[1], "x", 2, 1)


def on_device(
    sizes,
    inputs,
    slot_mask,
    ln1_gain,
    ln1_bias,
    qkv_weight,
    qv_bias,
    out_weight,
    out_bias,
    ln2_gain,
    ln2_bias,
    up_weight,
    up_bias,
    down_weight,
    down_bias,
    out_grad,
):
    seq, d = inputs.shape[1:]
    ny, nx, nc, nz = (sizes[a] for a in ("y", "x", "c", "z"))
    yi, xi, ci, zi = (lax.axis_index(a) for a in ("y", "x", "c", "z"))
    width = GROUP_HEADS * HEAD_DIM
    unit_width = up_weight.shape[1]
    cols = -(-unit_width // 128) * 128
    a_rows, f_rows = qkv_weight.shape[0], up_weight.shape[0]
    linked = ny == nx == nc == 2 and nz % 2 == 0 and a_rows % 16 == 0 and f_rows % 16 == 0

    attn_own = jnp.concatenate(
        [qkv_weight.reshape(a_rows, 3 * width).astype(BF16), out_weight.T.astype(BF16)], axis=1
    )
    spare = ((0, 0), (0, cols - unit_width))
    up_own = jnp.pad(up_weight.astype(BF16), spare)
    down_own = jnp.pad(down_weight.T.astype(BF16), spare)

    if linked:
        links = Links(sizes, a_rows)
        ffl = Links(sizes, f_rows)
        attn_pieces = links.gather_attn(attn_own)
        up_pieces, down_pieces = ffl.gather_ff(up_own), ffl.gather_ff(down_own)
        attn_plans = [Plan(e, attn_own.shape[1]) for e in links.attn_plans]
        ff_plan = Plan([e + (e[3] * cols,) for e in ffl.ff_entries], cols)
        attn_table = jnp.stack(
            [((yi ^ dy) * nz + (zi - dz) % nz) * a_rows for dy in range(2) for dz in range(nz)]
        )
        ff_table = jnp.stack(
            [
                (((yi ^ dy) * 2 + (xi ^ dx)) * 2 + (ci ^ dc)) * f_rows
                for dc in range(2)
                for dy in range(2)
                for dx in range(2)
            ]
        )
        turn_attn = jnp.stack(
            [((yi ^ b // nz) * nz + (zi - b % nz) % nz) * a_rows for b in range(2 * nz)]
        )
        turn_ff = jnp.stack(
            [
                ((ci ^ b % 2) * 4 + (yi ^ b // 4) * 2 + (xi ^ b // 2 % 2)) * f_rows
                for b in range(8)
            ]
        )
        halves = [[(xi ^ dx) * 2 + (ci ^ dc) for dx in range(2)] for dc in range(2)]
        zones = [(zi - dz) % nz for dz in range(nz)]
    else:
        heads = ("x", "c")
        whole_attn = lax.all_gather(attn_own, ("y", "z"), axis=0, tiled=True)
        whole_attn = lax.all_gather(whole_attn, heads, axis=0)
        attn_pieces = [[whole_attn[g] for g in range(nx * nc)]]
        spot = ("y", "x", "c")
        up_whole = lax.all_gather(up_own, spot, axis=0, tiled=True)
        up_whole = lax.all_gather(up_whole, "z", axis=0)
        down_whole = lax.all_gather(down_own, spot, axis=0, tiled=True)
        down_whole = lax.all_gather(down_whole, "z", axis=0)
        up_pieces = [up_whole[k] for k in range(nz)]
        down_pieces = [down_whole[k] for k in range(nz)]
        attn_plans = [Plan([(g, 0, d, g, 0, 0) for g in range(nx * nc)], attn_own.shape[1])]
        ff_plan = Plan([(k, 0, d, k, 0, k * cols) for k in range(nz)], cols)
        attn_table = ff_table = turn_attn = turn_ff = jnp.zeros((1,), jnp.int32)
        halves = [list(range(nx * nc))]
        zones = list(range(nz))

    valid = slot_mask[0].astype(F32)
    token_pad = ((0, PAD - seq), (0, 0))
    residual = jnp.pad(inputs[0], token_pad).astype(F32)
    real = lax.broadcasted_iota(jnp.int32, (PAD, 1), 0) < seq

    def norm(v, g, b):
        return jnp.where(real, layer_norm(v, g, b), 0.0)

    normed_a, back_a = jax.vjp(norm, residual, ln1_gain, ln1_bias)
    normed_a = normed_a.astype(BF16)

    def bias_rows(group):
        part = lax.dynamic_slice_in_dim(qv_bias, group * width, width, 1)
        return jnp.concatenate([part[0], jnp.zeros_like(part[0]), part[1]])[None]

    acc = None
    kept = []
    for pieces, plan, groups in zip(attn_pieces, attn_plans, halves):
        bias = jnp.stack([bias_rows(g) for g in groups])
        proj, mixed, lse, acc, w = attn_fwd(
            attn_table, normed_a, bias, pieces, plan, acc, seq, len(groups)
        )
        kept.append((proj, mixed, lse, w))
    hidden = residual + (acc + out_bias)

    normed_b, back_b = jax.vjp(norm, hidden, ln2_gain, ln2_bias)
    normed_b = normed_b.astype(BF16)
    grad_low = (valid * jnp.pad(out_grad[0], token_pad).astype(F32)).astype(BF16)
    shift = jnp.concatenate(
        [
            jnp.pad(lax.dynamic_slice_in_dim(up_bias, k * unit_width, unit_width), spare[1])
            for k in zones
        ]
    )[None]
    active, slope, up_full = ff_up(ff_table, normed_b, shift, up_pieces, ff_plan, nz)
    mlp, grad_upper, upper_sums = ff_down(
        ff_table, grad_low, active, slope, down_pieces, ff_plan, nz
    )
    output = (valid * (hidden + (mlp + down_bias)))[:seq].astype(BF16)[None]

    def swap(x):
        return hop(x, "c", 2, 1)

    nb_t, gl_t = turn(turn_ff, normed_b), turn(turn_ff, grad_low)
    if linked:
        half = d // 2
        down_lhs = [gl_t[:half], swap(gl_t[half:])]
        up_lhs = [nb_t[:half], swap(nb_t[half:])]
        down_parts = ff_grad(down_lhs, [active, swap(active)], nz, 4)
        down_sum = ffl.scatter_ff(down_parts)
        up_parts = ff_grad(up_lhs, [grad_upper, swap(grad_upper)], nz, 4)
        up_sum = ffl.scatter_ff(up_parts)
    else:
        spot = ("y", "x", "c")

        def spread(parts):
            part = lax.psum_scatter(parts[0], "z", scatter_dimension=0, tiled=True)[0]
            part = lax.psum_scatter(part, spot, scatter_dimension=0, tiled=True)
            return lax.optimization_barrier(part)

        down_sum = spread(ff_grad([gl_t], [active], nz, 1))
        up_sum = spread(ff_grad([nb_t], [grad_upper], nz, 1))

    grad_normed_b = ff_back(grad_upper, up_full)
    through, ln2_gain_grad, ln2_bias_grad = back_b(grad_normed_b)
    grad_hidden = grad_low.astype(F32) + through
    grad_attn = grad_hidden.astype(BF16)

    na_t, ga_t = turn(turn_attn, normed_a), turn(turn_attn, grad_attn)
    acc = None
    grads, sums = [], []
    for proj, mixed, lse, w in kept[::-1]:
        dproj, acc, part_sums = attn_bwd(proj, lse, grad_attn, w, acc, seq)
        grads.insert(0, dproj)
        sums.insert(0, part_sums)
    if linked:
        parts = attn_grad(
            [na_t, swap(na_t)],
            [grads[0], swap(grads[1])],
            [ga_t, swap(ga_t)],
            [kept[0][1], swap(kept[1][1])],
            2,
            nz,
        )
        attn_sum = links.scatter_attn(parts)
    else:
        part = attn_grad([na_t], grads, [ga_t], [kept[0][1]], 1, 1)[0][0]
        part = lax.psum_scatter(part, ("x", "c"), scatter_dimension=0, tiled=True)[0]
        attn_sum = lax.psum_scatter(part, ("y", "z"), scatter_dimension=0, tiled=True)
        attn_sum = lax.optimization_barrier(attn_sum)
    through, ln1_gain_grad, ln1_bias_grad = back_a(acc)
    input_grad = (grad_hidden + through)[:seq][None]

    qv_sum = jnp.zeros_like(qv_bias)
    for groups, part_sums in zip(halves, sums):
        for k, g in enumerate(groups):
            row = part_sums[k, 0]
            pair = jnp.stack([row[:width], row[2 * width :]])
            qv_sum = lax.dynamic_update_slice_in_dim(qv_sum, pair, g * width, 1)
    up_shift = jnp.zeros_like(up_bias)
    for slot, k in enumerate(zones):
        piece = upper_sums[0, slot * cols : slot * cols + unit_width]
        up_shift = lax.dynamic_update_slice_in_dim(up_shift, piece, k * unit_width, 0)
    vectors = [
        ln1_gain_grad,
        ln1_bias_grad,
        qv_sum.reshape(-1),
        jnp.sum(grad_attn.astype(F32), axis=0),
        ln2_gain_grad,
        ln2_bias_grad,
        up_shift,
        jnp.sum(grad_low.astype(F32), axis=0),
    ]
    lengths = [v.shape[0] for v in vectors]
    flat = jnp.concatenate(vectors)
    fill = -flat.shape[0] % 1024
    flat = total_sum(jnp.pad(flat, (0, fill)).reshape(-1, 128), sizes).reshape(-1)
    out = []
    start = 0
    for n in lengths:
        out.append(flat[start : start + n])
        start += n

    qkv_grad = attn_sum[:, : 3 * width].astype(F32).reshape(a_rows, 3, width)
    out_weight_grad = attn_sum[:, 3 * width :].astype(F32).T
    up_grad = up_sum[:, :unit_width].astype(F32)
    down_grad = down_sum[:, :unit_width].astype(F32).T
    return (
        output,
        input_grad,
        out[0],
        out[1],
        qkv_grad,
        out[2].reshape(qv_bias.shape),
        out_weight_grad,
        out[3],
        out[4],
        out[5],
        up_grad,
        out[6],
        down_grad,
        out[7],
    )


def solution(mesh):
    heads = mesh.shape["heads"]
    sizes = {"y": mesh.shape["fsdp"], "x": heads // 2, "c": 2, "z": mesh.shape["tensor"]}
    split = jax.sharding.Mesh(mesh.devices.reshape(tuple(sizes.values())), tuple(sizes))
    images = P(("y", "x", "c", "z"), None, None)
    attn_in = P(("y", "z"), None, ("x", "c"))
    attn_out = P(("x", "c"), ("y", "z"))
    up, down = P(("y", "x", "c"), "z"), P("z", ("y", "x", "c"))
    in_specs = (
        images,
        P(("y", "x", "c", "z")),
        P(),
        P(),
        attn_in,
        P(),
        attn_out,
        P(),
        P(),
        P(),
        up,
        P(),
        down,
        P(),
        images,
    )
    out_specs = (
        images,
        images,
        P(),
        P(),
        attn_in,
        P(),
        attn_out,
        P(),
        P(),
        P(),
        up,
        P(),
        down,
        P(),
    )
    return jax.shard_map(
        functools.partial(on_device, sizes),
        mesh=split,
        in_specs=in_specs,
        out_specs=out_specs,
        check_vma=False,
    )
```

time: 1410 us -> 705 us (0.50)
  waiting for transfers between devices: 931 us -> 280 us
  matrix products: 234 us -> 0 us
  Pallas kernels: 0 us -> 216 us
  blocking collectives: 83.6 us -> 0 us
  starting transfers between devices: 0.86 us -> 58.9 us
  local copies, waits for them, and re-layouts: 36.1 us -> 69.9 us
  other arithmetic: 96.3 us -> 71.8 us
  between operations: 17.1 us -> 2.37 us
    reduce_scatter x8 -> x0, waiting for transfers between devices: 585 us -> none  [the longest x1 211 us: on_device(): lax.psum_scatter(grad_normed_part, 'tensor', scatter_dimension=0, tiled=T...]
    all_gather x7 -> x0, waiting for transfers between devices: 346 us -> none  [the longest x1 125 us: on_device(): lax.all_gather(branch_grad, 'tensor', axis=0, tiled=True)]
    ppermute x0 -> x56, waiting for transfers between devices: none -> 280 us  [the longest x51 260 us: hop(): return lax.ppermute(x, axis, [(i, (i + step) % n) for i in range(n)])]
    dot_general x40 -> x0, matrix products: 234 us -> none  [the longest x1 25.4 us: mlp_backward(): jnp.einsum('bsd,fd->bsf', grad_low, down_matrix, preferred_element_type=j...]
    pallas_call x0 -> x14, Pallas kernels: none -> 216 us  [the longest x2 52.8 us: attn_bwd(): pl.pallas_call(functools.partial(attn_bwd_kernel, has_acc, seq, groups),...]
    ppermute x0 -> x56, starting transfers between devices: none -> 58.9 us  [the longest x51 56.4 us: hop(): return lax.ppermute(x, axis, [(i, (i + step) % n) for i in range(n)])]
    convert_element_type x12 -> x8, other arithmetic: 52.8 us -> 9.11 us  [the longest x1 2.25 us: on_device(): normed_a = normed_a.astype(BF16)]
    psum x1 -> x0, blocking collectives: 41.9 us -> none  [on_device(): lax.psum((ln1_gain_grad, ln1_bias_grad, bias_full, out_bias_grad, ln2_gai...]
  transfers between devices with their start and end apart: 15 -> 56, of which waited for: 12 -> 25; matrix products, arithmetic and copies ran while one was open for 18% -> 17% of each run, Pallas kernels for 0% -> 21%
where the time goes in v1:
time: 705 us; the launch traced here: 699 us
  waiting for transfers between devices  280 us (40%)
  Pallas kernels  216 us (31%)
  other arithmetic  71.8 us (10%)
  local copies, waits for them, and re-layouts  69.9 us (10%)
  starting transfers between devices  58.9 us (8%)
    ppermute x51, waiting for transfers between devices, hop(): return lax.ppermute(x, axis, [(i, (i + step) % n) for i in range(n)])  260 us
    ppermute x51, starting transfers between devices, hop(): return lax.ppermute(x, axis, [(i, (i + step) % n) for i in range(n)])  56.4 us
    pallas_call x2, Pallas kernels, attn_bwd(): pl.pallas_call(functools.partial(attn_bwd_kernel, has_acc, seq, groups),...  52.8 us
    pallas_call x2, Pallas kernels, attn_fwd(): pl.pallas_call(functools.partial(attn_fwd_kernel, plan, len(pieces), has_...  39.8 us
    pallas_call x1, Pallas kernels, ff_down(): pl.pallas_call(functools.partial(ff_down_kernel, plan, len(pieces), slots...  28.4 us
    pallas_call x2, Pallas kernels, ff_grad(): pl.pallas_call(functools.partial(ff_grad_kernel, total, parts, rows), gri...  27.1 us
    unnamed x102, local copies, waits for them, and re-layouts  22.6 us
    pallas_call x1, Pallas kernels, ff_up(): pl.pallas_call(functools.partial(ff_up_kernel, plan, len(pieces), slots,...  21.1 us
  transfers between devices with their start and end apart: 56, of which 25 were waited for; matrix products, arithmetic and copies ran while one was open for 17% of the time, Pallas kernels for 21%

profile of v1, /device:TPU:0, one launch (start us, length us, event | category | flops | bytes accessed | tf_op | source)
XLA Modules:
  0.0 699.4 jit_solution(16828752976529253647)
XLA Ops:
  4.3 2.9 collective-permute-start
  24.0 4.4 collective-permute-done.17
  37.7 11.9 %collective-permute-done.9 = bf16[144,1152]{1,0:T(8,128)(2,1)S(1)} collective-permute-done((bf16[144,1152]{1,0:T(8,128)(2,1)}, bf16[144,1152]{1,0:T(8,128)(2,1)S(1)}, u32[]{:S(2)}, u32[]{:S(2)}) %collective-permute-start.9) | collective-permute-done | bytes 331808 | tf_op jit(solution)/shard_map/ppermute | solution.py:542
  49.6 7.1 %collective-permute-done.18 = bf16[144,1152]{1,0:T(8,128)(2,1)S(1)} collective-permute-done((bf16[144,1152]{1,0:T(8,128)(2,1)}, bf16[144,1152]{1,0:T(8,128)(2,1)S(1)}, u32[]{:S(2)}, u32[]{:S(2)}) %collective-permute-start.18) | collective-permute-done | bytes 331808 | tf_op jit(solution)/shard_map/ppermute | solution.py:542
  61.3 2.6 collective-permute-done.10
  66.7 2.9 collective-permute-done.19
  71.7 15.2 %collective-permute-done.2.refs_5_ = bf16[288,1152]{1,0:T(8,128)(2,1)S(1)} collective-permute-done((bf16[288,1152]{1,0:T(8,128)(2,1)S(1)}, bf16[288,1152]{1,0:T(8,128)(2,1)S(1)}, u32[]{:S(2)}, u32[]{:S(2)}) %collective-permute-start.2) | collective-permute-done | bytes 663584 | tf_op jit(solution)/shard_map/ppermute | solution.py:542
  92.1 11.7 %collective-permute-done.3.refs_6_ = bf16[288,1152]{1,0:T(8,128)(2,1)S(1)} collective-permute-done((bf16[288,1152]{1,0:T(8,128)(2,1)S(1)}, bf16[288,1152]{1,0:T(8,128)(2,1)S(1)}, u32[]{:S(2)}, u32[]{:S(2)}) %collective-permute-start.3) | collective-permute-done | bytes 663584 | tf_op jit(solution)/shard_map/ppermute | solution.py:542
  108.8 11.4 %collective-permute-done.21 = bf16[288,1152]{1,0:T(8,128)(2,1)S(1)} collective-permute-done((bf16[288,1152]{1,0:T(8,128)(2,1)S(1)}, bf16[288,1152]{1,0:T(8,128)(2,1)S(1)}, u32[]{:S(2)}, u32[]{:S(2)}) %collective-permute-start.21) | collective-permute-done | bytes 663584 | tf_op jit(solution)/shard_map/ppermute | solution.py:542
  122.5 1.8 collective-permute-start.23
  124.2 20.7 %collective-permute-done.6.refs_8_ = bf16[576,1152]{1,0:T(8,128)(2,1)S(1)} collective-permute-done((bf16[576,1152]{1,0:T(8,128)(2,1)S(1)}, bf16[576,1152]{1,0:T(8,128)(2,1)S(1)}, u32[]{:S(2)}, u32[]{:S(2)}) %collective-permute-start.6) | collective-permute-done | bytes 1327136 | tf_op jit(solution)/shard_map/ppermute | solution.py:542
  145.0 1.8 pad_maximum_fusion
  147.3 2.2 fusion.8.refs_1_.x
  149.5 27.6 %collective-permute-done.14.refs_6_ = bf16[576,1152]{1,0:T(8,128)(2,1)S(1)} collective-permute-done((bf16[576,1152]{1,0:T(8,128)(2,1)S(1)}, bf16[576,1152]{1,0:T(8,128)(2,1)S(1)}, u32[]{:S(2)}, u32[]{:S(2)}) %collective-permute-start.14) | collective-permute-done | bytes 1327136 | tf_op jit(solution)/shard_map/ppermute | solution.py:542
  177.1 1.9 pad_maximum_fusion.1
  179.4 22.9 %collective-permute-done.23.refs_7_ = bf16[576,1152]{1,0:T(8,128)(2,1)S(1)} collective-permute-done((bf16[576,1152]{1,0:T(8,128)(2,1)S(1)}, bf16[576,1152]{1,0:T(8,128)(2,1)S(1)}, u32[]{:S(2)}, u32[]{:S(2)}) %collective-permute-start.23) | collective-permute-done | bytes 1327136 | tf_op jit(solution)/shard_map/ppermute | solution.py:542
  205.1 19.3 %attn_fwd.2 = (bf16[2,768,864]{2,1,0:T(8,128)(2,1)}, bf16[2,768,288]{2,1,0:T(8,128)(2,1)}, f32[2,8,768]{2,1,0:T(8,128)}, f32[768,1152]{1,0:T(8,128)}, bf16[2,1152,1152]{2,1,0:T(8,128)(2,1)}) custom-call(s32[8]{0:T(128)} %stack.140.refs_0_.table, bf16[768,1152]{1,0:T(8,128)(2,1)} %fusion.8.refs_1_.x, f32[2,1,864]{2,1,0:T(1,128)} %pad_maximum_fusion.18.refs_2_, ...), custom_call_target="tpu_custom_call" | custom-call | flops 8908701696 | bytes 17694720 | tf_op jit(solution)/shard_map/attn_fwd/pallas_call | solution.py:134
  224.5 20.5 %attn_fwd.3 = (bf16[2,768,864]{2,1,0:T(8,128)(2,1)}, bf16[2,768,288]{2,1,0:T(8,128)(2,1)}, f32[2,8,768]{2,1,0:T(8,128)}, f32[768,1152]{1,0:T(8,128)}, bf16[2,1152,1152]{2,1,0:T(8,128)(2,1)}) custom-call(s32[8]{0:T(128)} %stack.140.refs_0_.table, bf16[768,1152]{1,0:T(8,128)(2,1)} %fusion.8.refs_1_.x, f32[2,1,864]{2,1,0:T(1,128)} %pad_maximum_fusion.17.refs_2_, ...), custom_call_target="tpu_custom_call" | custom-call | flops 8908701696 | bytes 17694720 | tf_op jit(solution)/shard_map/attn_fwd/pallas_call | solution.py:134
  245.0 3.0 fusion.36
  248.8 2.1 select_convert_fusion.refs_1_.x
  250.9 21.1 %ff_up.1 = (bf16[768,4608]{1,0:T(8,128)(2,1)}, bf16[768,4608]{1,0:T(8,128)(2,1)}, bf16[1152,4608]{1,0:T(8,128)(2,1)}) custom-call(s32[8]{0:T(128)} %stack.151.refs_0_, bf16[768,1152]{1,0:T(8,128)(2,1)} %select_convert_fusion.refs_1_.x, f32[1,4608]{1,0:T(1,128)} %broadcast_in_dim.64.refs_2_, bf16[576,1152]{1,0:T(8,128)(2,1)} %copy-done.15, ...), custom_call_target="tpu_custom_call" | custom-call | flops 8153726976 | bytes 35389440 | tf_op jit(solution)/shard_map/ff_up/pallas_call | solution.py:310
  272.1 28.4 %ff_down.1 = (f32[768,1152]{1,0:T(8,128)}, bf16[768,4608]{1,0:T(8,128)(2,1)}, f32[1,4608]{1,0:T(1,128)}) custom-call(s32[8]{0:T(128)} %stack.151.refs_0_, bf16[768,1152]{1,0:T(8,128)(2,1)} %multiply_convert_fusion.refs_1_.x, bf16[768,4608]{1,0:T(8,128)(2,1)} %get-tuple-element.48.refs_2_, bf16[768,4608]{1,0:T(8,128)(2,1)} %get-tuple-element.49.refs_3_, ...), custom_call_target="tpu_custom_call" | custom-call | flops 16307453952 | bytes 31850496 | tf_op jit(solution)/shard_map/ff_down/pallas_call | solution.py:379
  300.6 15.8 %ff_back.1 = f32[768,1152]{1,0:T(8,128)} custom-call(bf16[768,4608]{1,0:T(8,128)(2,1)} %get-tuple-element.51.gu.refs_2_, bf16[1152,4608]{1,0:T(8,128)(2,1)} %get-tuple-element.52.w), custom_call_target="tpu_custom_call" | custom-call | flops 8153726976 | bytes 17694720 | tf_op jit(solution)/shard_map/ff_back/pallas_call | solution.py:424
  316.4 3.8 multiply_reduce_fusion
  321.9 3.8 convert_reduce_fusion.2
  325.6 26.0 %attn_bwd.2 = (bf16[2,768,864]{2,1,0:T(8,128)(2,1)}, f32[768,1152]{1,0:T(8,128)}, f32[2,1,864]{2,1,0:T(1,128)}) custom-call(bf16[2,768,864]{2,1,0:T(8,128)(2,1)} %get-tuple-element.56.refs_0_, f32[2,8,768]{2,1,0:T(8,128)} %get-tuple-element.57.refs_1_, bf16[768,1152]{1,0:T(8,128)(2,1)} %get-tuple-element.139.refs_2_.x, ...), custom_call_target="tpu_custom_call" | custom-call | flops 16156459008 | bytes 12386304 | tf_op jit(solution)/shard_map/attn_bwd/pallas_call | solution.py:228
  351.6 4.5 copy.36
  356.7 3.3 turn.4.refs_0_
  360.0 3.3 turn.5.refs_4_
  364.4 3.2 turn.7
  367.6 2.4 copy.37
  370.5 26.8 %attn_bwd.3 = (bf16[2,768,864]{2,1,0:T(8,128)(2,1)}, f32[768,1152]{1,0:T(8,128)}, f32[2,1,864]{2,1,0:T(1,128)}) custom-call(bf16[2,768,864]{2,1,0:T(8,128)(2,1)} %get-tuple-element.53.refs_0_, f32[2,8,768]{2,1,0:T(8,128)} %get-tuple-element.54.refs_1_, bf16[768,1152]{1,0:T(8,128)(2,1)} %get-tuple-element.139.refs_2_.x, ...), custom_call_target="tpu_custom_call" | custom-call | flops 16156459008 | bytes 12386304 | tf_op jit(solution)/shard_map/attn_bwd/pallas_call | solution.py:228
  397.5 2.3 copy.39.refs_7_
  399.8 4.5 copy.38.refs_3_
  404.3 17.9 %attn_grad.1 = (bf16[4,2,144,1152]{3,2,1,0:T(8,128)(2,1)}, bf16[4,2,144,1152]{3,2,1,0:T(8,128)(2,1)}) custom-call(bf16[1152,768]{1,0:T(8,128)(2,1)} %turn.4.refs_0_, bf16[1152,768]{1,0:T(8,128)(2,1)} %collective-permute-done.31.refs_1_, bf16[2,768,864]{2,1,0:T(8,128)(2,1)} %get-tuple-element.64.refs_2_, bf16[2,768,864]{2,1,0:T(8,128)(2,1)} %copy.38.refs_3_, ...), custom_call_target="tpu_custom_call" | custom-call | flops 8153726976 | bytes 12386304 | tf_op jit(solution)/shard_map/attn_grad/pallas_call | solution.py:514
  423.8 2.8 fusion.37
  447.7 4.2 fusion.9
  455.4 4.9 fusion.34
  460.3 3.3 turn.6
  463.6 20.0 %collective-permute-done.26 = f32[112,128]{1,0:T(8,128)S(1)} collective-permute-done((f32[112,128]{1,0:T(8,128)S(1)}, f32[112,128]{1,0:T(8,128)S(1)}, u32[]{:S(2)}, u32[]{:S(2)}) %collective-permute-start.26) | collective-permute-done | bytes 57376 | tf_op jit(solution)/shard_map/ppermute | solution.py:553
  484.7 3.3 add.391
  488.2 3.6 collective-permute-start.36
  494.2 11.9 %collective-permute-done.36 = bf16[2,144,1152]{2,1,0:T(8,128)(2,1)S(1)} collective-permute-done((bf16[2,144,1152]{2,1,0:T(8,128)(2,1)S(1)}, bf16[2,144,1152]{2,1,0:T(8,128)(2,1)S(1)}, u32[]{:S(2)}, u32[]{:S(2)}) %collective-permute-start.36) | collective-permute-done | bytes 663584 | tf_op jit(solution)/shard_map/ppermute | solution.py:542
  506.2 4.4 collective-permute-start.37
  510.6 2.1 fusion.12
  512.7 10.6 %collective-permute-done.37 = bf16[2,144,1152]{2,1,0:T(8,128)(2,1)S(1)} collective-permute-done((bf16[2,144,1152]{2,1,0:T(8,128)(2,1)S(1)}, bf16[2,144,1152]{2,1,0:T(8,128)(2,1)S(1)}, u32[]{:S(2)}, u32[]{:S(2)}) %collective-permute-start.37) | collective-permute-done | bytes 663584 | tf_op jit(solution)/shard_map/ppermute | solution.py:542
  525.9 3.6 collective-permute-start.38
  529.5 13.7 %ff_grad.2 = (bf16[4,144,1152]{2,1,0:T(8,128)(2,1)}, bf16[4,144,1152]{2,1,0:T(8,128)(2,1)}, bf16[4,144,1152]{2,1,0:T(8,128)(2,1)}, bf16[4,144,1152]{2,1,0:T(8,128)(2,1)}) custom-call(bf16[576,768]{1,0:T(8,128)(2,1)} %get-tuple-element.152.refs_0_, bf16[576,768]{1,0:T(8,128)(2,1)} %copy-done.43, bf16[768,4608]{1,0:T(8,128)(2,1)} %get-tuple-element.51.gu.refs_2_, ...), custom_call_target="tpu_custom_call" | custom-call | flops 8153726976 | bytes 19464192 | tf_op jit(solution)/shard_map/ff_grad/pallas_call | solution.py:474
  545.2 13.4 %ff_grad.3 = (bf16[4,144,1152]{2,1,0:T(8,128)(2,1)}, bf16[4,144,1152]{2,1,0:T(8,128)(2,1)}, bf16[4,144,1152]{2,1,0:T(8,128)(2,1)}, bf16[4,144,1152]{2,1,0:T(8,128)(2,1)}) custom-call(bf16[576,768]{1,0:T(8,128)(2,1)} %get-tuple-element.150.refs_0_, bf16[576,768]{1,0:T(8,128)(2,1)} %collective-permute-done.48.refs_1_, ...), custom_call_target="tpu_custom_call" | custom-call | flops 8153726976 | bytes 19464192 | tf_op jit(solution)/shard_map/ff_grad/pallas_call | solution.py:474
  562.9 12.7 %collective-permute-done.43 = bf16[4,144,1152]{2,1,0:T(8,128)(2,1)} collective-permute-done((bf16[4,144,1152]{2,1,0:T(8,128)(2,1)}, bf16[4,144,1152]{2,1,0:T(8,128)(2,1)}, u32[]{:S(2)}, u32[]{:S(2)}) %collective-permute-start.43) | collective-permute-done | bytes 1327136 | tf_op jit(solution)/shard_map/ppermute | solution.py:542
  575.5 2.7 add.409
  581.9 5.2 copy.40
  591.1 48.4 %collective-permute-done.39 = bf16[144,1152]{1,0:T(8,128)(2,1)} collective-permute-done((bf16[144,1152]{1,0:T(8,128)(2,1)}, bf16[144,1152]{1,0:T(8,128)(2,1)}, u32[]{:S(2)}, u32[]{:S(2)}) %collective-permute-start.39) | collective-permute-done | bytes 331808 | tf_op jit(solution)/shard_map/ppermute | solution.py:542
  645.6 2.0 add_add_fusion.3
  647.8 15.1 %collective-permute-done.50 = bf16[4,144,1152]{2,1,0:T(8,128)(2,1)} collective-permute-done((bf16[4,144,1152]{2,1,0:T(8,128)(2,1)}, bf16[4,144,1152]{2,1,0:T(8,128)(2,1)}, u32[]{:S(2)}, u32[]{:S(2)}) %collective-permute-start.50) | collective-permute-done | bytes 1327136 | tf_op jit(solution)/shard_map/ppermute | solution.py:542
  662.9 1.9 collective-permute-done.52
  667.0 2.5 collective-permute-start.46
  669.5 7.7 %collective-permute-done.53 = bf16[144,1152]{1,0:T(8,128)(2,1)S(1)} collective-permute-done((bf16[144,1152]{1,0:T(8,128)(2,1)S(1)}, bf16[144,1152]{1,0:T(8,128)(2,1)S(1)}, u32[]{:S(2)}, u32[]{:S(2)}) %collective-permute-start.53) | collective-permute-done | bytes 331808 | tf_op jit(solution)/shard_map/ppermute | solution.py:542
  677.3 2.2 collective-permute-start.54
  679.4 4.9 collective-permute-done.46
  684.3 2.2 collective-permute-start.47
  686.5 4.1 collective-permute-done.54
  690.7 2.9 collective-permute-start.55
  695.1 3.2 collective-permute-done.55
  (282 shorter events, 116.4 us)
Async XLA Ops:
  4.3 14.1 %collective-permute-start = (bf16[144,1152]{1,0:T(8,128)(2,1)}, bf16[144,1152]{1,0:T(8,128)(2,1)}, u32[]{:S(2)}, u32[]{:S(2)}) collective-permute-start(bf16[144,1152]{1,0:T(8,128)(2,1)} %get-tuple-element.148), channel_id=1, source_target_pairs={{0,8},{8,0},{1,9},{9,1},{2,10},{10,2},{3,11},{11,3},{4,12},{12,4},... | collective-permute-start | bytes 995336 | tf_op jit(solution)/shard_map/ppermute | solution.py:542
  8.4 12.8 %collective-permute-start.8 = (bf16[144,1152]{1,0:T(8,128)(2,1)}, bf16[144,1152]{1,0:T(8,128)(2,1)}, u32[]{:S(2)}, u32[]{:S(2)}) collective-permute-start(bf16[144,1152]{1,0:T(8,128)(2,1)} %get-tuple-element.169), channel_id=1, source_target_pairs={{0,1},{1,2},{2,3},{3,0},{4,5},{5,6},{6,7},{7,4},{8,9},{9,10},{10,1... | collective-permute-start | bytes 995336 | tf_op jit(solution)/shard_map/ppermute | solution.py:542
  10.0 18.4 %collective-permute-start.17 = (bf16[144,1152]{1,0:T(8,128)(2,1)}, bf16[144,1152]{1,0:T(8,128)(2,1)}, u32[]{:S(2)}, u32[]{:S(2)}) collective-permute-start(bf16[144,1152]{1,0:T(8,128)(2,1)} %get-tuple-element.191), channel_id=1, source_target_pairs={{0,1},{1,2},{2,3},{3,0},{4,5},{5,6},{6,7},{7,4},{8,9},{9,10},{10,1... | collective-permute-start | bytes 995336 | tf_op jit(solution)/shard_map/ppermute | solution.py:542
  18.3 301.9 %copy-start.35 = (pred[768]{0:T(1024)(128)(4,1)}, pred[768]{0:T(1024)(128)(4,1)S(1)}, u32[]{:S(2)}) copy-start(pred[768]{0:T(1024)(128)(4,1)S(1)} %iota_compare_fusion.6) | copy-start | bytes 2308
  19.5 38.0 %copy-start.29 = (bf16[288,1152]{1,0:T(8,128)(2,1)}, bf16[288,1152]{1,0:T(8,128)(2,1)S(1)}, u32[]{:S(2)}) copy-start(bf16[288,1152]{1,0:T(8,128)(2,1)S(1)} %pad_maximum_fusion.7.refs_3_) | copy-start | bytes 1990660
  19.5 38.8 %collective-permute-start.1 = (bf16[288,1152]{1,0:T(8,128)(2,1)S(1)}, bf16[288,1152]{1,0:T(8,128)(2,1)S(1)}, u32[]{:S(2)}, u32[]{:S(2)}) collective-permute-start(bf16[288,1152]{1,0:T(8,128)(2,1)S(1)} %pad_maximum_fusion.7.refs_3_), channel_id=1, source_target_pairs={{0,1},{1,2},{2,3},{3,0},{4,5},{5,6},{6,7},{7,4},{8,9},{9,10},{10,1... | collective-permute-start | bytes 1990664 | tf_op jit(solution)/shard_map/ppermute | solution.py:542
  22.4 65.7 %collective-permute-start.11 = (bf16[288,1152]{1,0:T(8,128)(2,1)S(1)}, bf16[288,1152]{1,0:T(8,128)(2,1)S(1)}, u32[]{:S(2)}, u32[]{:S(2)}) collective-permute-start(bf16[288,1152]{1,0:T(8,128)(2,1)S(1)} %pad_maximum_fusion.8), channel_id=1, source_target_pairs={{0,16},{16,0},{1,17},{17,1},{2,18},{18,2},{3,19},{19,3},{4,20},{20... | collective-permute-start | bytes 1990664 | tf_op jit(solution)/shard_map/ppermute | solution.py:542
  29.5 60.4 %collective-permute-start.20 = (bf16[288,1152]{1,0:T(8,128)(2,1)S(1)}, bf16[288,1152]{1,0:T(8,128)(2,1)S(1)}, u32[]{:S(2)}, u32[]{:S(2)}) collective-permute-start(bf16[288,1152]{1,0:T(8,128)(2,1)S(1)} %pad_maximum_fusion.10), channel_id=1, source_target_pairs={{0,16},{16,0},{1,17},{17,1},{2,18},{18,2},{3,19},{19,3},{4,20},{20... | collective-permute-start | bytes 1990664 | tf_op jit(solution)/shard_map/ppermute | solution.py:542
  31.1 18.5 %collective-permute-start.9 = (bf16[144,1152]{1,0:T(8,128)(2,1)}, bf16[144,1152]{1,0:T(8,128)(2,1)S(1)}, u32[]{:S(2)}, u32[]{:S(2)}) collective-permute-start(bf16[144,1152]{1,0:T(8,128)(2,1)} %collective-permute-done.8), channel_id=1, source_target_pairs={{0,1},{1,2},{2,3},{3,0},{4,5},{5,6},{6,7},{7,4},{8,9},{9,10},{10,1... | collective-permute-start | bytes 995336 | tf_op jit(solution)/shard_map/ppermute | solution.py:542
  31.1 25.6 %collective-permute-start.18 = (bf16[144,1152]{1,0:T(8,128)(2,1)}, bf16[144,1152]{1,0:T(8,128)(2,1)S(1)}, u32[]{:S(2)}, u32[]{:S(2)}) collective-permute-start(bf16[144,1152]{1,0:T(8,128)(2,1)} %collective-permute-done.17), channel_id=1, source_target_pairs={{0,1},{1,2},{2,3},{3,0},{4,5},{5,6},{6,7},{7,4},{8,9},{9,10},{10,1... | collective-permute-start | bytes 995336 | tf_op jit(solution)/shard_map/ppermute | solution.py:542
  49.6 14.2 %collective-permute-start.10 = (bf16[144,1152]{1,0:T(8,128)(2,1)S(1)}, bf16[144,1152]{1,0:T(8,128)(2,1)S(1)}, u32[]{:S(2)}, u32[]{:S(2)}) collective-permute-start(bf16[144,1152]{1,0:T(8,128)(2,1)S(1)} %collective-permute-done.9), channel_id=1, source_target_pairs={{0,1},{1,2},{2,3},{3,0},{4,5},{5,6},{6,7},{7,4},{8,9},{9,10},{10,1... | collective-permute-start | bytes 995336 | tf_op jit(solution)/shard_map/ppermute | solution.py:542
  56.7 12.8 %collective-permute-start.19 = (bf16[144,1152]{1,0:T(8,128)(2,1)S(1)}, bf16[144,1152]{1,0:T(8,128)(2,1)S(1)}, u32[]{:S(2)}, u32[]{:S(2)}) collective-permute-start(bf16[144,1152]{1,0:T(8,128)(2,1)S(1)} %collective-permute-done.18), channel_id=1, source_target_pairs={{0,1},{1,2},{2,3},{3,0},{4,5},{5,6},{6,7},{7,4},{8,9},{9,10},{10,1... | collective-permute-start | bytes 995336 | tf_op jit(solution)/shard_map/ppermute | solution.py:542
  58.3 47.2 %copy-start.10 = (bf16[288,1152]{1,0:T(8,128)(2,1)}, bf16[288,1152]{1,0:T(8,128)(2,1)S(1)}, u32[]{:S(2)}) copy-start(bf16[288,1152]{1,0:T(8,128)(2,1)S(1)} %collective-permute-done.1.refs_4_) | copy-start | bytes 1990660
  59.7 62.8 %collective-permute-start.5 = (bf16[576,1152]{1,0:T(8,128)(2,1)S(1)}, bf16[576,1152]{1,0:T(8,128)(2,1)S(1)}, u32[]{:S(2)}, u32[]{:S(2)}) collective-permute-start(bf16[576,1152]{1,0:T(8,128)(2,1)S(1)} %pad_maximum_fusion.3), channel_id=1, source_target_pairs={{0,16},{16,0},{1,17},{17,1},{2,18},{18,2},{3,19},{19,3},{4,20},{20... | collective-permute-start | bytes 3981320 | tf_op jit(solution)/shard_map/ppermute | solution.py:542
  63.9 42.5 %collective-permute-start.12 = (bf16[288,1152]{1,0:T(8,128)(2,1)S(1)}, bf16[288,1152]{1,0:T(8,128)(2,1)S(1)}, u32[]{:S(2)}, u32[]{:S(2)}) collective-permute-start(bf16[288,1152]{1,0:T(8,128)(2,1)S(1)} %pad_maximum_fusion.9), channel_id=1, source_target_pairs={{0,16},{16,0},{1,17},{17,1},{2,18},{18,2},{3,19},{19,3},{4,20},{20... | collective-permute-start | bytes 1990664 | tf_op jit(solution)/shard_map/ppermute | solution.py:542
  69.5 17.3 %collective-permute-start.2 = (bf16[288,1152]{1,0:T(8,128)(2,1)S(1)}, bf16[288,1152]{1,0:T(8,128)(2,1)S(1)}, u32[]{:S(2)}, u32[]{:S(2)}) collective-permute-start(bf16[288,1152]{1,0:T(8,128)(2,1)S(1)} %collective-permute-done.1.refs_4_), channel_id=1, source_target_pairs={{0,1},{1,2},{2,3},{3,0},{4,5},{5,6},{6,7},{7,4},{8,9},{9,10},{10,1... | collective-permute-start | bytes 1990664 | tf_op jit(solution)/shard_map/ppermute | solution.py:542
  70.7 35.7 %copy-start.14 = (bf16[576,1152]{1,0:T(8,128)(2,1)}, bf16[576,1152]{1,0:T(8,128)(2,1)S(1)}, u32[]{:S(2)}) copy-start(bf16[576,1152]{1,0:T(8,128)(2,1)S(1)} %pad_maximum_fusion.6.refs_4_) | copy-start | bytes 3981316
  86.9 16.9 %collective-permute-start.3 = (bf16[288,1152]{1,0:T(8,128)(2,1)S(1)}, bf16[288,1152]{1,0:T(8,128)(2,1)S(1)}, u32[]{:S(2)}, u32[]{:S(2)}) collective-permute-start(bf16[288,1152]{1,0:T(8,128)(2,1)S(1)} %collective-permute-done.2.refs_5_), channel_id=1, source_target_pairs={{0,1},{1,2},{2,3},{3,0},{4,5},{5,6},{6,7},{7,4},{8,9},{9,10},{10,1... | collective-permute-start | bytes 1990664 | tf_op jit(solution)/shard_map/ppermute | solution.py:542
  88.1 58.7 %collective-permute-start.13 = (bf16[576,1152]{1,0:T(8,128)(2,1)S(1)}, bf16[576,1152]{1,0:T(8,128)(2,1)S(1)}, u32[]{:S(2)}, u32[]{:S(2)}) collective-permute-start(bf16[576,1152]{1,0:T(8,128)(2,1)S(1)} %pad_maximum_fusion.5.refs_3_), channel_id=1, source_target_pairs={{0,8},{8,0},{1,9},{9,1},{2,10},{10,2},{3,11},{11,3},{4,12},{12,4},... | collective-permute-start | bytes 3981320 | tf_op jit(solution)/shard_map/ppermute | solution.py:542
  89.9 30.4 %collective-permute-start.21 = (bf16[288,1152]{1,0:T(8,128)(2,1)S(1)}, bf16[288,1152]{1,0:T(8,128)(2,1)S(1)}, u32[]{:S(2)}, u32[]{:S(2)}) collective-permute-start(bf16[288,1152]{1,0:T(8,128)(2,1)S(1)} %pad_maximum_fusion.11), channel_id=1, source_target_pairs={{0,16},{16,0},{1,17},{17,1},{2,18},{18,2},{3,19},{19,3},{4,20},{20... | collective-permute-start | bytes 1990664 | tf_op jit(solution)/shard_map/ppermute | solution.py:542
  103.9 41.1 %collective-permute-start.6 = (bf16[576,1152]{1,0:T(8,128)(2,1)S(1)}, bf16[576,1152]{1,0:T(8,128)(2,1)S(1)}, u32[]{:S(2)}, u32[]{:S(2)}) collective-permute-start(bf16[576,1152]{1,0:T(8,128)(2,1)S(1)} %pad_maximum_fusion.4), channel_id=1, source_target_pairs={{0,16},{16,0},{1,17},{17,1},{2,18},{18,2},{3,19},{19,3},{4,20},{20... | collective-permute-start | bytes 3981320 | tf_op jit(solution)/shard_map/ppermute | solution.py:542
  106.4 72.6 %collective-permute-start.22 = (bf16[576,1152]{1,0:T(8,128)(2,1)S(1)}, bf16[576,1152]{1,0:T(8,128)(2,1)S(1)}, u32[]{:S(2)}, u32[]{:S(2)}) collective-permute-start(bf16[576,1152]{1,0:T(8,128)(2,1)S(1)} %pad_maximum_fusion.6.refs_4_), channel_id=1, source_target_pairs={{0,8},{8,0},{1,9},{9,1},{2,10},{10,2},{3,11},{11,3},{4,12},{12,4},... | collective-permute-start | bytes 3981320 | tf_op jit(solution)/shard_map/ppermute | solution.py:542
  107.9 38.9 %copy-start.31 = (bf16[576,1152]{1,0:T(8,128)(2,1)}, bf16[576,1152]{1,0:T(8,128)(2,1)S(1)}, u32[]{:S(2)}) copy-start(bf16[576,1152]{1,0:T(8,128)(2,1)S(1)} %get-tuple-element.163.refs_4_) | copy-start | bytes 3981316
  120.2 56.8 %collective-permute-start.14 = (bf16[576,1152]{1,0:T(8,128)(2,1)S(1)}, bf16[576,1152]{1,0:T(8,128)(2,1)S(1)}, u32[]{:S(2)}, u32[]{:S(2)}) collective-permute-start(bf16[576,1152]{1,0:T(8,128)(2,1)S(1)} %get-tuple-element.163.refs_4_), channel_id=1, source_target_pairs={{0,8},{8,0},{1,9},{9,1},{2,10},{10,2},{3,11},{11,3},{4,12},{12,4},... | collective-permute-start | bytes 3981320 | tf_op jit(solution)/shard_map/ppermute | solution.py:542
  122.5 79.8 %collective-permute-start.23 = (bf16[576,1152]{1,0:T(8,128)(2,1)S(1)}, bf16[576,1152]{1,0:T(8,128)(2,1)S(1)}, u32[]{:S(2)}, u32[]{:S(2)}) collective-permute-start(bf16[576,1152]{1,0:T(8,128)(2,1)S(1)} %get-tuple-element.159.refs_5_), channel_id=1, source_target_pairs={{0,8},{8,0},{1,9},{9,1},{2,10},{10,2},{3,11},{11,3},{4,12},{12,4},... | collective-permute-start | bytes 3981320 | tf_op jit(solution)/shard_map/ppermute | solution.py:542
  145.0 79.4 %collective-permute-start.4 = (bf16[1152,1152]{1,0:T(8,128)(2,1)}, bf16[1152,1152]{1,0:T(8,128)(2,1)}, u32[]{:S(2)}, u32[]{:S(2)}) collective-permute-start(bf16[1152,1152]{1,0:T(8,128)(2,1)} %constant_dynamic-update-slice_fusion), channel_id=1, source_target_pairs={{0,4},{4,0},{1,5},{5,1},{2,6},{6,2},{3,7},{7,3},{8,12},{12,8},{9,1... | collective-permute-start | bytes 7962632 | tf_op jit(solution)/shard_map/ppermute | solution.py:542
  146.8 32.2 %copy-start.16 = (bf16[576,1152]{1,0:T(8,128)(2,1)}, bf16[576,1152]{1,0:T(8,128)(2,1)S(1)}, u32[]{:S(2)}) copy-start(bf16[576,1152]{1,0:T(8,128)(2,1)S(1)} %collective-permute-done.13.refs_5_) | copy-start | bytes 3981316
  146.8 77.7 %collective-permute-start.7 = (bf16[1152,1152]{1,0:T(8,128)(2,1)}, bf16[1152,1152]{1,0:T(8,128)(2,1)}, u32[]{:S(2)}, u32[]{:S(2)}) collective-permute-start(bf16[1152,1152]{1,0:T(8,128)(2,1)} %pad_maximum_fusion), channel_id=1, source_target_pairs={{0,4},{4,0},{1,5},{5,1},{2,6},{6,2},{3,7},{7,3},{8,12},{12,8},{9,1... | collective-permute-start | bytes 7962632 | tf_op jit(solution)/shard_map/ppermute | solution.py:542
  177.1 73.8 %collective-permute-start.15 = (bf16[1152,1152]{1,0:T(8,128)(2,1)}, bf16[1152,1152]{1,0:T(8,128)(2,1)}, u32[]{:S(2)}, u32[]{:S(2)}) collective-permute-start(bf16[1152,1152]{1,0:T(8,128)(2,1)} %get-tuple-element.162), channel_id=1, source_target_pairs={{0,4},{4,0},{1,5},{5,1},{2,6},{6,2},{3,7},{7,3},{8,12},{12,8},{9,1... | collective-permute-start | bytes 7962632 | tf_op jit(solution)/shard_map/ppermute | solution.py:542
  179.1 93.0 %collective-permute-start.24 = (bf16[1152,1152]{1,0:T(8,128)(2,1)}, bf16[1152,1152]{1,0:T(8,128)(2,1)}, u32[]{:S(2)}, u32[]{:S(2)}) collective-permute-start(bf16[1152,1152]{1,0:T(8,128)(2,1)} %get-tuple-element.158), channel_id=1, source_target_pairs={{0,4},{4,0},{1,5},{5,1},{2,6},{6,2},{3,7},{7,3},{8,12},{12,8},{9,1... | collective-permute-start | bytes 7962632 | tf_op jit(solution)/shard_map/ppermute | solution.py:542
  202.3 48.7 %collective-permute-start.16 = (bf16[1152,1152]{1,0:T(8,128)(2,1)}, bf16[1152,1152]{1,0:T(8,128)(2,1)}, u32[]{:S(2)}, u32[]{:S(2)}) collective-permute-start(bf16[1152,1152]{1,0:T(8,128)(2,1)} %pad_maximum_fusion.1), channel_id=1, source_target_pairs={{0,4},{4,0},{1,5},{5,1},{2,6},{6,2},{3,7},{7,3},{8,12},{12,8},{9,1... | collective-permute-start | bytes 7962632 | tf_op jit(solution)/shard_map/ppermute | solution.py:542
  224.4 47.7 %collective-permute-start.25 = (bf16[1152,1152]{1,0:T(8,128)(2,1)}, bf16[1152,1152]{1,0:T(8,128)(2,1)}, u32[]{:S(2)}, u32[]{:S(2)}) collective-permute-start(bf16[1152,1152]{1,0:T(8,128)(2,1)} %pad_maximum_fusion.2), channel_id=1, source_target_pairs={{0,4},{4,0},{1,5},{5,1},{2,6},{6,2},{3,7},{7,3},{8,12},{12,8},{9,1... | collective-permute-start | bytes 7962632 | tf_op jit(solution)/shard_map/ppermute | solution.py:542
  356.2 43.6 %collective-permute-start.32 = (bf16[2,768,864]{1,2,0:T(8,128)(2,1)}, bf16[2,768,864]{1,2,0:T(8,128)(2,1)}, u32[]{:S(2)}, u32[]{:S(2)}) collective-permute-start(bf16[2,768,864]{1,2,0:T(8,128)(2,1)} %copy.36), channel_id=1, source_target_pairs={{0,4},{4,0},{1,5},{5,1},{2,6},{6,2},{3,7},{7,3},{8,12},{12,8},{9,1... | collective-permute-start | bytes 7962632 | tf_op jit(solution)/shard_map/ppermute | solution.py:542
  359.9 44.3 %collective-permute-start.31 = (bf16[1152,768]{1,0:T(8,128)(2,1)}, bf16[1152,768]{1,0:T(8,128)(2,1)}, u32[]{:S(2)}, u32[]{:S(2)}) collective-permute-start(bf16[1152,768]{1,0:T(8,128)(2,1)} %turn.4.refs_0_), channel_id=1, source_target_pairs={{0,4},{4,0},{1,5},{5,1},{2,6},{6,2},{3,7},{7,3},{8,12},{12,8},{9,1... | collective-permute-start | bytes 5308424 | tf_op jit(solution)/shard_map/ppermute | solution.py:542
  363.2 41.0 %collective-permute-start.33 = (bf16[1152,768]{1,0:T(8,128)(2,1)}, bf16[1152,768]{1,0:T(8,128)(2,1)}, u32[]{:S(2)}, u32[]{:S(2)}) collective-permute-start(bf16[1152,768]{1,0:T(8,128)(2,1)} %turn.5.refs_4_), channel_id=1, source_target_pairs={{0,4},{4,0},{1,5},{5,1},{2,6},{6,2},{3,7},{7,3},{8,12},{12,8},{9,1... | collective-permute-start | bytes 5308424 | tf_op jit(solution)/shard_map/ppermute | solution.py:542
  367.6 161.9 %collective-permute-start.41 = (bf16[768,4608]{1,0:T(8,128)(2,1)}, bf16[768,4608]{1,0:T(8,128)(2,1)}, u32[]{:S(2)}, u32[]{:S(2)}) collective-permute-start(bf16[768,4608]{1,0:T(8,128)(2,1)} %get-tuple-element.51.gu.refs_2_), channel_id=1, source_target_pairs={{0,4},{4,0},{1,5},{5,1},{2,6},{6,2},{3,7},{7,3},{8,12},{12,8},{9,1... | collective-permute-start | bytes 21233672 | tf_op jit(solution)/shard_map/ppermute | solution.py:542
  370.1 27.3 %collective-permute-start.34 = (bf16[2,768,288]{1,2,0:T(8,128)(2,1)}, bf16[2,768,288]{1,2,0:T(8,128)(2,1)}, u32[]{:S(2)}, u32[]{:S(2)}) collective-permute-start(bf16[2,768,288]{1,2,0:T(8,128)(2,1)} %copy.37), channel_id=1, source_target_pairs={{0,4},{4,0},{1,5},{5,1},{2,6},{6,2},{3,7},{7,3},{8,12},{12,8},{9,1... | collective-permute-start | bytes 2654216 | tf_op jit(solution)/shard_map/ppermute | solution.py:542
  397.4 147.8 %collective-permute-start.49 = (bf16[768,4608]{1,0:T(8,128)(2,1)}, bf16[768,4608]{1,0:T(8,128)(2,1)}, u32[]{:S(2)}, u32[]{:S(2)}) collective-permute-start(bf16[768,4608]{1,0:T(8,128)(2,1)} %get-tuple-element.48.refs_2_), channel_id=1, source_target_pairs={{0,4},{4,0},{1,5},{5,1},{2,6},{6,2},{3,7},{7,3},{8,12},{12,8},{9,1... | collective-permute-start | bytes 21233672 | tf_op jit(solution)/shard_map/ppermute | solution.py:542
  422.2 62.6 %collective-permute-start.35 = (bf16[4,2,144,1152]{3,2,1,0:T(8,128)(2,1)}, bf16[4,2,144,1152]{3,2,1,0:T(8,128)(2,1)}, u32[]{:S(2)}, u32[]{:S(2)}) collective-permute-start(bf16[4,2,144,1152]{3,2,1,0:T(8,128)(2,1)} %get-tuple-element.69), channel_id=1, source_target_pairs={{0,16},{16,0},{1,17},{17,1},{2,18},{18,2},{3,19},{19,3},{4,20},{20... | collective-permute-start | bytes 7962632 | tf_op jit(solution)/shard_map/ppermute | solution.py:542
  454.2 29.4 %collective-permute-start.26 = (f32[112,128]{1,0:T(8,128)S(1)}, f32[112,128]{1,0:T(8,128)S(1)}, u32[]{:S(2)}, u32[]{:S(2)}) collective-permute-start(f32[112,128]{1,0:T(8,128)S(1)} %pad_bitcast_fusion), channel_id=1, source_target_pairs={{0,16},{16,0},{1,17},{17,1},{2,18},{18,2},{3,19},{19,3},{4,20},{20... | collective-permute-start | bytes 172040 | tf_op jit(solution)/shard_map/ppermute | solution.py:553
  483.6 9.2 %collective-permute-start.27 = (f32[112,128]{1,0:T(8,128)S(1)}, f32[112,128]{1,0:T(8,128)S(1)}, u32[]{:S(2)}, u32[]{:S(2)}) collective-permute-start(f32[112,128]{1,0:T(8,128)S(1)} %fusion.33), channel_id=1, source_target_pairs={{0,8},{8,0},{1,9},{9,1},{2,10},{10,2},{3,11},{11,3},{4,12},{12,4},... | collective-permute-start | bytes 172040 | tf_op jit(solution)/shard_map/ppermute | solution.py:553
  488.1 35.9 %copy-start.5 = (bf16[4,2,144,1152]{3,2,1,0:T(8,128)(2,1)}, bf16[4,2,144,1152]{3,2,1,0:T(8,128)(2,1)S(1)}, u32[]{:S(2)}) copy-start(bf16[4,2,144,1152]{3,2,1,0:T(8,128)(2,1)S(1)} %add.391) | copy-start | bytes 7962628
  488.2 17.9 %collective-permute-start.36 = (bf16[2,144,1152]{2,1,0:T(8,128)(2,1)S(1)}, bf16[2,144,1152]{2,1,0:T(8,128)(2,1)S(1)}, u32[]{:S(2)}, u32[]{:S(2)}) collective-permute-start(bf16[2,144,1152]{2,1,0:T(8,128)(2,1)S(1)} %slice_bitcast_fusion.3), channel_id=1, source_target_pairs={{0,3},{1,0},{2,1},{3,2},{4,7},{5,4},{6,5},{7,6},{8,11},{9,8},{10,9... | collective-permute-start | bytes 1990664 | tf_op jit(solution)/shard_map/ppermute | solution.py:542
  492.8 1.3 collective-permute-start.28
  492.9 32.0 %collective-permute-start.40 = (bf16[576,768]{1,0:T(8,128)(2,1)S(1)}, bf16[576,768]{1,0:T(8,128)(2,1)S(1)}, u32[]{:S(2)}, u32[]{:S(2)}) collective-permute-start(bf16[576,768]{1,0:T(8,128)(2,1)S(1)} %get-tuple-element.151), channel_id=1, source_target_pairs={{0,4},{4,0},{1,5},{5,1},{2,6},{6,2},{3,7},{7,3},{8,12},{12,8},{9,1... | collective-permute-start | bytes 2654216 | tf_op jit(solution)/shard_map/ppermute | solution.py:542
  494.2 18.5 %collective-permute-start.29 = (f32[112,128]{1,0:T(8,128)S(1)}, f32[112,128]{1,0:T(8,128)S(1)}, u32[]{:S(2)}, u32[]{:S(2)}) collective-permute-start(f32[112,128]{1,0:T(8,128)S(1)} %add.388), channel_id=1, source_target_pairs={{0,1},{1,0},{2,3},{3,2},{4,5},{5,4},{6,7},{7,6},{8,9},{9,8},{10,11... | collective-permute-start | bytes 172040 | tf_op jit(solution)/shard_map/ppermute | solution.py:553
  506.2 17.1 %collective-permute-start.37 = (bf16[2,144,1152]{2,1,0:T(8,128)(2,1)S(1)}, bf16[2,144,1152]{2,1,0:T(8,128)(2,1)S(1)}, u32[]{:S(2)}, u32[]{:S(2)}) collective-permute-start(bf16[2,144,1152]{2,1,0:T(8,128)(2,1)S(1)} %fusion.18), channel_id=1, source_target_pairs={{0,3},{1,0},{2,1},{3,2},{4,7},{5,4},{6,5},{7,6},{8,11},{9,8},{10,9... | collective-permute-start | bytes 1990664 | tf_op jit(solution)/shard_map/ppermute | solution.py:542
  512.7 31.4 %collective-permute-start.48 = (bf16[576,768]{1,0:T(8,128)(2,1)}, bf16[576,768]{1,0:T(8,128)(2,1)}, u32[]{:S(2)}, u32[]{:S(2)}) collective-permute-start(bf16[576,768]{1,0:T(8,128)(2,1)} %get-tuple-element.149), channel_id=1, source_target_pairs={{0,4},{4,0},{1,5},{5,1},{2,6},{6,2},{3,7},{7,3},{8,12},{12,8},{9,1... | collective-permute-start | bytes 2654216 | tf_op jit(solution)/shard_map/ppermute | solution.py:542
  523.3 63.7 %collective-permute-start.30 = (f32[112,128]{1,0:T(8,128)S(1)}, f32[112,128]{1,0:T(8,128)S(1)}, u32[]{:S(2)}, u32[]{:S(2)}) collective-permute-start(f32[112,128]{1,0:T(8,128)S(1)} %add.389), channel_id=1, source_target_pairs={{0,2},{1,3},{2,0},{3,1},{4,6},{5,7},{6,4},{7,5},{8,10},{9,11},{10,... | collective-permute-start | bytes 172040 | tf_op jit(solution)/shard_map/ppermute | solution.py:553
  525.9 33.8 %collective-permute-start.38 = (bf16[2,144,1152]{2,1,0:T(8,128)(2,1)}, bf16[2,144,1152]{2,1,0:T(8,128)(2,1)}, u32[]{:S(2)}, u32[]{:S(2)}) collective-permute-start(bf16[2,144,1152]{2,1,0:T(8,128)(2,1)} %fusion.17), channel_id=1, source_target_pairs={{0,3},{1,0},{2,1},{3,2},{4,7},{5,4},{6,5},{7,6},{8,11},{9,8},{10,9... | collective-permute-start | bytes 1990664 | tf_op jit(solution)/shard_map/ppermute | solution.py:542
  543.2 32.4 %collective-permute-start.43 = (bf16[4,144,1152]{2,1,0:T(8,128)(2,1)}, bf16[4,144,1152]{2,1,0:T(8,128)(2,1)}, u32[]{:S(2)}, u32[]{:S(2)}) collective-permute-start(bf16[4,144,1152]{2,1,0:T(8,128)(2,1)} %get-tuple-element.73), channel_id=1, source_target_pairs={{0,8},{8,0},{1,9},{9,1},{2,10},{10,2},{3,11},{11,3},{4,12},{12,4},... | collective-permute-start | bytes 3981320 | tf_op jit(solution)/shard_map/ppermute | solution.py:542
  544.1 101.5 %collective-permute-start.42 = (bf16[4,144,1152]{2,1,0:T(8,128)(2,1)}, bf16[4,144,1152]{2,1,0:T(8,128)(2,1)}, u32[]{:S(2)}, u32[]{:S(2)}) collective-permute-start(bf16[4,144,1152]{2,1,0:T(8,128)(2,1)} %get-tuple-element.71), channel_id=1, source_target_pairs={{0,8},{8,0},{1,9},{9,1},{2,10},{10,2},{3,11},{11,3},{4,12},{12,4},... | collective-permute-start | bytes 3981320 | tf_op jit(solution)/shard_map/ppermute | solution.py:542
  558.6 83.4 %collective-permute-start.51 = (bf16[4,144,1152]{2,1,0:T(8,128)(2,1)}, bf16[4,144,1152]{2,1,0:T(8,128)(2,1)}, u32[]{:S(2)}, u32[]{:S(2)}) collective-permute-start(bf16[4,144,1152]{2,1,0:T(8,128)(2,1)} %get-tuple-element.77), channel_id=1, source_target_pairs={{0,8},{8,0},{1,9},{9,1},{2,10},{10,2},{3,11},{11,3},{4,12},{12,4},... | collective-permute-start | bytes 3981320 | tf_op jit(solution)/shard_map/ppermute | solution.py:542
  561.8 77.7 %collective-permute-start.39 = (bf16[144,1152]{1,0:T(8,128)(2,1)}, bf16[144,1152]{1,0:T(8,128)(2,1)}, u32[]{:S(2)}, u32[]{:S(2)}) collective-permute-start(bf16[144,1152]{1,0:T(8,128)(2,1)} %slice_bitcast_fusion.12), channel_id=1, source_target_pairs={{0,8},{8,0},{1,9},{9,1},{2,10},{10,2},{3,11},{11,3},{4,12},{12,4},... | collective-permute-start | bytes 995336 | tf_op jit(solution)/shard_map/ppermute | solution.py:542
  578.3 67.3 %collective-permute-start.44 = (bf16[4,144,1152]{2,1,0:T(8,128)(2,1)}, bf16[4,144,1152]{2,1,0:T(8,128)(2,1)}, u32[]{:S(2)}, u32[]{:S(2)}) collective-permute-start(bf16[4,144,1152]{2,1,0:T(8,128)(2,1)} %add.409), channel_id=1, source_target_pairs={{0,16},{16,0},{1,17},{17,1},{2,18},{18,2},{3,19},{19,3},{4,20},{20... | collective-permute-start | bytes 3981320 | tf_op jit(solution)/shard_map/ppermute | solution.py:542
  587.1 55.0 %copy-start.24 = (bf16[4,144,1152]{2,1,0:T(8,128)(2,1)S(1)}, bf16[4,144,1152]{2,1,0:T(8,128)(2,1)}, u32[]{:S(2)}) copy-start(bf16[4,144,1152]{2,1,0:T(8,128)(2,1)} %get-tuple-element.76) | copy-start | bytes 3981316
  589.6 73.3 %collective-permute-start.50 = (bf16[4,144,1152]{2,1,0:T(8,128)(2,1)}, bf16[4,144,1152]{2,1,0:T(8,128)(2,1)}, u32[]{:S(2)}, u32[]{:S(2)}) collective-permute-start(bf16[4,144,1152]{2,1,0:T(8,128)(2,1)} %get-tuple-element.75), channel_id=1, source_target_pairs={{0,8},{8,0},{1,9},{9,1},{2,10},{10,2},{3,11},{11,3},{4,12},{12,4},... | collective-permute-start | bytes 3981320 | tf_op jit(solution)/shard_map/ppermute | solution.py:542
  643.7 21.1 %collective-permute-start.52 = (bf16[4,144,1152]{2,1,0:T(8,128)(2,1)S(1)}, bf16[4,144,1152]{2,1,0:T(8,128)(2,1)S(1)}, u32[]{:S(2)}, u32[]{:S(2)}) collective-permute-start(bf16[4,144,1152]{2,1,0:T(8,128)(2,1)S(1)} %add.415), channel_id=1, source_target_pairs={{0,16},{16,0},{1,17},{17,1},{2,18},{18,2},{3,19},{19,3},{4,20},{20... | collective-permute-start | bytes 3981320 | tf_op jit(solution)/shard_map/ppermute | solution.py:542
  647.7 19.3 %collective-permute-start.45 = (bf16[144,1152]{1,0:T(8,128)(2,1)S(1)}, bf16[144,1152]{1,0:T(8,128)(2,1)S(1)}, u32[]{:S(2)}, u32[]{:S(2)}) collective-permute-start(bf16[144,1152]{1,0:T(8,128)(2,1)S(1)} %get-tuple-element.156), channel_id=1, source_target_pairs={{0,3},{1,0},{2,1},{3,2},{4,7},{5,4},{6,5},{7,6},{8,11},{9,8},{10,9... | collective-permute-start | bytes 995336 | tf_op jit(solution)/shard_map/ppermute | solution.py:542
  666.4 10.8 %collective-permute-start.53 = (bf16[144,1152]{1,0:T(8,128)(2,1)S(1)}, bf16[144,1152]{1,0:T(8,128)(2,1)S(1)}, u32[]{:S(2)}, u32[]{:S(2)}) collective-permute-start(bf16[144,1152]{1,0:T(8,128)(2,1)S(1)} %get-tuple-element.154), channel_id=1, source_target_pairs={{0,3},{1,0},{2,1},{3,2},{4,7},{5,4},{6,5},{7,6},{8,11},{9,8},{10,9... | collective-permute-start | bytes 995336 | tf_op jit(solution)/shard_map/ppermute | solution.py:542
  667.0 17.3 %collective-permute-start.46 = (bf16[144,1152]{1,0:T(8,128)(2,1)S(1)}, bf16[144,1152]{1,0:T(8,128)(2,1)S(1)}, u32[]{:S(2)}, u32[]{:S(2)}) collective-permute-start(bf16[144,1152]{1,0:T(8,128)(2,1)S(1)} %fusion.23), channel_id=1, source_target_pairs={{0,3},{1,0},{2,1},{3,2},{4,7},{5,4},{6,5},{7,6},{8,11},{9,8},{10,9... | collective-permute-start | bytes 995336 | tf_op jit(solution)/shard_map/ppermute | solution.py:542
  677.3 13.4 %collective-permute-start.54 = (bf16[144,1152]{1,0:T(8,128)(2,1)S(1)}, bf16[144,1152]{1,0:T(8,128)(2,1)S(1)}, u32[]{:S(2)}, u32[]{:S(2)}) collective-permute-start(bf16[144,1152]{1,0:T(8,128)(2,1)S(1)} %fusion.20), channel_id=1, source_target_pairs={{0,3},{1,0},{2,1},{3,2},{4,7},{5,4},{6,5},{7,6},{8,11},{9,8},{10,9... | collective-permute-start | bytes 995336 | tf_op jit(solution)/shard_map/ppermute | solution.py:542
  684.3 9.9 %collective-permute-start.47 = (bf16[144,1152]{1,0:T(8,128)(2,1)S(1)}, bf16[144,1152]{1,0:T(8,128)(2,1)S(1)}, u32[]{:S(2)}, u32[]{:S(2)}) collective-permute-start(bf16[144,1152]{1,0:T(8,128)(2,1)S(1)} %fusion.22), channel_id=1, source_target_pairs={{0,3},{1,0},{2,1},{3,2},{4,7},{5,4},{6,5},{7,6},{8,11},{9,8},{10,9... | collective-permute-start | bytes 995336 | tf_op jit(solution)/shard_map/ppermute | solution.py:542
  690.7 7.6 %collective-permute-start.55 = (bf16[144,1152]{1,0:T(8,128)(2,1)S(1)}, bf16[144,1152]{1,0:T(8,128)(2,1)S(1)}, u32[]{:S(2)}, u32[]{:S(2)}) collective-permute-start(bf16[144,1152]{1,0:T(8,128)(2,1)S(1)} %fusion.19), channel_id=1, source_target_pairs={{0,3},{1,0},{2,1},{3,2},{4,7},{5,4},{6,5},{7,6},{8,11},{9,8},{10,9... | collective-permute-start | bytes 995336 | tf_op jit(solution)/shard_map/ppermute | solution.py:542
  (36 other events, 448.3 us)

commit v2 on v1

v2 whole, which is shorter than its diff:
```python
import functools
import math

import jax
import jax.numpy as jnp
from jax import lax
from jax.experimental import pallas as pl
from jax.experimental.pallas import tpu as pltpu
from jax.sharding import PartitionSpec as P

HEAD_DIM = 72
GROUP_HEADS = 4
PAD = 768
EPS = 1e-06
VMEM_BYTES = 60 * 1024 * 1024
BF16 = jnp.bfloat16
F32 = jnp.float32
LOG2E = math.log2(math.e)


def nn(a, b):
    return lax.dot_general(a, b, (((1,), (0,)), ((), ())), preferred_element_type=F32)


def nt(a, b):
    return lax.dot_general(a, b, (((1,), (1,)), ((), ())), preferred_element_type=F32)


def tn(a, b):
    return lax.dot_general(a, b, (((0,), (0,)), ((), ())), preferred_element_type=F32)


def params(**kw):
    return pltpu.CompilerParams(vmem_limit_bytes=VMEM_BYTES, **kw)


def cost(flops, bytes_, scale=64):
    return pl.CostEstimate(
        flops=int(flops * scale), bytes_accessed=int(bytes_ * scale), transcendentals=0
    )


def whole(shape):
    zeros = (0,) * len(shape)
    return pl.BlockSpec(shape, lambda *_: zeros)


class Plan:
    def __init__(self, entries, columns):
        self.entries = entries
        self.columns = columns

    def copies(self, slot, pieces, table, dst, sems):
        for number, (piece, src, rows, to, entry, inside, column) in enumerate(self.entries):
            if to != slot:
                continue
            row = pl.multiple_of(table[entry] + inside, 16)
            yield pltpu.make_async_copy(
                pieces[piece].at[pl.ds(src, rows), :],
                dst.at[pl.ds(row, rows), pl.ds(column, self.columns)],
                sems.at[number],
            )


class ZonePlan:
    def __init__(self, slots, rows, columns):
        self.entries = range(slots)
        self.rows = rows
        self.columns = columns

    def copies(self, slot, pieces, table, dst, sems):
        row = pl.multiple_of(table[slot], 16)
        yield pltpu.make_async_copy(
            pieces[0].at[pl.ds(row, self.rows), :],
            dst.at[:, pl.ds(slot * self.columns, self.columns)],
            sems.at[slot],
        )


def masked_tail(values, low, seq):
    tail = values[low:]
    rows = lax.broadcasted_iota(jnp.int32, tail.shape, 0)
    return jnp.where(rows < seq - low, tail, -1e30)


def attn_fwd_kernel(plan, pieces_total, has_acc, seq, *refs):
    table, x, bias = refs[:3]
    pieces = refs[3 : 3 + pieces_total]
    rest = refs[3 + pieces_total :]
    if has_acc:
        acc_in, rest = rest[0], rest[1:]
    proj, mixed, lse, acc, w, mixed_t, sems = rest
    width = GROUP_HEADS * HEAD_DIM
    keys = -(-seq // 16) * 16
    low = seq // 8 * 8
    scale = HEAD_DIM**-0.5 * LOG2E

    for c in plan.copies(0, pieces, table, w, sems):
        c.start()
    for c in plan.copies(0, pieces, table, w, sems):
        c.wait()

    proj[...] = (nn(x[...], w[:, 0 : 3 * width]) + bias[...]).astype(BF16)
    for h in range(GROUP_HEADS):
        q = proj[:, h * HEAD_DIM : (h + 1) * HEAD_DIM]
        k = proj[0:keys, width + h * HEAD_DIM : width + (h + 1) * HEAD_DIM]
        v = proj[0:keys, 2 * width + h * HEAD_DIM : 2 * width + (h + 1) * HEAD_DIM]
        s = nt(k, q)
        tail = masked_tail(s, low, seq)
        top = jnp.maximum(
            jnp.max(s[0:low], axis=0, keepdims=True), jnp.max(tail, axis=0, keepdims=True)
        )
        shift = top * scale
        p = jnp.exp2(jnp.concatenate([s[0:low], tail], axis=0) * scale - shift)
        total = jnp.sum(p, axis=0, keepdims=True)
        mixed_t[h * HEAD_DIM : (h + 1) * HEAD_DIM, :] = tn(v, p.astype(BF16)) / total
        lse[h : h + 1, :] = shift + jnp.log2(total)
    mixed[...] = mixed_t[...].T.astype(BF16)
    part = nt(mixed[...], w[:, 3 * width : 4 * width])
    acc[...] = part + acc_in[...] if has_acc else part


def attn_fwd(table, x, bias, pieces, plan, acc_in, seq):
    d = x.shape[1]
    gw = plan.columns
    width = GROUP_HEADS * HEAD_DIM
    has_acc = acc_in is not None
    vmem = pl.BlockSpec(memory_space=pltpu.VMEM)
    return pl.pallas_call(
        functools.partial(attn_fwd_kernel, plan, len(pieces), has_acc, seq),
        in_specs=[
            pl.BlockSpec(memory_space=pltpu.SMEM),
            vmem,
            vmem,
            *[pl.BlockSpec(memory_space=pl.ANY) for _ in pieces],
            *([vmem] if has_acc else []),
        ],
        out_specs=[vmem] * 5,
        out_shape=[
            jax.ShapeDtypeStruct((PAD, 3 * width), BF16),
            jax.ShapeDtypeStruct((PAD, width), BF16),
            jax.ShapeDtypeStruct((8, PAD), F32),
            jax.ShapeDtypeStruct((PAD, d), F32),
            jax.ShapeDtypeStruct((d, gw), BF16),
        ],
        scratch_shapes=[
            pltpu.VMEM((width, PAD), F32),
            pltpu.SemaphoreType.DMA((len(plan.entries),)),
        ],
        compiler_params=params(),
        cost_estimate=cost(
            2 * PAD * (d * 4 * width + 8 * PAD * 256), d * gw * 4 + PAD * d * 8, 0.05),
        name="attn_fwd",
    )(table, x, bias, *pieces, *([acc_in] if has_acc else []))


def attn_bwd_kernel(has_acc, seq, *refs):
    proj, mixed, lse, ga, w = refs[:5]
    rest = refs[5:]
    if has_acc:
        acc_in, rest = rest[0], rest[1:]
    grads, acc, sums, gm, dq_t = rest
    width = GROUP_HEADS * HEAD_DIM
    keys = -(-seq // 16) * 16
    low = seq // 8 * 8
    factor = HEAD_DIM**-0.5
    scale = factor * LOG2E
    gm[...] = nn(ga[...], w[:, 3 * width : 4 * width]).astype(BF16)
    for h in range(GROUP_HEADS):
        sl = slice(h * HEAD_DIM, (h + 1) * HEAD_DIM)
        q = proj[:, h * HEAD_DIM : (h + 1) * HEAD_DIM]
        k = proj[0:keys, width + h * HEAD_DIM : width + (h + 1) * HEAD_DIM]
        v = proj[0:keys, 2 * width + h * HEAD_DIM : 2 * width + (h + 1) * HEAD_DIM]
        do = gm[:, sl]
        e = nt(k, q) * scale - lse[h : h + 1, :]
        p = jnp.exp2(jnp.concatenate([e[0:low], masked_tail(e, low, seq)], axis=0))
        dp = nt(v, do)
        delta = jnp.sum(p * dp, axis=0, keepdims=True)
        ds = (p * (dp - delta)).astype(BF16)
        dv = nn(p.astype(BF16), do)
        dk = nn(ds, q)
        dq_t[sl, :] = tn(k, ds)
        grads[0:keys, width + h * HEAD_DIM : width + (h + 1) * HEAD_DIM] = (dk * factor).astype(
            BF16
        )
        grads[0:keys, 2 * width + h * HEAD_DIM : 2 * width + (h + 1) * HEAD_DIM] = dv.astype(BF16)
    grads[keys:PAD, width : 3 * width] = jnp.zeros((PAD - keys, 2 * width), BF16)
    grads[:, 0:width] = (dq_t[...] * factor).T.astype(BF16)
    value = grads[:, 0 : 3 * width]
    sums[...] = jnp.sum(value.astype(F32), axis=0, keepdims=True)
    part = nt(value, w[:, 0 : 3 * width])
    grads[:, 3 * width : 4 * width] = mixed[...]
    acc[...] = part + acc_in[...] if has_acc else part


def attn_bwd(proj, mixed, lse, ga, w, acc_in, seq):
    d, gw = w.shape
    width = GROUP_HEADS * HEAD_DIM
    has_acc = acc_in is not None
    vmem = pl.BlockSpec(memory_space=pltpu.VMEM)
    return pl.pallas_call(
        functools.partial(attn_bwd_kernel, has_acc, seq),
        in_specs=[vmem] * (6 if has_acc else 5),
        out_specs=[vmem] * 3,
        out_shape=[
            jax.ShapeDtypeStruct((PAD, gw), BF16),
            jax.ShapeDtypeStruct((PAD, d), F32),
            jax.ShapeDtypeStruct((1, 3 * width), F32),
        ],
        scratch_shapes=[pltpu.VMEM((PAD, width), BF16), pltpu.VMEM((width, PAD), F32)],
        compiler_params=params(),
        cost_estimate=cost(
            2 * PAD * (d * 4 * width + 20 * PAD * 256), d * gw * 2 + PAD * d * 8
        ),
        name="attn_bwd",
    )(proj, mixed, lse, ga, w, *([acc_in] if has_acc else []))


def tile_of(units):
    return next(t for t in (1024, 768, 512, 256, 128) if units % t == 0)


def first_need(tile, columns, slots):
    return [slot * columns // tile for slot in range(slots)]


def ff_up_kernel(plan, pieces_total, slots, tile, *refs):
    table, x, bias = refs[:3]
    pieces = refs[3 : 3 + pieces_total]
    active, slope, w_out, w, sems, out_sems = refs[3 + pieces_total :]
    n = pl.program_id(0)
    cols = plan.columns

    @pl.when(n == 0)
    def _():
        for slot in range(slots):
            for c in plan.copies(slot, pieces, table, w, sems):
                c.start()

    def out_copy(slot):
        part = pl.ds(slot * cols, cols)
        return pltpu.make_async_copy(w.at[:, part], w_out.at[:, part], out_sems.at[slot])

    for slot, step in enumerate(first_need(tile, cols, slots)):

        @pl.when(n == step)
        def _(slot=slot):
            for c in plan.copies(slot, pieces, table, w, sems):
                c.wait()
            out_copy(slot).start()

    u = nn(x[...], w[:, pl.ds(pl.multiple_of(n * tile, tile), tile)]) + bias[...]
    root = math.sqrt(2.0 / math.pi)
    square = u * u
    t = jnp.tanh(u * (root + (root * 0.044715) * square))
    half = 0.5 * (1.0 + t)
    active[...] = (u * half).astype(BF16)
    slope[...] = (
        half + (0.5 * u) * (1.0 - t * t) * (root + (3.0 * root * 0.044715) * square)
    ).astype(BF16)

    @pl.when(n == pl.num_programs(0) - 1)
    def _():
        for slot in range(slots):
            out_copy(slot).wait()


def ff_up(table, x, bias, pieces, plan, slots):
    d = x.shape[1]
    units = slots * plan.columns
    tile = tile_of(units)
    return pl.pallas_call(
        functools.partial(ff_up_kernel, plan, len(pieces), slots, tile),
        grid=(units // tile,),
        in_specs=[
            pl.BlockSpec(memory_space=pltpu.SMEM),
            whole((PAD, d)),
            pl.BlockSpec((1, tile), lambda n: (0, n)),
            *[pl.BlockSpec(memory_space=pl.ANY) for _ in pieces],
        ],
        out_specs=[
            pl.BlockSpec((PAD, tile), lambda n: (0, n)),
            pl.BlockSpec((PAD, tile), lambda n: (0, n)),
            pl.BlockSpec(memory_space=pl.ANY),
        ],
        out_shape=[
            jax.ShapeDtypeStruct((PAD, units), BF16),
            jax.ShapeDtypeStruct((PAD, units), BF16),
            jax.ShapeDtypeStruct((d, units), BF16),
        ],
        scratch_shapes=[
            pltpu.VMEM((d, units), BF16),
            pltpu.SemaphoreType.DMA((len(plan.entries),)),
            pltpu.SemaphoreType.DMA((slots,)),
        ],
        compiler_params=params(),
        cost_estimate=cost(2 * PAD * d * units, 4 * d * units + 4 * PAD * units, 0.05),
        name="ff_up",
    )(table, x, bias, *pieces)


def ff_down_kernel(plan, pieces_total, slots, tile, *refs):
    table, gl, active, slope = refs[:4]
    pieces = refs[4 : 4 + pieces_total]
    acc, gu, sums, w, sems = refs[4 + pieces_total :]
    n = pl.program_id(0)
    cols = plan.columns

    @pl.when(n == 0)
    def _():
        for slot in range(slots):
            for c in plan.copies(slot, pieces, table, w, sems):
                c.start()

    for slot, step in enumerate(first_need(tile, cols, slots)):

        @pl.when(n == step)
        def _(slot=slot):
            for c in plan.copies(slot, pieces, table, w, sems):
                c.wait()

    wt = w[:, pl.ds(pl.multiple_of(n * tile, tile), tile)]
    grad = (nn(gl[...], wt) * slope[...].astype(F32)).astype(BF16)
    gu[...] = grad
    sums[...] = jnp.sum(grad.astype(F32), axis=0, keepdims=True)
    part = nt(active[...], wt)

    @pl.when(n == 0)
    def _():
        acc[...] = part

    @pl.when(n > 0)
    def _():
        acc[...] += part


def ff_down(table, gl, active, slope, pieces, plan, slots):
    d = gl.shape[1]
    units = slots * plan.columns
    tile = tile_of(units)
    return pl.pallas_call(
        functools.partial(ff_down_kernel, plan, len(pieces), slots, tile),
        grid=(units // tile,),
        in_specs=[
            pl.BlockSpec(memory_space=pltpu.SMEM),
            whole((PAD, d)),
            pl.BlockSpec((PAD, tile), lambda n: (0, n)),
            pl.BlockSpec((PAD, tile), lambda n: (0, n)),
            *[pl.BlockSpec(memory_space=pl.ANY) for _ in pieces],
        ],
        out_specs=[
            whole((PAD, d)),
            pl.BlockSpec((PAD, tile), lambda n: (0, n)),
            pl.BlockSpec((1, tile), lambda n: (0, n)),
        ],
        out_shape=[
            jax.ShapeDtypeStruct((PAD, d), F32),
            jax.ShapeDtypeStruct((PAD, units), BF16),
            jax.ShapeDtypeStruct((1, units), F32),
        ],
        scratch_shapes=[
            pltpu.VMEM((d, units), BF16),
            pltpu.SemaphoreType.DMA((len(plan.entries),)),
        ],
        compiler_params=params(),
        cost_estimate=cost(4 * PAD * d * units, 2 * d * units + 6 * PAD * units, 0.05),
        name="ff_down",
    )(table, gl, active, slope, *pieces)


def ff_back_kernel(gu, w, acc):
    part = nt(gu[...], w[...])

    @pl.when(pl.program_id(0) == 0)
    def _():
        acc[...] = part

    @pl.when(pl.program_id(0) > 0)
    def _():
        acc[...] += part


def ff_back(gu, w):
    d, units = w.shape
    tile = tile_of(units)
    return pl.pallas_call(
        ff_back_kernel,
        grid=(units // tile,),
        in_specs=[
            pl.BlockSpec((PAD, tile), lambda n: (0, n)),
            pl.BlockSpec((d, tile), lambda n: (0, n)),
        ],
        out_specs=whole((PAD, d)),
        out_shape=jax.ShapeDtypeStruct((PAD, d), F32),
        compiler_params=params(),
        cost_estimate=cost(2 * PAD * d * units, 2 * d * units + 2 * PAD * units),
        name="ff_back",
    )(gu, w)


def put_turned(table, blocks, value, out):
    t = value.T
    rows = t.shape[0] // blocks
    for b in range(blocks):
        out[pl.ds(pl.multiple_of(table[b], 16), rows), :] = t[b * rows : (b + 1) * rows, :]


def turn_kernel(blocks, table, x, out, sums):
    value = x[...]
    put_turned(table, blocks, value, out)
    sums[...] = jnp.sum(value.astype(F32), axis=0, keepdims=True)


def specs(total):
    return [pl.BlockSpec(memory_space=pltpu.SMEM)] + [pl.BlockSpec(memory_space=pltpu.VMEM)] * total


def turn(table, x):
    d = x.shape[1]
    return pl.pallas_call(
        functools.partial(turn_kernel, table.shape[0]),
        in_specs=specs(1),
        out_specs=specs(2)[1:],
        out_shape=[jax.ShapeDtypeStruct((d, PAD), BF16), jax.ShapeDtypeStruct((1, d), F32)],
        compiler_params=params(),
        cost_estimate=cost(PAD * d * 8, PAD * d * 4, 0.05),
        name="turn",
    )(table, x)


def centered(v):
    c = v - jnp.mean(v, axis=-1, keepdims=True)
    return c, lax.rsqrt(jnp.mean(c * c, axis=-1, keepdims=True) + EPS)


def norm_kernel(blocks, seq, has_acc, *refs):
    if has_acc:
        table, base, acc, extra, gain, bias, hidden, normed, turned = refs
        v = base[...].astype(F32) + (acc[...] + extra[...])
        hidden[...] = v
    else:
        table, base, gain, bias, normed, turned = refs
        v = base[...].astype(F32)
    c, r = centered(v)
    value = c * r * gain[...] + bias[...]
    rows = lax.broadcasted_iota(jnp.int32, value.shape, 0)
    low = jnp.where(rows < seq, value, 0.0).astype(BF16)
    normed[...] = low
    put_turned(table, blocks, low, turned)


def norm(table, base, acc, extra, gain, bias, seq):
    d = base.shape[1]
    has_acc = acc is not None
    args = [base] + ([acc, extra[None]] if has_acc else []) + [gain[None], bias[None]]
    outs = [jax.ShapeDtypeStruct((PAD, d), BF16), jax.ShapeDtypeStruct((d, PAD), BF16)]
    if has_acc:
        outs = [jax.ShapeDtypeStruct((PAD, d), F32)] + outs
    return pl.pallas_call(
        functools.partial(norm_kernel, table.shape[0], seq, has_acc),
        in_specs=specs(len(args)),
        out_specs=specs(len(outs))[1:],
        out_shape=outs,
        compiler_params=params(),
        cost_estimate=cost(PAD * d * 16, PAD * d * 10, 0.05),
        name="norm",
    )(table, *args)


def norm_back_kernel(blocks, seq, with_low, *refs):
    table, v, e, gain, base, grad, gain_sum, bias_sum, *low_refs = refs
    c, r = centered(v[...].astype(F32))
    u = c * r
    scaled = e[...] * gain[...]
    inner = jnp.mean(scaled * u, axis=-1, keepdims=True)
    value = base[...].astype(F32) + r * (
        scaled - jnp.mean(scaled, axis=-1, keepdims=True) - u * inner
    )
    gain_sum[...] = jnp.sum(e[...] * u, axis=0, keepdims=True)
    bias_sum[...] = jnp.sum(e[...], axis=0, keepdims=True)
    if with_low:
        grad[...] = value
        low, turned, low_sum = low_refs
        rounded = value.astype(BF16)
        low[...] = rounded
        put_turned(table, blocks, rounded, turned)
        low_sum[...] = jnp.sum(rounded.astype(F32), axis=0, keepdims=True)
    else:
        grad[...] = value[0:seq]


def norm_back(table, v, e, gain, base, seq, with_low):
    d = v.shape[1]
    row = jax.ShapeDtypeStruct((1, d), F32)
    outs = [jax.ShapeDtypeStruct((PAD if with_low else seq, d), F32), row, row]
    if with_low:
        outs += [
            jax.ShapeDtypeStruct((PAD, d), BF16),
            jax.ShapeDtypeStruct((d, PAD), BF16),
            row,
        ]
    return pl.pallas_call(
        functools.partial(norm_back_kernel, table.shape[0], seq, with_low),
        in_specs=specs(4),
        out_specs=specs(len(outs))[1:],
        out_shape=outs,
        compiler_params=params(),
        cost_estimate=cost(PAD * d * 24, PAD * d * 18),
        name="norm_back",
    )(table, v, e, gain[None], base)


def ff_grad_kernel(total, parts, rows, *refs):
    lhs, rhs, outs = refs[:total], refs[total : 2 * total], refs[2 * total :]
    value = nn(lhs[0][...], rhs[0][...])
    for a, b in zip(lhs[1:], rhs[1:]):
        value += nn(a[...], b[...])
    for number in range(parts):
        outs[number][0] = value[number * rows : (number + 1) * rows].astype(BF16)


def ff_grad(lhs, rhs, slots, parts):
    total = len(lhs)
    height = lhs[0].shape[0]
    rows = height // parts
    cols = rhs[0].shape[1] // slots
    return pl.pallas_call(
        functools.partial(ff_grad_kernel, total, parts, rows),
        grid=(slots,),
        in_specs=[
            *[whole((height, PAD)) for _ in lhs],
            *[pl.BlockSpec((PAD, cols), lambda n: (0, n)) for _ in rhs],
        ],
        out_specs=[pl.BlockSpec((1, rows, cols), lambda n: (n, 0, 0)) for _ in range(parts)],
        out_shape=[jax.ShapeDtypeStruct((slots, rows, cols), BF16) for _ in range(parts)],
        compiler_params=params(),
        cost_estimate=cost(
            2 * total * PAD * height * slots * cols, 2 * slots * cols * (total * PAD + height)
        ),
        name="ff_grad",
    )(*lhs, *rhs)


def attn_grad_kernel(total, parts, has_more, *refs):
    na, ga, g = refs[:total], refs[total : 2 * total], refs[2 * total : 3 * total]
    more, outs = refs[3 * total : -parts], refs[-parts:]
    cut = 3 * GROUP_HEADS * HEAD_DIM
    rows = na[0].shape[0] // parts
    for part in range(parts):
        block = slice(part * rows, (part + 1) * rows)
        for lhs, columns in ((na, slice(0, cut)), (ga, slice(cut, None))):
            value = nn(lhs[0][block, :], g[0][:, columns])
            for i in range(1, total):
                value += nn(lhs[i][block, :], g[i][:, columns])
            if has_more:
                value += more[part][:, columns].astype(F32)
            outs[part][:, columns] = value.astype(BF16)


def attn_grad(na, ga, grads, parts, more=()):
    total = len(na)
    d = na[0].shape[0]
    cols = grads[0].shape[1]
    args = [*na, *ga, *grads, *more]
    return pl.pallas_call(
        functools.partial(attn_grad_kernel, total, parts, len(more) > 0),
        in_specs=specs(len(args))[1:],
        out_specs=specs(parts)[1:],
        out_shape=[jax.ShapeDtypeStruct((d // parts, cols), BF16) for _ in range(parts)],
        compiler_params=params(),
        cost_estimate=cost(2 * total * PAD * d * cols, 2 * cols * (total * PAD + 2 * d)),
        name="attn_grad",
    )(*args)


def hop(x, axis, n, step):
    return lax.ppermute(x, axis, [(i, (i + step) % n) for i in range(n)])


def cat(*arrays):
    return jnp.concatenate(arrays, axis=0)


def after(x, *others):
    return lax.optimization_barrier((x, others))[0]


def total_sum(value, sizes):
    for axis, n in sizes.items():
        step = 1
        while step < n:
            value = value + lax.ppermute(value, axis, [(i, i ^ step) for i in range(n)])
            step *= 2
    return value


def attn_entries(nz, rows, h):
    g = rows - h
    plans = {}
    for dc in range(2):
        for dx in range(2):
            entries = []
            for dy in range(2):
                for dz in range(nz):
                    if dy == 0:
                        one = (dz, dz * 2 * rows, dx * h)
                    else:
                        one = (nz + dz // 2, dz // 2 * 4 * h, dz % 2 * 2 * h + dx * h)
                    if dx == 0:
                        two = (dz, dz * 2 * rows, 2 * h + dy * g)
                    else:
                        two = (
                            nz + nz // 2 + dz // 2,
                            2 * nz * h + dz // 2 * 4 * g,
                            dz % 2 * 2 * g + dy * g,
                        )
                    for (piece, base, at), size, inside in ((one, h, 0), (two, g, h)):
                        if dc == 1:
                            piece, at = (0 if piece < nz else 1), base + at
                        entries.append((piece, at, size, 0, dy * nz + dz, inside, 0))
            plans[dc, dx] = entries
    return plans


def ff_entries(nz, rows, cols):
    entries = []
    for dz in range(nz):
        for dy in range(2):
            for dx in range(2):
                if dy == 0:
                    if dx == 0:
                        near = dz, 0
                    elif dz == 0:
                        near = nz, 0
                    else:
                        near = nz + 1, dz - 1
                    far = nz + 5, dx * nz + dz
                elif dz == 0:
                    near = nz + 2, dx
                    far = nz + 6, dx
                elif dx == 0:
                    near = nz + 3, dz - 1
                    far = nz + 6, 1 + dz
                else:
                    near = nz + 4, dz - 1
                    far = nz + 7, dz - 1
                for dc, (piece, at) in enumerate((near, far)):
                    entries.append(
                        (piece, at * rows, rows, dz, dc * 4 + dy * 2 + dx, 0, dz * cols)
                    )
    return entries


def on_device(
    sizes,
    inputs,
    slot_mask,
    ln1_gain,
    ln1_bias,
    qkv_weight,
    qv_bias,
    out_weight,
    out_bias,
    ln2_gain,
    ln2_bias,
    up_weight,
    up_bias,
    down_weight,
    down_bias,
    out_grad,
):
    seq, d = inputs.shape[1:]
    ny, nx, nc, nz = (sizes[a] for a in ("y", "x", "c", "z"))
    yi, xi, ci, zi = (lax.axis_index(a) for a in ("y", "x", "c", "z"))
    width = GROUP_HEADS * HEAD_DIM
    unit_width = up_weight.shape[1]
    cols = -(-unit_width // 128) * 128
    a_rows, f_rows = qkv_weight.shape[0], up_weight.shape[0]
    linked = ny == nx == nc == 2 and nz % 2 == 0 and a_rows % 16 == 0 and f_rows % 16 == 0

    attn_own = jnp.concatenate(
        [qkv_weight.reshape(a_rows, 3 * width).astype(BF16), out_weight.T.astype(BF16)], axis=1
    )
    spare = ((0, 0), (0, cols - unit_width))
    up_own = jnp.pad(up_weight.astype(BF16), spare)
    down_own = jnp.pad(down_weight.T.astype(BF16), spare)

    def swap(x, axis="c"):
        return hop(x, axis, 2, 1)

    if linked:
        h = -(-a_rows // 32) * 16
        order = [(dc, dx) for dc in range(2) for dx in range(2)]
        entries = attn_entries(nz, a_rows, h)
        attn_plans = [Plan(entries[o], 4 * width) for o in order]
        groups = [(xi ^ dx) * 2 + (ci ^ dc) for dc, dx in order]
        down_plan = Plan(ff_entries(nz, f_rows, cols), cols)
        zones = [(zi - dz) % nz for dz in range(nz)]
        attn_table = jnp.stack(
            [((yi ^ dy) * nz + (zi - dz) % nz) * a_rows for dy in range(2) for dz in range(nz)]
        )
        ff_table = jnp.stack(
            [
                (((yi ^ dy) * 2 + (xi ^ dx)) * 2 + (ci ^ dc)) * f_rows
                for dc in range(2)
                for dy in range(2)
                for dx in range(2)
            ]
        )
        turn_attn = jnp.stack(
            [((yi ^ b // nz) * nz + (zi - b % nz) % nz) * a_rows for b in range(2 * nz)]
        )
        turn_ff = jnp.stack(
            [
                ((ci ^ b % 2) * 4 + (yi ^ b // 4) * 2 + (xi ^ b // 2 % 2)) * f_rows
                for b in range(8)
            ]
        )
    else:
        whole_attn = lax.all_gather(attn_own, ("y", "z"), axis=0, tiled=True)
        whole_attn = lax.all_gather(whole_attn, ("x", "c"), axis=0)
        down_whole = lax.all_gather(down_own, ("z", "y", "x", "c"), axis=0, tiled=True)
        up_whole = lax.all_gather(up_own, ("z", "y", "x", "c"), axis=0, tiled=True)
        attn_pieces = [[whole_attn[g]] for g in range(nx * nc)]
        attn_plans = [Plan([(0, 0, d, 0, 0, 0, 0)], 4 * width)] * (nx * nc)
        attn_table = ff_table = turn_attn = turn_ff = jnp.zeros((1,), jnp.int32)
        groups = list(range(nx * nc))
        zones = list(range(nz))
    up_plan = ZonePlan(nz, d, cols)
    zone_table = jnp.stack([jnp.asarray(k, jnp.int32) * d for k in zones])

    valid = slot_mask[0].astype(F32)
    token_pad = ((0, PAD - seq), (0, 0))
    base = jnp.pad(inputs[0], token_pad)
    grad_low = (valid * jnp.pad(out_grad[0], token_pad).astype(F32)).astype(BF16)
    bias_rows = []
    for g in groups:
        part = lax.dynamic_slice_in_dim(qv_bias, g * width, width, 1)
        bias_rows.append(jnp.concatenate([part[0], jnp.zeros_like(part[0]), part[1]])[None])
    shift = jnp.concatenate(
        [
            jnp.pad(lax.dynamic_slice_in_dim(up_bias, k * unit_width, unit_width), spare[1])
            for k in zones
        ]
    )[None]
    normed_a, na_t = norm(turn_attn, base, None, None, ln1_gain, ln1_bias, seq)
    gl_t, down_bias_sum = turn(turn_ff, grad_low)

    together = lax.optimization_barrier
    if linked:
        half = d // 2
        px, py, down_xa = together(
            (swap(attn_own[:h], "x"), swap(attn_own[h:], "y"), swap(down_own, "x"))
        )
        s = [cat(attn_own[:h], px, attn_own[h:], py)]
        s1, down_ya, na_far = together(
            (
                hop(s[0], "z", nz, 1),
                swap(cat(down_own, after(down_xa, px)), "y"),
                swap(after(na_t, px)),
            )
        )
        s.append(s1)
        y_parts, x_parts = [], []
        gl_first = gl_t[half:]
        for k in range(2, nz):
            moves = [hop(s[-1], "z", nz, 1)]
            if k % 2 == 0:
                moves.append(swap(cat(s[k - 2][: 2 * h], s[k - 1][: 2 * h]), "y"))
                moves.append(swap(cat(s[k - 2][2 * h :], s[k - 1][2 * h :]), "x"))
            elif k == 3:
                gl_far = swap(after(gl_first, s[-1]))
                moves.append(gl_far)
            moves = together(tuple(moves))
            s.append(moves[0])
            if k % 2 == 0:
                y_parts.append(moves[1])
                x_parts.append(moves[2])
            elif k == 3:
                gl_far = moves[1]
        moves = together(
            (
                swap(cat(s[-2][: 2 * h], s[-1][: 2 * h]), "y"),
                swap(cat(s[-2][2 * h :], s[-1][2 * h :]), "x"),
                swap(cat(*s)),
            )
        )
        y_parts.append(moves[0])
        x_parts.append(moves[1])
        up_whole = lax.all_gather(after(up_own, s[2]), ("z", "y", "x", "c"), axis=0, tiled=True)
        near = [*s, *y_parts, *x_parts]
        far = [moves[2], swap(cat(*y_parts, *x_parts))]
        down_first = after(down_own, moves[2])
        down_z = [down_own] + [hop(down_first, "z", nz, k) for k in range(1, nz)]

        kept = []
        acc = None
        for number in range(4):
            pieces = near if number < 2 else far
            proj, mixed, lse, acc, w = attn_fwd(
                attn_table, normed_a, bias_rows[number], pieces, attn_plans[number], acc, seq
            )
            kept.append((proj, mixed, lse, w))
            if number == 1:
                acc, down_z, far = together((acc, down_z, far))
                down_xb = swap(cat(*down_z[1:]), "x")
                down_yb = swap(cat(*down_z[1:]), "y")
            if number == 3:
                acc, down_xb, down_yb = together((acc, down_xb, down_yb))
                down_yc = swap(down_xb, "y")
                down_c0 = swap(cat(*down_z, down_xa, down_xb))
                down_c1 = swap(cat(down_ya, down_yb))
    else:
        kept = []
        acc = None
        for number, g in enumerate(groups):
            proj, mixed, lse, acc, w = attn_fwd(
                attn_table,
                normed_a,
                bias_rows[number],
                attn_pieces[number],
                attn_plans[number],
                acc,
                seq,
            )
            kept.append((proj, mixed, lse, w))

    hidden, normed_b, nb_t = norm(turn_ff, base, acc, out_bias, ln2_gain, ln2_bias, seq)
    if linked:
        nb_far = swap(nb_t[half:])
    active, slope, up_full = ff_up(zone_table, normed_b, shift, [up_whole], up_plan, nz)
    if linked:
        active, down_yc, down_c0, down_c1, nb_far = together(
            (active, down_yc, down_c0, down_c1, nb_far)
        )
        down_c2 = swap(down_yc)
        down_pieces = [*down_z, down_xa, down_xb, down_ya, down_yb, down_yc]
        down_pieces += [down_c0, down_c1, down_c2]
        active_far = swap(active)
    else:
        down_plan, ff_table, down_pieces = up_plan, zone_table, [down_whole]
    mlp, grad_upper, upper_sums = ff_down(
        ff_table, grad_low, active, slope, down_pieces, down_plan, nz
    )
    output = (valid * (hidden + (mlp + down_bias)))[:seq].astype(BF16)[None]

    def plus(*values):
        return sum(v.astype(F32) for v in values).astype(BF16)

    if linked:
        grad_upper, active_far = together((grad_upper, active_far))
        upper_far = swap(grad_upper)
        down_parts = ff_grad([gl_t[:half], gl_far], [active, active_far], nz, 4)
        down_one, down_two = swap(down_parts[3], "x"), swap(down_parts[1], "x")
        grad_normed_b = ff_back(after(grad_upper, down_parts), up_full)
    else:
        spot = ("y", "x", "c")

        def spread(parts):
            part = lax.psum_scatter(parts[0], "z", scatter_dimension=0, tiled=True)[0]
            part = lax.psum_scatter(part, spot, scatter_dimension=0, tiled=True)
            return lax.optimization_barrier(part).astype(F32)

        down_sum = spread(ff_grad([gl_t], [active], nz, 1))
        up_sum = spread(ff_grad([nb_t], [grad_upper], nz, 1))
        grad_normed_b = ff_back(grad_upper, up_full)

    grad_hidden, ln2_gain_grad, ln2_bias_grad, grad_attn, ga_t, out_bias_sum = norm_back(
        turn_attn, hidden, grad_normed_b, ln2_gain, grad_low, seq, True
    )

    acc = None
    sums = [None] * len(groups)
    if linked:
        grads = {}
        ga_far = swap(ga_t)

        def back(number, acc):
            proj, mixed, lse, w = kept[number]
            grads[number], acc, sums[number] = attn_bwd(proj, mixed, lse, ga_first, w, acc, seq)
            return acc

        ga_first, down_one = together((grad_attn, down_one))
        down_one = plus(down_parts[2], down_one)
        down_other = swap(down_one, "y")
        ga_first = after(ga_first, down_one)
        acc = back(3, None)
        far_grads = swap(grads[3])
        acc = back(1, acc)
        acc, far_grads, ga_far, down_two, down_other = together(
            (acc, far_grads, ga_far, down_two, down_other)
        )
        down_value = plus(down_parts[0], down_two, down_other)
        down_line = hop(down_value[nz - 1], "z", nz, -1)
        more = attn_grad(
            [after(na_t, down_value), na_far], [ga_t, ga_far], [grads[1], far_grads], 2
        )
        more_one, more_two = swap(more[1], "x"), swap(more[0], "x")
        upper_first, upper_far = together((grad_upper, upper_far, more))[:2]
        up_parts = ff_grad([nb_t[:half], nb_far], [upper_first, upper_far], nz, 4)
        up_parts, down_line, acc = together((up_parts, down_line, acc))
        up_one, up_two = swap(up_parts[3], "y"), swap(up_parts[2], "y")
        down_line = hop(plus(down_line, down_value[nz - 2]), "z", nz, -1)
        acc = back(2, acc)
        far_grads = swap(grads[2])
        acc, more_one, down_line = together((acc, more_one, down_line))
        for k in range(nz - 3, 0, -1):
            down_line = hop(plus(down_line, down_value[k]), "z", nz, -1)
        acc = back(0, acc)
        acc, far_grads, up_one, down_line = together((acc, far_grads, up_one, down_line))
        up_one = plus(up_parts[1], up_one)
        up_other = swap(up_one, "x")
        input_grad, ln1_gain_grad, ln1_bias_grad = norm_back(
            turn_attn, base, after(acc, up_one), ln1_gain, grad_hidden, seq, False
        )
        na_first, more_two, up_two, up_other, input_grad = together(
            (na_t, more_two, up_two, up_other, input_grad)
        )
        total = attn_grad(
            [na_first, na_far], [ga_t, ga_far], [grads[0], far_grads], 2, (more_two, more_one)
        )
        far_y = swap(total[1], "y")
        up_value = plus(up_parts[0], up_two, up_other)
        up_line = hop(after(up_value[nz - 1], total[0]), "z", nz, -1)
        for k in range(nz - 2, 0, -1):
            up_line = hop(plus(up_line, up_value[k]), "z", nz, -1)
        far_y, up_line, near_y = together((far_y, up_line, total[0]))
        last = plus(near_y, far_y).reshape(nz, a_rows, 4 * width)
        last_far = [hop(last[k], "z", nz, -k) for k in range(1, nz)]
        down_sum = down_line.astype(F32) + down_value[0].astype(F32)
        up_sum = up_line.astype(F32) + up_value[0].astype(F32)
        attn_sum = sum(v.astype(F32) for v in (last[0], *last_far))
    else:
        parts = []
        for number, (proj, mixed, lse, w) in enumerate(kept):
            g, acc, sums[number] = attn_bwd(proj, mixed, lse, grad_attn, w, acc, seq)
            parts.append(attn_grad([na_t], [ga_t], [g], 1)[0])
        part = lax.psum_scatter(jnp.stack(parts), ("x", "c"), scatter_dimension=0, tiled=True)[0]
        part = lax.psum_scatter(part, ("y", "z"), scatter_dimension=0, tiled=True)
        attn_sum = lax.optimization_barrier(part).astype(F32)
        input_grad, ln1_gain_grad, ln1_bias_grad = norm_back(
            turn_attn, base, acc, ln1_gain, grad_hidden, seq, False
        )

    def in_place(rows, places):
        at = jnp.arange(len(rows))[:, None]
        return sum(jnp.where(at == p, r, 0.0) for r, p in zip(rows, places))

    wide = max(d, 3 * width, cols)

    def fit(x):
        return jnp.pad(x, ((0, 0), (0, wide - x.shape[1])))

    vectors = [
        ln1_gain_grad,
        ln1_bias_grad,
        out_bias_sum,
        ln2_gain_grad,
        ln2_bias_grad,
        down_bias_sum,
        in_place(sums, groups),
        in_place(
            [upper_sums[:, slot * cols : (slot + 1) * cols] for slot in range(nz)], zones
        ),
    ]
    table = cat(*[fit(v) for v in vectors])
    fill = -table.shape[0] % 8
    table = total_sum(jnp.pad(table, ((0, fill), (0, 0))), sizes)
    singles = [table[k, :d] for k in range(6)]
    qv = table[6 : 6 + len(groups)]
    qv_grad = jnp.stack([qv[:, :width].reshape(-1), qv[:, 2 * width : 3 * width].reshape(-1)])
    up_bias_grad = table[6 + len(groups) : 6 + len(groups) + nz, :unit_width].reshape(-1)

    qkv_grad = attn_sum[:, : 3 * width].reshape(a_rows, 3, width)
    out_weight_grad = attn_sum[:, 3 * width :].T
    up_grad = up_sum[:, :unit_width]
    down_grad = down_sum[:, :unit_width].T
    return (
        output,
        input_grad[None],
        singles[0],
        singles[1],
        qkv_grad,
        qv_grad,
        out_weight_grad,
        singles[2],
        singles[3],
        singles[4],
        up_grad,
        up_bias_grad,
        down_grad,
        singles[5],
    )


def solution(mesh):
    heads = mesh.shape["heads"]
    sizes = {"y": mesh.shape["fsdp"], "x": heads // 2, "c": 2, "z": mesh.shape["tensor"]}
    split = jax.sharding.Mesh(mesh.devices.reshape(tuple(sizes.values())), tuple(sizes))
    images = P(("y", "x", "c", "z"), None, None)
    attn_in = P(("y", "z"), None, ("x", "c"))
    attn_out = P(("x", "c"), ("y", "z"))
    up, down = P(("y", "x", "c"), "z"), P("z", ("y", "x", "c"))
    in_specs = (
        images,
        P(("y", "x", "c", "z")),
        P(),
        P(),
        attn_in,
        P(),
        attn_out,
        P(),
        P(),
        P(),
        up,
        P(),
        down,
        P(),
        images,
    )
    out_specs = (
        images,
        images,
        P(),
        P(),
        attn_in,
        P(),
        attn_out,
        P(),
        P(),
        P(),
        up,
        P(),
        down,
        P(),
    )
    return jax.shard_map(
        functools.partial(on_device, sizes),
        mesh=split,
        in_specs=in_specs,
        out_specs=out_specs,
        check_vma=False,
    )
```

time: 705 us -> 609 us (0.86)
  waiting for transfers between devices: 280 us -> 161 us
  Pallas kernels: 216 us -> 265 us
  local copies, waits for them, and re-layouts: 69.9 us -> 44.1 us
  other arithmetic: 71.8 us -> 48.5 us
  between operations: 2.37 us -> 16.3 us
  starting transfers between devices: 58.9 us -> 66.6 us
    ppermute x51 -> x48, waiting for transfers between devices: 260 us -> 139 us  [hop(): return lax.ppermute(x, axis, [(i, (i + step) % n) for i in range(n)])]
    pallas_call x7 -> x11, Pallas kernels: 83.7 us -> 120 us  [the longest x4 64.1 us: attn_bwd(): pl.pallas_call(functools.partial(attn_bwd_kernel, has_acc, seq), in_specs...]
    reduce_sum x9 -> x0, other arithmetic: 22.6 us -> none  [the longest x4 9.81 us: layer_norm(): center = values - jnp.mean(values, axis=-1, keepdims=True)]
    add x13 -> x4, other arithmetic: 15.1 us -> 1.26 us  [the longest x1 0.92 us: on_device(): up_sum = up_line.astype(F32) + up_value[0].astype(F32)]
    pallas_call x2 -> x4, Pallas kernels: 39.8 us -> 53.1 us  [attn_fwd(): pl.pallas_call(functools.partial(attn_fwd_kernel, plan, len(pieces), has_...]
    convert_element_type x3 -> x9, other arithmetic: 5.26 us -> 17.7 us  [plus(): return sum((v.astype(F32) for v in values)).astype(BF16)]
    dynamic_update_slice x8 -> x0, local copies, waits for them, and re-layouts: 11.5 us -> none  [the longest x4 5.8 us: on_device(): lax.dynamic_update_slice_in_dim(up_shift, piece, k * unit_width, 0)]
    ppermute x51 -> x48, starting transfers between devices: 56.4 us -> 61.9 us  [hop(): return lax.ppermute(x, axis, [(i, (i + step) % n) for i in range(n)])]
  transfers between devices with their start and end apart: 56 -> 54, of which waited for: 25 -> 20; matrix products, arithmetic and copies ran while one was open for 17% -> 14% of each run, Pallas kernels for 21% -> 42%
where the time goes in v2:
time: 609 us; the launch traced here: 601 us
  Pallas kernels  265 us (44%)
  waiting for transfers between devices  161 us (26%)
  starting transfers between devices  66.6 us (11%)
  other arithmetic  48.5 us (8%)
  local copies, waits for them, and re-layouts  44.1 us (7%)
  between operations  16.3 us (3%)
    ppermute x48, waiting for transfers between devices, hop(): return lax.ppermute(x, axis, [(i, (i + step) % n) for i in range(n)])  139 us
    pallas_call x4, Pallas kernels, attn_bwd(): pl.pallas_call(functools.partial(attn_bwd_kernel, has_acc, seq), in_specs...  64.1 us
    ppermute x48, starting transfers between devices, hop(): return lax.ppermute(x, axis, [(i, (i + step) % n) for i in range(n)])  61.9 us
    pallas_call x4, Pallas kernels, attn_fwd(): pl.pallas_call(functools.partial(attn_fwd_kernel, plan, len(pieces), has_...  53.1 us
    pallas_call x1, Pallas kernels, ff_down(): pl.pallas_call(functools.partial(ff_down_kernel, plan, len(pieces), slots...  28.2 us
    pallas_call x2, Pallas kernels, ff_grad(): pl.pallas_call(functools.partial(ff_grad_kernel, total, parts, rows), gri...  26.8 us
    pallas_call x2, Pallas kernels, attn_grad(): pl.pallas_call(functools.partial(attn_grad_kernel, total, parts, len(more...  22.7 us
    ppermute x5, waiting for transfers between devices, total_sum(): value = value + lax.ppermute(value, axis, [(i, i ^ step) for i in range(n)])  22 us
  transfers between devices with their start and end apart: 54, of which 20 were waited for; matrix products, arithmetic and copies ran while one was open for 14% of the time, Pallas kernels for 42%

profile of v2, /device:TPU:0, one launch (start us, length us, event | category | flops | bytes accessed | tf_op | source)
XLA Modules:
  0.0 601.0 jit_solution(4462587532784856419)
XLA Ops:
  10.6 2.9 collective-permute-start
  15.5 2.1 collective-permute-start.1
  20.8 4.6 norm.2
  29.9 15.0 %collective-permute-done.3.refs_4_ = bf16[288,1152]{1,0:T(8,128)(2,1)S(1)} collective-permute-done((bf16[288,1152]{1,0:T(8,128)(2,1)S(1)}, bf16[288,1152]{1,0:T(8,128)(2,1)S(1)}, u32[]{:S(2)}, u32[]{:S(2)}) %collective-permute-start.3) | collective-permute-done | bytes 663584 | tf_op jit(solution)/shard_map/ppermute | solution.py:577
  53.6 12.0 %collective-permute-done.8.refs_9_ = bf16[256,1152]{1,0:T(8,128)(2,1)S(1)} collective-permute-done((bf16[256,1152]{1,0:T(8,128)(2,1)}, bf16[256,1152]{1,0:T(8,128)(2,1)S(1)}, u32[]{:S(2)}, u32[]{:S(2)}) %collective-permute-start.8) | collective-permute-done | bytes 589856 | tf_op jit(solution)/shard_map/ppermute | solution.py:577
  67.3 3.0 multiply_convert_fusion.x.refs_1_.refs_4_
  71.0 3.4 turn.1
  74.3 2.7 fusion.17
  79.0 23.5 %collective-permute-done.9.refs_6_ = bf16[288,1152]{1,0:T(8,128)(2,1)S(1)} collective-permute-done((bf16[288,1152]{1,0:T(8,128)(2,1)S(1)}, bf16[288,1152]{1,0:T(8,128)(2,1)S(1)}, u32[]{:S(2)}, u32[]{:S(2)}) %collective-permute-start.9) | collective-permute-done | bytes 663584 | tf_op jit(solution)/shard_map/ppermute | solution.py:577
  106.9 13.8 %collective-permute-done.12.refs_10_ = bf16[256,1152]{1,0:T(8,128)(2,1)S(1)} collective-permute-done((bf16[256,1152]{1,0:T(8,128)(2,1)S(1)}, bf16[256,1152]{1,0:T(8,128)(2,1)S(1)}, u32[]{:S(2)}, u32[]{:S(2)}) %collective-permute-start.12) | collective-permute-done | bytes 589856 | tf_op jit(solution)/shard_map/ppermute | solution.py:577
  121.9 6.1 %pad_maximum_fusion = bf16[1152,1152]{1,0:T(8,128)(2,1)} fusion(bf16[256,1152]{1,0:T(8,128)(2,1)S(1)} %collective-permute-done.12.refs_10_, bf16[256,1152]{1,0:T(8,128)(2,1)S(1)} %collective-permute-done.8.refs_9_, bf16[320,1152]{1,0:T(8,128)(2,1)S(1)} %collective-permute-done.11.refs_8_, bf16[320,1152]{1,0:T(8,128)(2,1)S(1)} %collective-permute-done.7.refs_7_), kind=kLoop, calls=%fused_computation.5 | loop fusion | flops 10616832 | bytes 5308416 | tf_op jit(solution)/shard_map/concatenate | solution.py:581
  129.0 2.4 collective-permute-start.15
  134.4 12.4 %attn_fwd.4 = (bf16[768,864]{1,0:T(8,128)(2,1)}, bf16[768,288]{1,0:T(8,128)(2,1)}, f32[8,768]{1,0:T(8,128)}, f32[768,1152]{1,0:T(8,128)}, bf16[1152,1152]{1,0:T(8,128)(2,1)}) custom-call(s32[8]{0:T(128)} %stack.125.refs_0_, bf16[768,1152]{1,0:T(8,128)(2,1)} %get-tuple-element.151.refs_1_, f32[1,864]{1,0:T(1,128)} %broadcast_in_dim.167.refs_2_, ...), custom_call_target="tpu_custom_call" | custom-call | flops 222717536 | bytes 619315 | tf_op jit(solution)/shard_map/attn_fwd/pallas_call | solution.py:129
  146.9 13.5 %attn_fwd.5 = (bf16[768,864]{1,0:T(8,128)(2,1)}, bf16[768,288]{1,0:T(8,128)(2,1)}, f32[8,768]{1,0:T(8,128)}, f32[768,1152]{1,0:T(8,128)}, bf16[1152,1152]{1,0:T(8,128)(2,1)}) custom-call(s32[8]{0:T(128)} %stack.125.refs_0_, bf16[768,1152]{1,0:T(8,128)(2,1)} %get-tuple-element.151.refs_1_, f32[1,864]{1,0:T(1,128)} %broadcast_in_dim.166.refs_2_, ...), custom_call_target="tpu_custom_call" | custom-call | flops 222717536 | bytes 619315 | tf_op jit(solution)/shard_map/attn_fwd/pallas_call | solution.py:129
  160.4 11.1 %collective-permute-done.15.refs_6_ = bf16[144,1152]{1,0:T(8,128)(2,1)} collective-permute-done((bf16[144,1152]{1,0:T(8,128)(2,1)}, bf16[144,1152]{1,0:T(8,128)(2,1)}, u32[]{:S(2)}, u32[]{:S(2)}) %collective-permute-start.15) | collective-permute-done | bytes 331808 | tf_op jit(solution)/shard_map/ppermute | solution.py:577
  172.1 2.0 constant_dynamic-update-slice_fusion.15
  175.0 1.9 constant_dynamic-update-slice_fusion.13
  176.9 1.9 constant_dynamic-update-slice_fusion.12
  182.4 13.7 %attn_fwd.6 = (bf16[768,864]{1,0:T(8,128)(2,1)}, bf16[768,288]{1,0:T(8,128)(2,1)}, f32[8,768]{1,0:T(8,128)}, f32[768,1152]{1,0:T(8,128)}, bf16[1152,1152]{1,0:T(8,128)(2,1)}) custom-call(s32[8]{0:T(128)} %stack.125.refs_0_, bf16[768,1152]{1,0:T(8,128)(2,1)} %get-tuple-element.151.refs_1_, f32[1,864]{1,0:T(1,128)} %broadcast_in_dim.168.refs_2_, ...), custom_call_target="tpu_custom_call" | custom-call | flops 222717536 | bytes 619315 | tf_op jit(solution)/shard_map/attn_fwd/pallas_call | solution.py:129
  196.1 13.5 %attn_fwd.7 = (bf16[768,864]{1,0:T(8,128)(2,1)}, bf16[768,288]{1,0:T(8,128)(2,1)}, f32[8,768]{1,0:T(8,128)}, f32[768,1152]{1,0:T(8,128)}, bf16[1152,1152]{1,0:T(8,128)(2,1)}) custom-call(s32[8]{0:T(128)} %stack.125.refs_0_, bf16[768,1152]{1,0:T(8,128)(2,1)} %get-tuple-element.151.refs_1_, f32[1,864]{1,0:T(1,128)} %broadcast_in_dim.165.refs_2_, ...), custom_call_target="tpu_custom_call" | custom-call | flops 222717536 | bytes 619315 | tf_op jit(solution)/shard_map/attn_fwd/pallas_call | solution.py:129
  210.4 2.2 constant_dynamic-update-slice_fusion.10
  212.7 2.5 pad_maximum_fusion.1
  218.0 6.9 %norm.3 = (f32[768,1152]{1,0:T(8,128)}, bf16[768,1152]{1,0:T(8,128)(2,1)}, bf16[1152,768]{1,0:T(8,128)(2,1)}) custom-call(s32[8]{0:T(128)} %stack.116.table.refs_0_, bf16[768,1152]{1,0:T(8,128)(2,1)} %pad.35.refs_1_, f32[768,1152]{1,0:T(8,128)} %get-tuple-element.179.refs_2_, f32[1,1152]{1,0:T(1,128)} %broadcast_in_dim.169.refs_3_, ...), custom_call_target="tpu_custom_call" | custom-call | flops 707788 | bytes 442368 | tf_op jit(solution)/shard_map/norm/pallas_call | solution.py:459
  224.9 2.5 fusion.16
  229.9 20.8 %ff_up.1 = (bf16[768,4608]{1,0:T(8,128)(2,1)}, bf16[768,4608]{1,0:T(8,128)(2,1)}, bf16[1152,4608]{1,0:T(8,128)(2,1)}) custom-call(s32[4]{0:T(128)} %pad_add_fusion.refs_0_, bf16[768,1152]{1,0:T(8,128)(2,1)} %get-tuple-element.181.refs_1_, f32[1,4608]{1,0:T(1,128)} %broadcast_in_dim.172.refs_2_, bf16[4608,1152]{1,0:T(8,128)(2,1)} %all-gather.2.cloned.1.call-done.refs_3_), custom_call_target="tpu_custom_call" | custom-call | flops 407686336 | bytes 1769472 | tf_op jit(solution)/shard_map/ff_up/pallas_call | solution.py:272
  254.4 9.6 %collective-permute-done.24.refs_15_ = bf16[432,1152]{1,0:T(8,128)(2,1)} collective-permute-done((bf16[432,1152]{1,0:T(8,128)(2,1)}, bf16[432,1152]{1,0:T(8,128)(2,1)}, u32[]{:S(2)}, u32[]{:S(2)}) %collective-permute-start.24) | collective-permute-done | bytes 995360 | tf_op jit(solution)/shard_map/ppermute | solution.py:577
  264.1 28.2 %ff_down.1 = (f32[768,1152]{1,0:T(8,128)}, bf16[768,4608]{1,0:T(8,128)(2,1)}, f32[1,4608]{1,0:T(1,128)}) custom-call(s32[8]{0:T(128)} %stack.134.refs_0_, bf16[768,1152]{1,0:T(8,128)(2,1)} %multiply_convert_fusion.x.refs_1_.refs_4_, bf16[768,4608]{1,0:T(8,128)(2,1)} %get-tuple-element.189.refs_2_, bf16[768,4608]{1,0:T(8,128)(2,1)} %get-tuple-element.190.refs_3_, ...), custom_call_target="tpu_custom_call" | custom-call | flops 815372672 | bytes 1592524 | tf_op jit(solution)/shard_map/ff_down/pallas_call | solution.py:341
  293.7 13.4 %ff_grad.2 = (bf16[4,144,1152]{2,1,0:T(8,128)(2,1)}, bf16[4,144,1152]{2,1,0:T(8,128)(2,1)}, bf16[4,144,1152]{2,1,0:T(8,128)(2,1)}, bf16[4,144,1152]{2,1,0:T(8,128)(2,1)}) custom-call(bf16[576,768]{1,0:T(8,128)(2,1)} %get-tuple-element.338.refs_0_, bf16[576,768]{1,0:T(8,128)(2,1)} %copy-done.59, bf16[768,4608]{1,0:T(8,128)(2,1)} %get-tuple-element.189.refs_2_, ...), custom_call_target="tpu_custom_call" | custom-call | flops 521838526464 | bytes 1245708288 | tf_op jit(solution)/shard_map/ff_grad/pallas_call | solution.py:527
  309.1 16.0 %ff_back.1.refs_2_ = f32[768,1152]{1,0:T(8,128)} custom-call(bf16[768,4608]{1,0:T(8,128)(2,1)} %get-tuple-element.231.gu.refs_2_, bf16[1152,4608]{1,0:T(8,128)(2,1)} %get-tuple-element.207.w), custom_call_target="tpu_custom_call" | custom-call | flops 521838526464 | bytes 1132462080 | tf_op jit(solution)/shard_map/ff_back/pallas_call | solution.py:386
  325.1 9.6 %norm_back.2 = (f32[768,1152]{1,0:T(8,128)}, f32[1,1152]{1,0:T(1,128)}, f32[1,1152]{1,0:T(1,128)}, bf16[768,1152]{1,0:T(8,128)(2,1)}, bf16[1152,768]{1,0:T(8,128)(2,1)}, /*index=5*/f32[1,1152]{1,0:T(1,128)}) custom-call(s32[8]{0:T(128)} %stack.125.refs_0_, f32[768,1152]{1,0:T(8,128)} %get-tuple-element.180.refs_1_, f32[768,1152]{1,0:T(8,128)} %ff_back.1.refs_2_, ...), custom_call_target="tpu_custom_call" | custom-call | flops 1358954496 | bytes 1019215872 | tf_op jit(solution)/shard_map/norm_back/pallas_call | solution.py:502
  335.2 4.1 collective-permute-done.26
  339.3 2.7 add_convert_fusion.4
  343.6 15.6 %attn_bwd.4 = (bf16[768,1152]{1,0:T(8,128)(2,1)}, f32[768,1152]{1,0:T(8,128)}, f32[1,864]{1,0:T(1,128)}) custom-call(bf16[768,864]{1,0:T(8,128)(2,1)} %get-tuple-element.213.refs_0_, bf16[768,288]{1,0:T(8,128)(2,1)} %get-tuple-element.214.refs_1_, f32[8,768]{1,0:T(8,128)} %get-tuple-element.215.refs_2_, bf16[768,1152]{1,0:T(8,128)(2,1)} %get-tuple-element.211.refs_3_, ...), custom_call_target="tpu_custom_call" | custom-call | flops 517006688256 | bytes 622854144 | tf_op jit(solution)/shard_map/attn_bwd/pallas_call | solution.py:201
  359.2 16.2 %attn_bwd.5 = (bf16[768,1152]{1,0:T(8,128)(2,1)}, f32[768,1152]{1,0:T(8,128)}, f32[1,864]{1,0:T(1,128)}) custom-call(bf16[768,864]{1,0:T(8,128)(2,1)} %get-tuple-element.199.refs_0_, bf16[768,288]{1,0:T(8,128)(2,1)} %get-tuple-element.200.refs_1_, f32[8,768]{1,0:T(8,128)} %get-tuple-element.201.refs_2_, bf16[768,1152]{1,0:T(8,128)(2,1)} %get-tuple-element.211.refs_3_, ...), custom_call_target="tpu_custom_call" | custom-call | flops 517006688256 | bytes 622854144 | tf_op jit(solution)/shard_map/attn_bwd/pallas_call | solution.py:201
  375.4 2.2 add_convert_fusion.3
  379.6 12.9 %collective-permute-start.33 = (bf16[144,1152]{1,0:T(8,128)(2,1)}, bf16[144,1152]{1,0:T(8,128)(2,1)}, u32[]{:S(2)}, u32[]{:S(2)}) collective-permute-start(bf16[144,1152]{1,0:T(8,128)(2,1)} %get-tuple-element.341), channel_id=1, source_target_pairs={{0,3},{1,0},{2,1},{3,2},{4,7},{5,4},{6,5},{7,6},{8,11},{9,8},{10,9... | collective-permute-start | bytes 995336 | tf_op jit(solution)/shard_map/ppermute | solution.py:577
  392.5 10.9 %attn_grad.2 = (bf16[576,1152]{1,0:T(8,128)(2,1)}, bf16[576,1152]{1,0:T(8,128)(2,1)}) custom-call(bf16[1152,768]{1,0:T(8,128)(2,1)} %get-tuple-element.273.refs_0_, bf16[1152,768]{1,0:T(8,128)(2,1)} %copy-done.58, bf16[1152,768]{1,0:T(8,128)(2,1)} %get-tuple-element.220.refs_2_, bf16[1152,768]{1,0:T(8,128)(2,1)} %collective-permute-done.28.refs_3_, ...), custom_call_target="tpu_custom_call" | custom-call | flops 260919263232 | bytes 566231040 | tf_op jit(solution)/shard_map/attn_grad/pallas_call | solution.py:565
  405.4 13.5 %ff_grad.3 = (bf16[4,144,1152]{2,1,0:T(8,128)(2,1)}, bf16[4,144,1152]{2,1,0:T(8,128)(2,1)}, bf16[4,144,1152]{2,1,0:T(8,128)(2,1)}, bf16[4,144,1152]{2,1,0:T(8,128)(2,1)}) custom-call(bf16[576,768]{1,0:T(8,128)(2,1)} %get-tuple-element.336.refs_0_, bf16[576,768]{1,0:T(8,128)(2,1)} %collective-permute-done.23.refs_1_, ...), custom_call_target="tpu_custom_call" | custom-call | flops 521838526464 | bytes 1245708288 | tf_op jit(solution)/shard_map/ff_grad/pallas_call | solution.py:527
  418.8 1.9 fusion.7
  420.7 16.1 %attn_bwd.6 = (bf16[768,1152]{1,0:T(8,128)(2,1)}, f32[768,1152]{1,0:T(8,128)}, f32[1,864]{1,0:T(1,128)}) custom-call(bf16[768,864]{1,0:T(8,128)(2,1)} %get-tuple-element.244.refs_0_, bf16[768,288]{1,0:T(8,128)(2,1)} %get-tuple-element.245.refs_1_, f32[8,768]{1,0:T(8,128)} %get-tuple-element.246.refs_2_, bf16[768,1152]{1,0:T(8,128)(2,1)} %get-tuple-element.211.refs_3_, ...), custom_call_target="tpu_custom_call" | custom-call | flops 517006688256 | bytes 622854144 | tf_op jit(solution)/shard_map/attn_bwd/pallas_call | solution.py:201
  438.9 1.9 fusion.6
  440.8 2.2 collective-permute-start.39
  443.0 16.2 %attn_bwd.7 = (bf16[768,1152]{1,0:T(8,128)(2,1)}, f32[768,1152]{1,0:T(8,128)}, f32[1,864]{1,0:T(1,128)}) custom-call(bf16[768,864]{1,0:T(8,128)(2,1)} %get-tuple-element.240.refs_0_, bf16[768,288]{1,0:T(8,128)(2,1)} %get-tuple-element.241.refs_1_, f32[8,768]{1,0:T(8,128)} %get-tuple-element.242.refs_2_, bf16[768,1152]{1,0:T(8,128)(2,1)} %get-tuple-element.211.refs_3_, ...), custom_call_target="tpu_custom_call" | custom-call | flops 517006688256 | bytes 622854144 | tf_op jit(solution)/shard_map/attn_bwd/pallas_call | solution.py:201
  459.4 9.7 %collective-permute-done.38 = bf16[4,144,1152]{2,1,0:T(8,128)(2,1)} collective-permute-done((bf16[4,144,1152]{2,1,0:T(8,128)(2,1)}, bf16[4,144,1152]{2,1,0:T(8,128)(2,1)}, u32[]{:S(2)}, u32[]{:S(2)}) %collective-permute-start.38) | collective-permute-done | bytes 1327136 | tf_op jit(solution)/shard_map/ppermute | solution.py:577
  469.1 2.7 add_convert_fusion.2
  472.8 8.4 %norm_back.3 = (f32[729,1152]{1,0:T(8,128)}, f32[1,1152]{1,0:T(1,128)}, f32[1,1152]{1,0:T(1,128)}) custom-call(s32[8]{0:T(128)} %stack.125.refs_0_, bf16[768,1152]{1,0:T(8,128)(2,1)} %pad.35.refs_1_, f32[768,1152]{1,0:T(8,128)} %get-tuple-element.258.refs_2_, f32[1,1152]{1,0:T(1,128)} %broadcast_in_dim.163.refs_2_.refs_3_, ...), custom_call_target="tpu_custom_call" | custom-call | flops 1358954496 | bytes 1019215872 | tf_op jit(solution)/shard_map/norm_back/pallas_call | solution.py:502
  482.6 16.0 %collective-permute-done.41 = f32[16,1152]{1,0:T(8,128)S(1)} collective-permute-done((f32[16,1152]{1,0:T(8,128)S(1)}, f32[16,1152]{1,0:T(8,128)S(1)}, u32[]{:S(2)}, u32[]{:S(2)}) %collective-permute-start.41) | collective-permute-done | bytes 73760 | tf_op jit(solution)/shard_map/ppermute | solution.py:592
  499.3 4.7 collective-permute-done.42
  506.0 2.0 collective-permute-start.44
  508.0 1.8 add_convert_fusion.1
  511.1 11.8 %attn_grad.3 = (bf16[576,1152]{1,0:T(8,128)(2,1)}, bf16[576,1152]{1,0:T(8,128)(2,1)}) custom-call(bf16[1152,768]{1,0:T(8,128)(2,1)} %get-tuple-element.273.refs_0_, bf16[1152,768]{1,0:T(8,128)(2,1)} %copy-done.58, bf16[1152,768]{1,0:T(8,128)(2,1)} %get-tuple-element.220.refs_2_, bf16[1152,768]{1,0:T(8,128)(2,1)} %collective-permute-done.28.refs_3_, ...), custom_call_target="tpu_custom_call" | custom-call | flops 260919263232 | bytes 566231040 | tf_op jit(solution)/shard_map/attn_grad/pallas_call | solution.py:565
  522.9 3.6 fusion.2
  529.7 3.6 collective-permute-done.47
  533.2 1.8 fusion.5
  535.0 2.4 collective-permute-start.48
  537.5 1.9 fusion.3
  540.3 3.1 collective-permute-done.48
  544.6 4.5 collective-permute-start.49
  550.4 5.2 copy.33
  555.6 4.5 collective-permute-done.46
  560.1 1.6 add_convert_fusion
  561.8 2.7 collective-permute-start.50
  566.3 6.5 %collective-permute-done.50 = bf16[144,1152]{1,0:T(8,128)(2,1)S(1)} collective-permute-done((bf16[144,1152]{1,0:T(8,128)(2,1)S(1)}, bf16[144,1152]{1,0:T(8,128)(2,1)S(1)}, u32[]{:S(2)}, u32[]{:S(2)}) %collective-permute-start.50) | collective-permute-done | bytes 331808 | tf_op jit(solution)/shard_map/ppermute | solution.py:577
  572.8 18.8 %collective-permute-done.51 = bf16[144,1152]{1,0:T(8,128)(2,1)S(1)} collective-permute-done((bf16[144,1152]{1,0:T(8,128)(2,1)S(1)}, bf16[144,1152]{1,0:T(8,128)(2,1)S(1)}, u32[]{:S(2)}, u32[]{:S(2)}) %collective-permute-start.51) | collective-permute-done | bytes 331808 | tf_op jit(solution)/shard_map/ppermute | solution.py:577
  (291 shorter events, 77.8 us)
Async XLA Ops:
  7.2 222.4 %all-gather.2.cloned.1.call-start = ((), (), s32[]{:S(2)}) async-start(), calls=%async_computation | async-start | bytes 10948608 | tf_op jit(solution)/shard_map/all_gather | solution.py:790
  10.6 14.8 %collective-permute-start = (bf16[80,1152]{1,0:T(8,128)(2,1)S(1)}, bf16[80,1152]{1,0:T(8,128)(2,1)S(1)}, u32[]{:S(2)}, u32[]{:S(2)}) collective-permute-start(bf16[80,1152]{1,0:T(8,128)(2,1)S(1)} %get-tuple-element.335), channel_id=1, source_target_pairs={{0,8},{8,0},{1,9},{9,1},{2,10},{10,2},{3,11},{11,3},{4,12},{12,4},... | collective-permute-start | bytes 552968 | tf_op jit(solution)/shard_map/ppermute | solution.py:577
  15.4 10.0 %collective-permute-start.2 = (bf16[144,1152]{1,0:T(8,128)(2,1)}, bf16[144,1152]{1,0:T(8,128)(2,1)S(1)}, u32[]{:S(2)}, u32[]{:S(2)}) collective-permute-start(bf16[144,1152]{1,0:T(8,128)(2,1)} %pad.36.refs_4_), channel_id=1, source_target_pairs={{0,8},{8,0},{1,9},{9,1},{2,10},{10,2},{3,11},{11,3},{4,12},{12,4},... | collective-permute-start | bytes 995336 | tf_op jit(solution)/shard_map/ppermute | solution.py:577
  15.5 9.9 %collective-permute-start.1 = (bf16[64,1152]{1,0:T(8,128)(2,1)S(1)}, bf16[64,1152]{1,0:T(8,128)(2,1)S(1)}, u32[]{:S(2)}, u32[]{:S(2)}) collective-permute-start(bf16[64,1152]{1,0:T(8,128)(2,1)S(1)} %pad_maximum_fusion.8), channel_id=1, source_target_pairs={{0,16},{16,0},{1,17},{17,1},{2,18},{18,2},{3,19},{19,3},{4,20},{20... | collective-permute-start | bytes 442376 | tf_op jit(solution)/shard_map/ppermute | solution.py:577
  25.4 184.2 %copy-start.13 = (bf16[144,1152]{1,0:T(8,128)(2,1)}, bf16[144,1152]{1,0:T(8,128)(2,1)S(1)}, u32[]{:S(2)}) copy-start(bf16[144,1152]{1,0:T(8,128)(2,1)S(1)} %collective-permute-done.2.refs_8_) | copy-start | bytes 995332
  25.4 19.9 %collective-permute-start.5 = (bf16[1152,768]{1,0:T(8,128)(2,1)}, bf16[1152,768]{1,0:T(8,128)(2,1)S(1)}, u32[]{:S(2)}, u32[]{:S(2)}) collective-permute-start(bf16[1152,768]{1,0:T(8,128)(2,1)} %get-tuple-element.273.refs_0_), channel_id=1, source_target_pairs={{0,4},{4,0},{1,5},{5,1},{2,6},{6,2},{3,7},{7,3},{8,12},{12,8},{9,1... | collective-permute-start | bytes 5308424 | tf_op jit(solution)/shard_map/ppermute | solution.py:577
  25.6 27.1 %copy-start.29 = (f32[144,1076]{1,0:T(8,128)S(1)}, f32[144,1076]{1,0:T(8,128)}, u32[]{:S(2)}) copy-start(f32[144,1076]{1,0:T(8,128)} %param.25) | copy-start | bytes 1859332
  25.6 19.2 %collective-permute-start.3 = (bf16[288,1152]{1,0:T(8,128)(2,1)S(1)}, bf16[288,1152]{1,0:T(8,128)(2,1)S(1)}, u32[]{:S(2)}, u32[]{:S(2)}) collective-permute-start(bf16[288,1152]{1,0:T(8,128)(2,1)S(1)} %pad_maximum_fusion.4.refs_3_), channel_id=1, source_target_pairs={{0,1},{1,2},{2,3},{3,0},{4,5},{5,6},{6,7},{7,4},{8,9},{9,10},{10,1... | collective-permute-start | bytes 1990664 | tf_op jit(solution)/shard_map/ppermute | solution.py:577
  28.3 17.1 %collective-permute-start.4 = (bf16[288,1152]{1,0:T(8,128)(2,1)S(1)}, bf16[288,1152]{1,0:T(8,128)(2,1)S(1)}, u32[]{:S(2)}, u32[]{:S(2)}) collective-permute-start(bf16[288,1152]{1,0:T(8,128)(2,1)S(1)} %pad_maximum_fusion.5), channel_id=1, source_target_pairs={{0,16},{16,0},{1,17},{17,1},{2,18},{18,2},{3,19},{19,3},{4,20},{20... | collective-permute-start | bytes 1990664 | tf_op jit(solution)/shard_map/ppermute | solution.py:577
  44.8 34.0 %copy-start.1 = (bf16[288,1152]{1,0:T(8,128)(2,1)}, bf16[288,1152]{1,0:T(8,128)(2,1)S(1)}, u32[]{:S(2)}) copy-start(bf16[288,1152]{1,0:T(8,128)(2,1)S(1)} %collective-permute-done.3.refs_4_) | copy-start | bytes 1990660
  46.3 19.2 %collective-permute-start.6 = (bf16[288,1152]{1,0:T(8,128)(2,1)S(1)}, bf16[288,1152]{1,0:T(8,128)(2,1)S(1)}, u32[]{:S(2)}, u32[]{:S(2)}) collective-permute-start(bf16[288,1152]{1,0:T(8,128)(2,1)S(1)} %collective-permute-done.3.refs_4_), channel_id=1, source_target_pairs={{0,1},{1,2},{2,3},{3,0},{4,5},{5,6},{6,7},{7,4},{8,9},{9,10},{10,1... | collective-permute-start | bytes 1990664 | tf_op jit(solution)/shard_map/ppermute | solution.py:577
  48.9 17.7 %collective-permute-start.7 = (bf16[320,1152]{1,0:T(8,128)(2,1)}, bf16[320,1152]{1,0:T(8,128)(2,1)S(1)}, u32[]{:S(2)}, u32[]{:S(2)}) collective-permute-start(bf16[320,1152]{1,0:T(8,128)(2,1)} %pad_maximum_fusion.2), channel_id=1, source_target_pairs={{0,16},{16,0},{1,17},{17,1},{2,18},{18,2},{3,19},{19,3},{4,20},{20... | collective-permute-start | bytes 2211848 | tf_op jit(solution)/shard_map/ppermute | solution.py:577
  51.2 14.3 %collective-permute-start.8 = (bf16[256,1152]{1,0:T(8,128)(2,1)}, bf16[256,1152]{1,0:T(8,128)(2,1)S(1)}, u32[]{:S(2)}, u32[]{:S(2)}) collective-permute-start(bf16[256,1152]{1,0:T(8,128)(2,1)} %pad_maximum_fusion.6), channel_id=1, source_target_pairs={{0,8},{8,0},{1,9},{9,1},{2,10},{10,2},{3,11},{11,3},{4,12},{12,4},... | collective-permute-start | bytes 1769480 | tf_op jit(solution)/shard_map/ppermute | solution.py:577
  65.5 56.3 %copy-start.8 = (bf16[256,1152]{1,0:T(8,128)(2,1)}, bf16[256,1152]{1,0:T(8,128)(2,1)S(1)}, u32[]{:S(2)}) copy-start(bf16[256,1152]{1,0:T(8,128)(2,1)S(1)} %collective-permute-done.8.refs_9_) | copy-start | bytes 1769476
  65.5 37.2 %copy-start.2 = (bf16[288,1152]{1,0:T(8,128)(2,1)}, bf16[288,1152]{1,0:T(8,128)(2,1)S(1)}, u32[]{:S(2)}) copy-start(bf16[288,1152]{1,0:T(8,128)(2,1)S(1)} %collective-permute-done.6.refs_5_) | copy-start | bytes 1990660
  66.6 55.3 %copy-start.5 = (bf16[320,1152]{1,0:T(8,128)(2,1)}, bf16[320,1152]{1,0:T(8,128)(2,1)S(1)}, u32[]{:S(2)}) copy-start(bf16[320,1152]{1,0:T(8,128)(2,1)S(1)} %collective-permute-done.7.refs_7_) | copy-start | bytes 2211844
  77.1 25.4 %collective-permute-start.10 = (bf16[576,768]{1,0:T(8,128)(2,1)S(1)}, bf16[576,768]{1,0:T(8,128)(2,1)S(1)}, u32[]{:S(2)}, u32[]{:S(2)}) collective-permute-start(bf16[576,768]{1,0:T(8,128)(2,1)S(1)} %get-tuple-element.161), channel_id=1, source_target_pairs={{0,4},{4,0},{1,5},{5,1},{2,6},{6,2},{3,7},{7,3},{8,12},{12,8},{9,1... | collective-permute-start | bytes 2654216 | tf_op jit(solution)/shard_map/ppermute | solution.py:577
  77.2 25.3 %collective-permute-start.9 = (bf16[288,1152]{1,0:T(8,128)(2,1)S(1)}, bf16[288,1152]{1,0:T(8,128)(2,1)S(1)}, u32[]{:S(2)}, u32[]{:S(2)}) collective-permute-start(bf16[288,1152]{1,0:T(8,128)(2,1)S(1)} %collective-permute-done.6.refs_5_), channel_id=1, source_target_pairs={{0,1},{1,2},{2,3},{3,0},{4,5},{5,6},{6,7},{7,4},{8,9},{9,10},{10,1... | collective-permute-start | bytes 1990664 | tf_op jit(solution)/shard_map/ppermute | solution.py:577
  102.6 19.3 %collective-permute-start.13 = (bf16[1152,1152]{1,0:T(8,128)(2,1)S(1)}, bf16[1152,1152]{1,0:T(8,128)(2,1)}, u32[]{:S(2)}, u32[]{:S(2)}) collective-permute-start(bf16[1152,1152]{1,0:T(8,128)(2,1)S(1)} %constant_dynamic-update-slice_fusion), channel_id=1, source_target_pairs={{0,4},{4,0},{1,5},{5,1},{2,6},{6,2},{3,7},{7,3},{8,12},{12,8},{9,1... | collective-permute-start | bytes 7962632 | tf_op jit(solution)/shard_map/ppermute | solution.py:577
  103.8 18.1 %collective-permute-start.11 = (bf16[320,1152]{1,0:T(8,128)(2,1)S(1)}, bf16[320,1152]{1,0:T(8,128)(2,1)S(1)}, u32[]{:S(2)}, u32[]{:S(2)}) collective-permute-start(bf16[320,1152]{1,0:T(8,128)(2,1)S(1)} %pad_maximum_fusion.3), channel_id=1, source_target_pairs={{0,16},{16,0},{1,17},{17,1},{2,18},{18,2},{3,19},{19,3},{4,20},{20... | collective-permute-start | bytes 2211848 | tf_op jit(solution)/shard_map/ppermute | solution.py:577
  105.4 27.6 %copy-start.34 = (f32[2,1152]{1,0:T(2,128)S(1)}, f32[2,1152]{1,0:T(2,128)}, u32[]{:S(2)}) copy-start(f32[2,1152]{1,0:T(2,128)} %param.20) | copy-start | bytes 27652
  105.4 15.3 %collective-permute-start.12 = (bf16[256,1152]{1,0:T(8,128)(2,1)S(1)}, bf16[256,1152]{1,0:T(8,128)(2,1)S(1)}, u32[]{:S(2)}, u32[]{:S(2)}) collective-permute-start(bf16[256,1152]{1,0:T(8,128)(2,1)S(1)} %pad_maximum_fusion.7), channel_id=1, source_target_pairs={{0,8},{8,0},{1,9},{9,1},{2,10},{10,2},{3,11},{11,3},{4,12},{12,4},... | collective-permute-start | bytes 1769480 | tf_op jit(solution)/shard_map/ppermute | solution.py:577
  128.0 44.1 %collective-permute-start.17 = (bf16[1152,1152]{1,0:T(8,128)(2,1)}, bf16[1152,1152]{1,0:T(8,128)(2,1)S(1)}, u32[]{:S(2)}, u32[]{:S(2)}) collective-permute-start(bf16[1152,1152]{1,0:T(8,128)(2,1)} %pad_maximum_fusion), channel_id=1, source_target_pairs={{0,4},{4,0},{1,5},{5,1},{2,6},{6,2},{3,7},{7,3},{8,12},{12,8},{9,1... | collective-permute-start | bytes 7962632 | tf_op jit(solution)/shard_map/ppermute | solution.py:577
  128.0 32.4 %collective-permute-start.14 = (bf16[144,1152]{1,0:T(8,128)(2,1)}, bf16[144,1152]{1,0:T(8,128)(2,1)S(1)}, u32[]{:S(2)}, u32[]{:S(2)}) collective-permute-start(bf16[144,1152]{1,0:T(8,128)(2,1)} %pad.36.refs_4_), channel_id=1, source_target_pairs={{0,1},{1,2},{2,3},{3,0},{4,5},{5,6},{6,7},{7,4},{8,9},{9,10},{10,1... | collective-permute-start | bytes 995336 | tf_op jit(solution)/shard_map/ppermute | solution.py:577
  129.0 42.4 %collective-permute-start.15 = (bf16[144,1152]{1,0:T(8,128)(2,1)}, bf16[144,1152]{1,0:T(8,128)(2,1)}, u32[]{:S(2)}, u32[]{:S(2)}) collective-permute-start(bf16[144,1152]{1,0:T(8,128)(2,1)} %pad.36.refs_4_), channel_id=1, source_target_pairs={{0,2},{1,3},{2,0},{3,1},{4,6},{5,7},{6,4},{7,5},{8,10},{9,11},{10,... | collective-permute-start | bytes 995336 | tf_op jit(solution)/shard_map/ppermute | solution.py:577
  131.4 40.7 %collective-permute-start.16 = (bf16[144,1152]{1,0:T(8,128)(2,1)}, bf16[144,1152]{1,0:T(8,128)(2,1)}, u32[]{:S(2)}, u32[]{:S(2)}) collective-permute-start(bf16[144,1152]{1,0:T(8,128)(2,1)} %pad.36.refs_4_), channel_id=1, source_target_pairs={{0,3},{1,0},{2,1},{3,2},{4,7},{5,4},{6,5},{7,6},{8,11},{9,8},{10,9... | collective-permute-start | bytes 995336 | tf_op jit(solution)/shard_map/ppermute | solution.py:577
  160.4 35.8 %copy-start.18 = (bf16[144,1152]{1,0:T(8,128)(2,1)}, bf16[144,1152]{1,0:T(8,128)(2,1)S(1)}, u32[]{:S(2)}) copy-start(bf16[144,1152]{1,0:T(8,128)(2,1)S(1)} %collective-permute-done.14.refs_5_) | copy-start | bytes 995332
  178.7 31.7 %collective-permute-start.18 = (bf16[432,1152]{1,0:T(8,128)(2,1)}, bf16[432,1152]{1,0:T(8,128)(2,1)}, u32[]{:S(2)}, u32[]{:S(2)}) collective-permute-start(bf16[432,1152]{1,0:T(8,128)(2,1)} %get-tuple-element.348), channel_id=1, source_target_pairs={{0,8},{8,0},{1,9},{9,1},{2,10},{10,2},{3,11},{11,3},{4,12},{12,4},... | collective-permute-start | bytes 2985992 | tf_op jit(solution)/shard_map/ppermute | solution.py:577
  179.7 30.7 %collective-permute-start.19 = (bf16[432,1152]{1,0:T(8,128)(2,1)}, bf16[432,1152]{1,0:T(8,128)(2,1)}, u32[]{:S(2)}, u32[]{:S(2)}) collective-permute-start(bf16[432,1152]{1,0:T(8,128)(2,1)} %get-tuple-element.348), channel_id=1, source_target_pairs={{0,16},{16,0},{1,17},{17,1},{2,18},{18,2},{3,19},{19,3},{4,20},{20... | collective-permute-start | bytes 2985992 | tf_op jit(solution)/shard_map/ppermute | solution.py:577
  212.7 38.1 %collective-permute-start.21 = (bf16[1152,1152]{1,0:T(8,128)(2,1)}, bf16[1152,1152]{1,0:T(8,128)(2,1)S(1)}, u32[]{:S(2)}, u32[]{:S(2)}) collective-permute-start(bf16[1152,1152]{1,0:T(8,128)(2,1)} %constant_dynamic-update-slice_fusion.10), channel_id=1, source_target_pairs={{0,4},{4,0},{1,5},{5,1},{2,6},{6,2},{3,7},{7,3},{8,12},{12,8},{9,1... | collective-permute-start | bytes 7962632 | tf_op jit(solution)/shard_map/ppermute | solution.py:577
  215.2 35.6 %collective-permute-start.22 = (bf16[720,1152]{1,0:T(8,128)(2,1)}, bf16[720,1152]{1,0:T(8,128)(2,1)}, u32[]{:S(2)}, u32[]{:S(2)}) collective-permute-start(bf16[720,1152]{1,0:T(8,128)(2,1)} %pad_maximum_fusion.1), channel_id=1, source_target_pairs={{0,4},{4,0},{1,5},{5,1},{2,6},{6,2},{3,7},{7,3},{8,12},{12,8},{9,1... | collective-permute-start | bytes 4976648 | tf_op jit(solution)/shard_map/ppermute | solution.py:577
  217.5 33.3 %collective-permute-start.20 = (bf16[432,1152]{1,0:T(8,128)(2,1)}, bf16[432,1152]{1,0:T(8,128)(2,1)}, u32[]{:S(2)}, u32[]{:S(2)}) collective-permute-start(bf16[432,1152]{1,0:T(8,128)(2,1)} %collective-permute-done.18.refs_9_), channel_id=1, source_target_pairs={{0,16},{16,0},{1,17},{17,1},{2,18},{18,2},{3,19},{19,3},{4,20},{20... | collective-permute-start | bytes 2985992 | tf_op jit(solution)/shard_map/ppermute | solution.py:577
  227.4 23.4 %collective-permute-start.23 = (bf16[576,768]{1,0:T(8,128)(2,1)S(1)}, bf16[576,768]{1,0:T(8,128)(2,1)}, u32[]{:S(2)}, u32[]{:S(2)}) collective-permute-start(bf16[576,768]{1,0:T(8,128)(2,1)S(1)} %get-tuple-element.337), channel_id=1, source_target_pairs={{0,4},{4,0},{1,5},{5,1},{2,6},{6,2},{3,7},{7,3},{8,12},{12,8},{9,1... | collective-permute-start | bytes 2654216 | tf_op jit(solution)/shard_map/ppermute | solution.py:577
  250.8 42.8 %collective-permute-start.25 = (bf16[768,4608]{1,0:T(8,128)(2,1)}, bf16[768,4608]{1,0:T(8,128)(2,1)}, u32[]{:S(2)}, u32[]{:S(2)}) collective-permute-start(bf16[768,4608]{1,0:T(8,128)(2,1)} %get-tuple-element.189.refs_2_), channel_id=1, source_target_pairs={{0,4},{4,0},{1,5},{5,1},{2,6},{6,2},{3,7},{7,3},{8,12},{12,8},{9,1... | collective-permute-start | bytes 21233672 | tf_op jit(solution)/shard_map/ppermute | solution.py:577
  251.4 12.7 %collective-permute-start.24 = (bf16[432,1152]{1,0:T(8,128)(2,1)}, bf16[432,1152]{1,0:T(8,128)(2,1)}, u32[]{:S(2)}, u32[]{:S(2)}) collective-permute-start(bf16[432,1152]{1,0:T(8,128)(2,1)} %collective-permute-done.20.refs_12_), channel_id=1, source_target_pairs={{0,4},{4,0},{1,5},{5,1},{2,6},{6,2},{3,7},{7,3},{8,12},{12,8},{9,1... | collective-permute-start | bytes 2985992 | tf_op jit(solution)/shard_map/ppermute | solution.py:577
  307.1 32.3 %collective-permute-start.26 = (bf16[4,144,1152]{2,1,0:T(8,128)(2,1)}, bf16[4,144,1152]{2,1,0:T(8,128)(2,1)}, u32[]{:S(2)}, u32[]{:S(2)}) collective-permute-start(bf16[4,144,1152]{2,1,0:T(8,128)(2,1)} %get-tuple-element.205), channel_id=1, source_target_pairs={{0,8},{8,0},{1,9},{9,1},{2,10},{10,2},{3,11},{11,3},{4,12},{12,4},... | collective-permute-start | bytes 3981320 | tf_op jit(solution)/shard_map/ppermute | solution.py:577
  308.1 67.3 %collective-permute-start.29 = (bf16[4,144,1152]{2,1,0:T(8,128)(2,1)}, bf16[4,144,1152]{2,1,0:T(8,128)(2,1)}, u32[]{:S(2)}, u32[]{:S(2)}) collective-permute-start(bf16[4,144,1152]{2,1,0:T(8,128)(2,1)} %get-tuple-element.203), channel_id=1, source_target_pairs={{0,8},{8,0},{1,9},{9,1},{2,10},{10,2},{3,11},{11,3},{4,12},{12,4},... | collective-permute-start | bytes 3981320 | tf_op jit(solution)/shard_map/ppermute | solution.py:577
  309.1 96.3 %collective-permute-start.32 = (bf16[768,4608]{1,0:T(8,128)(2,1)}, bf16[768,4608]{1,0:T(8,128)(2,1)}, u32[]{:S(2)}, u32[]{:S(2)}) collective-permute-start(bf16[768,4608]{1,0:T(8,128)(2,1)} %get-tuple-element.231.gu.refs_2_), channel_id=1, source_target_pairs={{0,4},{4,0},{1,5},{5,1},{2,6},{6,2},{3,7},{7,3},{8,12},{12,8},{9,1... | collective-permute-start | bytes 21233672 | tf_op jit(solution)/shard_map/ppermute | solution.py:577
  334.7 40.7 %collective-permute-start.28 = (bf16[1152,768]{1,0:T(8,128)(2,1)}, bf16[1152,768]{1,0:T(8,128)(2,1)}, u32[]{:S(2)}, u32[]{:S(2)}) collective-permute-start(bf16[1152,768]{1,0:T(8,128)(2,1)} %get-tuple-element.220.refs_2_), channel_id=1, source_target_pairs={{0,4},{4,0},{1,5},{5,1},{2,6},{6,2},{3,7},{7,3},{8,12},{12,8},{9,1... | collective-permute-start | bytes 5308424 | tf_op jit(solution)/shard_map/ppermute | solution.py:577
  342.0 33.4 %collective-permute-start.30 = (bf16[4,144,1152]{2,1,0:T(8,128)(2,1)}, bf16[4,144,1152]{2,1,0:T(8,128)(2,1)}, u32[]{:S(2)}, u32[]{:S(2)}) collective-permute-start(bf16[4,144,1152]{2,1,0:T(8,128)(2,1)} %add_convert_fusion.4), channel_id=1, source_target_pairs={{0,16},{16,0},{1,17},{17,1},{2,18},{18,2},{3,19},{19,3},{4,20},{20... | collective-permute-start | bytes 3981320 | tf_op jit(solution)/shard_map/ppermute | solution.py:577
  359.2 16.3 %collective-permute-start.27 = (bf16[768,1152]{1,0:T(8,128)(2,1)}, bf16[768,1152]{1,0:T(8,128)(2,1)}, u32[]{:S(2)}, u32[]{:S(2)}) collective-permute-start(bf16[768,1152]{1,0:T(8,128)(2,1)} %get-tuple-element.219), channel_id=1, source_target_pairs={{0,4},{4,0},{1,5},{5,1},{2,6},{6,2},{3,7},{7,3},{8,12},{12,8},{9,1... | collective-permute-start | bytes 5308424 | tf_op jit(solution)/shard_map/ppermute | solution.py:577
  379.6 39.2 %collective-permute-start.33 = (bf16[144,1152]{1,0:T(8,128)(2,1)}, bf16[144,1152]{1,0:T(8,128)(2,1)}, u32[]{:S(2)}, u32[]{:S(2)}) collective-permute-start(bf16[144,1152]{1,0:T(8,128)(2,1)} %get-tuple-element.341), channel_id=1, source_target_pairs={{0,3},{1,0},{2,1},{3,2},{4,7},{5,4},{6,5},{7,6},{8,11},{9,8},{10,9... | collective-permute-start | bytes 995336 | tf_op jit(solution)/shard_map/ppermute | solution.py:577
  403.4 34.1 %collective-permute-start.35 = (bf16[576,1152]{1,0:T(8,128)(2,1)}, bf16[576,1152]{1,0:T(8,128)(2,1)}, u32[]{:S(2)}, u32[]{:S(2)}) collective-permute-start(bf16[576,1152]{1,0:T(8,128)(2,1)} %get-tuple-element.230), channel_id=1, source_target_pairs={{0,8},{8,0},{1,9},{9,1},{2,10},{10,2},{3,11},{11,3},{4,12},{12,4},... | collective-permute-start | bytes 3981320 | tf_op jit(solution)/shard_map/ppermute | solution.py:577
  403.9 104.1 %collective-permute-start.31 = (bf16[576,1152]{1,0:T(8,128)(2,1)}, bf16[576,1152]{1,0:T(8,128)(2,1)}, u32[]{:S(2)}, u32[]{:S(2)}) collective-permute-start(bf16[576,1152]{1,0:T(8,128)(2,1)} %get-tuple-element.228), channel_id=1, source_target_pairs={{0,8},{8,0},{1,9},{9,1},{2,10},{10,2},{3,11},{11,3},{4,12},{12,4},... | collective-permute-start | bytes 3981320 | tf_op jit(solution)/shard_map/ppermute | solution.py:577
  420.7 18.2 %collective-permute-start.36 = (bf16[144,1152]{1,0:T(8,128)(2,1)}, bf16[144,1152]{1,0:T(8,128)(2,1)}, u32[]{:S(2)}, u32[]{:S(2)}) collective-permute-start(bf16[144,1152]{1,0:T(8,128)(2,1)} %fusion.7), channel_id=1, source_target_pairs={{0,3},{1,0},{2,1},{3,2},{4,7},{5,4},{6,5},{7,6},{8,11},{9,8},{10,9... | collective-permute-start | bytes 995336 | tf_op jit(solution)/shard_map/ppermute | solution.py:577
  436.9 32.2 %collective-permute-start.37 = (bf16[768,1152]{1,0:T(8,128)(2,1)}, bf16[768,1152]{1,0:T(8,128)(2,1)}, u32[]{:S(2)}, u32[]{:S(2)}) collective-permute-start(bf16[768,1152]{1,0:T(8,128)(2,1)} %get-tuple-element.253), channel_id=1, source_target_pairs={{0,4},{4,0},{1,5},{5,1},{2,6},{6,2},{3,7},{7,3},{8,12},{12,8},{9,1... | collective-permute-start | bytes 5308424 | tf_op jit(solution)/shard_map/ppermute | solution.py:577
  436.9 32.2 %collective-permute-start.38 = (bf16[4,144,1152]{2,1,0:T(8,128)(2,1)}, bf16[4,144,1152]{2,1,0:T(8,128)(2,1)}, u32[]{:S(2)}, u32[]{:S(2)}) collective-permute-start(bf16[4,144,1152]{2,1,0:T(8,128)(2,1)} %get-tuple-element.254), channel_id=1, source_target_pairs={{0,16},{16,0},{1,17},{17,1},{2,18},{18,2},{3,19},{19,3},{4,20},{20... | collective-permute-start | bytes 3981320 | tf_op jit(solution)/shard_map/ppermute | solution.py:577
  437.4 70.6 %collective-permute-start.34 = (bf16[4,144,1152]{2,1,0:T(8,128)(2,1)}, bf16[4,144,1152]{2,1,0:T(8,128)(2,1)}, u32[]{:S(2)}, u32[]{:S(2)}) collective-permute-start(bf16[4,144,1152]{2,1,0:T(8,128)(2,1)} %get-tuple-element.238), channel_id=1, source_target_pairs={{0,16},{16,0},{1,17},{17,1},{2,18},{18,2},{3,19},{19,3},{4,20},{20... | collective-permute-start | bytes 3981320 | tf_op jit(solution)/shard_map/ppermute | solution.py:577
  440.8 18.6 %collective-permute-start.39 = (bf16[144,1152]{1,0:T(8,128)(2,1)}, bf16[144,1152]{1,0:T(8,128)(2,1)}, u32[]{:S(2)}, u32[]{:S(2)}) collective-permute-start(bf16[144,1152]{1,0:T(8,128)(2,1)} %fusion.6), channel_id=1, source_target_pairs={{0,3},{1,0},{2,1},{3,2},{4,7},{5,4},{6,5},{7,6},{8,11},{9,8},{10,9... | collective-permute-start | bytes 995336 | tf_op jit(solution)/shard_map/ppermute | solution.py:577
  443.0 26.1 %copy-start.25 = (bf16[4,144,1152]{2,1,0:T(8,128)(2,1)S(1)}, bf16[4,144,1152]{2,1,0:T(8,128)(2,1)}, u32[]{:S(2)}) copy-start(bf16[4,144,1152]{2,1,0:T(8,128)(2,1)} %get-tuple-element.239) | copy-start | bytes 3981316
  471.8 36.2 %collective-permute-start.40 = (bf16[4,144,1152]{2,1,0:T(8,128)(2,1)}, bf16[4,144,1152]{2,1,0:T(8,128)(2,1)S(1)}, u32[]{:S(2)}, u32[]{:S(2)}) collective-permute-start(bf16[4,144,1152]{2,1,0:T(8,128)(2,1)} %add_convert_fusion.2), channel_id=1, source_target_pairs={{0,8},{8,0},{1,9},{9,1},{2,10},{10,2},{3,11},{11,3},{4,12},{12,4},... | collective-permute-start | bytes 3981320 | tf_op jit(solution)/shard_map/ppermute | solution.py:577
  472.8 35.2 %copy-start.22 = (bf16[4,144,1152]{2,1,0:T(8,128)(2,1)S(1)}, bf16[4,144,1152]{2,1,0:T(8,128)(2,1)}, u32[]{:S(2)}) copy-start(bf16[4,144,1152]{2,1,0:T(8,128)(2,1)} %get-tuple-element.279) | copy-start | bytes 3981316
  482.2 16.5 %collective-permute-start.41 = (f32[16,1152]{1,0:T(8,128)S(1)}, f32[16,1152]{1,0:T(8,128)S(1)}, u32[]{:S(2)}, u32[]{:S(2)}) collective-permute-start(f32[16,1152]{1,0:T(8,128)S(1)} %pad.44), channel_id=1, source_target_pairs={{0,16},{16,0},{1,17},{17,1},{2,18},{18,2},{3,19},{19,3},{4,20},{20... | collective-permute-start | bytes 221192 | tf_op jit(solution)/shard_map/ppermute | solution.py:592
  498.6 5.3 collective-permute-start.42
  504.0 1.3 collective-permute-start.43
  506.0 20.6 %collective-permute-start.44 = (f32[16,1152]{1,0:T(8,128)}, f32[16,1152]{1,0:T(8,128)}, u32[]{:S(2)}, u32[]{:S(2)}) collective-permute-start(f32[16,1152]{1,0:T(8,128)} %add.357), channel_id=1, source_target_pairs={{0,1},{1,0},{2,3},{3,2},{4,5},{5,4},{6,7},{7,6},{8,9},{9,8},{10,11... | collective-permute-start | bytes 221192 | tf_op jit(solution)/shard_map/ppermute | solution.py:592
  522.9 10.4 %collective-permute-start.47 = (bf16[144,1152]{1,0:T(8,128)(2,1)}, bf16[144,1152]{1,0:T(8,128)(2,1)S(1)}, u32[]{:S(2)}, u32[]{:S(2)}) collective-permute-start(bf16[144,1152]{1,0:T(8,128)(2,1)} %get-tuple-element.283), channel_id=1, source_target_pairs={{0,3},{1,0},{2,1},{3,2},{4,7},{5,4},{6,5},{7,6},{8,11},{9,8},{10,9... | collective-permute-start | bytes 995336 | tf_op jit(solution)/shard_map/ppermute | solution.py:577
  527.6 11.7 %collective-permute-start.45 = (f32[16,1152]{1,0:T(8,128)S(1)}, f32[16,1152]{1,0:T(8,128)S(1)}, u32[]{:S(2)}, u32[]{:S(2)}) collective-permute-start(f32[16,1152]{1,0:T(8,128)S(1)} %add.358), channel_id=1, source_target_pairs={{0,2},{1,3},{2,0},{3,1},{4,6},{5,7},{6,4},{7,5},{8,10},{9,11},{10,... | collective-permute-start | bytes 221192 | tf_op jit(solution)/shard_map/ppermute | solution.py:592
  529.1 30.9 %collective-permute-start.46 = (bf16[576,1152]{1,0:T(8,128)(2,1)}, bf16[576,1152]{1,0:T(8,128)(2,1)}, u32[]{:S(2)}, u32[]{:S(2)}) collective-permute-start(bf16[576,1152]{1,0:T(8,128)(2,1)} %get-tuple-element.278), channel_id=1, source_target_pairs={{0,16},{16,0},{1,17},{17,1},{2,18},{18,2},{3,19},{19,3},{4,20},{20... | collective-permute-start | bytes 3981320 | tf_op jit(solution)/shard_map/ppermute | solution.py:577
  535.0 8.4 %collective-permute-start.48 = (bf16[144,1152]{1,0:T(8,128)(2,1)}, bf16[144,1152]{1,0:T(8,128)(2,1)}, u32[]{:S(2)}, u32[]{:S(2)}) collective-permute-start(bf16[144,1152]{1,0:T(8,128)(2,1)} %fusion.5), channel_id=1, source_target_pairs={{0,3},{1,0},{2,1},{3,2},{4,7},{5,4},{6,5},{7,6},{8,11},{9,8},{10,9... | collective-permute-start | bytes 995336 | tf_op jit(solution)/shard_map/ppermute | solution.py:577
  544.6 11.0 %collective-permute-start.49 = (bf16[144,1152]{1,0:T(8,128)(2,1)S(1)}, bf16[144,1152]{1,0:T(8,128)(2,1)S(1)}, u32[]{:S(2)}, u32[]{:S(2)}) collective-permute-start(bf16[144,1152]{1,0:T(8,128)(2,1)S(1)} %fusion.4), channel_id=1, source_target_pairs={{0,3},{1,0},{2,1},{3,2},{4,7},{5,4},{6,5},{7,6},{8,11},{9,8},{10,9... | collective-permute-start | bytes 995336 | tf_op jit(solution)/shard_map/ppermute | solution.py:577
  561.8 11.0 %collective-permute-start.50 = (bf16[144,1152]{1,0:T(8,128)(2,1)S(1)}, bf16[144,1152]{1,0:T(8,128)(2,1)S(1)}, u32[]{:S(2)}, u32[]{:S(2)}) collective-permute-start(bf16[144,1152]{1,0:T(8,128)(2,1)S(1)} %get-tuple-element.344), channel_id=1, source_target_pairs={{0,3},{1,0},{2,1},{3,2},{4,7},{5,4},{6,5},{7,6},{8,11},{9,8},{10,9... | collective-permute-start | bytes 995336 | tf_op jit(solution)/shard_map/ppermute | solution.py:577
  564.5 27.1 %collective-permute-start.51 = (bf16[144,1152]{1,0:T(8,128)(2,1)S(1)}, bf16[144,1152]{1,0:T(8,128)(2,1)S(1)}, u32[]{:S(2)}, u32[]{:S(2)}) collective-permute-start(bf16[144,1152]{1,0:T(8,128)(2,1)S(1)} %get-tuple-element.346), channel_id=1, source_target_pairs={{0,2},{1,3},{2,0},{3,1},{4,6},{5,7},{6,4},{7,5},{8,10},{9,11},{10,... | collective-permute-start | bytes 995336 | tf_op jit(solution)/shard_map/ppermute | solution.py:577
  564.5 27.1 %collective-permute-start.52 = (bf16[144,1152]{1,0:T(8,128)(2,1)S(1)}, bf16[144,1152]{1,0:T(8,128)(2,1)S(1)}, u32[]{:S(2)}, u32[]{:S(2)}) collective-permute-start(bf16[144,1152]{1,0:T(8,128)(2,1)S(1)} %get-tuple-element.345), channel_id=1, source_target_pairs={{0,1},{1,2},{2,3},{3,0},{4,5},{5,6},{6,7},{7,4},{8,9},{9,10},{10,1... | collective-permute-start | bytes 995336 | tf_op jit(solution)/shard_map/ppermute | solution.py:577
  (50 other events, 508.4 us)
Sparse Core Ops, SparseCore 0:
  66.7 115.0 all-gather.1

commit v3 on v2

--- a/solution.py
+++ b/solution.py
@@ -77,143 +77,136 @@
         )
 
 
-def masked_tail(values, low, seq):
+def cut_rows(values, low, seq):
     tail = values[low:]
     rows = lax.broadcasted_iota(jnp.int32, tail.shape, 0)
-    return jnp.where(rows < seq - low, tail, -1e30)
-
-
-def attn_fwd_kernel(plan, pieces_total, has_acc, seq, *refs):
+    return values[0:low], jnp.where(rows < seq - low, tail, -1e30)
+
+
+def attn_fwd_kernel(plan, pieces_total, seq, *refs):
     table, x, bias = refs[:3]
     pieces = refs[3 : 3 + pieces_total]
-    rest = refs[3 + pieces_total :]
-    if has_acc:
-        acc_in, rest = rest[0], rest[1:]
-    proj, mixed, lse, acc, w, mixed_t, sems = rest
+    proj, mixed, lse, w_out, wo, w, mixed_t, probs, sems, out_sem = refs[3 + pieces_total :]
     width = GROUP_HEADS * HEAD_DIM
     keys = -(-seq // 16) * 16
-    low = seq // 8 * 8
+    low = seq // 16 * 16
     scale = HEAD_DIM**-0.5 * LOG2E
 
     for c in plan.copies(0, pieces, table, w, sems):
         c.start()
     for c in plan.copies(0, pieces, table, w, sems):
         c.wait()
+    keep = pltpu.make_async_copy(w, w_out, out_sem)
+    keep.start()
 
     proj[...] = (nn(x[...], w[:, 0 : 3 * width]) + bias[...]).astype(BF16)
+    wo[...] = w[:, 3 * width : 4 * width]
     for h in range(GROUP_HEADS):
         q = proj[:, h * HEAD_DIM : (h + 1) * HEAD_DIM]
         k = proj[0:keys, width + h * HEAD_DIM : width + (h + 1) * HEAD_DIM]
         v = proj[0:keys, 2 * width + h * HEAD_DIM : 2 * width + (h + 1) * HEAD_DIM]
-        s = nt(k, q)
-        tail = masked_tail(s, low, seq)
-        top = jnp.maximum(
-            jnp.max(s[0:low], axis=0, keepdims=True), jnp.max(tail, axis=0, keepdims=True)
-        )
+        parts = cut_rows(nt(k, q), low, seq)
+        top = functools.reduce(jnp.maximum, [jnp.max(t, axis=0, keepdims=True) for t in parts])
         shift = top * scale
-        p = jnp.exp2(jnp.concatenate([s[0:low], tail], axis=0) * scale - shift)
-        total = jnp.sum(p, axis=0, keepdims=True)
-        mixed_t[h * HEAD_DIM : (h + 1) * HEAD_DIM, :] = tn(v, p.astype(BF16)) / total
+        total = jnp.zeros_like(top)
+        for t, rows in zip(parts, (slice(0, low), slice(low, keys))):
+            p = jnp.exp2(t * scale - shift)
+            total += jnp.sum(p, axis=0, keepdims=True)
+            probs[rows, :] = p.astype(BF16)
+        mixed_t[h * HEAD_DIM : (h + 1) * HEAD_DIM, :] = tn(v, probs[...]) / total
         lse[h : h + 1, :] = shift + jnp.log2(total)
     mixed[...] = mixed_t[...].T.astype(BF16)
-    part = nt(mixed[...], w[:, 3 * width : 4 * width])
-    acc[...] = part + acc_in[...] if has_acc else part
-
-
-def attn_fwd(table, x, bias, pieces, plan, acc_in, seq):
+    keep.wait()
+
+
+def attn_fwd(table, x, bias, pieces, plan, seq):
     d = x.shape[1]
     gw = plan.columns
     width = GROUP_HEADS * HEAD_DIM
-    has_acc = acc_in is not None
+    keys = -(-seq // 16) * 16
     vmem = pl.BlockSpec(memory_space=pltpu.VMEM)
+    anywhere = pl.BlockSpec(memory_space=pl.ANY)
     return pl.pallas_call(
-        functools.partial(attn_fwd_kernel, plan, len(pieces), has_acc, seq),
-        in_specs=[
-            pl.BlockSpec(memory_space=pltpu.SMEM),
-            vmem,
-            vmem,
-            *[pl.BlockSpec(memory_space=pl.ANY) for _ in pieces],
-            *([vmem] if has_acc else []),
-        ],
-        out_specs=[vmem] * 5,
+        functools.partial(attn_fwd_kernel, plan, len(pieces), seq),
+        in_specs=[pl.BlockSpec(memory_space=pltpu.SMEM), vmem, vmem, *[anywhere for _ in pieces]],
+        out_specs=[vmem, vmem, vmem, anywhere, vmem],
         out_shape=[
             jax.ShapeDtypeStruct((PAD, 3 * width), BF16),
             jax.ShapeDtypeStruct((PAD, width), BF16),
             jax.ShapeDtypeStruct((8, PAD), F32),
-            jax.ShapeDtypeStruct((PAD, d), F32),
             jax.ShapeDtypeStruct((d, gw), BF16),
+            jax.ShapeDtypeStruct((d, width), BF16),
         ],
         scratch_shapes=[
+            pltpu.VMEM((d, gw), BF16),
             pltpu.VMEM((width, PAD), F32),
+            pltpu.VMEM((keys, PAD), BF16),
             pltpu.SemaphoreType.DMA((len(plan.entries),)),
+            pltpu.SemaphoreType.DMA,
         ],
         compiler_params=params(),
-        cost_estimate=cost(
-            2 * PAD * (d * 4 * width + 8 * PAD * 256), d * gw * 4 + PAD * d * 8, 0.05),
+        cost_estimate=cost(2 * PAD * (d * 4 * width + 8 * PAD * 256), d * gw * 4, 0.05),
         name="attn_fwd",
-    )(table, x, bias, *pieces, *([acc_in] if has_acc else []))
-
-
-def attn_bwd_kernel(has_acc, seq, *refs):
-    proj, mixed, lse, ga, w = refs[:5]
-    rest = refs[5:]
-    if has_acc:
-        acc_in, rest = rest[0], rest[1:]
-    grads, acc, sums, gm, dq_t = rest
+    )(table, x, bias, *pieces)
+
+
+def attn_bwd_kernel(seq, proj, mixed, lse, ga, wo, grads, sums, gm, dq_t, probs, slopes):
     width = GROUP_HEADS * HEAD_DIM
     keys = -(-seq // 16) * 16
-    low = seq // 8 * 8
+    low = seq // 16 * 16
     factor = HEAD_DIM**-0.5
     scale = factor * LOG2E
-    gm[...] = nn(ga[...], w[:, 3 * width : 4 * width]).astype(BF16)
+    gm[...] = nn(ga[...], wo[...]).astype(BF16)
     for h in range(GROUP_HEADS):
         sl = slice(h * HEAD_DIM, (h + 1) * HEAD_DIM)
         q = proj[:, h * HEAD_DIM : (h + 1) * HEAD_DIM]
         k = proj[0:keys, width + h * HEAD_DIM : width + (h + 1) * HEAD_DIM]
         v = proj[0:keys, 2 * width + h * HEAD_DIM : 2 * width + (h + 1) * HEAD_DIM]
         do = gm[:, sl]
-        e = nt(k, q) * scale - lse[h : h + 1, :]
-        p = jnp.exp2(jnp.concatenate([e[0:low], masked_tail(e, low, seq)], axis=0))
+        parts = cut_rows(nt(k, q) * scale - lse[h : h + 1, :], low, seq)
         dp = nt(v, do)
-        delta = jnp.sum(p * dp, axis=0, keepdims=True)
-        ds = (p * (dp - delta)).astype(BF16)
-        dv = nn(p.astype(BF16), do)
-        dk = nn(ds, q)
-        dq_t[sl, :] = tn(k, ds)
+        cuts = (slice(0, low), slice(low, keys))
+        p = [jnp.exp2(t) for t in parts]
+        delta = sum(
+            jnp.sum(t * dp[rows], axis=0, keepdims=True) for t, rows in zip(p, cuts)
+        )
+        for t, rows in zip(p, cuts):
+            probs[rows, :] = t.astype(BF16)
+            slopes[rows, :] = (t * (dp[rows] - delta)).astype(BF16)
+        dv = nn(probs[...], do)
+        dk = nn(slopes[...], q)
+        dq_t[sl, :] = tn(k, slopes[...])
         grads[0:keys, width + h * HEAD_DIM : width + (h + 1) * HEAD_DIM] = (dk * factor).astype(
             BF16
         )
         grads[0:keys, 2 * width + h * HEAD_DIM : 2 * width + (h + 1) * HEAD_DIM] = dv.astype(BF16)
     grads[keys:PAD, width : 3 * width] = jnp.zeros((PAD - keys, 2 * width), BF16)
     grads[:, 0:width] = (dq_t[...] * factor).T.astype(BF16)
-    value = grads[:, 0 : 3 * width]
-    sums[...] = jnp.sum(value.astype(F32), axis=0, keepdims=True)
-    part = nt(value, w[:, 0 : 3 * width])
+    sums[...] = jnp.sum(grads[:, 0 : 3 * width].astype(F32), axis=0, keepdims=True)
     grads[:, 3 * width : 4 * width] = mixed[...]
-    acc[...] = part + acc_in[...] if has_acc else part
-
-
-def attn_bwd(proj, mixed, lse, ga, w, acc_in, seq):
-    d, gw = w.shape
-    width = GROUP_HEADS * HEAD_DIM
-    has_acc = acc_in is not None
-    vmem = pl.BlockSpec(memory_space=pltpu.VMEM)
+
+
+def attn_bwd(proj, mixed, lse, ga, wo, seq):
+    d, width = wo.shape
+    keys = -(-seq // 16) * 16
     return pl.pallas_call(
-        functools.partial(attn_bwd_kernel, has_acc, seq),
-        in_specs=[vmem] * (6 if has_acc else 5),
-        out_specs=[vmem] * 3,
+        functools.partial(attn_bwd_kernel, seq),
+        in_specs=specs(5)[1:],
+        out_specs=specs(2)[1:],
         out_shape=[
-            jax.ShapeDtypeStruct((PAD, gw), BF16),
-            jax.ShapeDtypeStruct((PAD, d), F32),
+            jax.ShapeDtypeStruct((PAD, 4 * width), BF16),
             jax.ShapeDtypeStruct((1, 3 * width), F32),
         ],
-        scratch_shapes=[pltpu.VMEM((PAD, width), BF16), pltpu.VMEM((width, PAD), F32)],
+        scratch_shapes=[
+            pltpu.VMEM((PAD, width), BF16),
+            pltpu.VMEM((width, PAD), F32),
+            pltpu.VMEM((keys, PAD), BF16),
+            pltpu.VMEM((keys, PAD), BF16),
+        ],
         compiler_params=params(),
-        cost_estimate=cost(
-            2 * PAD * (d * 4 * width + 20 * PAD * 256), d * gw * 2 + PAD * d * 8
-        ),
+        cost_estimate=cost(2 * PAD * (d * width + 20 * PAD * 256), d * width * 2 + PAD * d * 8),
         name="attn_bwd",
-    )(proj, mixed, lse, ga, w, *([acc_in] if has_acc else []))
+    )(proj, mixed, lse, ga, wo)
 
 
 def tile_of(units):
@@ -249,15 +242,18 @@
                 c.wait()
             out_copy(slot).start()
 
-    u = nn(x[...], w[:, pl.ds(pl.multiple_of(n * tile, tile), tile)]) + bias[...]
     root = math.sqrt(2.0 / math.pi)
-    square = u * u
-    t = jnp.tanh(u * (root + (root * 0.044715) * square))
-    half = 0.5 * (1.0 + t)
-    active[...] = (u * half).astype(BF16)
-    slope[...] = (
-        half + (0.5 * u) * (1.0 - t * t) * (root + (3.0 * root * 0.044715) * square)
-    ).astype(BF16)
+    for r in range(0, PAD, PAD // 3):
+        rows = slice(r, r + PAD // 3)
+        u = nn(x[rows, :], w[:, pl.ds(pl.multiple_of(n * tile, tile), tile)]) + bias[...]
+        square = u * u
+        t = jnp.tanh(u * (root + (root * 0.044715) * square))
+        half = 0.5 + 0.5 * t
+        value = u * half
+        active[rows, :] = value.astype(BF16)
+        slope[rows, :] = (
+            half + (value * (1.0 - half)) * (2.0 * root + (6.0 * root * 0.044715) * square)
+        ).astype(BF16)
 
     @pl.when(n == pl.num_programs(0) - 1)
     def _():
@@ -368,36 +364,6 @@
     )(table, gl, active, slope, *pieces)
 
 
-def ff_back_kernel(gu, w, acc):
-    part = nt(gu[...], w[...])
-
-    @pl.when(pl.program_id(0) == 0)
-    def _():
-        acc[...] = part
-
-    @pl.when(pl.program_id(0) > 0)
-    def _():
-        acc[...] += part
-
-
-def ff_back(gu, w):
-    d, units = w.shape
-    tile = tile_of(units)
-    return pl.pallas_call(
-        ff_back_kernel,
-        grid=(units // tile,),
-        in_specs=[
-            pl.BlockSpec((PAD, tile), lambda n: (0, n)),
-            pl.BlockSpec((d, tile), lambda n: (0, n)),
-        ],
-        out_specs=whole((PAD, d)),
-        out_shape=jax.ShapeDtypeStruct((PAD, d), F32),
-        compiler_params=params(),
-        cost_estimate=cost(2 * PAD * d * units, 2 * d * units + 2 * PAD * units),
-        name="ff_back",
-    )(gu, w)
-
-
 def put_turned(table, blocks, value, out):
     t = value.T
     rows = t.shape[0] // blocks
@@ -433,10 +399,14 @@
     return c, lax.rsqrt(jnp.mean(c * c, axis=-1, keepdims=True) + EPS)
 
 
-def norm_kernel(blocks, seq, has_acc, *refs):
-    if has_acc:
-        table, base, acc, extra, gain, bias, hidden, normed, turned = refs
-        v = base[...].astype(F32) + (acc[...] + extra[...])
+def norm_kernel(blocks, seq, groups, *refs):
+    if groups:
+        table, base, extra, gain, bias = refs[:5]
+        mixed, wo = refs[5 : 5 + groups], refs[5 + groups : 5 + 2 * groups]
+        hidden, normed, turned = refs[5 + 2 * groups :]
+        v = base[...].astype(F32) + extra[...]
+        for m, o in zip(mixed, wo):
+            v += nt(m[...], o[...])
         hidden[...] = v
     else:
         table, base, gain, bias, normed, turned = refs
@@ -449,15 +419,14 @@
     put_turned(table, blocks, low, turned)
 
 
-def norm(table, base, acc, extra, gain, bias, seq):
+def norm(table, base, extra, gain, bias, seq, mixed=(), wo=()):
     d = base.shape[1]
-    has_acc = acc is not None
-    args = [base] + ([acc, extra[None]] if has_acc else []) + [gain[None], bias[None]]
+    args = [base] + ([extra[None]] if mixed else []) + [gain[None], bias[None], *mixed, *wo]
     outs = [jax.ShapeDtypeStruct((PAD, d), BF16), jax.ShapeDtypeStruct((d, PAD), BF16)]
-    if has_acc:
+    if mixed:
         outs = [jax.ShapeDtypeStruct((PAD, d), F32)] + outs
     return pl.pallas_call(
-        functools.partial(norm_kernel, table.shape[0], seq, has_acc),
+        functools.partial(norm_kernel, table.shape[0], seq, len(mixed)),
         in_specs=specs(len(args)),
         out_specs=specs(len(outs))[1:],
         out_shape=outs,
@@ -467,47 +436,96 @@
     )(table, *args)
 
 
-def norm_back_kernel(blocks, seq, with_low, *refs):
-    table, v, e, gain, base, grad, gain_sum, bias_sum, *low_refs = refs
-    c, r = centered(v[...].astype(F32))
+def through_norm(v, e, gain, base):
+    c, r = centered(v)
     u = c * r
-    scaled = e[...] * gain[...]
+    scaled = e * gain
     inner = jnp.mean(scaled * u, axis=-1, keepdims=True)
-    value = base[...].astype(F32) + r * (
-        scaled - jnp.mean(scaled, axis=-1, keepdims=True) - u * inner
-    )
-    gain_sum[...] = jnp.sum(e[...] * u, axis=0, keepdims=True)
-    bias_sum[...] = jnp.sum(e[...], axis=0, keepdims=True)
-    if with_low:
+    value = base + r * (scaled - jnp.mean(scaled, axis=-1, keepdims=True) - u * inner)
+    return value, jnp.sum(e * u, axis=0, keepdims=True), jnp.sum(e, axis=0, keepdims=True)
+
+
+def ff_back_kernel(blocks, *refs):
+    table, gu, w, v, gain, base, grad, gain_sum, bias_sum, low, turned, low_sum, acc = refs
+    n = pl.program_id(0)
+    part = nt(gu[...], w[...])
+
+    @pl.when(n == 0)
+    def _():
+        acc[...] = part
+
+    @pl.when(n > 0)
+    def _():
+        acc[...] += part
+
+    @pl.when(n == pl.num_programs(0) - 1)
+    def _():
+        value, gain_sum[...], bias_sum[...] = through_norm(
+            v[...], acc[...], gain[...], base[...].astype(F32)
+        )
         grad[...] = value
-        low, turned, low_sum = low_refs
         rounded = value.astype(BF16)
         low[...] = rounded
         put_turned(table, blocks, rounded, turned)
         low_sum[...] = jnp.sum(rounded.astype(F32), axis=0, keepdims=True)
-    else:
-        grad[...] = value[0:seq]
-
-
-def norm_back(table, v, e, gain, base, seq, with_low):
+
+
+def ff_back(table, gu, w, v, gain, base):
+    d, units = w.shape
+    tile = tile_of(units)
+    row = jax.ShapeDtypeStruct((1, d), F32)
+    outs = [
+        jax.ShapeDtypeStruct((PAD, d), F32),
+        row,
+        row,
+        jax.ShapeDtypeStruct((PAD, d), BF16),
+        jax.ShapeDtypeStruct((d, PAD), BF16),
+        row,
+    ]
+    return pl.pallas_call(
+        functools.partial(ff_back_kernel, table.shape[0]),
+        grid=(units // tile,),
+        in_specs=[
+            pl.BlockSpec(memory_space=pltpu.SMEM),
+            pl.BlockSpec((PAD, tile), lambda n: (0, n)),
+            pl.BlockSpec((d, tile), lambda n: (0, n)),
+            *specs(3)[1:],
+        ],
+        out_specs=specs(len(outs))[1:],
+        out_shape=outs,
+        scratch_shapes=[pltpu.VMEM((PAD, d), F32)],
+        compiler_params=params(),
+        cost_estimate=cost(2 * PAD * d * units, 2 * d * units + 2 * PAD * units),
+        name="ff_back",
+    )(table, gu, w, v, gain[None], base)
+
+
+def attn_back_kernel(seq, groups, *refs):
+    grads, ws = refs[:groups], refs[groups : 2 * groups]
+    v, gain, base, grad, gain_sum, bias_sum = refs[2 * groups :]
+    cut = 3 * GROUP_HEADS * HEAD_DIM
+    e = nt(grads[0][:, 0:cut], ws[0][:, 0:cut])
+    for g, w in zip(grads[1:], ws[1:]):
+        e += nt(g[:, 0:cut], w[:, 0:cut])
+    value, gain_sum[...], bias_sum[...] = through_norm(
+        v[...].astype(F32), e, gain[...], base[...]
+    )
+    grad[...] = value[0:seq]
+
+
+def attn_back(grads, ws, v, gain, base, seq):
     d = v.shape[1]
     row = jax.ShapeDtypeStruct((1, d), F32)
-    outs = [jax.ShapeDtypeStruct((PAD if with_low else seq, d), F32), row, row]
-    if with_low:
-        outs += [
-            jax.ShapeDtypeStruct((PAD, d), BF16),
-            jax.ShapeDtypeStruct((d, PAD), BF16),
-            row,
-        ]
+    args = [*grads, *ws, v, gain[None], base]
     return pl.pallas_call(
-        functools.partial(norm_back_kernel, table.shape[0], seq, with_low),
-        in_specs=specs(4),
-        out_specs=specs(len(outs))[1:],
-        out_shape=outs,
+        functools.partial(attn_back_kernel, seq, len(grads)),
+        in_specs=specs(len(args))[1:],
+        out_specs=specs(3)[1:],
+        out_shape=[jax.ShapeDtypeStruct((seq, d), F32), row, row],
         compiler_params=params(),
-        cost_estimate=cost(PAD * d * 24, PAD * d * 18),
-        name="norm_back",
-    )(table, v, e, gain[None], base)
+        cost_estimate=cost(6 * PAD * d * d, PAD * d * 18),
+        name="attn_back",
+    )(*args)
 
 
 def ff_grad_kernel(total, parts, rows, *refs):
@@ -582,7 +600,8 @@
 
 
 def after(x, *others):
-    return lax.optimization_barrier((x, others))[0]
+    others = [o for o in others if o is not None]
+    return lax.optimization_barrier((x, others))[0] if others else x
 
 
 def total_sum(value, sizes):
@@ -596,29 +615,19 @@
 
 def attn_entries(nz, rows, h):
     g = rows - h
-    plans = {}
-    for dc in range(2):
-        for dx in range(2):
-            entries = []
-            for dy in range(2):
-                for dz in range(nz):
-                    if dy == 0:
-                        one = (dz, dz * 2 * rows, dx * h)
-                    else:
-                        one = (nz + dz // 2, dz // 2 * 4 * h, dz % 2 * 2 * h + dx * h)
-                    if dx == 0:
-                        two = (dz, dz * 2 * rows, 2 * h + dy * g)
-                    else:
-                        two = (
-                            nz + nz // 2 + dz // 2,
-                            2 * nz * h + dz // 2 * 4 * g,
-                            dz % 2 * 2 * g + dy * g,
-                        )
-                    for (piece, base, at), size, inside in ((one, h, 0), (two, g, h)):
-                        if dc == 1:
-                            piece, at = (0 if piece < nz else 1), base + at
-                        entries.append((piece, at, size, 0, dy * nz + dz, inside, 0))
-            plans[dc, dx] = entries
+    plans = []
+    for dx in range(2):
+        entries = []
+        for dy in range(2):
+            for dz in range(nz):
+                one = (dz, dx * h) if dy == 0 else (nz + dz // 2, dz % 2 * 2 * h + dx * h)
+                if dx == 0:
+                    two = dz, 2 * h + dy * g
+                else:
+                    two = nz + nz // 2 + dz // 2, dz % 2 * 2 * g + dy * g
+                for (piece, at), size, inside in ((one, h, 0), (two, g, h)):
+                    entries.append((piece, at, size, 0, dy * nz + dz, inside, 0))
+        plans.append(entries)
     return plans
 
 
@@ -627,26 +636,11 @@
     for dz in range(nz):
         for dy in range(2):
             for dx in range(2):
-                if dy == 0:
-                    if dx == 0:
-                        near = dz, 0
-                    elif dz == 0:
-                        near = nz, 0
-                    else:
-                        near = nz + 1, dz - 1
-                    far = nz + 5, dx * nz + dz
-                elif dz == 0:
-                    near = nz + 2, dx
-                    far = nz + 6, dx
-                elif dx == 0:
-                    near = nz + 3, dz - 1
-                    far = nz + 6, 1 + dz
-                else:
-                    near = nz + 4, dz - 1
-                    far = nz + 7, dz - 1
-                for dc, (piece, at) in enumerate((near, far)):
+                piece, at = (dx * nz + dz, 0) if dy == 0 else (2 * nz + dz, dx)
+                far = 3 * nz + dz // 2, dz % 2 * 4 + dy * 2 + dx
+                for dc, (p, block) in enumerate(((piece, at), far)):
                     entries.append(
-                        (piece, at * rows, rows, dz, dc * 4 + dy * 2 + dx, 0, dz * cols)
+                        (p, block * rows, rows, dz, dc * 4 + dy * 2 + dx, 0, dz * cols)
                     )
     return entries
 
@@ -691,8 +685,7 @@
     if linked:
         h = -(-a_rows // 32) * 16
         order = [(dc, dx) for dc in range(2) for dx in range(2)]
-        entries = attn_entries(nz, a_rows, h)
-        attn_plans = [Plan(entries[o], 4 * width) for o in order]
+        attn_plans = [Plan(e, 4 * width) for e in attn_entries(nz, a_rows, h)] * 2
         groups = [(xi ^ dx) * 2 + (ci ^ dc) for dc, dx in order]
         down_plan = Plan(ff_entries(nz, f_rows, cols), cols)
         zones = [(zi - dz) % nz for dz in range(nz)]
@@ -743,99 +736,149 @@
             for k in zones
         ]
     )[None]
-    normed_a, na_t = norm(turn_attn, base, None, None, ln1_gain, ln1_bias, seq)
+    normed_a, na_t = norm(turn_attn, base, None, ln1_gain, ln1_bias, seq)
     gl_t, down_bias_sum = turn(turn_ff, grad_low)
 
     together = lax.optimization_barrier
+    spots = ("z", "y", "x", "c")
     if linked:
         half = d // 2
-        px, py, down_xa = together(
-            (swap(attn_own[:h], "x"), swap(attn_own[h:], "y"), swap(down_own, "x"))
-        )
+        down_z, down_x, down_y, down_c = [down_own], [], [], []
+
+        def down_pair(k):
+            return swap(cat(down_z[k], down_x[k]), "y")
+
+        def down_core(k):
+            return swap(
+                cat(*[t for j in (k, k + 1) for t in (down_z[j], down_x[j], down_y[j])])
+            )
+
+        px, py, dx0, dz1, normed_a = together(
+            (
+                swap(attn_own[:h], "x"),
+                swap(attn_own[h:], "y"),
+                swap(down_own, "x"),
+                hop(down_own, "z", nz, 1),
+                normed_a,
+            )
+        )
+        down_x.append(dx0)
+        down_z.append(dz1)
         s = [cat(attn_own[:h], px, attn_own[h:], py)]
-        s1, down_ya, na_far = together(
+        s1, dy0, dx1, na_far, sc0, gl_t, na_t = together(
             (
                 hop(s[0], "z", nz, 1),
-                swap(cat(down_own, after(down_xa, px)), "y"),
+                down_pair(0),
+                swap(down_z[1], "x"),
                 swap(after(na_t, px)),
+                swap(s[0]),
+                gl_t,
+                na_t,
             )
         )
+        down_y.append(dy0)
+        down_x.append(dx1)
         s.append(s1)
-        y_parts, x_parts = [], []
-        gl_first = gl_t[half:]
+        s_far = [sc0]
+        y_parts, x_parts, y_far, x_far = [], [], [], []
         for k in range(2, nz):
-            moves = [hop(s[-1], "z", nz, 1)]
+            moves = [hop(s[-1], "z", nz, 1), swap(s[-1])]
             if k % 2 == 0:
                 moves.append(swap(cat(s[k - 2][: 2 * h], s[k - 1][: 2 * h]), "y"))
                 moves.append(swap(cat(s[k - 2][2 * h :], s[k - 1][2 * h :]), "x"))
-            elif k == 3:
-                gl_far = swap(after(gl_first, s[-1]))
-                moves.append(gl_far)
+                if k == 2:
+                    moves.append(swap(after(gl_t, s1)[half:]))
+            else:
+                moves += [swap(y_parts[-1]), swap(x_parts[-1])]
+                if k == 3:
+                    moves.append(down_pair(1))
             moves = together(tuple(moves))
             s.append(moves[0])
+            s_far.append(moves[1])
             if k % 2 == 0:
-                y_parts.append(moves[1])
-                x_parts.append(moves[2])
-            elif k == 3:
-                gl_far = moves[1]
-        moves = together(
+                y_parts.append(moves[2])
+                x_parts.append(moves[3])
+                if k == 2:
+                    gl_far = moves[4]
+            else:
+                y_far.append(moves[2])
+                x_far.append(moves[3])
+                if k == 3:
+                    down_y.append(moves[4])
+        up_whole = lax.all_gather(after(up_own, s[-1]), spots, axis=0, tiled=True)
+        y1, x1, sc3, dz2 = together(
             (
                 swap(cat(s[-2][: 2 * h], s[-1][: 2 * h]), "y"),
                 swap(cat(s[-2][2 * h :], s[-1][2 * h :]), "x"),
-                swap(cat(*s)),
+                swap(s[-1]),
+                hop(after(down_z[1], s[-1]), "z", nz, 1),
             )
         )
-        y_parts.append(moves[0])
-        x_parts.append(moves[1])
-        up_whole = lax.all_gather(after(up_own, s[2]), ("z", "y", "x", "c"), axis=0, tiled=True)
+        y_parts.append(y1)
+        x_parts.append(x1)
+        s_far.append(sc3)
+        down_z.append(dz2)
         near = [*s, *y_parts, *x_parts]
-        far = [moves[2], swap(cat(*y_parts, *x_parts))]
-        down_first = after(down_own, moves[2])
-        down_z = [down_own] + [hop(down_first, "z", nz, k) for k in range(1, nz)]
+        y_far.append(swap(y1))
+        x_far.append(swap(x1))
+        far = [*s_far, *y_far, *x_far]
 
         kept = []
-        acc = None
         for number in range(4):
             pieces = near if number < 2 else far
-            proj, mixed, lse, acc, w = attn_fwd(
-                attn_table, normed_a, bias_rows[number], pieces, attn_plans[number], acc, seq
+            out = attn_fwd(
+                attn_table, normed_a, bias_rows[number], pieces, attn_plans[number], seq
             )
-            kept.append((proj, mixed, lse, w))
+            kept.append(out)
+            if number == 0:
+                dz3 = hop(down_z[2], "z", nz, 1)
+                dx2 = swap(down_z[2], "x")
+                normed_a, dz3, dx2, far, _ = together((normed_a, dz3, dx2, far, out))
+                down_z.append(dz3)
+                down_x.append(dx2)
             if number == 1:
-                acc, down_z, far = together((acc, down_z, far))
-                down_xb = swap(cat(*down_z[1:]), "x")
-                down_yb = swap(cat(*down_z[1:]), "y")
-            if number == 3:
-                acc, down_xb, down_yb = together((acc, down_xb, down_yb))
-                down_yc = swap(down_xb, "y")
-                down_c0 = swap(cat(*down_z, down_xa, down_xb))
-                down_c1 = swap(cat(down_ya, down_yb))
+                dx3, dy2 = swap(down_z[3], "x"), down_pair(2)
+                down_c.append(down_core(0))
+                normed_a = after(normed_a, out)
+            if number == 2:
+                normed_a, dx3, dy2, down_c[0], _ = together(
+                    (normed_a, dx3, dy2, down_c[0], out)
+                )
+                down_x.append(dx3)
+                down_y.append(dy2)
+                down_y.append(down_pair(3))
     else:
         kept = []
-        acc = None
         for number, g in enumerate(groups):
-            proj, mixed, lse, acc, w = attn_fwd(
-                attn_table,
-                normed_a,
-                bias_rows[number],
-                attn_pieces[number],
-                attn_plans[number],
-                acc,
-                seq,
+            kept.append(
+                attn_fwd(
+                    attn_table,
+                    normed_a,
+                    bias_rows[number],
+                    attn_pieces[number],
+                    attn_plans[number],
+                    seq,
+                )
             )
-            kept.append((proj, mixed, lse, w))
-
-    hidden, normed_b, nb_t = norm(turn_ff, base, acc, out_bias, ln2_gain, ln2_bias, seq)
+
+    hidden, normed_b, nb_t = norm(
+        turn_ff,
+        base,
+        out_bias,
+        ln2_gain,
+        ln2_bias,
+        seq,
+        [out[1] for out in kept],
+        [out[4] for out in kept],
+    )
     if linked:
+        normed_b, down_y[3] = together((normed_b, down_y[3]))
+        down_c.append(down_core(2))
         nb_far = swap(nb_t[half:])
     active, slope, up_full = ff_up(zone_table, normed_b, shift, [up_whole], up_plan, nz)
     if linked:
-        active, down_yc, down_c0, down_c1, nb_far = together(
-            (active, down_yc, down_c0, down_c1, nb_far)
-        )
-        down_c2 = swap(down_yc)
-        down_pieces = [*down_z, down_xa, down_xb, down_ya, down_yb, down_yc]
-        down_pieces += [down_c0, down_c1, down_c2]
+        active, down_c[1], nb_far = together((active, down_c[1], nb_far))
+        down_pieces = [*down_z, *down_x, *down_y, *down_c]
         active_far = swap(active)
     else:
         down_plan, ff_table, down_pieces = up_plan, zone_table, [down_whole]
@@ -852,7 +895,7 @@
         upper_far = swap(grad_upper)
         down_parts = ff_grad([gl_t[:half], gl_far], [active, active_far], nz, 4)
         down_one, down_two = swap(down_parts[3], "x"), swap(down_parts[1], "x")
-        grad_normed_b = ff_back(after(grad_upper, down_parts), up_full)
+        grad_upper_first = after(grad_upper, down_parts)
     else:
         spot = ("y", "x", "c")
 
@@ -863,83 +906,92 @@
 
         down_sum = spread(ff_grad([gl_t], [active], nz, 1))
         up_sum = spread(ff_grad([nb_t], [grad_upper], nz, 1))
-        grad_normed_b = ff_back(grad_upper, up_full)
-
-    grad_hidden, ln2_gain_grad, ln2_bias_grad, grad_attn, ga_t, out_bias_sum = norm_back(
-        turn_attn, hidden, grad_normed_b, ln2_gain, grad_low, seq, True
+        grad_upper_first = grad_upper
+
+    grad_hidden, ln2_gain_grad, ln2_bias_grad, grad_attn, ga_t, out_bias_sum = ff_back(
+        turn_attn, grad_upper_first, up_full, hidden, ln2_gain, grad_low
     )
 
-    acc = None
     sums = [None] * len(groups)
     if linked:
         grads = {}
         ga_far = swap(ga_t)
 
-        def back(number, acc):
-            proj, mixed, lse, w = kept[number]
-            grads[number], acc, sums[number] = attn_bwd(proj, mixed, lse, ga_first, w, acc, seq)
-            return acc
-
-        ga_first, down_one = together((grad_attn, down_one))
+        def back(number):
+            proj, mixed, lse, _, wo = kept[number]
+            grads[number], sums[number] = attn_bwd(proj, mixed, lse, ga_first, wo, seq)
+
+        ga_first, upper_far = together((grad_attn, upper_far))
+        back(3)
+        far_grads = swap(grads[3])
+        ga_first, down_one, _ = together((ga_first, down_one, grads[3]))
         down_one = plus(down_parts[2], down_one)
         down_other = swap(down_one, "y")
-        ga_first = after(ga_first, down_one)
-        acc = back(3, None)
-        far_grads = swap(grads[3])
-        acc = back(1, acc)
-        acc, far_grads, ga_far, down_two, down_other = together(
-            (acc, far_grads, ga_far, down_two, down_other)
-        )
-        down_value = plus(down_parts[0], down_two, down_other)
-        down_line = hop(down_value[nz - 1], "z", nz, -1)
-        more = attn_grad(
-            [after(na_t, down_value), na_far], [ga_t, ga_far], [grads[1], far_grads], 2
-        )
+        back(1)
+        grads[1], far_grads, ga_far, down_one = together((grads[1], far_grads, ga_far, down_one))
+        more = attn_grad([na_t, na_far], [ga_t, ga_far], [grads[1], far_grads], 2)
         more_one, more_two = swap(more[1], "x"), swap(more[0], "x")
         upper_first, upper_far = together((grad_upper, upper_far, more))[:2]
         up_parts = ff_grad([nb_t[:half], nb_far], [upper_first, upper_far], nz, 4)
-        up_parts, down_line, acc = together((up_parts, down_line, acc))
+        up_parts, down_two, down_other, ga_first = together(
+            (up_parts, down_two, down_other, ga_first)
+        )
         up_one, up_two = swap(up_parts[3], "y"), swap(up_parts[2], "y")
-        down_line = hop(plus(down_line, down_value[nz - 2]), "z", nz, -1)
-        acc = back(2, acc)
+        down_value = plus(down_parts[0], down_two, down_other)
+        down_line = hop(down_value[nz - 1], "z", nz, -1)
+        ga_first = after(ga_first, down_value)
+        back(2)
         far_grads = swap(grads[2])
-        acc, more_one, down_line = together((acc, more_one, down_line))
-        for k in range(nz - 3, 0, -1):
+        grads[2], down_line, ga_first = together((grads[2], down_line, ga_first))
+        for k in range(nz - 2, 0, -1):
             down_line = hop(plus(down_line, down_value[k]), "z", nz, -1)
-        acc = back(0, acc)
-        acc, far_grads, up_one, down_line = together((acc, far_grads, up_one, down_line))
+        back(0)
+        grads[0], far_grads, more_one = together((grads[0], far_grads, more_one))
+        input_grad, ln1_gain_grad, ln1_bias_grad = attn_back(
+            [grads[k] for k in range(4)],
+            [out[3] for out in kept],
+            base,
+            ln1_gain,
+            grad_hidden,
+            seq,
+        )
+        input_grad, up_one, more_two, down_line = together(
+            (input_grad, up_one, more_two, down_line)
+        )
         up_one = plus(up_parts[1], up_one)
         up_other = swap(up_one, "x")
-        input_grad, ln1_gain_grad, ln1_bias_grad = norm_back(
-            turn_attn, base, after(acc, up_one), ln1_gain, grad_hidden, seq, False
-        )
-        na_first, more_two, up_two, up_other, input_grad = together(
-            (na_t, more_two, up_two, up_other, input_grad)
-        )
+        na_first = after(na_t, up_one)
         total = attn_grad(
             [na_first, na_far], [ga_t, ga_far], [grads[0], far_grads], 2, (more_two, more_one)
         )
         far_y = swap(total[1], "y")
+        up_two, up_other, near_y = together((up_two, up_other, total[0]))
         up_value = plus(up_parts[0], up_two, up_other)
-        up_line = hop(after(up_value[nz - 1], total[0]), "z", nz, -1)
+        up_line = hop(up_value[nz - 1], "z", nz, -1)
+        far_y, up_line, near_y = together((far_y, up_line, near_y))
+        last = plus(near_y, far_y).reshape(nz, a_rows, 4 * width)
+        last_far = [hop(last[k], "z", nz, -k) for k in range(1, nz)]
         for k in range(nz - 2, 0, -1):
             up_line = hop(plus(up_line, up_value[k]), "z", nz, -1)
-        far_y, up_line, near_y = together((far_y, up_line, total[0]))
-        last = plus(near_y, far_y).reshape(nz, a_rows, 4 * width)
-        last_far = [hop(last[k], "z", nz, -k) for k in range(1, nz)]
         down_sum = down_line.astype(F32) + down_value[0].astype(F32)
         up_sum = up_line.astype(F32) + up_value[0].astype(F32)
         attn_sum = sum(v.astype(F32) for v in (last[0], *last_far))
     else:
         parts = []
-        for number, (proj, mixed, lse, w) in enumerate(kept):
-            g, acc, sums[number] = attn_bwd(proj, mixed, lse, grad_attn, w, acc, seq)
-            parts.append(attn_grad([na_t], [ga_t], [g], 1)[0])
+        grads = {}
+        for number, (proj, mixed, lse, _, wo) in enumerate(kept):
+            grads[number], sums[number] = attn_bwd(proj, mixed, lse, grad_attn, wo, seq)
+            parts.append(attn_grad([na_t], [ga_t], [grads[number]], 1)[0])
         part = lax.psum_scatter(jnp.stack(parts), ("x", "c"), scatter_dimension=0, tiled=True)[0]
         part = lax.psum_scatter(part, ("y", "z"), scatter_dimension=0, tiled=True)
         attn_sum = lax.optimization_barrier(part).astype(F32)
-        input_grad, ln1_gain_grad, ln1_bias_grad = norm_back(
-            turn_attn, base, acc, ln1_gain, grad_hidden, seq, False
+        input_grad, ln1_gain_grad, ln1_bias_grad = attn_back(
+            [grads[k] for k in range(len(groups))],
+            [out[3] for out in kept],
+            base,
+            ln1_gain,
+            grad_hidden,
+            seq,
         )
 
     def in_place(rows, places):

time: 609 us -> 531 us (0.87)
  the two profiles are of different devices: /device:TPU:0 before, /device:TPU:25 now
where the time goes in v3:
time: 531 us; the launch traced here: 524 us
  Pallas kernels  246 us (46%)
  waiting for transfers between devices  127 us (24%)
  starting transfers between devices  55 us (10%)
  local copies, waits for them, and re-layouts  41.8 us (8%)
  other arithmetic  38.5 us (7%)
  between operations  16 us (3%)
    ppermute x56, waiting for transfers between devices, hop(): return lax.ppermute(x, axis, [(i, (i + step) % n) for i in range(n)])  127 us
    ppermute x56, starting transfers between devices, hop(): return lax.ppermute(x, axis, [(i, (i + step) % n) for i in range(n)])  49.7 us
    pallas_call x4, Pallas kernels, attn_bwd(): pl.pallas_call(functools.partial(attn_bwd_kernel, seq), in_specs=specs(5)...  45.3 us
    pallas_call x4, Pallas kernels, attn_fwd(): pl.pallas_call(functools.partial(attn_fwd_kernel, plan, len(pieces), seq)...  43.1 us
    pallas_call x1, Pallas kernels, ff_down(): pl.pallas_call(functools.partial(ff_down_kernel, plan, len(pieces), slots...  28.2 us
    pallas_call x2, Pallas kernels, ff_grad(): pl.pallas_call(functools.partial(ff_grad_kernel, total, parts, rows), gri...  27 us
    pallas_call x2, Pallas kernels, attn_grad(): pl.pallas_call(functools.partial(attn_grad_kernel, total, parts, len(more...  22.7 us
    pallas_call x1, Pallas kernels, ff_back(): pl.pallas_call(functools.partial(ff_back_kernel, table.shape[0]), grid=(u...  22.2 us
  transfers between devices with their start and end apart: 62, of which 18 were waited for; matrix products, arithmetic and copies ran while one was open for 14% of the time, Pallas kernels for 47%

profile of v3, /device:TPU:25, one launch (start us, length us, event | category | flops | bytes accessed | tf_op | source)
XLA Modules:
  0.0 524.4 jit_solution(9768600634128863067)
XLA Ops:
  12.5 1.3 collective-permute-start.1
  15.0 1.4 pad.35.refs_1_.refs_8_
  16.9 4.6 norm.2
  22.0 1.6 collective-permute-start.7
  29.8 3.0 multiply_convert_fusion.x.refs_1_.refs_5_
  33.4 3.3 turn.1
  37.3 3.5 collective-permute-done.4.refs_4_
  40.8 1.5 collective-permute-done.5.refs_12_
  42.4 1.3 collective-permute-start.9
  43.7 2.0 collective-permute-start.10
  49.8 13.0 %collective-permute-done.12.refs_9_ = bf16[256,1152]{1,0:T(8,128)(2,1)} collective-permute-done((bf16[256,1152]{1,0:T(8,128)(2,1)S(1)}, bf16[256,1152]{1,0:T(8,128)(2,1)}, u32[]{:S(2)}, u32[]{:S(2)}) %collective-permute-start.12) | collective-permute-done | bytes 589856 | tf_op jit(solution)/shard_map/ppermute | solution.py:595
  62.8 3.1 collective-permute-done.11.refs_7_
  65.9 1.3 collective-permute-start.16
  71.1 13.8 %collective-permute-done.18.refs_13_ = bf16[288,1152]{1,0:T(8,128)(2,1)} collective-permute-done((bf16[288,1152]{1,0:T(8,128)(2,1)}, bf16[288,1152]{1,0:T(8,128)(2,1)}, u32[]{:S(2)}, u32[]{:S(2)}) %collective-permute-start.18) | collective-permute-done | bytes 663584 | tf_op jit(solution)/shard_map/ppermute | solution.py:595
  85.9 2.0 constant_dynamic-update-slice_fusion.3
  90.5 2.0 constant_dynamic-update-slice_fusion
  95.1 3.1 collective-permute-start.22
  98.2 12.9 %collective-permute-done.22.refs_6_ = bf16[144,1152]{1,0:T(8,128)(2,1)S(1)} collective-permute-done((bf16[144,1152]{1,0:T(8,128)(2,1)S(1)}, bf16[144,1152]{1,0:T(8,128)(2,1)S(1)}, u32[]{:S(2)}, u32[]{:S(2)}) %collective-permute-start.22) | collective-permute-done | bytes 331808 | tf_op jit(solution)/shard_map/ppermute | solution.py:595
  111.1 1.5 collective-permute-done.19.refs_8_
  112.6 1.3 collective-permute-start.25
  113.9 3.0 collective-permute-start.23
  118.9 10.7 %attn_fwd.4 = (bf16[768,864]{1,0:T(8,128)(2,1)}, bf16[768,288]{1,0:T(8,128)(2,1)}, f32[8,768]{1,0:T(8,128)}, bf16[1152,1152]{1,0:T(8,128)(2,1)}, bf16[1152,288]{1,0:T(8,128)(2,1)}) custom-call(s32[8]{0:T(128)} %stack.125.refs_0_, bf16[768,1152]{1,0:T(8,128)(2,1)} %get-tuple-element.220.refs_1_, f32[1,864]{1,0:T(1,128)} %broadcast_in_dim.168.refs_2_, ...), custom_call_target="tpu_custom_call" | custom-call | flops 222717536 | bytes 265420 | tf_op jit(solution)/shard_map/attn_fwd/pallas_call | solution.py:129
  129.6 1.4 collective-permute-done.23.refs_7_
  131.0 2.6 collective-permute-done.24.refs_10_
  138.2 1.5 collective-permute-start.27
  140.4 10.7 %attn_fwd.5 = (bf16[768,864]{1,0:T(8,128)(2,1)}, bf16[768,288]{1,0:T(8,128)(2,1)}, f32[8,768]{1,0:T(8,128)}, bf16[1152,1152]{1,0:T(8,128)(2,1)}, bf16[1152,288]{1,0:T(8,128)(2,1)}) custom-call(s32[8]{0:T(128)} %stack.125.refs_0_, bf16[768,1152]{1,0:T(8,128)(2,1)} %get-tuple-element.220.refs_1_, f32[1,864]{1,0:T(1,128)} %broadcast_in_dim.169.refs_2_, ...), custom_call_target="tpu_custom_call" | custom-call | flops 222717536 | bytes 265420 | tf_op jit(solution)/shard_map/attn_fwd/pallas_call | solution.py:129
  151.1 11.1 %attn_fwd.6 = (bf16[768,864]{1,0:T(8,128)(2,1)}, bf16[768,288]{1,0:T(8,128)(2,1)}, f32[8,768]{1,0:T(8,128)}, bf16[1152,1152]{1,0:T(8,128)(2,1)}, bf16[1152,288]{1,0:T(8,128)(2,1)}) custom-call(s32[8]{0:T(128)} %stack.125.refs_0_, bf16[768,1152]{1,0:T(8,128)(2,1)} %get-tuple-element.220.refs_1_, f32[1,864]{1,0:T(1,128)} %broadcast_in_dim.170.refs_2_, ...), custom_call_target="tpu_custom_call" | custom-call | flops 222717536 | bytes 265420 | tf_op jit(solution)/shard_map/attn_fwd/pallas_call | solution.py:129
  164.1 10.6 %attn_fwd.7 = (bf16[768,864]{1,0:T(8,128)(2,1)}, bf16[768,288]{1,0:T(8,128)(2,1)}, f32[8,768]{1,0:T(8,128)}, bf16[1152,1152]{1,0:T(8,128)(2,1)}, bf16[1152,288]{1,0:T(8,128)(2,1)}) custom-call(s32[8]{0:T(128)} %stack.125.refs_0_, bf16[768,1152]{1,0:T(8,128)(2,1)} %get-tuple-element.220.refs_1_, f32[1,864]{1,0:T(1,128)} %broadcast_in_dim.171.refs_2_, ...), custom_call_target="tpu_custom_call" | custom-call | flops 222717536 | bytes 265420 | tf_op jit(solution)/shard_map/attn_fwd/pallas_call | solution.py:129
  174.7 10.6 %norm.3 = (f32[768,1152]{1,0:T(8,128)}, bf16[768,1152]{1,0:T(8,128)(2,1)}, bf16[1152,768]{1,0:T(8,128)(2,1)}) custom-call(s32[8]{0:T(128)} %stack.116.table.refs_0_, bf16[768,1152]{1,0:T(8,128)(2,1)} %pad.35.refs_1_.refs_8_, f32[1,1152]{1,0:T(1,128)} %broadcast_in_dim.163.refs_2_, f32[1,1152]{1,0:T(1,128)} %broadcast_in_dim.164.refs_3_.refs_4_, ...), custom_call_target="tpu_custom_call" | custom-call | flops 707788 | bytes 442368 | tf_op jit(solution)/shard_map/norm/pallas_call | solution.py:428
  188.7 2.2 collective-permute-start.31
  193.3 19.9 %ff_up.1 = (bf16[768,4608]{1,0:T(8,128)(2,1)}, bf16[768,4608]{1,0:T(8,128)(2,1)}, bf16[1152,4608]{1,0:T(8,128)(2,1)}) custom-call(s32[4]{0:T(128)} %pad_add_fusion.refs_0_, bf16[768,1152]{1,0:T(8,128)(2,1)} %get-tuple-element.226.refs_1_, f32[1,4608]{1,0:T(1,128)} %broadcast_in_dim.172.refs_2_, bf16[4608,1152]{1,0:T(8,128)(2,1)} %all-gather.2.cloned.1.call-done.refs_3_), custom_call_target="tpu_custom_call" | custom-call | flops 407686336 | bytes 1769472 | tf_op jit(solution)/shard_map/ff_up/pallas_call | solution.py:268
  216.6 28.2 %ff_down.1 = (f32[768,1152]{1,0:T(8,128)}, bf16[768,4608]{1,0:T(8,128)(2,1)}, f32[1,4608]{1,0:T(1,128)}) custom-call(s32[8]{0:T(128)} %stack.134.refs_0_, bf16[768,1152]{1,0:T(8,128)(2,1)} %multiply_convert_fusion.x.refs_1_.refs_5_, bf16[768,4608]{1,0:T(8,128)(2,1)} %get-tuple-element.232.refs_2_, bf16[768,4608]{1,0:T(8,128)(2,1)} %get-tuple-element.233.refs_3_, ...), custom_call_target="tpu_custom_call" | custom-call | flops 815372672 | bytes 1592524 | tf_op jit(solution)/shard_map/ff_down/pallas_call | solution.py:337
  246.4 13.5 %ff_grad.2 = (bf16[4,144,1152]{2,1,0:T(8,128)(2,1)}, bf16[4,144,1152]{2,1,0:T(8,128)(2,1)}, bf16[4,144,1152]{2,1,0:T(8,128)(2,1)}, bf16[4,144,1152]{2,1,0:T(8,128)(2,1)}) custom-call(bf16[576,768]{1,0:T(8,128)(2,1)} %slice.184.refs_0_, bf16[576,768]{1,0:T(8,128)(2,1)} %copy-done.61, bf16[768,4608]{1,0:T(8,128)(2,1)} %get-tuple-element.232.refs_2_, ...), custom_call_target="tpu_custom_call" | custom-call | flops 521838526464 | bytes 1245708288 | tf_op jit(solution)/shard_map/ff_grad/pallas_call | solution.py:545
  261.3 22.2 %ff_back.1 = (f32[768,1152]{1,0:T(8,128)}, f32[1,1152]{1,0:T(1,128)}, f32[1,1152]{1,0:T(1,128)}, bf16[768,1152]{1,0:T(8,128)(2,1)}, bf16[1152,768]{1,0:T(8,128)(2,1)}, /*index=5*/f32[1,1152]{1,0:T(1,128)}) custom-call(s32[8]{0:T(128)} %stack.125.refs_0_, bf16[768,4608]{1,0:T(8,128)(2,1)} %get-tuple-element.265.refs_1_.refs_2_, ...), custom_call_target="tpu_custom_call" | custom-call | flops 521838526464 | bytes 1132462080 | tf_op jit(solution)/shard_map/ff_back/pallas_call | solution.py:485
  284.5 11.2 %attn_bwd.4 = (bf16[768,1152]{1,0:T(8,128)(2,1)}, f32[1,864]{1,0:T(1,128)}) custom-call(bf16[768,864]{1,0:T(8,128)(2,1)} %get-tuple-element.254.proj, bf16[768,288]{1,0:T(8,128)(2,1)} %get-tuple-element.221.refs_8_.mixed, f32[8,768]{1,0:T(8,128)} %get-tuple-element.255.lse, bf16[768,1152]{1,0:T(8,128)(2,1)} %get-tuple-element.276.ga, ...), custom_call_target="tpu_custom_call" | custom-call | flops 419161964544 | bytes 495452160 | tf_op jit(solution)/shard_map/attn_bwd/pallas_call | solution.py:192
  295.7 11.7 %attn_bwd.5 = (bf16[768,1152]{1,0:T(8,128)(2,1)}, f32[1,864]{1,0:T(1,128)}) custom-call(bf16[768,864]{1,0:T(8,128)(2,1)} %get-tuple-element.198.proj, bf16[768,288]{1,0:T(8,128)(2,1)} %get-tuple-element.197.refs_6_.mixed, f32[8,768]{1,0:T(8,128)} %get-tuple-element.199.lse, bf16[768,1152]{1,0:T(8,128)(2,1)} %get-tuple-element.276.ga, ...), custom_call_target="tpu_custom_call" | custom-call | flops 419161964544 | bytes 495452160 | tf_op jit(solution)/shard_map/attn_bwd/pallas_call | solution.py:192
  307.4 2.7 add_convert_fusion.4
  311.5 10.9 %attn_grad.2 = (bf16[576,1152]{1,0:T(8,128)(2,1)}, bf16[576,1152]{1,0:T(8,128)(2,1)}) custom-call(bf16[1152,768]{1,0:T(8,128)(2,1)} %get-tuple-element.299.refs_0_, bf16[1152,768]{1,0:T(8,128)(2,1)} %collective-permute-done.7.refs_1_, bf16[1152,768]{1,0:T(8,128)(2,1)} %get-tuple-element.252.refs_2_, bf16[1152,768]{1,0:T(8,128)(2,1)} %collective-permute-done.37.refs_3_, ...), custom_call_target="tpu_custom_call" | custom-call | flops 260919263232 | bytes 566231040 | tf_op jit(solution)/shard_map/attn_grad/pallas_call | solution.py:583
  322.5 1.3 collective-permute-start.44
  323.8 13.5 %ff_grad.3 = (bf16[4,144,1152]{2,1,0:T(8,128)(2,1)}, bf16[4,144,1152]{2,1,0:T(8,128)(2,1)}, bf16[4,144,1152]{2,1,0:T(8,128)(2,1)}, bf16[4,144,1152]{2,1,0:T(8,128)(2,1)}) custom-call(bf16[576,768]{1,0:T(8,128)(2,1)} %get-tuple-element.360.refs_0_, bf16[576,768]{1,0:T(8,128)(2,1)} %copy-done.62, bf16[768,4608]{1,0:T(8,128)(2,1)} %get-tuple-element.265.refs_1_.refs_2_, ...), custom_call_target="tpu_custom_call" | custom-call | flops 521838526464 | bytes 1245708288 | tf_op jit(solution)/shard_map/ff_grad/pallas_call | solution.py:545
  337.4 3.3 collective-permute-done.39
  340.7 2.2 add_convert_fusion.3
  345.0 11.1 %attn_bwd.6 = (bf16[768,1152]{1,0:T(8,128)(2,1)}, f32[1,864]{1,0:T(1,128)}) custom-call(bf16[768,864]{1,0:T(8,128)(2,1)} %get-tuple-element.216.proj, bf16[768,288]{1,0:T(8,128)(2,1)} %get-tuple-element.211.refs_7_.mixed, f32[8,768]{1,0:T(8,128)} %get-tuple-element.217.lse, bf16[768,1152]{1,0:T(8,128)(2,1)} %get-tuple-element.276.ga, ...), custom_call_target="tpu_custom_call" | custom-call | flops 419161964544 | bytes 495452160 | tf_op jit(solution)/shard_map/attn_bwd/pallas_call | solution.py:192
  356.1 1.6 collective-permute-start.41
  359.1 11.4 %attn_bwd.7 = (bf16[768,1152]{1,0:T(8,128)(2,1)}, f32[1,864]{1,0:T(1,128)}) custom-call(bf16[768,864]{1,0:T(8,128)(2,1)} %get-tuple-element.192.proj, bf16[768,288]{1,0:T(8,128)(2,1)} %get-tuple-element.184.refs_5_.mixed, f32[8,768]{1,0:T(8,128)} %get-tuple-element.193.lse, bf16[768,1152]{1,0:T(8,128)(2,1)} %get-tuple-element.276.ga, ...), custom_call_target="tpu_custom_call" | custom-call | flops 419161964544 | bytes 495452160 | tf_op jit(solution)/shard_map/attn_bwd/pallas_call | solution.py:192
  370.5 1.9 fusion.7
  374.6 19.0 %attn_back.1 = (f32[729,1152]{1,0:T(8,128)}, f32[1,1152]{1,0:T(1,128)}, f32[1,1152]{1,0:T(1,128)}) custom-call(bf16[768,1152]{1,0:T(8,128)(2,1)} %get-tuple-element.278.refs_0_.refs_4_, bf16[768,1152]{1,0:T(8,128)(2,1)} %get-tuple-element.261.refs_4_.refs_1_, bf16[768,1152]{1,0:T(8,128)(2,1)} %get-tuple-element.279.refs_2_, ...), custom_call_target="tpu_custom_call" | custom-call | flops 391378894848 | bytes 1019215872 | tf_op jit(solution)/shard_map/attn_back/pallas_call | solution.py:520
  394.6 1.5 collective-permute-start.47
  397.2 1.4 collective-permute-start.46
  399.6 4.7 fusion.2
  404.3 1.5 collective-permute-start.53
  405.8 2.1 collective-permute-done.46
  407.9 1.8 collective-permute-start.49
  409.7 2.7 add_convert_fusion.2
  412.4 1.7 collective-permute-start.54
  414.7 11.7 %attn_grad.3 = (bf16[576,1152]{1,0:T(8,128)(2,1)}, bf16[576,1152]{1,0:T(8,128)(2,1)}) custom-call(bf16[1152,768]{1,0:T(8,128)(2,1)} %get-tuple-element.299.refs_0_, bf16[1152,768]{1,0:T(8,128)(2,1)} %collective-permute-done.7.refs_1_, bf16[1152,768]{1,0:T(8,128)(2,1)} %get-tuple-element.252.refs_2_, bf16[1152,768]{1,0:T(8,128)(2,1)} %collective-permute-done.37.refs_3_, ...), custom_call_target="tpu_custom_call" | custom-call | flops 260919263232 | bytes 566231040 | tf_op jit(solution)/shard_map/attn_grad/pallas_call | solution.py:583
  429.4 7.3 %copy.33 = f32[1,729,1152]{2,0,1:T(1,128)} copy(f32[1,729,1152]{2,1,0:T(8,128)} %bitcast.72) | data formatting | bytes 6718464
  437.7 6.1 %collective-permute-done.54 = bf16[4,144,1152]{2,1,0:T(8,128)(2,1)} collective-permute-done((bf16[4,144,1152]{2,1,0:T(8,128)(2,1)}, bf16[4,144,1152]{2,1,0:T(8,128)(2,1)}, u32[]{:S(2)}, u32[]{:S(2)}) %collective-permute-start.54) | collective-permute-done | bytes 1327136 | tf_op jit(solution)/shard_map/ppermute | solution.py:595
  443.8 2.2 add_convert_fusion.1
  447.4 19.2 %collective-permute-done.52 = bf16[576,1152]{1,0:T(8,128)(2,1)S(1)} collective-permute-done((bf16[576,1152]{1,0:T(8,128)(2,1)}, bf16[576,1152]{1,0:T(8,128)(2,1)S(1)}, u32[]{:S(2)}, u32[]{:S(2)}) %collective-permute-start.52) | collective-permute-done | bytes 1327136 | tf_op jit(solution)/shard_map/ppermute | solution.py:595
  468.0 2.5 collective-permute-start.58
  471.6 4.7 collective-permute-done.59
  476.4 7.8 %collective-permute-done.58 = bf16[144,1152]{1,0:T(8,128)(2,1)S(1)} collective-permute-done((bf16[144,1152]{1,0:T(8,128)(2,1)S(1)}, bf16[144,1152]{1,0:T(8,128)(2,1)S(1)}, u32[]{:S(2)}, u32[]{:S(2)}) %collective-permute-start.58) | collective-permute-done | bytes 331808 | tf_op jit(solution)/shard_map/ppermute | solution.py:595
  484.2 29.7 %collective-permute-done.57 = bf16[144,1152]{1,0:T(8,128)(2,1)S(1)} collective-permute-done((bf16[144,1152]{1,0:T(8,128)(2,1)S(1)}, bf16[144,1152]{1,0:T(8,128)(2,1)S(1)}, u32[]{:S(2)}, u32[]{:S(2)}) %collective-permute-start.57) | collective-permute-done | bytes 331808 | tf_op jit(solution)/shard_map/ppermute | solution.py:595
  (313 shorter events, 72.3 us)
Async XLA Ops:
  7.2 186.1 %all-gather.2.cloned.1.call-start = ((), (), s32[]{:S(2)}) async-start(), calls=%async_computation | async-start | bytes 10948608 | tf_op jit(solution)/shard_map/all_gather | solution.py:808
  9.2 12.7 %collective-permute-start.2 = (bf16[144,1152]{1,0:T(8,128)(2,1)S(1)}, bf16[144,1152]{1,0:T(8,128)(2,1)S(1)}, u32[]{:S(2)}, u32[]{:S(2)}) collective-permute-start(bf16[144,1152]{1,0:T(8,128)(2,1)S(1)} %get-tuple-element.370.refs_4_), channel_id=1, source_target_pairs={{0,8},{8,0},{1,9},{9,1},{2,10},{10,2},{3,11},{11,3},{4,12},{12,4},... | collective-permute-start | bytes 995336 | tf_op jit(solution)/shard_map/ppermute | solution.py:595
  10.4 11.5 %collective-permute-start.3 = (bf16[144,1152]{1,0:T(8,128)(2,1)S(1)}, bf16[144,1152]{1,0:T(8,128)(2,1)S(1)}, u32[]{:S(2)}, u32[]{:S(2)}) collective-permute-start(bf16[144,1152]{1,0:T(8,128)(2,1)S(1)} %get-tuple-element.370.refs_4_), channel_id=1, source_target_pairs={{0,1},{1,2},{2,3},{3,0},{4,5},{5,6},{6,7},{7,4},{8,9},{9,10},{10,1... | collective-permute-start | bytes 995336 | tf_op jit(solution)/shard_map/ppermute | solution.py:595
  12.0 9.9 %collective-permute-start = (bf16[80,1152]{1,0:T(8,128)(2,1)S(1)}, bf16[80,1152]{1,0:T(8,128)(2,1)}, u32[]{:S(2)}, u32[]{:S(2)}) collective-permute-start(bf16[80,1152]{1,0:T(8,128)(2,1)S(1)} %fusion.8), channel_id=1, source_target_pairs={{0,8},{8,0},{1,9},{9,1},{2,10},{10,2},{3,11},{11,3},{4,12},{12,4},... | collective-permute-start | bytes 552968 | tf_op jit(solution)/shard_map/ppermute | solution.py:595
  12.5 9.0 %collective-permute-start.1 = (bf16[64,1152]{1,0:T(8,128)(2,1)S(1)}, bf16[64,1152]{1,0:T(8,128)(2,1)S(1)}, u32[]{:S(2)}, u32[]{:S(2)}) collective-permute-start(bf16[64,1152]{1,0:T(8,128)(2,1)S(1)} %pad_maximum_fusion.9), channel_id=1, source_target_pairs={{0,16},{16,0},{1,17},{17,1},{2,18},{18,2},{3,19},{19,3},{4,20},{20... | collective-permute-start | bytes 442376 | tf_op jit(solution)/shard_map/ppermute | solution.py:595
  21.9 63.1 %copy-start.6 = (bf16[144,1152]{1,0:T(8,128)(2,1)}, bf16[144,1152]{1,0:T(8,128)(2,1)S(1)}, u32[]{:S(2)}) copy-start(bf16[144,1152]{1,0:T(8,128)(2,1)S(1)} %collective-permute-done.2.refs_8_) | copy-start | bytes 995332
  22.0 73.1 %copy-start.7 = (bf16[144,1152]{1,0:T(8,128)(2,1)}, bf16[144,1152]{1,0:T(8,128)(2,1)S(1)}, u32[]{:S(2)}) copy-start(bf16[144,1152]{1,0:T(8,128)(2,1)S(1)} %collective-permute-done.3.refs_5_) | copy-start | bytes 995332
  22.0 20.4 %collective-permute-start.7 = (bf16[1152,768]{1,0:T(8,128)(2,1)}, bf16[1152,768]{1,0:T(8,128)(2,1)}, u32[]{:S(2)}, u32[]{:S(2)}) collective-permute-start(bf16[1152,768]{1,0:T(8,128)(2,1)} %get-tuple-element.299.refs_0_), channel_id=1, source_target_pairs={{0,4},{4,0},{1,5},{5,1},{2,6},{6,2},{3,7},{7,3},{8,12},{12,8},{9,1... | collective-permute-start | bytes 5308424 | tf_op jit(solution)/shard_map/ppermute | solution.py:595
  24.6 16.3 %collective-permute-start.4 = (bf16[288,1152]{1,0:T(8,128)(2,1)S(1)}, bf16[288,1152]{1,0:T(8,128)(2,1)S(1)}, u32[]{:S(2)}, u32[]{:S(2)}) collective-permute-start(bf16[288,1152]{1,0:T(8,128)(2,1)S(1)} %pad_maximum_fusion.2.refs_3_), channel_id=1, source_target_pairs={{0,1},{1,2},{2,3},{3,0},{4,5},{5,6},{6,7},{7,4},{8,9},{9,10},{10,1... | collective-permute-start | bytes 1990664 | tf_op jit(solution)/shard_map/ppermute | solution.py:595
  26.6 15.8 %collective-permute-start.5 = (bf16[288,1152]{1,0:T(8,128)(2,1)}, bf16[288,1152]{1,0:T(8,128)(2,1)S(1)}, u32[]{:S(2)}, u32[]{:S(2)}) collective-permute-start(bf16[288,1152]{1,0:T(8,128)(2,1)} %pad_maximum_fusion.3), channel_id=1, source_target_pairs={{0,16},{16,0},{1,17},{17,1},{2,18},{18,2},{3,19},{19,3},{4,20},{20... | collective-permute-start | bytes 1990664 | tf_op jit(solution)/shard_map/ppermute | solution.py:595
  26.9 15.5 %collective-permute-start.8 = (bf16[288,1152]{1,0:T(8,128)(2,1)S(1)}, bf16[288,1152]{1,0:T(8,128)(2,1)}, u32[]{:S(2)}, u32[]{:S(2)}) collective-permute-start(bf16[288,1152]{1,0:T(8,128)(2,1)S(1)} %pad_maximum_fusion.2.refs_3_), channel_id=1, source_target_pairs={{0,4},{4,0},{1,5},{5,1},{2,6},{6,2},{3,7},{7,3},{8,12},{12,8},{9,1... | collective-permute-start | bytes 1990664 | tf_op jit(solution)/shard_map/ppermute | solution.py:595
  27.9 9.4 %collective-permute-start.6 = (bf16[144,1152]{1,0:T(8,128)(2,1)S(1)}, bf16[144,1152]{1,0:T(8,128)(2,1)S(1)}, u32[]{:S(2)}, u32[]{:S(2)}) collective-permute-start(bf16[144,1152]{1,0:T(8,128)(2,1)S(1)} %collective-permute-done.3.refs_5_), channel_id=1, source_target_pairs={{0,8},{8,0},{1,9},{9,1},{2,10},{10,2},{3,11},{11,3},{4,12},{12,4},... | collective-permute-start | bytes 995336 | tf_op jit(solution)/shard_map/ppermute | solution.py:595
  42.4 20.4 %collective-permute-start.9 = (bf16[288,1152]{1,0:T(8,128)(2,1)S(1)}, bf16[288,1152]{1,0:T(8,128)(2,1)S(1)}, u32[]{:S(2)}, u32[]{:S(2)}) collective-permute-start(bf16[288,1152]{1,0:T(8,128)(2,1)S(1)} %collective-permute-done.4.refs_4_), channel_id=1, source_target_pairs={{0,1},{1,2},{2,3},{3,0},{4,5},{5,6},{6,7},{7,4},{8,9},{9,10},{10,1... | collective-permute-start | bytes 1990664 | tf_op jit(solution)/shard_map/ppermute | solution.py:595
  43.7 19.1 %collective-permute-start.10 = (bf16[288,1152]{1,0:T(8,128)(2,1)S(1)}, bf16[288,1152]{1,0:T(8,128)(2,1)S(1)}, u32[]{:S(2)}, u32[]{:S(2)}) collective-permute-start(bf16[288,1152]{1,0:T(8,128)(2,1)S(1)} %collective-permute-done.4.refs_4_), channel_id=1, source_target_pairs={{0,4},{4,0},{1,5},{5,1},{2,6},{6,2},{3,7},{7,3},{8,12},{12,8},{9,1... | collective-permute-start | bytes 1990664 | tf_op jit(solution)/shard_map/ppermute | solution.py:595
  47.1 18.9 %collective-permute-start.13 = (bf16[576,768]{1,0:T(8,128)(2,1)S(1)}, bf16[576,768]{1,0:T(8,128)(2,1)S(1)}, u32[]{:S(2)}, u32[]{:S(2)}) collective-permute-start(bf16[576,768]{1,0:T(8,128)(2,1)S(1)} %slice.170), channel_id=1, source_target_pairs={{0,4},{4,0},{1,5},{5,1},{2,6},{6,2},{3,7},{7,3},{8,12},{12,8},{9,1... | collective-permute-start | bytes 2654216 | tf_op jit(solution)/shard_map/ppermute | solution.py:595
  48.2 17.7 %collective-permute-start.11 = (bf16[320,1152]{1,0:T(8,128)(2,1)S(1)}, bf16[320,1152]{1,0:T(8,128)(2,1)}, u32[]{:S(2)}, u32[]{:S(2)}) collective-permute-start(bf16[320,1152]{1,0:T(8,128)(2,1)S(1)} %pad_maximum_fusion), channel_id=1, source_target_pairs={{0,16},{16,0},{1,17},{17,1},{2,18},{18,2},{3,19},{19,3},{4,20},{20... | collective-permute-start | bytes 2211848 | tf_op jit(solution)/shard_map/ppermute | solution.py:595
  48.5 14.3 %collective-permute-start.12 = (bf16[256,1152]{1,0:T(8,128)(2,1)S(1)}, bf16[256,1152]{1,0:T(8,128)(2,1)}, u32[]{:S(2)}, u32[]{:S(2)}) collective-permute-start(bf16[256,1152]{1,0:T(8,128)(2,1)S(1)} %pad_maximum_fusion.7), channel_id=1, source_target_pairs={{0,8},{8,0},{1,9},{9,1},{2,10},{10,2},{3,11},{11,3},{4,12},{12,4},... | collective-permute-start | bytes 1769480 | tf_op jit(solution)/shard_map/ppermute | solution.py:595
  65.9 19.0 %collective-permute-start.16 = (bf16[320,1152]{1,0:T(8,128)(2,1)}, bf16[320,1152]{1,0:T(8,128)(2,1)S(1)}, u32[]{:S(2)}, u32[]{:S(2)}) collective-permute-start(bf16[320,1152]{1,0:T(8,128)(2,1)} %collective-permute-done.11.refs_7_), channel_id=1, source_target_pairs={{0,4},{4,0},{1,5},{5,1},{2,6},{6,2},{3,7},{7,3},{8,12},{12,8},{9,1... | collective-permute-start | bytes 2211848 | tf_op jit(solution)/shard_map/ppermute | solution.py:595
  68.2 16.8 %collective-permute-start.18 = (bf16[288,1152]{1,0:T(8,128)(2,1)}, bf16[288,1152]{1,0:T(8,128)(2,1)}, u32[]{:S(2)}, u32[]{:S(2)}) collective-permute-start(bf16[288,1152]{1,0:T(8,128)(2,1)} %pad_maximum_fusion.4), channel_id=1, source_target_pairs={{0,16},{16,0},{1,17},{17,1},{2,18},{18,2},{3,19},{19,3},{4,20},{20... | collective-permute-start | bytes 1990664 | tf_op jit(solution)/shard_map/ppermute | solution.py:595
  68.4 16.6 %collective-permute-start.14 = (bf16[288,1152]{1,0:T(8,128)(2,1)S(1)}, bf16[288,1152]{1,0:T(8,128)(2,1)S(1)}, u32[]{:S(2)}, u32[]{:S(2)}) collective-permute-start(bf16[288,1152]{1,0:T(8,128)(2,1)S(1)} %collective-permute-done.9.refs_5_), channel_id=1, source_target_pairs={{0,1},{1,2},{2,3},{3,0},{4,5},{5,6},{6,7},{7,4},{8,9},{9,10},{10,1... | collective-permute-start | bytes 1990664 | tf_op jit(solution)/shard_map/ppermute | solution.py:595
  69.7 15.3 %collective-permute-start.15 = (bf16[288,1152]{1,0:T(8,128)(2,1)S(1)}, bf16[288,1152]{1,0:T(8,128)(2,1)}, u32[]{:S(2)}, u32[]{:S(2)}) collective-permute-start(bf16[288,1152]{1,0:T(8,128)(2,1)S(1)} %collective-permute-done.9.refs_5_), channel_id=1, source_target_pairs={{0,4},{4,0},{1,5},{5,1},{2,6},{6,2},{3,7},{7,3},{8,12},{12,8},{9,1... | collective-permute-start | bytes 1990664 | tf_op jit(solution)/shard_map/ppermute | solution.py:595
  70.3 14.6 %collective-permute-start.17 = (bf16[256,1152]{1,0:T(8,128)(2,1)}, bf16[256,1152]{1,0:T(8,128)(2,1)}, u32[]{:S(2)}, u32[]{:S(2)}) collective-permute-start(bf16[256,1152]{1,0:T(8,128)(2,1)} %collective-permute-done.12.refs_9_), channel_id=1, source_target_pairs={{0,4},{4,0},{1,5},{5,1},{2,6},{6,2},{3,7},{7,3},{8,12},{12,8},{9,1... | collective-permute-start | bytes 1769480 | tf_op jit(solution)/shard_map/ppermute | solution.py:595
  89.6 21.5 %collective-permute-start.21 = (bf16[288,1152]{1,0:T(8,128)(2,1)S(1)}, bf16[288,1152]{1,0:T(8,128)(2,1)S(1)}, u32[]{:S(2)}, u32[]{:S(2)}) collective-permute-start(bf16[288,1152]{1,0:T(8,128)(2,1)S(1)} %collective-permute-done.14.refs_6_), channel_id=1, source_target_pairs={{0,4},{4,0},{1,5},{5,1},{2,6},{6,2},{3,7},{7,3},{8,12},{12,8},{9,1... | collective-permute-start | bytes 1990664 | tf_op jit(solution)/shard_map/ppermute | solution.py:595
  92.5 70.5 %collective-permute-start.29 = (bf16[1152,1152]{1,0:T(8,128)(2,1)}, bf16[1152,1152]{1,0:T(8,128)(2,1)}, u32[]{:S(2)}, u32[]{:S(2)}) collective-permute-start(bf16[1152,1152]{1,0:T(8,128)(2,1)} %constant_dynamic-update-slice_fusion), channel_id=1, source_target_pairs={{0,4},{4,0},{1,5},{5,1},{2,6},{6,2},{3,7},{7,3},{8,12},{12,8},{9,1... | collective-permute-start | bytes 7962632 | tf_op jit(solution)/shard_map/ppermute | solution.py:595
  92.6 20.0 %collective-permute-start.19 = (bf16[320,1152]{1,0:T(8,128)(2,1)S(1)}, bf16[320,1152]{1,0:T(8,128)(2,1)S(1)}, u32[]{:S(2)}, u32[]{:S(2)}) collective-permute-start(bf16[320,1152]{1,0:T(8,128)(2,1)S(1)} %pad_maximum_fusion.1), channel_id=1, source_target_pairs={{0,16},{16,0},{1,17},{17,1},{2,18},{18,2},{3,19},{19,3},{4,20},{20... | collective-permute-start | bytes 2211848 | tf_op jit(solution)/shard_map/ppermute | solution.py:595
  93.8 17.2 %collective-permute-start.20 = (bf16[256,1152]{1,0:T(8,128)(2,1)S(1)}, bf16[256,1152]{1,0:T(8,128)(2,1)}, u32[]{:S(2)}, u32[]{:S(2)}) collective-permute-start(bf16[256,1152]{1,0:T(8,128)(2,1)S(1)} %pad_maximum_fusion.8), channel_id=1, source_target_pairs={{0,8},{8,0},{1,9},{9,1},{2,10},{10,2},{3,11},{11,3},{4,12},{12,4},... | collective-permute-start | bytes 1769480 | tf_op jit(solution)/shard_map/ppermute | solution.py:595
  95.1 16.0 %collective-permute-start.22 = (bf16[144,1152]{1,0:T(8,128)(2,1)S(1)}, bf16[144,1152]{1,0:T(8,128)(2,1)S(1)}, u32[]{:S(2)}, u32[]{:S(2)}) collective-permute-start(bf16[144,1152]{1,0:T(8,128)(2,1)S(1)} %collective-permute-done.3.refs_5_), channel_id=1, source_target_pairs={{0,1},{1,2},{2,3},{3,0},{4,5},{5,6},{6,7},{7,4},{8,9},{9,10},{10,1... | collective-permute-start | bytes 995336 | tf_op jit(solution)/shard_map/ppermute | solution.py:595
  112.6 21.1 %collective-permute-start.25 = (bf16[320,1152]{1,0:T(8,128)(2,1)S(1)}, bf16[320,1152]{1,0:T(8,128)(2,1)S(1)}, u32[]{:S(2)}, u32[]{:S(2)}) collective-permute-start(bf16[320,1152]{1,0:T(8,128)(2,1)S(1)} %collective-permute-done.19.refs_8_), channel_id=1, source_target_pairs={{0,4},{4,0},{1,5},{5,1},{2,6},{6,2},{3,7},{7,3},{8,12},{12,8},{9,1... | collective-permute-start | bytes 2211848 | tf_op jit(solution)/shard_map/ppermute | solution.py:595
  113.9 19.7 %collective-permute-start.26 = (bf16[256,1152]{1,0:T(8,128)(2,1)}, bf16[256,1152]{1,0:T(8,128)(2,1)}, u32[]{:S(2)}, u32[]{:S(2)}) collective-permute-start(bf16[256,1152]{1,0:T(8,128)(2,1)} %collective-permute-done.20.refs_10_), channel_id=1, source_target_pairs={{0,4},{4,0},{1,5},{5,1},{2,6},{6,2},{3,7},{7,3},{8,12},{12,8},{9,1... | collective-permute-start | bytes 1769480 | tf_op jit(solution)/shard_map/ppermute | solution.py:595
  113.9 17.1 %collective-permute-start.23 = (bf16[144,1152]{1,0:T(8,128)(2,1)S(1)}, bf16[144,1152]{1,0:T(8,128)(2,1)S(1)}, u32[]{:S(2)}, u32[]{:S(2)}) collective-permute-start(bf16[144,1152]{1,0:T(8,128)(2,1)S(1)} %collective-permute-done.22.refs_6_), channel_id=1, source_target_pairs={{0,1},{1,2},{2,3},{3,0},{4,5},{5,6},{6,7},{7,4},{8,9},{9,10},{10,1... | collective-permute-start | bytes 995336 | tf_op jit(solution)/shard_map/ppermute | solution.py:595
  117.0 16.7 %collective-permute-start.24 = (bf16[144,1152]{1,0:T(8,128)(2,1)S(1)}, bf16[144,1152]{1,0:T(8,128)(2,1)S(1)}, u32[]{:S(2)}, u32[]{:S(2)}) collective-permute-start(bf16[144,1152]{1,0:T(8,128)(2,1)S(1)} %collective-permute-done.22.refs_6_), channel_id=1, source_target_pairs={{0,8},{8,0},{1,9},{9,1},{2,10},{10,2},{3,11},{11,3},{4,12},{12,4},... | collective-permute-start | bytes 995336 | tf_op jit(solution)/shard_map/ppermute | solution.py:595
  134.6 28.4 %collective-permute-start.28 = (bf16[288,1152]{1,0:T(8,128)(2,1)}, bf16[288,1152]{1,0:T(8,128)(2,1)S(1)}, u32[]{:S(2)}, u32[]{:S(2)}) collective-permute-start(bf16[288,1152]{1,0:T(8,128)(2,1)} %pad_maximum_fusion.5), channel_id=1, source_target_pairs={{0,16},{16,0},{1,17},{17,1},{2,18},{18,2},{3,19},{19,3},{4,20},{20... | collective-permute-start | bytes 1990664 | tf_op jit(solution)/shard_map/ppermute | solution.py:595
  138.2 24.8 %collective-permute-start.27 = (bf16[144,1152]{1,0:T(8,128)(2,1)S(1)}, bf16[144,1152]{1,0:T(8,128)(2,1)S(1)}, u32[]{:S(2)}, u32[]{:S(2)}) collective-permute-start(bf16[144,1152]{1,0:T(8,128)(2,1)S(1)} %collective-permute-done.23.refs_7_), channel_id=1, source_target_pairs={{0,8},{8,0},{1,9},{9,1},{2,10},{10,2},{3,11},{11,3},{4,12},{12,4},... | collective-permute-start | bytes 995336 | tf_op jit(solution)/shard_map/ppermute | solution.py:595
  163.1 24.7 %collective-permute-start.30 = (bf16[288,1152]{1,0:T(8,128)(2,1)S(1)}, bf16[288,1152]{1,0:T(8,128)(2,1)S(1)}, u32[]{:S(2)}, u32[]{:S(2)}) collective-permute-start(bf16[288,1152]{1,0:T(8,128)(2,1)S(1)} %pad_maximum_fusion.6), channel_id=1, source_target_pairs={{0,16},{16,0},{1,17},{17,1},{2,18},{18,2},{3,19},{19,3},{4,20},{20... | collective-permute-start | bytes 1990664 | tf_op jit(solution)/shard_map/ppermute | solution.py:595
  188.7 24.5 %collective-permute-start.31 = (bf16[1152,1152]{1,0:T(8,128)(2,1)}, bf16[1152,1152]{1,0:T(8,128)(2,1)}, u32[]{:S(2)}, u32[]{:S(2)}) collective-permute-start(bf16[1152,1152]{1,0:T(8,128)(2,1)} %constant_dynamic-update-slice_fusion.6), channel_id=1, source_target_pairs={{0,4},{4,0},{1,5},{5,1},{2,6},{6,2},{3,7},{7,3},{8,12},{12,8},{9,1... | collective-permute-start | bytes 7962632 | tf_op jit(solution)/shard_map/ppermute | solution.py:595
  191.9 21.3 %collective-permute-start.32 = (bf16[576,768]{1,0:T(8,128)(2,1)S(1)}, bf16[576,768]{1,0:T(8,128)(2,1)S(1)}, u32[]{:S(2)}, u32[]{:S(2)}) collective-permute-start(bf16[576,768]{1,0:T(8,128)(2,1)S(1)} %get-tuple-element.361), channel_id=1, source_target_pairs={{0,4},{4,0},{1,5},{5,1},{2,6},{6,2},{3,7},{7,3},{8,12},{12,8},{9,1... | collective-permute-start | bytes 2654216 | tf_op jit(solution)/shard_map/ppermute | solution.py:595
  213.2 33.0 %collective-permute-start.33 = (bf16[768,4608]{1,0:T(8,128)(2,1)}, bf16[768,4608]{1,0:T(8,128)(2,1)}, u32[]{:S(2)}, u32[]{:S(2)}) collective-permute-start(bf16[768,4608]{1,0:T(8,128)(2,1)} %get-tuple-element.232.refs_2_), channel_id=1, source_target_pairs={{0,4},{4,0},{1,5},{5,1},{2,6},{6,2},{3,7},{7,3},{8,12},{12,8},{9,1... | collective-permute-start | bytes 21233672 | tf_op jit(solution)/shard_map/ppermute | solution.py:595
  246.2 38.2 %collective-permute-start.34 = (bf16[768,4608]{1,0:T(8,128)(2,1)}, bf16[768,4608]{1,0:T(8,128)(2,1)}, u32[]{:S(2)}, u32[]{:S(2)}) collective-permute-start(bf16[768,4608]{1,0:T(8,128)(2,1)} %get-tuple-element.265.refs_1_.refs_2_), channel_id=1, source_target_pairs={{0,4},{4,0},{1,5},{5,1},{2,6},{6,2},{3,7},{7,3},{8,12},{12,8},{9,1... | collective-permute-start | bytes 21233672 | tf_op jit(solution)/shard_map/ppermute | solution.py:595
  259.8 35.8 %collective-permute-start.35 = (bf16[4,144,1152]{2,1,0:T(8,128)(2,1)}, bf16[4,144,1152]{2,1,0:T(8,128)(2,1)}, u32[]{:S(2)}, u32[]{:S(2)}) collective-permute-start(bf16[4,144,1152]{2,1,0:T(8,128)(2,1)} %get-tuple-element.245), channel_id=1, source_target_pairs={{0,8},{8,0},{1,9},{9,1},{2,10},{10,2},{3,11},{11,3},{4,12},{12,4},... | collective-permute-start | bytes 3981320 | tf_op jit(solution)/shard_map/ppermute | solution.py:595
  260.1 77.3 %collective-permute-start.38 = (bf16[4,144,1152]{2,1,0:T(8,128)(2,1)}, bf16[4,144,1152]{2,1,0:T(8,128)(2,1)}, u32[]{:S(2)}, u32[]{:S(2)}) collective-permute-start(bf16[4,144,1152]{2,1,0:T(8,128)(2,1)} %get-tuple-element.243), channel_id=1, source_target_pairs={{0,8},{8,0},{1,9},{9,1},{2,10},{10,2},{3,11},{11,3},{4,12},{12,4},... | collective-permute-start | bytes 3981320 | tf_op jit(solution)/shard_map/ppermute | solution.py:595
  283.5 28.0 %collective-permute-start.37 = (bf16[1152,768]{1,0:T(8,128)(2,1)}, bf16[1152,768]{1,0:T(8,128)(2,1)}, u32[]{:S(2)}, u32[]{:S(2)}) collective-permute-start(bf16[1152,768]{1,0:T(8,128)(2,1)} %get-tuple-element.252.refs_2_), channel_id=1, source_target_pairs={{0,4},{4,0},{1,5},{5,1},{2,6},{6,2},{3,7},{7,3},{8,12},{12,8},{9,1... | collective-permute-start | bytes 5308424 | tf_op jit(solution)/shard_map/ppermute | solution.py:595
  295.6 15.8 %collective-permute-start.36 = (bf16[768,1152]{1,0:T(8,128)(2,1)}, bf16[768,1152]{1,0:T(8,128)(2,1)}, u32[]{:S(2)}, u32[]{:S(2)}) collective-permute-start(bf16[768,1152]{1,0:T(8,128)(2,1)} %get-tuple-element.256.refs_3_), channel_id=1, source_target_pairs={{0,4},{4,0},{1,5},{5,1},{2,6},{6,2},{3,7},{7,3},{8,12},{12,8},{9,1... | collective-permute-start | bytes 5308424 | tf_op jit(solution)/shard_map/ppermute | solution.py:595
  310.1 30.5 %collective-permute-start.39 = (bf16[4,144,1152]{2,1,0:T(8,128)(2,1)}, bf16[4,144,1152]{2,1,0:T(8,128)(2,1)}, u32[]{:S(2)}, u32[]{:S(2)}) collective-permute-start(bf16[4,144,1152]{2,1,0:T(8,128)(2,1)} %add_convert_fusion.4), channel_id=1, source_target_pairs={{0,16},{16,0},{1,17},{17,1},{2,18},{18,2},{3,19},{19,3},{4,20},{20... | collective-permute-start | bytes 3981320 | tf_op jit(solution)/shard_map/ppermute | solution.py:595
  322.4 52.1 %collective-permute-start.42 = (bf16[576,1152]{1,0:T(8,128)(2,1)}, bf16[576,1152]{1,0:T(8,128)(2,1)}, u32[]{:S(2)}, u32[]{:S(2)}) collective-permute-start(bf16[576,1152]{1,0:T(8,128)(2,1)} %get-tuple-element.264), channel_id=1, source_target_pairs={{0,8},{8,0},{1,9},{9,1},{2,10},{10,2},{3,11},{11,3},{4,12},{12,4},... | collective-permute-start | bytes 3981320 | tf_op jit(solution)/shard_map/ppermute | solution.py:595
  322.5 85.3 %collective-permute-start.44 = (bf16[576,1152]{1,0:T(8,128)(2,1)}, bf16[576,1152]{1,0:T(8,128)(2,1)}, u32[]{:S(2)}, u32[]{:S(2)}) collective-permute-start(bf16[576,1152]{1,0:T(8,128)(2,1)} %get-tuple-element.263), channel_id=1, source_target_pairs={{0,8},{8,0},{1,9},{9,1},{2,10},{10,2},{3,11},{11,3},{4,12},{12,4},... | collective-permute-start | bytes 3981320 | tf_op jit(solution)/shard_map/ppermute | solution.py:595
  344.8 14.2 %collective-permute-start.40 = (bf16[144,1152]{1,0:T(8,128)(2,1)}, bf16[144,1152]{1,0:T(8,128)(2,1)}, u32[]{:S(2)}, u32[]{:S(2)}) collective-permute-start(bf16[144,1152]{1,0:T(8,128)(2,1)} %get-tuple-element.363), channel_id=1, source_target_pairs={{0,3},{1,0},{2,1},{3,2},{4,7},{5,4},{6,5},{7,6},{8,11},{9,8},{10,9... | collective-permute-start | bytes 995336 | tf_op jit(solution)/shard_map/ppermute | solution.py:595
  356.1 18.4 %collective-permute-start.41 = (bf16[768,1152]{1,0:T(8,128)(2,1)}, bf16[768,1152]{1,0:T(8,128)(2,1)}, u32[]{:S(2)}, u32[]{:S(2)}) collective-permute-start(bf16[768,1152]{1,0:T(8,128)(2,1)} %get-tuple-element.279.refs_2_), channel_id=1, source_target_pairs={{0,4},{4,0},{1,5},{5,1},{2,6},{6,2},{3,7},{7,3},{8,12},{12,8},{9,1... | collective-permute-start | bytes 5308424 | tf_op jit(solution)/shard_map/ppermute | solution.py:595
  357.8 50.1 %collective-permute-start.43 = (bf16[4,144,1152]{2,1,0:T(8,128)(2,1)}, bf16[4,144,1152]{2,1,0:T(8,128)(2,1)}, u32[]{:S(2)}, u32[]{:S(2)}) collective-permute-start(bf16[4,144,1152]{2,1,0:T(8,128)(2,1)} %get-tuple-element.283), channel_id=1, source_target_pairs={{0,16},{16,0},{1,17},{17,1},{2,18},{18,2},{3,19},{19,3},{4,20},{20... | collective-permute-start | bytes 3981320 | tf_op jit(solution)/shard_map/ppermute | solution.py:595
  372.3 23.8 %collective-permute-start.45 = (bf16[144,1152]{1,0:T(8,128)(2,1)}, bf16[144,1152]{1,0:T(8,128)(2,1)}, u32[]{:S(2)}, u32[]{:S(2)}) collective-permute-start(bf16[144,1152]{1,0:T(8,128)(2,1)} %fusion.7), channel_id=1, source_target_pairs={{0,3},{1,0},{2,1},{3,2},{4,7},{5,4},{6,5},{7,6},{8,11},{9,8},{10,9... | collective-permute-start | bytes 995336 | tf_op jit(solution)/shard_map/ppermute | solution.py:595
  394.6 4.1 collective-permute-start.47
  397.2 10.6 %collective-permute-start.46 = (bf16[144,1152]{1,0:T(8,128)(2,1)S(1)}, bf16[144,1152]{1,0:T(8,128)(2,1)S(1)}, u32[]{:S(2)}, u32[]{:S(2)}) collective-permute-start(bf16[144,1152]{1,0:T(8,128)(2,1)S(1)} %fusion.6), channel_id=1, source_target_pairs={{0,3},{1,0},{2,1},{3,2},{4,7},{5,4},{6,5},{7,6},{8,11},{9,8},{10,9... | collective-permute-start | bytes 995336 | tf_op jit(solution)/shard_map/ppermute | solution.py:595
  398.7 9.1 %collective-permute-start.48 = (f32[16,1152]{1,0:T(8,128)S(1)}, f32[16,1152]{1,0:T(8,128)S(1)}, u32[]{:S(2)}, u32[]{:S(2)}) collective-permute-start(f32[16,1152]{1,0:T(8,128)S(1)} %pad_add_fusion.1), channel_id=1, source_target_pairs={{0,8},{8,0},{1,9},{9,1},{2,10},{10,2},{3,11},{11,3},{4,12},{12,4},... | collective-permute-start | bytes 221192 | tf_op jit(solution)/shard_map/ppermute | solution.py:611
  404.3 33.4 %collective-permute-start.53 = (bf16[4,144,1152]{2,1,0:T(8,128)(2,1)}, bf16[4,144,1152]{2,1,0:T(8,128)(2,1)}, u32[]{:S(2)}, u32[]{:S(2)}) collective-permute-start(bf16[4,144,1152]{2,1,0:T(8,128)(2,1)} %get-tuple-element.305), channel_id=1, source_target_pairs={{0,16},{16,0},{1,17},{17,1},{2,18},{18,2},{3,19},{19,3},{4,20},{20... | collective-permute-start | bytes 3981320 | tf_op jit(solution)/shard_map/ppermute | solution.py:595
  407.9 6.2 %collective-permute-start.49 = (f32[16,1152]{1,0:T(8,128)S(1)}, f32[16,1152]{1,0:T(8,128)S(1)}, u32[]{:S(2)}, u32[]{:S(2)}) collective-permute-start(f32[16,1152]{1,0:T(8,128)S(1)} %add.355), channel_id=1, source_target_pairs={{0,4},{4,0},{1,5},{5,1},{2,6},{6,2},{3,7},{7,3},{8,12},{12,8},{9,1... | collective-permute-start | bytes 221192 | tf_op jit(solution)/shard_map/ppermute | solution.py:611
  412.4 31.4 %collective-permute-start.54 = (bf16[4,144,1152]{2,1,0:T(8,128)(2,1)}, bf16[4,144,1152]{2,1,0:T(8,128)(2,1)}, u32[]{:S(2)}, u32[]{:S(2)}) collective-permute-start(bf16[4,144,1152]{2,1,0:T(8,128)(2,1)} %add_convert_fusion.2), channel_id=1, source_target_pairs={{0,8},{8,0},{1,9},{9,1},{2,10},{10,2},{3,11},{11,3},{4,12},{12,4},... | collective-permute-start | bytes 3981320 | tf_op jit(solution)/shard_map/ppermute | solution.py:595
  414.7 11.8 %collective-permute-start.50 = (f32[16,1152]{1,0:T(8,128)}, f32[16,1152]{1,0:T(8,128)}, u32[]{:S(2)}, u32[]{:S(2)}) collective-permute-start(f32[16,1152]{1,0:T(8,128)} %add.356), channel_id=1, source_target_pairs={{0,1},{1,0},{2,3},{3,2},{4,5},{5,4},{6,7},{7,6},{8,9},{9,8},{10,11... | collective-permute-start | bytes 221192 | tf_op jit(solution)/shard_map/ppermute | solution.py:611
  427.4 9.3 %collective-permute-start.51 = (f32[16,1152]{1,0:T(8,128)S(1)}, f32[16,1152]{1,0:T(8,128)S(1)}, u32[]{:S(2)}, u32[]{:S(2)}) collective-permute-start(f32[16,1152]{1,0:T(8,128)S(1)} %add.357), channel_id=1, source_target_pairs={{0,2},{1,3},{2,0},{3,1},{4,6},{5,7},{6,4},{7,5},{8,10},{9,11},{10,... | collective-permute-start | bytes 221192 | tf_op jit(solution)/shard_map/ppermute | solution.py:611
  436.7 30.0 %collective-permute-start.52 = (bf16[576,1152]{1,0:T(8,128)(2,1)}, bf16[576,1152]{1,0:T(8,128)(2,1)S(1)}, u32[]{:S(2)}, u32[]{:S(2)}) collective-permute-start(bf16[576,1152]{1,0:T(8,128)(2,1)} %get-tuple-element.303), channel_id=1, source_target_pairs={{0,16},{16,0},{1,17},{17,1},{2,18},{18,2},{3,19},{19,3},{4,20},{20... | collective-permute-start | bytes 3981320 | tf_op jit(solution)/shard_map/ppermute | solution.py:595
  446.1 20.6 %collective-permute-start.55 = (bf16[144,1152]{1,0:T(8,128)(2,1)S(1)}, bf16[144,1152]{1,0:T(8,128)(2,1)S(1)}, u32[]{:S(2)}, u32[]{:S(2)}) collective-permute-start(bf16[144,1152]{1,0:T(8,128)(2,1)S(1)} %get-tuple-element.365), channel_id=1, source_target_pairs={{0,3},{1,0},{2,1},{3,2},{4,7},{5,4},{6,5},{7,6},{8,11},{9,8},{10,9... | collective-permute-start | bytes 995336 | tf_op jit(solution)/shard_map/ppermute | solution.py:595
  466.8 9.5 %collective-permute-start.59 = (bf16[144,1152]{1,0:T(8,128)(2,1)S(1)}, bf16[144,1152]{1,0:T(8,128)(2,1)S(1)}, u32[]{:S(2)}, u32[]{:S(2)}) collective-permute-start(bf16[144,1152]{1,0:T(8,128)(2,1)S(1)} %fusion.5), channel_id=1, source_target_pairs={{0,3},{1,0},{2,1},{3,2},{4,7},{5,4},{6,5},{7,6},{8,11},{9,8},{10,9... | collective-permute-start | bytes 995336 | tf_op jit(solution)/shard_map/ppermute | solution.py:595
  468.0 16.2 %collective-permute-start.58 = (bf16[144,1152]{1,0:T(8,128)(2,1)S(1)}, bf16[144,1152]{1,0:T(8,128)(2,1)S(1)}, u32[]{:S(2)}, u32[]{:S(2)}) collective-permute-start(bf16[144,1152]{1,0:T(8,128)(2,1)S(1)} %get-tuple-element.367), channel_id=1, source_target_pairs={{0,1},{1,2},{2,3},{3,0},{4,5},{5,6},{6,7},{7,4},{8,9},{9,10},{10,1... | collective-permute-start | bytes 995336 | tf_op jit(solution)/shard_map/ppermute | solution.py:595
  470.6 43.3 %collective-permute-start.57 = (bf16[144,1152]{1,0:T(8,128)(2,1)S(1)}, bf16[144,1152]{1,0:T(8,128)(2,1)S(1)}, u32[]{:S(2)}, u32[]{:S(2)}) collective-permute-start(bf16[144,1152]{1,0:T(8,128)(2,1)S(1)} %get-tuple-element.368), channel_id=1, source_target_pairs={{0,2},{1,3},{2,0},{3,1},{4,6},{5,7},{6,4},{7,5},{8,10},{9,11},{10,... | collective-permute-start | bytes 995336 | tf_op jit(solution)/shard_map/ppermute | solution.py:595
  470.6 43.3 %collective-permute-start.56 = (bf16[144,1152]{1,0:T(8,128)(2,1)S(1)}, bf16[144,1152]{1,0:T(8,128)(2,1)S(1)}, u32[]{:S(2)}, u32[]{:S(2)}) collective-permute-start(bf16[144,1152]{1,0:T(8,128)(2,1)S(1)} %get-tuple-element.366), channel_id=1, source_target_pairs={{0,3},{1,0},{2,1},{3,2},{4,7},{5,4},{6,5},{7,6},{8,11},{9,8},{10,9... | collective-permute-start | bytes 995336 | tf_op jit(solution)/shard_map/ppermute | solution.py:595
  476.4 39.9 %collective-permute-start.60 = (bf16[144,1152]{1,0:T(8,128)(2,1)S(1)}, bf16[144,1152]{1,0:T(8,128)(2,1)S(1)}, u32[]{:S(2)}, u32[]{:S(2)}) collective-permute-start(bf16[144,1152]{1,0:T(8,128)(2,1)S(1)} %fusion.4), channel_id=1, source_target_pairs={{0,3},{1,0},{2,1},{3,2},{4,7},{5,4},{6,5},{7,6},{8,11},{9,8},{10,9... | collective-permute-start | bytes 995336 | tf_op jit(solution)/shard_map/ppermute | solution.py:595
  (61 other events, 925.6 us)
Sparse Core Ops, SparseCore 0:
  85.1 103.2 all-gather.1

commit v4 on v3

--- a/solution.py
+++ b/solution.py
@@ -209,8 +209,8 @@
     )(proj, mixed, lse, ga, wo)
 
 
-def tile_of(units):
-    return next(t for t in (1024, 768, 512, 256, 128) if units % t == 0)
+def tile_of(units, most=1024):
+    return next(t for t in (1536, 1024, 768, 512, 256, 128) if units % t == 0 and t <= most)
 
 
 def first_need(tile, columns, slots):
@@ -472,7 +472,7 @@
 
 def ff_back(table, gu, w, v, gain, base):
     d, units = w.shape
-    tile = tile_of(units)
+    tile = tile_of(units, 1536)
     row = jax.ShapeDtypeStruct((1, d), F32)
     outs = [
         jax.ShapeDtypeStruct((PAD, d), F32),
@@ -528,35 +528,49 @@
     )(*args)
 
 
-def ff_grad_kernel(total, parts, rows, *refs):
+def ff_grad_kernel(total, parts, sets, size, rows, *refs):
     lhs, rhs, outs = refs[:total], refs[total : 2 * total], refs[2 * total :]
     value = nn(lhs[0][...], rhs[0][...])
     for a, b in zip(lhs[1:], rhs[1:]):
         value += nn(a[...], b[...])
-    for number in range(parts):
-        outs[number][0] = value[number * rows : (number + 1) * rows].astype(BF16)
-
-
-def ff_grad(lhs, rhs, slots, parts):
+    low = value.astype(BF16)
+    n = pl.program_id(0)
+    for s in range(sets):
+
+        @pl.when((n >= s * size) & (n < (s + 1) * size))
+        def _(s=s):
+            for number in range(parts):
+                outs[number * sets + s][0] = low[number * rows : (number + 1) * rows]
+
+
+def ff_grad(lhs, rhs, slots, parts, sets):
     total = len(lhs)
     height = lhs[0].shape[0]
     rows = height // parts
     cols = rhs[0].shape[1] // slots
-    return pl.pallas_call(
-        functools.partial(ff_grad_kernel, total, parts, rows),
+    size = slots // sets
+
+    def place(s):
+        return lambda n: (jnp.clip(n - s * size, 0, size - 1), 0, 0)
+
+    outs = pl.pallas_call(
+        functools.partial(ff_grad_kernel, total, parts, sets, size, rows),
         grid=(slots,),
         in_specs=[
             *[whole((height, PAD)) for _ in lhs],
             *[pl.BlockSpec((PAD, cols), lambda n: (0, n)) for _ in rhs],
         ],
-        out_specs=[pl.BlockSpec((1, rows, cols), lambda n: (n, 0, 0)) for _ in range(parts)],
-        out_shape=[jax.ShapeDtypeStruct((slots, rows, cols), BF16) for _ in range(parts)],
+        out_specs=[
+            pl.BlockSpec((1, rows, cols), place(s)) for _ in range(parts) for s in range(sets)
+        ],
+        out_shape=[jax.ShapeDtypeStruct((size, rows, cols), BF16)] * (parts * sets),
         compiler_params=params(),
         cost_estimate=cost(
             2 * total * PAD * height * slots * cols, 2 * slots * cols * (total * PAD + height)
         ),
         name="ff_grad",
     )(*lhs, *rhs)
+    return [outs[p * sets : (p + 1) * sets] for p in range(parts)]
 
 
 def attn_grad_kernel(total, parts, has_more, *refs):
@@ -605,7 +619,8 @@
 
 
 def total_sum(value, sizes):
-    for axis, n in sizes.items():
+    for axis in ("c", "x", "y", "z"):
+        n = sizes[axis]
         step = 1
         while step < n:
             value = value + lax.ppermute(value, axis, [(i, i ^ step) for i in range(n)])
@@ -634,13 +649,12 @@
 def ff_entries(nz, rows, cols):
     entries = []
     for dz in range(nz):
-        for dy in range(2):
-            for dx in range(2):
-                piece, at = (dx * nz + dz, 0) if dy == 0 else (2 * nz + dz, dx)
-                far = 3 * nz + dz // 2, dz % 2 * 4 + dy * 2 + dx
-                for dc, (p, block) in enumerate(((piece, at), far)):
+        for dc in range(2):
+            for dy in range(2):
+                for dx in range(2):
+                    piece = (dc * 2 + dy) * nz + dz
                     entries.append(
-                        (p, block * rows, rows, dz, dc * 4 + dy * 2 + dx, 0, dz * cols)
+                        (piece, dx * rows, rows, dz, dc * 4 + dy * 2 + dx, 0, dz * cols)
                     )
     return entries
 
@@ -670,7 +684,7 @@
     unit_width = up_weight.shape[1]
     cols = -(-unit_width // 128) * 128
     a_rows, f_rows = qkv_weight.shape[0], up_weight.shape[0]
-    linked = ny == nx == nc == 2 and nz % 2 == 0 and a_rows % 16 == 0 and f_rows % 16 == 0
+    linked = ny == nx == nc == 2 and nz == 4 and a_rows % 16 == 0 and f_rows % 16 == 0
 
     attn_own = jnp.concatenate(
         [qkv_weight.reshape(a_rows, 3 * width).astype(BF16), out_weight.T.astype(BF16)], axis=1
@@ -743,41 +757,31 @@
     spots = ("z", "y", "x", "c")
     if linked:
         half = d // 2
-        down_z, down_x, down_y, down_c = [down_own], [], [], []
-
-        def down_pair(k):
-            return swap(cat(down_z[k], down_x[k]), "y")
-
-        def down_core(k):
-            return swap(
-                cat(*[t for j in (k, k + 1) for t in (down_z[j], down_x[j], down_y[j])])
-            )
-
-        px, py, dx0, dz1, normed_a = together(
+        down_z, pairs, down_y, pair_far, y_far_down = [down_own], [], [], [], []
+
+        px, py, dx0, dz1 = together(
             (
                 swap(attn_own[:h], "x"),
                 swap(attn_own[h:], "y"),
                 swap(down_own, "x"),
                 hop(down_own, "z", nz, 1),
-                normed_a,
             )
         )
-        down_x.append(dx0)
+        pairs.append(cat(down_own, dx0))
         down_z.append(dz1)
         s = [cat(attn_own[:h], px, attn_own[h:], py)]
-        s1, dy0, dx1, na_far, sc0, gl_t, na_t = together(
+        s1, dy0, dx1, sc0, gl_t, na_t = together(
             (
                 hop(s[0], "z", nz, 1),
-                down_pair(0),
+                swap(pairs[0], "y"),
                 swap(down_z[1], "x"),
-                swap(after(na_t, px)),
                 swap(s[0]),
                 gl_t,
                 na_t,
             )
         )
         down_y.append(dy0)
-        down_x.append(dx1)
+        pairs.append(cat(down_z[1], dx1))
         s.append(s1)
         s_far = [sc0]
         y_parts, x_parts, y_far, x_far = [], [], [], []
@@ -787,11 +791,11 @@
                 moves.append(swap(cat(s[k - 2][: 2 * h], s[k - 1][: 2 * h]), "y"))
                 moves.append(swap(cat(s[k - 2][2 * h :], s[k - 1][2 * h :]), "x"))
                 if k == 2:
-                    moves.append(swap(after(gl_t, s1)[half:]))
+                    moves.append(swap(na_t))
             else:
                 moves += [swap(y_parts[-1]), swap(x_parts[-1])]
                 if k == 3:
-                    moves.append(down_pair(1))
+                    moves.append(swap(pairs[1], "y"))
             moves = together(tuple(moves))
             s.append(moves[0])
             s_far.append(moves[1])
@@ -799,25 +803,26 @@
                 y_parts.append(moves[2])
                 x_parts.append(moves[3])
                 if k == 2:
-                    gl_far = moves[4]
+                    na_far = moves[4]
             else:
                 y_far.append(moves[2])
                 x_far.append(moves[3])
                 if k == 3:
                     down_y.append(moves[4])
         up_whole = lax.all_gather(after(up_own, s[-1]), spots, axis=0, tiled=True)
-        y1, x1, sc3, dz2 = together(
+        y1, x1, sc3, dz2, dz3 = together(
             (
                 swap(cat(s[-2][: 2 * h], s[-1][: 2 * h]), "y"),
                 swap(cat(s[-2][2 * h :], s[-1][2 * h :]), "x"),
                 swap(s[-1]),
                 hop(after(down_z[1], s[-1]), "z", nz, 1),
+                hop(after(down_own, s[-1]), "z", nz, -1),
             )
         )
         y_parts.append(y1)
         x_parts.append(x1)
         s_far.append(sc3)
-        down_z.append(dz2)
+        down_z += [dz2, dz3]
         near = [*s, *y_parts, *x_parts]
         y_far.append(swap(y1))
         x_far.append(swap(x1))
@@ -830,23 +835,24 @@
                 attn_table, normed_a, bias_rows[number], pieces, attn_plans[number], seq
             )
             kept.append(out)
+            normed_a = after(normed_a, out)
             if number == 0:
-                dz3 = hop(down_z[2], "z", nz, 1)
-                dx2 = swap(down_z[2], "x")
-                normed_a, dz3, dx2, far, _ = together((normed_a, dz3, dx2, far, out))
-                down_z.append(dz3)
-                down_x.append(dx2)
+                dx2, p0, y0 = swap(down_z[2], "x"), swap(pairs[0]), swap(after(down_y[0], s[-1]))
+                normed_a, dx2, far, p0, y0 = together((normed_a, dx2, far, p0, y0))
+                pair_far.append(p0)
+                y_far_down.append(y0)
+                pairs.append(cat(down_z[2], dx2))
             if number == 1:
-                dx3, dy2 = swap(down_z[3], "x"), down_pair(2)
-                down_c.append(down_core(0))
-                normed_a = after(normed_a, out)
+                dx3, dy2 = swap(down_z[3], "x"), swap(pairs[2], "y")
+                p1, y1 = swap(pairs[1]), swap(down_y[1])
             if number == 2:
-                normed_a, dx3, dy2, down_c[0], _ = together(
-                    (normed_a, dx3, dy2, down_c[0], out)
-                )
-                down_x.append(dx3)
+                normed_a, dx3, dy2, p1, y1 = together((normed_a, dx3, dy2, p1, y1))
+                pair_far.append(p1)
+                y_far_down.append(y1)
+                pairs.append(cat(down_z[3], dx3))
                 down_y.append(dy2)
-                down_y.append(down_pair(3))
+                dy3 = swap(pairs[3], "y")
+                p2, y2, gl_far = swap(pairs[2]), swap(dy2), swap(after(gl_t[half:], out))
     else:
         kept = []
         for number, g in enumerate(groups):
@@ -872,20 +878,23 @@
         [out[4] for out in kept],
     )
     if linked:
-        normed_b, down_y[3] = together((normed_b, down_y[3]))
-        down_c.append(down_core(2))
+        normed_b, dy3, p2, y2, gl_far = together((normed_b, dy3, p2, y2, gl_far))
+        down_y.append(dy3)
+        p3, y3 = swap(pairs[3]), swap(dy3)
         nb_far = swap(nb_t[half:])
     active, slope, up_full = ff_up(zone_table, normed_b, shift, [up_whole], up_plan, nz)
     if linked:
-        active, down_c[1], nb_far = together((active, down_c[1], nb_far))
-        down_pieces = [*down_z, *down_x, *down_y, *down_c]
+        active, p3, y3, nb_far = together((active, p3, y3, nb_far))
+        down_pieces = [*pairs, *down_y, *pair_far, p2, p3, *y_far_down, y2, y3]
         active_far = swap(active)
     else:
         down_plan, ff_table, down_pieces = up_plan, zone_table, [down_whole]
     mlp, grad_upper, upper_sums = ff_down(
         ff_table, grad_low, active, slope, down_pieces, down_plan, nz
     )
-    output = (valid * (hidden + (mlp + down_bias)))[:seq].astype(BF16)[None]
+
+    def finish(rows):
+        return (valid * (hidden + (rows + down_bias)))[:seq].astype(BF16)[None]
 
     def plus(*values):
         return sum(v.astype(F32) for v in values).astype(BF16)
@@ -893,7 +902,9 @@
     if linked:
         grad_upper, active_far = together((grad_upper, active_far))
         upper_far = swap(grad_upper)
-        down_parts = ff_grad([gl_t[:half], gl_far], [active, active_far], nz, 4)
+        down_parts = [
+            p[0] for p in ff_grad([gl_t[:half], gl_far], [active, active_far], nz, 4, 1)
+        ]
         down_one, down_two = swap(down_parts[3], "x"), swap(down_parts[1], "x")
         grad_upper_first = after(grad_upper, down_parts)
     else:
@@ -904,13 +915,39 @@
             part = lax.psum_scatter(part, spot, scatter_dimension=0, tiled=True)
             return lax.optimization_barrier(part).astype(F32)
 
-        down_sum = spread(ff_grad([gl_t], [active], nz, 1))
-        up_sum = spread(ff_grad([nb_t], [grad_upper], nz, 1))
+        down_sum = spread(ff_grad([gl_t], [active], nz, 1, 1)[0])
+        up_sum = spread(ff_grad([nb_t], [grad_upper], nz, 1, 1)[0])
         grad_upper_first = grad_upper
 
     grad_hidden, ln2_gain_grad, ln2_bias_grad, grad_attn, ga_t, out_bias_sum = ff_back(
         turn_attn, grad_upper_first, up_full, hidden, ln2_gain, grad_low
     )
+
+    def in_place(rows, places):
+        at = jnp.arange(len(rows))[:, None]
+        return sum(jnp.where(at == p, r, 0.0) for r, p in zip(rows, places))
+
+    wide = max(d, 3 * width, cols)
+
+    def fit(x):
+        return jnp.pad(x, ((0, 0), (0, wide - x.shape[1])))
+
+    def early_rows():
+        vectors = [
+            out_bias_sum,
+            ln2_gain_grad,
+            ln2_bias_grad,
+            down_bias_sum,
+            in_place(sums, groups),
+            in_place(
+                [upper_sums[:, slot * cols : (slot + 1) * cols] for slot in range(nz)], zones
+            ),
+        ]
+        rows = cat(*[fit(v) for v in vectors])
+        return jnp.pad(rows, ((0, -(rows.shape[0] + 2) % 8), (0, 0)))
+
+    def fold(value, axis, step):
+        return lax.ppermute(value, axis, [(i, i ^ step) for i in range(sizes[axis])])
 
     sums = [None] * len(groups)
     if linked:
@@ -929,54 +966,89 @@
         down_other = swap(down_one, "y")
         back(1)
         grads[1], far_grads, ga_far, down_one = together((grads[1], far_grads, ga_far, down_one))
-        more = attn_grad([na_t, na_far], [ga_t, ga_far], [grads[1], far_grads], 2)
-        more_one, more_two = swap(more[1], "x"), swap(more[0], "x")
+        more = attn_grad([na_t, na_far], [ga_t, ga_far], [grads[1], far_grads], 4)
+        more_in = [None, None, swap(more[2], "x"), swap(more[3], "x")]
         upper_first, upper_far = together((grad_upper, upper_far, more))[:2]
-        up_parts = ff_grad([nb_t[:half], nb_far], [upper_first, upper_far], nz, 4)
+        up_parts = ff_grad([nb_t[:half], nb_far], [upper_first, upper_far], nz, 4, 2)
         up_parts, down_two, down_other, ga_first = together(
             (up_parts, down_two, down_other, ga_first)
         )
-        up_one, up_two = swap(up_parts[3], "y"), swap(up_parts[2], "y")
+        up_near = [swap(up_parts[3][1], "y")]
         down_value = plus(down_parts[0], down_two, down_other)
+        ga_first = after(ga_first, down_value)
         down_line = hop(down_value[nz - 1], "z", nz, -1)
-        ga_first = after(ga_first, down_value)
         back(2)
+        grads[2], down_line, more_in[2], more_in[3], up_near[0], ga_first = together(
+            (grads[2], down_line, more_in[2], more_in[3], up_near[0], ga_first)
+        )
         far_grads = swap(grads[2])
-        grads[2], down_line, ga_first = together((grads[2], down_line, ga_first))
-        for k in range(nz - 2, 0, -1):
-            down_line = hop(plus(down_line, down_value[k]), "z", nz, -1)
+        more_in[1] = swap(after(more[1], more_in[3]), "x")
+        up_near.append(swap(after(up_parts[2][1], grads[2]), "y"))
+        down_line = plus(down_line, down_value[nz - 2])
+        up_one = [None, plus(up_parts[1][1], up_near[0])]
+        ga_first = after(ga_first, down_line, up_one[1])
+        down_line = hop(down_line, "z", nz, -1)
         back(0)
-        grads[0], far_grads, more_one = together((grads[0], far_grads, more_one))
+        early = early_rows()
+        grads[0], far_grads, up_near[1], down_line, more_in[1], early = together(
+            (grads[0], far_grads, up_near[1], down_line, more_in[1], early)
+        )
+        more_in[0] = swap(after(more[0], grads[0]), "x")
+        up_near.append(swap(after(up_parts[3][0], grads[0]), "y"))
+        down_line = plus(down_line, down_value[nz - 3])
+        grads_first = after(grads[0], down_line)
+        down_line = hop(down_line, "z", nz, -1)
         input_grad, ln1_gain_grad, ln1_bias_grad = attn_back(
-            [grads[k] for k in range(4)],
+            [grads_first] + [grads[k] for k in range(1, 4)],
             [out[3] for out in kept],
             base,
             ln1_gain,
             grad_hidden,
             seq,
         )
-        input_grad, up_one, more_two, down_line = together(
-            (input_grad, up_one, more_two, down_line)
-        )
-        up_one = plus(up_parts[1], up_one)
-        up_other = swap(up_one, "x")
-        na_first = after(na_t, up_one)
+        na_first, more_in[0], up_near[2], down_line, input_grad = together(
+            (na_t, more_in[0], up_near[2], down_line, input_grad)
+        )
+        up_near.append(swap(after(up_parts[2][0], na_first), "y"))
+        up_other = [None, swap(after(up_one[1], na_first), "x")]
         total = attn_grad(
-            [na_first, na_far], [ga_t, ga_far], [grads[0], far_grads], 2, (more_two, more_one)
-        )
-        far_y = swap(total[1], "y")
-        up_two, up_other, near_y = together((up_two, up_other, total[0]))
-        up_value = plus(up_parts[0], up_two, up_other)
-        up_line = hop(up_value[nz - 1], "z", nz, -1)
-        far_y, up_line, near_y = together((far_y, up_line, near_y))
-        last = plus(near_y, far_y).reshape(nz, a_rows, 4 * width)
-        last_far = [hop(last[k], "z", nz, -k) for k in range(1, nz)]
-        for k in range(nz - 2, 0, -1):
-            up_line = hop(plus(up_line, up_value[k]), "z", nz, -1)
+            [na_first, na_far], [ga_t, ga_far], [grads[0], far_grads], 4, more_in
+        )
+        table = after(cat(fit(ln1_gain_grad), fit(ln1_bias_grad), early), na_first)
+        total, up_near[3], up_other[1], other = together(
+            (total, up_near[3], up_other[1], fold(table, "z", 1))
+        )
+        table = table + other
+        far_y = [None, swap(total[3], "y")]
+        up_one[0] = plus(up_parts[1][0], up_near[2])
+        up_other[0] = swap(up_one[0], "x")
+        up_high = plus(up_parts[0][1], up_near[1], up_other[1])
+        up_line = hop(up_high[1], "z", nz, -1)
+        far_y[1], up_line, up_other[0], near_y, other = together(
+            (far_y[1], up_line, up_other[0], total[1], fold(table, "z", 2))
+        )
+        table = table + other
+        far_y[0] = swap(after(total[2], near_y), "y")
+        high = plus(near_y, far_y[1]).reshape(2, a_rows, 4 * width)
+        last_far = [hop(high[k], "z", nz, -2 - k) for k in range(2)]
+        up_line = hop(plus(up_line, up_high[0]), "z", nz, -1)
+        output = finish(after(mlp, near_y))
+        input_grad = after(input_grad, near_y)
+        far_y[0], up_line, other, last_far, near_y = together(
+            (far_y[0], up_line, fold(table, "x", 1), last_far, after(total[0], near_y))
+        )
+        table = table + other
+        table = table + fold(table, "y", 1)
+        table = table + fold(table, "c", 1)
+        low = plus(near_y, far_y[0]).reshape(2, a_rows, 4 * width)
+        last_far.append(hop(low[1], "z", nz, -1))
+        up_low = plus(up_parts[0][0], up_near[3], up_other[0])
+        up_line = hop(plus(up_line, up_low[1]), "z", nz, -1)
         down_sum = down_line.astype(F32) + down_value[0].astype(F32)
-        up_sum = up_line.astype(F32) + up_value[0].astype(F32)
-        attn_sum = sum(v.astype(F32) for v in (last[0], *last_far))
+        up_sum = up_line.astype(F32) + up_low[0].astype(F32)
+        attn_sum = sum(v.astype(F32) for v in (low[0], *last_far))
     else:
+        output = finish(mlp)
         parts = []
         grads = {}
         for number, (proj, mixed, lse, _, wo) in enumerate(kept):
@@ -994,30 +1066,9 @@
             seq,
         )
 
-    def in_place(rows, places):
-        at = jnp.arange(len(rows))[:, None]
-        return sum(jnp.where(at == p, r, 0.0) for r, p in zip(rows, places))
-
-    wide = max(d, 3 * width, cols)
-
-    def fit(x):
-        return jnp.pad(x, ((0, 0), (0, wide - x.shape[1])))
-
-    vectors = [
-        ln1_gain_grad,
-        ln1_bias_grad,
-        out_bias_sum,
-        ln2_gain_grad,
-        ln2_bias_grad,
-        down_bias_sum,
-        in_place(sums, groups),
-        in_place(
-            [upper_sums[:, slot * cols : (slot + 1) * cols] for slot in range(nz)], zones
-        ),
-    ]
-    table = cat(*[fit(v) for v in vectors])
-    fill = -table.shape[0] % 8
-    table = total_sum(jnp.pad(table, ((0, fill), (0, 0))), sizes)
+
+    if not linked:
+        table = total_sum(cat(fit(ln1_gain_grad), fit(ln1_bias_grad), early_rows()), sizes)
     singles = [table[k, :d] for k in range(6)]
     qv = table[6 : 6 + len(groups)]
     qv_grad = jnp.stack([qv[:, :width].reshape(-1), qv[:, 2 * width : 3 * width].reshape(-1)])

time: 531 us -> 514 us (0.968)
  the two profiles are of different devices: /device:TPU:25 before, /device:TPU:0 now
where the time goes in v4:
time: 514 us; the launch traced here: 508 us
  Pallas kernels  247 us (48%)
  waiting for transfers between devices  99.9 us (19%)
  starting transfers between devices  71 us (14%)
  local copies, waits for them, and re-layouts  38.7 us (8%)
  other arithmetic  35.8 us (7%)
  between operations  16 us (3%)
    ppermute x68, waiting for transfers between devices, hop(): return lax.ppermute(x, axis, [(i, (i + step) % n) for i in range(n)])  95.6 us
    ppermute x68, starting transfers between devices, hop(): return lax.ppermute(x, axis, [(i, (i + step) % n) for i in range(n)])  63.2 us
    pallas_call x4, Pallas kernels, attn_bwd(): pl.pallas_call(functools.partial(attn_bwd_kernel, seq), in_specs=specs(5)...  45.3 us
    pallas_call x4, Pallas kernels, attn_fwd(): pl.pallas_call(functools.partial(attn_fwd_kernel, plan, len(pieces), seq)...  43.5 us
    pallas_call x2, Pallas kernels, ff_grad(): pl.pallas_call(functools.partial(ff_grad_kernel, total, parts, sets, size...  28.9 us
    pallas_call x1, Pallas kernels, ff_down(): pl.pallas_call(functools.partial(ff_down_kernel, plan, len(pieces), slots...  28.2 us
    pallas_call x2, Pallas kernels, attn_grad(): pl.pallas_call(functools.partial(attn_grad_kernel, total, parts, len(more...  22.3 us
    pallas_call x1, Pallas kernels, ff_back(): pl.pallas_call(functools.partial(ff_back_kernel, table.shape[0]), grid=(u...  21.2 us
  transfers between devices with their start and end apart: 74, of which 22 were waited for; matrix products, arithmetic and copies ran while one was open for 13% of the time, Pallas kernels for 49%

profile of v4, /device:TPU:0, one launch (start us, length us, event | category | flops | bytes accessed | tf_op | source)
XLA Modules:
  0.0 507.9 jit_solution(208536490150755470)
XLA Ops:
  8.5 3.0 collective-permute-start.2
  16.0 3.6 collective-permute-done.1
  19.6 3.6 collective-permute-done
  23.3 1.9 collective-permute-start.4
  29.0 3.0 multiply_convert_fusion.x.refs_1_.refs_5_
  32.6 3.3 turn.1
  35.9 2.9 pad.35.refs_1_.refs_8_
  40.6 4.6 norm.2
  48.6 1.7 constant_dynamic-update-slice_fusion.1
  50.3 13.3 %collective-permute-done.11.refs_9_ = bf16[256,1152]{1,0:T(8,128)(2,1)} collective-permute-done((bf16[256,1152]{1,0:T(8,128)(2,1)S(1)}, bf16[256,1152]{1,0:T(8,128)(2,1)}, u32[]{:S(2)}, u32[]{:S(2)}) %collective-permute-start.11) | collective-permute-done | bytes 589856 | tf_op jit(solution)/shard_map/ppermute | solution.py:609
  64.5 1.8 collective-permute-done.10.refs_7_
  70.6 14.1 %collective-permute-done.17.refs_9_ = bf16[288,1152]{1,0:T(8,128)(2,1)} collective-permute-done((bf16[288,1152]{1,0:T(8,128)(2,1)}, bf16[288,1152]{1,0:T(8,128)(2,1)}, u32[]{:S(2)}, u32[]{:S(2)}) %collective-permute-start.17) | collective-permute-done | bytes 663584 | tf_op jit(solution)/shard_map/ppermute | solution.py:609
  84.8 1.7 collective-permute-done.13.refs_6_
  89.9 4.0 collective-permute-start.22
  93.9 13.8 %collective-permute-done.21 = bf16[144,1152]{1,0:T(8,128)(2,1)S(1)} collective-permute-done((bf16[144,1152]{1,0:T(8,128)(2,1)}, bf16[144,1152]{1,0:T(8,128)(2,1)S(1)}, u32[]{:S(2)}, u32[]{:S(2)}) %collective-permute-start.21) | collective-permute-done | bytes 331808 | tf_op jit(solution)/shard_map/ppermute | solution.py:609
  107.7 6.3 %collective-permute-done.22 = bf16[144,1152]{1,0:T(8,128)(2,1)} collective-permute-done((bf16[144,1152]{1,0:T(8,128)(2,1)S(1)}, bf16[144,1152]{1,0:T(8,128)(2,1)}, u32[]{:S(2)}, u32[]{:S(2)}) %collective-permute-start.22) | collective-permute-done | bytes 331808 | tf_op jit(solution)/shard_map/ppermute | solution.py:609
  117.6 10.7 %attn_fwd.4 = (bf16[768,864]{1,0:T(8,128)(2,1)}, bf16[768,288]{1,0:T(8,128)(2,1)}, f32[8,768]{1,0:T(8,128)}, bf16[1152,1152]{1,0:T(8,128)(2,1)}, bf16[1152,288]{1,0:T(8,128)(2,1)}) custom-call(s32[8]{0:T(128)} %stack.125.refs_0_, bf16[768,1152]{1,0:T(8,128)(2,1)} %get-tuple-element.272.refs_1_, f32[1,864]{1,0:T(1,128)} %broadcast_in_dim.168.refs_2_, ...), custom_call_target="tpu_custom_call" | custom-call | flops 222717536 | bytes 265420 | tf_op jit(solution)/shard_map/attn_fwd/pallas_call | solution.py:129
  129.5 2.7 collective-permute-done.23
  132.2 2.0 constant_dynamic-update-slice_fusion.2.refs_6_
  135.4 2.1 collective-permute-start.28
  137.5 2.8 fusion.16
  141.3 10.6 %attn_fwd.5 = (bf16[768,864]{1,0:T(8,128)(2,1)}, bf16[768,288]{1,0:T(8,128)(2,1)}, f32[8,768]{1,0:T(8,128)}, bf16[1152,1152]{1,0:T(8,128)(2,1)}, bf16[1152,288]{1,0:T(8,128)(2,1)}) custom-call(s32[8]{0:T(128)} %stack.125.refs_0_, bf16[768,1152]{1,0:T(8,128)(2,1)} %get-tuple-element.272.refs_1_, f32[1,864]{1,0:T(1,128)} %broadcast_in_dim.169.refs_2_, ...), custom_call_target="tpu_custom_call" | custom-call | flops 222717536 | bytes 265420 | tf_op jit(solution)/shard_map/attn_fwd/pallas_call | solution.py:129
  152.0 11.3 %attn_fwd.6 = (bf16[768,864]{1,0:T(8,128)(2,1)}, bf16[768,288]{1,0:T(8,128)(2,1)}, f32[8,768]{1,0:T(8,128)}, bf16[1152,1152]{1,0:T(8,128)(2,1)}, bf16[1152,288]{1,0:T(8,128)(2,1)}) custom-call(s32[8]{0:T(128)} %stack.125.refs_0_, bf16[768,1152]{1,0:T(8,128)(2,1)} %get-tuple-element.272.refs_1_, f32[1,864]{1,0:T(1,128)} %broadcast_in_dim.170.refs_2_, ...), custom_call_target="tpu_custom_call" | custom-call | flops 222717536 | bytes 265420 | tf_op jit(solution)/shard_map/attn_fwd/pallas_call | solution.py:129
  164.9 2.1 collective-permute-start.32
  169.4 10.9 %attn_fwd.7 = (bf16[768,864]{1,0:T(8,128)(2,1)}, bf16[768,288]{1,0:T(8,128)(2,1)}, f32[8,768]{1,0:T(8,128)}, bf16[1152,1152]{1,0:T(8,128)(2,1)}, bf16[1152,288]{1,0:T(8,128)(2,1)}) custom-call(s32[8]{0:T(128)} %stack.125.refs_0_, bf16[768,1152]{1,0:T(8,128)(2,1)} %get-tuple-element.272.refs_1_, f32[1,864]{1,0:T(1,128)} %broadcast_in_dim.171.refs_2_, ...), custom_call_target="tpu_custom_call" | custom-call | flops 222717536 | bytes 265420 | tf_op jit(solution)/shard_map/attn_fwd/pallas_call | solution.py:129
  180.3 10.4 %norm.3 = (f32[768,1152]{1,0:T(8,128)}, bf16[768,1152]{1,0:T(8,128)(2,1)}, bf16[1152,768]{1,0:T(8,128)(2,1)}) custom-call(s32[8]{0:T(128)} %stack.116.table.refs_0_, bf16[768,1152]{1,0:T(8,128)(2,1)} %pad.35.refs_1_.refs_8_, f32[1,1152]{1,0:T(1,128)} %broadcast_in_dim.163.refs_2_, f32[1,1152]{1,0:T(1,128)} %broadcast_in_dim.164.refs_3_.refs_4_, ...), custom_call_target="tpu_custom_call" | custom-call | flops 707788 | bytes 442368 | tf_op jit(solution)/shard_map/norm/pallas_call | solution.py:428
  190.8 2.5 fusion.15
  195.8 19.7 %ff_up.1 = (bf16[768,4608]{1,0:T(8,128)(2,1)}, bf16[768,4608]{1,0:T(8,128)(2,1)}, bf16[1152,4608]{1,0:T(8,128)(2,1)}) custom-call(s32[4]{0:T(128)} %pad_add_fusion.refs_0_, bf16[768,1152]{1,0:T(8,128)(2,1)} %get-tuple-element.281.refs_1_, f32[1,4608]{1,0:T(1,128)} %broadcast_in_dim.172.refs_2_, bf16[4608,1152]{1,0:T(8,128)(2,1)} %all-gather.2.cloned.1.call-done.refs_3_), custom_call_target="tpu_custom_call" | custom-call | flops 407686336 | bytes 1769472 | tf_op jit(solution)/shard_map/ff_up/pallas_call | solution.py:268
  217.7 28.2 %ff_down.1 = (f32[768,1152]{1,0:T(8,128)}, bf16[768,4608]{1,0:T(8,128)(2,1)}, f32[1,4608]{1,0:T(1,128)}) custom-call(s32[8]{0:T(128)} %stack.134.refs_0_, bf16[768,1152]{1,0:T(8,128)(2,1)} %multiply_convert_fusion.x.refs_1_.refs_5_, bf16[768,4608]{1,0:T(8,128)(2,1)} %get-tuple-element.286.refs_2_, bf16[768,4608]{1,0:T(8,128)(2,1)} %get-tuple-element.287.refs_3_, ...), custom_call_target="tpu_custom_call" | custom-call | flops 815372672 | bytes 1592524 | tf_op jit(solution)/shard_map/ff_down/pallas_call | solution.py:337
  247.8 14.1 %ff_grad.2 = (bf16[4,144,1152]{2,1,0:T(8,128)(2,1)}, bf16[4,144,1152]{2,1,0:T(8,128)(2,1)}, bf16[4,144,1152]{2,1,0:T(8,128)(2,1)}, bf16[4,144,1152]{2,1,0:T(8,128)(2,1)}) custom-call(bf16[576,768]{1,0:T(8,128)(2,1)} %get-tuple-element.464.refs_0_, bf16[576,768]{1,0:T(8,128)(2,1)} %collective-permute-done.35.refs_1_, ...), custom_call_target="tpu_custom_call" | custom-call | flops 521838526464 | bytes 1245708288 | tf_op jit(solution)/shard_map/ff_grad/pallas_call | solution.py:556
  261.9 2.0 collective-permute-start.44
  264.0 21.2 %ff_back.1 = (f32[768,1152]{1,0:T(8,128)}, f32[1,1152]{1,0:T(1,128)}, f32[1,1152]{1,0:T(1,128)}, bf16[768,1152]{1,0:T(8,128)(2,1)}, bf16[1152,768]{1,0:T(8,128)(2,1)}, /*index=5*/f32[1,1152]{1,0:T(1,128)}) custom-call(s32[8]{0:T(128)} %stack.125.refs_0_, bf16[768,4608]{1,0:T(8,128)(2,1)} %get-tuple-element.326.refs_1_.refs_2_, ...), custom_call_target="tpu_custom_call" | custom-call | flops 521838526464 | bytes 1132462080 | tf_op jit(solution)/shard_map/ff_back/pallas_call | solution.py:485
  285.2 11.1 %attn_bwd.4 = (bf16[768,1152]{1,0:T(8,128)(2,1)}, f32[1,864]{1,0:T(1,128)}) custom-call(bf16[768,864]{1,0:T(8,128)(2,1)} %get-tuple-element.311.proj, bf16[768,288]{1,0:T(8,128)(2,1)} %get-tuple-element.273.refs_8_.mixed, f32[8,768]{1,0:T(8,128)} %get-tuple-element.312.lse, bf16[768,1152]{1,0:T(8,128)(2,1)} %get-tuple-element.346.ga, ...), custom_call_target="tpu_custom_call" | custom-call | flops 419161964544 | bytes 495452160 | tf_op jit(solution)/shard_map/attn_bwd/pallas_call | solution.py:192
  296.9 11.7 %attn_bwd.5 = (bf16[768,1152]{1,0:T(8,128)(2,1)}, f32[1,864]{1,0:T(1,128)}) custom-call(bf16[768,864]{1,0:T(8,128)(2,1)} %get-tuple-element.250.proj, bf16[768,288]{1,0:T(8,128)(2,1)} %get-tuple-element.249.refs_6_.mixed, f32[8,768]{1,0:T(8,128)} %get-tuple-element.251.lse, bf16[768,1152]{1,0:T(8,128)(2,1)} %get-tuple-element.346.ga, ...), custom_call_target="tpu_custom_call" | custom-call | flops 419161964544 | bytes 495452160 | tf_op jit(solution)/shard_map/attn_bwd/pallas_call | solution.py:192
  308.5 2.8 add_convert_fusion.1
  312.5 10.7 %attn_grad.2 = (bf16[288,1152]{1,0:T(8,128)(2,1)}, bf16[288,1152]{1,0:T(8,128)(2,1)}, bf16[288,1152]{1,0:T(8,128)(2,1)}, bf16[288,1152]{1,0:T(8,128)(2,1)}) custom-call(bf16[1152,768]{1,0:T(8,128)(2,1)} %get-tuple-element.371.refs_0_, bf16[1152,768]{1,0:T(8,128)(2,1)} %copy-done.69, bf16[1152,768]{1,0:T(8,128)(2,1)} %get-tuple-element.308.refs_2_, ...), custom_call_target="tpu_custom_call" | custom-call | flops 260919263232 | bytes 566231040 | tf_op jit(solution)/shard_map/attn_grad/pallas_call | solution.py:597
  323.3 2.0 collective-permute-start.48
  325.2 14.8 %ff_grad.3 = (bf16[2,144,1152]{2,1,0:T(8,128)(2,1)}, bf16[2,144,1152]{2,1,0:T(8,128)(2,1)}, bf16[2,144,1152]{2,1,0:T(8,128)(2,1)}, bf16[2,144,1152]{2,1,0:T(8,12...) custom-call(bf16[576,768]{1,0:T(8,128)(2,1)} %get-tuple-element.462., ...), custom_call_target="tpu_custom_call" | custom-call | flops 521838526464 | bytes 1245708288 | tf_op jit(solution)/shard_map/ff_grad/pallas_call | solution.py:556
  340.0 2.7 collective-permute-done.45
  342.7 2.2 add_convert_fusion
  348.2 11.2 %attn_bwd.6 = (bf16[768,1152]{1,0:T(8,128)(2,1)}, f32[1,864]{1,0:T(1,128)}) custom-call(bf16[768,864]{1,0:T(8,128)(2,1)} %get-tuple-element.264.proj, bf16[768,288]{1,0:T(8,128)(2,1)} %get-tuple-element.263.refs_7_.mixed, f32[8,768]{1,0:T(8,128)} %get-tuple-element.265.lse, bf16[768,1152]{1,0:T(8,128)(2,1)} %get-tuple-element.346.ga, ...), custom_call_target="tpu_custom_call" | custom-call | flops 419161964544 | bytes 495452160 | tf_op jit(solution)/shard_map/attn_bwd/pallas_call | solution.py:192
  360.8 3.2 collective-permute-done.49
  364.0 1.9 fusion.7
  365.9 2.6 collective-permute-start.52
  368.5 2.1 add_convert_fusion.7
  371.2 11.2 %attn_bwd.7 = (bf16[768,1152]{1,0:T(8,128)(2,1)}, f32[1,864]{1,0:T(1,128)}) custom-call(bf16[768,864]{1,0:T(8,128)(2,1)} %get-tuple-element.234.proj, bf16[768,288]{1,0:T(8,128)(2,1)} %get-tuple-element.233.refs_5_.mixed, f32[8,768]{1,0:T(8,128)} %get-tuple-element.235.lse, bf16[768,1152]{1,0:T(8,128)(2,1)} %get-tuple-element.346.ga, ...), custom_call_target="tpu_custom_call" | custom-call | flops 419161964544 | bytes 495452160 | tf_op jit(solution)/shard_map/attn_bwd/pallas_call | solution.py:192
  384.1 4.2 collective-permute-done.51
  388.4 1.9 fusion.6
  392.9 19.1 %attn_back.1 = (f32[729,1152]{1,0:T(8,128)}, f32[1,1152]{1,0:T(1,128)}, f32[1,1152]{1,0:T(1,128)}) custom-call(bf16[768,1152]{1,0:T(8,128)(2,1)} %get-tuple-element.367.refs_0_.refs_4_, bf16[768,1152]{1,0:T(8,128)(2,1)} %get-tuple-element.318.refs_4_.refs_1_, bf16[768,1152]{1,0:T(8,128)(2,1)} %get-tuple-element.348.refs_2_, ...), custom_call_target="tpu_custom_call" | custom-call | flops 391378894848 | bytes 1019215872 | tf_op jit(solution)/shard_map/attn_back/pallas_call | solution.py:520
  413.8 1.7 collective-permute-start.58
  417.2 2.1 add_convert_fusion.5
  419.6 11.6 %attn_grad.3 = (bf16[288,1152]{1,0:T(8,128)(2,1)}, bf16[288,1152]{1,0:T(8,128)(2,1)}, bf16[288,1152]{1,0:T(8,128)(2,1)}, bf16[288,1152]{1,0:T(8,128)(2,1)}) custom-call(bf16[1152,768]{1,0:T(8,128)(2,1)} %get-tuple-element.371.refs_0_, bf16[1152,768]{1,0:T(8,128)(2,1)} %copy-done.69, bf16[1152,768]{1,0:T(8,128)(2,1)} %get-tuple-element.308.refs_2_, ...), custom_call_target="tpu_custom_call" | custom-call | flops 260919263232 | bytes 566231040 | tf_op jit(solution)/shard_map/attn_grad/pallas_call | solution.py:597
  433.6 1.7 add_convert_fusion.6
  437.5 2.0 collective-permute-start.63
  439.5 1.9 fusion.3
  441.4 2.3 collective-permute-done.62
  445.2 1.9 collective-permute-done.60
  448.9 2.5 collective-permute-start.66
  456.7 5.2 %copy.33 = f32[1,729,1152]{2,0,1:T(1,128)} copy(f32[1,729,1152]{2,1,0:T(8,128)S(1)} %bitcast.72) | data formatting | bytes 6718464
  461.9 13.6 %collective-permute-done.67 = bf16[144,1152]{1,0:T(8,128)(2,1)S(1)} collective-permute-done((bf16[144,1152]{1,0:T(8,128)(2,1)S(1)}, bf16[144,1152]{1,0:T(8,128)(2,1)S(1)}, u32[]{:S(2)}, u32[]{:S(2)}) %collective-permute-start.67) | collective-permute-done | bytes 331808 | tf_op jit(solution)/shard_map/ppermute | solution.py:609
  477.2 2.7 collective-permute-done.69
  480.2 9.3 %collective-permute-start.72 = (bf16[144,1152]{1,0:T(8,128)(2,1)S(1)}, bf16[144,1152]{1,0:T(8,128)(2,1)S(1)}, u32[]{:S(2)}, u32[]{:S(2)}) collective-permute-start(bf16[144,1152]{1,0:T(8,128)(2,1)S(1)} %fusion.4), channel_id=1, source_target_pairs={{0,3},{1,0},{2,1},{3,2},{4,7},{5,4},{6,5},{7,6},{8,11},{9,8},{10,9... | collective-permute-start | bytes 995336 | tf_op jit(solution)/shard_map/ppermute | solution.py:609
  491.8 2.9 collective-permute-done.71
  498.0 2.0 collective-permute-done.72
  (350 shorter events, 77.0 us)
Async XLA Ops:
  7.2 188.7 %all-gather.2.cloned.1.call-start = ((), (), s32[]{:S(2)}) async-start(), calls=%async_computation | async-start | bytes 10948608 | tf_op jit(solution)/shard_map/all_gather | solution.py:812
  8.5 14.8 %collective-permute-start.2 = (bf16[144,1152]{1,0:T(8,128)(2,1)S(1)}, bf16[144,1152]{1,0:T(8,128)(2,1)S(1)}, u32[]{:S(2)}, u32[]{:S(2)}) collective-permute-start(bf16[144,1152]{1,0:T(8,128)(2,1)S(1)} %pad.36), channel_id=1, source_target_pairs={{0,8},{8,0},{1,9},{9,1},{2,10},{10,2},{3,11},{11,3},{4,12},{12,4},... | collective-permute-start | bytes 995336 | tf_op jit(solution)/shard_map/ppermute | solution.py:609
  23.3 21.9 %collective-permute-start.4 = (bf16[288,1152]{1,0:T(8,128)(2,1)S(1)}, bf16[288,1152]{1,0:T(8,128)(2,1)S(1)}, u32[]{:S(2)}, u32[]{:S(2)}) collective-permute-start(bf16[288,1152]{1,0:T(8,128)(2,1)S(1)} %pad_maximum_fusion.2.refs_3_), channel_id=1, source_target_pairs={{0,1},{1,2},{2,3},{3,0},{4,5},{5,6},{6,7},{7,4},{8,9},{9,10},{10,1... | collective-permute-start | bytes 1990664 | tf_op jit(solution)/shard_map/ppermute | solution.py:609
  25.3 20.0 %collective-permute-start.5 = (bf16[288,1152]{1,0:T(8,128)(2,1)S(1)}, bf16[288,1152]{1,0:T(8,128)(2,1)}, u32[]{:S(2)}, u32[]{:S(2)}) collective-permute-start(bf16[288,1152]{1,0:T(8,128)(2,1)S(1)} %pad_maximum_fusion.3.refs_4_), channel_id=1, source_target_pairs={{0,16},{16,0},{1,17},{17,1},{2,18},{18,2},{3,19},{19,3},{4,20},{20... | collective-permute-start | bytes 1990664 | tf_op jit(solution)/shard_map/ppermute | solution.py:609
  26.9 18.4 %collective-permute-start.7 = (bf16[288,1152]{1,0:T(8,128)(2,1)S(1)}, bf16[288,1152]{1,0:T(8,128)(2,1)S(1)}, u32[]{:S(2)}, u32[]{:S(2)}) collective-permute-start(bf16[288,1152]{1,0:T(8,128)(2,1)S(1)} %pad_maximum_fusion.2.refs_3_), channel_id=1, source_target_pairs={{0,4},{4,0},{1,5},{5,1},{2,6},{6,2},{3,7},{7,3},{8,12},{12,8},{9,1... | collective-permute-start | bytes 1990664 | tf_op jit(solution)/shard_map/ppermute | solution.py:609
  26.9 18.3 %collective-permute-start.6 = (bf16[144,1152]{1,0:T(8,128)(2,1)}, bf16[144,1152]{1,0:T(8,128)(2,1)S(1)}, u32[]{:S(2)}, u32[]{:S(2)}) collective-permute-start(bf16[144,1152]{1,0:T(8,128)(2,1)} %collective-permute-done.3), channel_id=1, source_target_pairs={{0,8},{8,0},{1,9},{9,1},{2,10},{10,2},{3,11},{11,3},{4,12},{12,4},... | collective-permute-start | bytes 995336 | tf_op jit(solution)/shard_map/ppermute | solution.py:609
  45.3 21.0 %collective-permute-start.12 = (bf16[1152,768]{1,0:T(8,128)(2,1)}, bf16[1152,768]{1,0:T(8,128)(2,1)S(1)}, u32[]{:S(2)}, u32[]{:S(2)}) collective-permute-start(bf16[1152,768]{1,0:T(8,128)(2,1)} %get-tuple-element.371.refs_0_), channel_id=1, source_target_pairs={{0,4},{4,0},{1,5},{5,1},{2,6},{6,2},{3,7},{7,3},{8,12},{12,8},{9,1... | collective-permute-start | bytes 5308424 | tf_op jit(solution)/shard_map/ppermute | solution.py:609
  45.6 18.9 %collective-permute-start.8 = (bf16[288,1152]{1,0:T(8,128)(2,1)S(1)}, bf16[288,1152]{1,0:T(8,128)(2,1)S(1)}, u32[]{:S(2)}, u32[]{:S(2)}) collective-permute-start(bf16[288,1152]{1,0:T(8,128)(2,1)S(1)} %collective-permute-done.4.refs_4_), channel_id=1, source_target_pairs={{0,1},{1,2},{2,3},{3,0},{4,5},{5,6},{6,7},{7,4},{8,9},{9,10},{10,1... | collective-permute-start | bytes 1990664 | tf_op jit(solution)/shard_map/ppermute | solution.py:609
  47.1 17.3 %collective-permute-start.9 = (bf16[288,1152]{1,0:T(8,128)(2,1)S(1)}, bf16[288,1152]{1,0:T(8,128)(2,1)S(1)}, u32[]{:S(2)}, u32[]{:S(2)}) collective-permute-start(bf16[288,1152]{1,0:T(8,128)(2,1)S(1)} %collective-permute-done.4.refs_4_), channel_id=1, source_target_pairs={{0,4},{4,0},{1,5},{5,1},{2,6},{6,2},{3,7},{7,3},{8,12},{12,8},{9,1... | collective-permute-start | bytes 1990664 | tf_op jit(solution)/shard_map/ppermute | solution.py:609
  47.3 19.0 %collective-permute-start.10 = (bf16[320,1152]{1,0:T(8,128)(2,1)S(1)}, bf16[320,1152]{1,0:T(8,128)(2,1)S(1)}, u32[]{:S(2)}, u32[]{:S(2)}) collective-permute-start(bf16[320,1152]{1,0:T(8,128)(2,1)S(1)} %pad_maximum_fusion), channel_id=1, source_target_pairs={{0,16},{16,0},{1,17},{17,1},{2,18},{18,2},{3,19},{19,3},{4,20},{20... | collective-permute-start | bytes 2211848 | tf_op jit(solution)/shard_map/ppermute | solution.py:609
  48.0 15.6 %collective-permute-start.11 = (bf16[256,1152]{1,0:T(8,128)(2,1)S(1)}, bf16[256,1152]{1,0:T(8,128)(2,1)}, u32[]{:S(2)}, u32[]{:S(2)}) collective-permute-start(bf16[256,1152]{1,0:T(8,128)(2,1)S(1)} %pad_maximum_fusion.4), channel_id=1, source_target_pairs={{0,8},{8,0},{1,9},{9,1},{2,10},{10,2},{3,11},{11,3},{4,12},{12,4},... | collective-permute-start | bytes 1769480 | tf_op jit(solution)/shard_map/ppermute | solution.py:609
  66.3 20.2 %collective-permute-start.15 = (bf16[320,1152]{1,0:T(8,128)(2,1)S(1)}, bf16[320,1152]{1,0:T(8,128)(2,1)S(1)}, u32[]{:S(2)}, u32[]{:S(2)}) collective-permute-start(bf16[320,1152]{1,0:T(8,128)(2,1)S(1)} %collective-permute-done.10.refs_7_), channel_id=1, source_target_pairs={{0,4},{4,0},{1,5},{5,1},{2,6},{6,2},{3,7},{7,3},{8,12},{12,8},{9,1... | collective-permute-start | bytes 2211848 | tf_op jit(solution)/shard_map/ppermute | solution.py:609
  67.2 17.6 %collective-permute-start.17 = (bf16[288,1152]{1,0:T(8,128)(2,1)}, bf16[288,1152]{1,0:T(8,128)(2,1)}, u32[]{:S(2)}, u32[]{:S(2)}) collective-permute-start(bf16[288,1152]{1,0:T(8,128)(2,1)} %constant_dynamic-update-slice_fusion.refs_5_), channel_id=1, source_target_pairs={{0,16},{16,0},{1,17},{17,1},{2,18},{18,2},{3,19},{19,3},{4,20},{20... | collective-permute-start | bytes 1990664 | tf_op jit(solution)/shard_map/ppermute | solution.py:609
  67.7 18.8 %collective-permute-start.13 = (bf16[288,1152]{1,0:T(8,128)(2,1)S(1)}, bf16[288,1152]{1,0:T(8,128)(2,1)S(1)}, u32[]{:S(2)}, u32[]{:S(2)}) collective-permute-start(bf16[288,1152]{1,0:T(8,128)(2,1)S(1)} %collective-permute-done.8.refs_5_), channel_id=1, source_target_pairs={{0,1},{1,2},{2,3},{3,0},{4,5},{5,6},{6,7},{7,4},{8,9},{9,10},{10,1... | collective-permute-start | bytes 1990664 | tf_op jit(solution)/shard_map/ppermute | solution.py:609
  69.3 17.2 %collective-permute-start.14 = (bf16[288,1152]{1,0:T(8,128)(2,1)S(1)}, bf16[288,1152]{1,0:T(8,128)(2,1)}, u32[]{:S(2)}, u32[]{:S(2)}) collective-permute-start(bf16[288,1152]{1,0:T(8,128)(2,1)S(1)} %collective-permute-done.8.refs_5_), channel_id=1, source_target_pairs={{0,4},{4,0},{1,5},{5,1},{2,6},{6,2},{3,7},{7,3},{8,12},{12,8},{9,1... | collective-permute-start | bytes 1990664 | tf_op jit(solution)/shard_map/ppermute | solution.py:609
  69.3 15.5 %collective-permute-start.16 = (bf16[256,1152]{1,0:T(8,128)(2,1)}, bf16[256,1152]{1,0:T(8,128)(2,1)}, u32[]{:S(2)}, u32[]{:S(2)}) collective-permute-start(bf16[256,1152]{1,0:T(8,128)(2,1)} %collective-permute-done.11.refs_9_), channel_id=1, source_target_pairs={{0,4},{4,0},{1,5},{5,1},{2,6},{6,2},{3,7},{7,3},{8,12},{12,8},{9,1... | collective-permute-start | bytes 1769480 | tf_op jit(solution)/shard_map/ppermute | solution.py:609
  87.6 26.5 %collective-permute-start.20 = (bf16[288,1152]{1,0:T(8,128)(2,1)S(1)}, bf16[288,1152]{1,0:T(8,128)(2,1)S(1)}, u32[]{:S(2)}, u32[]{:S(2)}) collective-permute-start(bf16[288,1152]{1,0:T(8,128)(2,1)S(1)} %collective-permute-done.13.refs_6_), channel_id=1, source_target_pairs={{0,4},{4,0},{1,5},{5,1},{2,6},{6,2},{3,7},{7,3},{8,12},{12,8},{9,1... | collective-permute-start | bytes 1990664 | tf_op jit(solution)/shard_map/ppermute | solution.py:609
  87.7 26.4 %collective-permute-start.18 = (bf16[320,1152]{1,0:T(8,128)(2,1)S(1)}, bf16[320,1152]{1,0:T(8,128)(2,1)S(1)}, u32[]{:S(2)}, u32[]{:S(2)}) collective-permute-start(bf16[320,1152]{1,0:T(8,128)(2,1)S(1)} %pad_maximum_fusion.1), channel_id=1, source_target_pairs={{0,16},{16,0},{1,17},{17,1},{2,18},{18,2},{3,19},{19,3},{4,20},{20... | collective-permute-start | bytes 2211848 | tf_op jit(solution)/shard_map/ppermute | solution.py:609
  89.3 24.8 %collective-permute-start.19 = (bf16[256,1152]{1,0:T(8,128)(2,1)S(1)}, bf16[256,1152]{1,0:T(8,128)(2,1)}, u32[]{:S(2)}, u32[]{:S(2)}) collective-permute-start(bf16[256,1152]{1,0:T(8,128)(2,1)S(1)} %pad_maximum_fusion.5), channel_id=1, source_target_pairs={{0,8},{8,0},{1,9},{9,1},{2,10},{10,2},{3,11},{11,3},{4,12},{12,4},... | collective-permute-start | bytes 1769480 | tf_op jit(solution)/shard_map/ppermute | solution.py:609
  89.9 17.8 %collective-permute-start.21 = (bf16[144,1152]{1,0:T(8,128)(2,1)}, bf16[144,1152]{1,0:T(8,128)(2,1)S(1)}, u32[]{:S(2)}, u32[]{:S(2)}) collective-permute-start(bf16[144,1152]{1,0:T(8,128)(2,1)} %collective-permute-done.3), channel_id=1, source_target_pairs={{0,1},{1,2},{2,3},{3,0},{4,5},{5,6},{6,7},{7,4},{8,9},{9,10},{10,1... | collective-permute-start | bytes 995336 | tf_op jit(solution)/shard_map/ppermute | solution.py:609
  89.9 24.2 %collective-permute-start.22 = (bf16[144,1152]{1,0:T(8,128)(2,1)S(1)}, bf16[144,1152]{1,0:T(8,128)(2,1)}, u32[]{:S(2)}, u32[]{:S(2)}) collective-permute-start(bf16[144,1152]{1,0:T(8,128)(2,1)S(1)} %copy-done.21), channel_id=1, source_target_pairs={{0,3},{1,0},{2,1},{3,2},{4,7},{5,4},{6,5},{7,6},{8,11},{9,8},{10,9... | collective-permute-start | bytes 995336 | tf_op jit(solution)/shard_map/ppermute | solution.py:609
  114.1 18.1 %collective-permute-start.24 = (bf16[320,1152]{1,0:T(8,128)(2,1)S(1)}, bf16[320,1152]{1,0:T(8,128)(2,1)S(1)}, u32[]{:S(2)}, u32[]{:S(2)}) collective-permute-start(bf16[320,1152]{1,0:T(8,128)(2,1)S(1)} %collective-permute-done.18.refs_8_), channel_id=1, source_target_pairs={{0,4},{4,0},{1,5},{5,1},{2,6},{6,2},{3,7},{7,3},{8,12},{12,8},{9,1... | collective-permute-start | bytes 2211848 | tf_op jit(solution)/shard_map/ppermute | solution.py:609
  114.2 14.8 %collective-permute-start.26 = (bf16[288,1152]{1,0:T(8,128)(2,1)S(1)}, bf16[288,1152]{1,0:T(8,128)(2,1)}, u32[]{:S(2)}, u32[]{:S(2)}) collective-permute-start(bf16[288,1152]{1,0:T(8,128)(2,1)S(1)} %pad_maximum_fusion.3.refs_4_), channel_id=1, source_target_pairs={{0,4},{4,0},{1,5},{5,1},{2,6},{6,2},{3,7},{7,3},{8,12},{12,8},{9,1... | collective-permute-start | bytes 1990664 | tf_op jit(solution)/shard_map/ppermute | solution.py:609
  114.7 14.3 %collective-permute-start.27 = (bf16[288,1152]{1,0:T(8,128)(2,1)}, bf16[288,1152]{1,0:T(8,128)(2,1)}, u32[]{:S(2)}, u32[]{:S(2)}) collective-permute-start(bf16[288,1152]{1,0:T(8,128)(2,1)} %collective-permute-done.5.refs_8_), channel_id=1, source_target_pairs={{0,4},{4,0},{1,5},{5,1},{2,6},{6,2},{3,7},{7,3},{8,12},{12,8},{9,1... | collective-permute-start | bytes 1990664 | tf_op jit(solution)/shard_map/ppermute | solution.py:609
  114.8 17.4 %collective-permute-start.25 = (bf16[256,1152]{1,0:T(8,128)(2,1)}, bf16[256,1152]{1,0:T(8,128)(2,1)S(1)}, u32[]{:S(2)}, u32[]{:S(2)}) collective-permute-start(bf16[256,1152]{1,0:T(8,128)(2,1)} %collective-permute-done.19.refs_10_), channel_id=1, source_target_pairs={{0,4},{4,0},{1,5},{5,1},{2,6},{6,2},{3,7},{7,3},{8,12},{12,8},{9,1... | collective-permute-start | bytes 1769480 | tf_op jit(solution)/shard_map/ppermute | solution.py:609
  115.3 16.9 %collective-permute-start.23 = (bf16[144,1152]{1,0:T(8,128)(2,1)}, bf16[144,1152]{1,0:T(8,128)(2,1)}, u32[]{:S(2)}, u32[]{:S(2)}) collective-permute-start(bf16[144,1152]{1,0:T(8,128)(2,1)} %copy-done.41), channel_id=1, source_target_pairs={{0,8},{8,0},{1,9},{9,1},{2,10},{10,2},{3,11},{11,3},{4,12},{12,4},... | collective-permute-start | bytes 995336 | tf_op jit(solution)/shard_map/ppermute | solution.py:609
  129.0 34.3 %collective-permute-start.30 = (bf16[288,1152]{1,0:T(8,128)(2,1)}, bf16[288,1152]{1,0:T(8,128)(2,1)S(1)}, u32[]{:S(2)}, u32[]{:S(2)}) collective-permute-start(bf16[288,1152]{1,0:T(8,128)(2,1)} %constant_dynamic-update-slice_fusion.refs_5_), channel_id=1, source_target_pairs={{0,4},{4,0},{1,5},{5,1},{2,6},{6,2},{3,7},{7,3},{8,12},{12,8},{9,1... | collective-permute-start | bytes 1990664 | tf_op jit(solution)/shard_map/ppermute | solution.py:609
  129.0 34.9 %collective-permute-start.31 = (bf16[288,1152]{1,0:T(8,128)(2,1)}, bf16[288,1152]{1,0:T(8,128)(2,1)}, u32[]{:S(2)}, u32[]{:S(2)}) collective-permute-start(bf16[288,1152]{1,0:T(8,128)(2,1)} %collective-permute-done.17.refs_9_), channel_id=1, source_target_pairs={{0,4},{4,0},{1,5},{5,1},{2,6},{6,2},{3,7},{7,3},{8,12},{12,8},{9,1... | collective-permute-start | bytes 1990664 | tf_op jit(solution)/shard_map/ppermute | solution.py:609
  134.2 29.7 %collective-permute-start.29 = (bf16[288,1152]{1,0:T(8,128)(2,1)}, bf16[288,1152]{1,0:T(8,128)(2,1)}, u32[]{:S(2)}, u32[]{:S(2)}) collective-permute-start(bf16[288,1152]{1,0:T(8,128)(2,1)} %constant_dynamic-update-slice_fusion.2.refs_6_), channel_id=1, source_target_pairs={{0,16},{16,0},{1,17},{17,1},{2,18},{18,2},{3,19},{19,3},{4,20},{20... | collective-permute-start | bytes 1990664 | tf_op jit(solution)/shard_map/ppermute | solution.py:609
  135.4 28.5 %collective-permute-start.28 = (bf16[144,1152]{1,0:T(8,128)(2,1)}, bf16[144,1152]{1,0:T(8,128)(2,1)}, u32[]{:S(2)}, u32[]{:S(2)}) collective-permute-start(bf16[144,1152]{1,0:T(8,128)(2,1)} %collective-permute-done.22), channel_id=1, source_target_pairs={{0,8},{8,0},{1,9},{9,1},{2,10},{10,2},{3,11},{11,3},{4,12},{12,4},... | collective-permute-start | bytes 995336 | tf_op jit(solution)/shard_map/ppermute | solution.py:609
  141.3 52.6 %collective-permute-start.33 = (bf16[288,1152]{1,0:T(8,128)(2,1)}, bf16[288,1152]{1,0:T(8,128)(2,1)S(1)}, u32[]{:S(2)}, u32[]{:S(2)}) collective-permute-start(bf16[288,1152]{1,0:T(8,128)(2,1)} %constant_dynamic-update-slice_fusion.2.refs_6_), channel_id=1, source_target_pairs={{0,4},{4,0},{1,5},{5,1},{2,6},{6,2},{3,7},{7,3},{8,12},{12,8},{9,1... | collective-permute-start | bytes 1990664 | tf_op jit(solution)/shard_map/ppermute | solution.py:609
  163.3 30.6 %collective-permute-start.35 = (bf16[576,768]{1,0:T(8,128)(2,1)S(1)}, bf16[576,768]{1,0:T(8,128)(2,1)}, u32[]{:S(2)}, u32[]{:S(2)}) collective-permute-start(bf16[576,768]{1,0:T(8,128)(2,1)S(1)} %copy-done.25), channel_id=1, source_target_pairs={{0,4},{4,0},{1,5},{5,1},{2,6},{6,2},{3,7},{7,3},{8,12},{12,8},{9,1... | collective-permute-start | bytes 2654216 | tf_op jit(solution)/shard_map/ppermute | solution.py:609
  164.9 29.0 %collective-permute-start.32 = (bf16[288,1152]{1,0:T(8,128)(2,1)S(1)}, bf16[288,1152]{1,0:T(8,128)(2,1)}, u32[]{:S(2)}, u32[]{:S(2)}) collective-permute-start(bf16[288,1152]{1,0:T(8,128)(2,1)S(1)} %constant_dynamic-update-slice_fusion.4.refs_7_), channel_id=1, source_target_pairs={{0,16},{16,0},{1,17},{17,1},{2,18},{18,2},{3,19},{19,3},{4,20},{20... | collective-permute-start | bytes 1990664 | tf_op jit(solution)/shard_map/ppermute | solution.py:609
  167.0 26.9 %collective-permute-start.34 = (bf16[288,1152]{1,0:T(8,128)(2,1)}, bf16[288,1152]{1,0:T(8,128)(2,1)}, u32[]{:S(2)}, u32[]{:S(2)}) collective-permute-start(bf16[288,1152]{1,0:T(8,128)(2,1)} %collective-permute-done.29.refs_10_), channel_id=1, source_target_pairs={{0,4},{4,0},{1,5},{5,1},{2,6},{6,2},{3,7},{7,3},{8,12},{12,8},{9,1... | collective-permute-start | bytes 1990664 | tf_op jit(solution)/shard_map/ppermute | solution.py:609
  193.3 22.4 %collective-permute-start.38 = (bf16[576,768]{1,0:T(8,128)(2,1)S(1)}, bf16[576,768]{1,0:T(8,128)(2,1)}, u32[]{:S(2)}, u32[]{:S(2)}) collective-permute-start(bf16[576,768]{1,0:T(8,128)(2,1)S(1)} %get-tuple-element.463), channel_id=1, source_target_pairs={{0,4},{4,0},{1,5},{5,1},{2,6},{6,2},{3,7},{7,3},{8,12},{12,8},{9,1... | collective-permute-start | bytes 2654216 | tf_op jit(solution)/shard_map/ppermute | solution.py:609
  193.9 21.8 %collective-permute-start.36 = (bf16[288,1152]{1,0:T(8,128)(2,1)S(1)}, bf16[288,1152]{1,0:T(8,128)(2,1)S(1)}, u32[]{:S(2)}, u32[]{:S(2)}) collective-permute-start(bf16[288,1152]{1,0:T(8,128)(2,1)S(1)} %constant_dynamic-update-slice_fusion.4.refs_7_), channel_id=1, source_target_pairs={{0,4},{4,0},{1,5},{5,1},{2,6},{6,2},{3,7},{7,3},{8,12},{12,8},{9,1... | collective-permute-start | bytes 1990664 | tf_op jit(solution)/shard_map/ppermute | solution.py:609
  194.0 21.7 %collective-permute-start.37 = (bf16[288,1152]{1,0:T(8,128)(2,1)}, bf16[288,1152]{1,0:T(8,128)(2,1)}, u32[]{:S(2)}, u32[]{:S(2)}) collective-permute-start(bf16[288,1152]{1,0:T(8,128)(2,1)} %collective-permute-done.32.refs_11_), channel_id=1, source_target_pairs={{0,4},{4,0},{1,5},{5,1},{2,6},{6,2},{3,7},{7,3},{8,12},{12,8},{9,1... | collective-permute-start | bytes 1990664 | tf_op jit(solution)/shard_map/ppermute | solution.py:609
  215.7 31.8 %collective-permute-start.39 = (bf16[768,4608]{1,0:T(8,128)(2,1)}, bf16[768,4608]{1,0:T(8,128)(2,1)}, u32[]{:S(2)}, u32[]{:S(2)}) collective-permute-start(bf16[768,4608]{1,0:T(8,128)(2,1)} %get-tuple-element.286.refs_2_), channel_id=1, source_target_pairs={{0,4},{4,0},{1,5},{5,1},{2,6},{6,2},{3,7},{7,3},{8,12},{12,8},{9,1... | collective-permute-start | bytes 21233672 | tf_op jit(solution)/shard_map/ppermute | solution.py:609
  247.4 37.8 %collective-permute-start.40 = (bf16[768,4608]{1,0:T(8,128)(2,1)}, bf16[768,4608]{1,0:T(8,128)(2,1)}, u32[]{:S(2)}, u32[]{:S(2)}) collective-permute-start(bf16[768,4608]{1,0:T(8,128)(2,1)} %get-tuple-element.326.refs_1_.refs_2_), channel_id=1, source_target_pairs={{0,4},{4,0},{1,5},{5,1},{2,6},{6,2},{3,7},{7,3},{8,12},{12,8},{9,1... | collective-permute-start | bytes 21233672 | tf_op jit(solution)/shard_map/ppermute | solution.py:609
  261.9 34.9 %collective-permute-start.41 = (bf16[4,144,1152]{2,1,0:T(8,128)(2,1)}, bf16[4,144,1152]{2,1,0:T(8,128)(2,1)}, u32[]{:S(2)}, u32[]{:S(2)}) collective-permute-start(bf16[4,144,1152]{2,1,0:T(8,128)(2,1)} %get-tuple-element.305), channel_id=1, source_target_pairs={{0,8},{8,0},{1,9},{9,1},{2,10},{10,2},{3,11},{11,3},{4,12},{12,4},... | collective-permute-start | bytes 3981320 | tf_op jit(solution)/shard_map/ppermute | solution.py:609
  261.9 78.0 %collective-permute-start.44 = (bf16[4,144,1152]{2,1,0:T(8,128)(2,1)}, bf16[4,144,1152]{2,1,0:T(8,128)(2,1)}, u32[]{:S(2)}, u32[]{:S(2)}) collective-permute-start(bf16[4,144,1152]{2,1,0:T(8,128)(2,1)} %get-tuple-element.303), channel_id=1, source_target_pairs={{0,8},{8,0},{1,9},{9,1},{2,10},{10,2},{3,11},{11,3},{4,12},{12,4},... | collective-permute-start | bytes 3981320 | tf_op jit(solution)/shard_map/ppermute | solution.py:609
  285.1 27.4 %collective-permute-start.43 = (bf16[1152,768]{1,0:T(8,128)(2,1)}, bf16[1152,768]{1,0:T(8,128)(2,1)}, u32[]{:S(2)}, u32[]{:S(2)}) collective-permute-start(bf16[1152,768]{1,0:T(8,128)(2,1)} %get-tuple-element.308.refs_2_), channel_id=1, source_target_pairs={{0,4},{4,0},{1,5},{5,1},{2,6},{6,2},{3,7},{7,3},{8,12},{12,8},{9,1... | collective-permute-start | bytes 5308424 | tf_op jit(solution)/shard_map/ppermute | solution.py:609
  296.4 16.1 %collective-permute-start.42 = (bf16[768,1152]{1,0:T(8,128)(2,1)}, bf16[768,1152]{1,0:T(8,128)(2,1)}, u32[]{:S(2)}, u32[]{:S(2)}) collective-permute-start(bf16[768,1152]{1,0:T(8,128)(2,1)} %get-tuple-element.313.refs_3_), channel_id=1, source_target_pairs={{0,4},{4,0},{1,5},{5,1},{2,6},{6,2},{3,7},{7,3},{8,12},{12,8},{9,1... | collective-permute-start | bytes 5308424 | tf_op jit(solution)/shard_map/ppermute | solution.py:609
  311.3 31.4 %collective-permute-start.45 = (bf16[4,144,1152]{2,1,0:T(8,128)(2,1)}, bf16[4,144,1152]{2,1,0:T(8,128)(2,1)}, u32[]{:S(2)}, u32[]{:S(2)}) collective-permute-start(bf16[4,144,1152]{2,1,0:T(8,128)(2,1)} %add_convert_fusion.1), channel_id=1, source_target_pairs={{0,16},{16,0},{1,17},{17,1},{2,18},{18,2},{3,19},{19,3},{4,20},{20... | collective-permute-start | bytes 3981320 | tf_op jit(solution)/shard_map/ppermute | solution.py:609
  323.2 37.6 %collective-permute-start.47 = (bf16[288,1152]{1,0:T(8,128)(2,1)}, bf16[288,1152]{1,0:T(8,128)(2,1)}, u32[]{:S(2)}, u32[]{:S(2)}) collective-permute-start(bf16[288,1152]{1,0:T(8,128)(2,1)} %get-tuple-element.324), channel_id=1, source_target_pairs={{0,8},{8,0},{1,9},{9,1},{2,10},{10,2},{3,11},{11,3},{4,12},{12,4},... | collective-permute-start | bytes 1990664 | tf_op jit(solution)/shard_map/ppermute | solution.py:609
  323.3 37.5 %collective-permute-start.48 = (bf16[288,1152]{1,0:T(8,128)(2,1)}, bf16[288,1152]{1,0:T(8,128)(2,1)}, u32[]{:S(2)}, u32[]{:S(2)}) collective-permute-start(bf16[288,1152]{1,0:T(8,128)(2,1)} %get-tuple-element.325), channel_id=1, source_target_pairs={{0,8},{8,0},{1,9},{9,1},{2,10},{10,2},{3,11},{11,3},{4,12},{12,4},... | collective-permute-start | bytes 1990664 | tf_op jit(solution)/shard_map/ppermute | solution.py:609
  348.0 16.0 %collective-permute-start.49 = (bf16[2,144,1152]{2,1,0:T(8,128)(2,1)}, bf16[2,144,1152]{2,1,0:T(8,128)(2,1)}, u32[]{:S(2)}, u32[]{:S(2)}) collective-permute-start(bf16[2,144,1152]{2,1,0:T(8,128)(2,1)} %get-tuple-element.341), channel_id=1, source_target_pairs={{0,16},{16,0},{1,17},{17,1},{2,18},{18,2},{3,19},{19,3},{4,20},{20... | collective-permute-start | bytes 1990664 | tf_op jit(solution)/shard_map/ppermute | solution.py:609
  365.9 18.2 %collective-permute-start.52 = (bf16[144,1152]{1,0:T(8,128)(2,1)}, bf16[144,1152]{1,0:T(8,128)(2,1)}, u32[]{:S(2)}, u32[]{:S(2)}) collective-permute-start(bf16[144,1152]{1,0:T(8,128)(2,1)} %fusion.7), channel_id=1, source_target_pairs={{0,3},{1,0},{2,1},{3,2},{4,7},{5,4},{6,5},{7,6},{8,11},{9,8},{10,9... | collective-permute-start | bytes 995336 | tf_op jit(solution)/shard_map/ppermute | solution.py:609
  370.6 17.8 %collective-permute-start.50 = (bf16[768,1152]{1,0:T(8,128)(2,1)}, bf16[768,1152]{1,0:T(8,128)(2,1)}, u32[]{:S(2)}, u32[]{:S(2)}) collective-permute-start(bf16[768,1152]{1,0:T(8,128)(2,1)} %get-tuple-element.348.refs_2_), channel_id=1, source_target_pairs={{0,4},{4,0},{1,5},{5,1},{2,6},{6,2},{3,7},{7,3},{8,12},{12,8},{9,1... | collective-permute-start | bytes 5308424 | tf_op jit(solution)/shard_map/ppermute | solution.py:609
  370.6 17.6 %collective-permute-start.51 = (bf16[2,144,1152]{2,1,0:T(8,128)(2,1)}, bf16[2,144,1152]{2,1,0:T(8,128)(2,1)}, u32[]{:S(2)}, u32[]{:S(2)}) collective-permute-start(bf16[2,144,1152]{2,1,0:T(8,128)(2,1)} %get-tuple-element.350), channel_id=1, source_target_pairs={{0,16},{16,0},{1,17},{17,1},{2,18},{18,2},{3,19},{19,3},{4,20},{20... | collective-permute-start | bytes 1990664 | tf_op jit(solution)/shard_map/ppermute | solution.py:609
  371.0 17.4 %collective-permute-start.53 = (bf16[288,1152]{1,0:T(8,128)(2,1)}, bf16[288,1152]{1,0:T(8,128)(2,1)}, u32[]{:S(2)}, u32[]{:S(2)}) collective-permute-start(bf16[288,1152]{1,0:T(8,128)(2,1)} %get-tuple-element.352), channel_id=1, source_target_pairs={{0,8},{8,0},{1,9},{9,1},{2,10},{10,2},{3,11},{11,3},{4,12},{12,4},... | collective-permute-start | bytes 1990664 | tf_op jit(solution)/shard_map/ppermute | solution.py:609
  390.3 23.1 %collective-permute-start.56 = (bf16[144,1152]{1,0:T(8,128)(2,1)}, bf16[144,1152]{1,0:T(8,128)(2,1)}, u32[]{:S(2)}, u32[]{:S(2)}) collective-permute-start(bf16[144,1152]{1,0:T(8,128)(2,1)} %fusion.6), channel_id=1, source_target_pairs={{0,3},{1,0},{2,1},{3,2},{4,7},{5,4},{6,5},{7,6},{8,11},{9,8},{10,9... | collective-permute-start | bytes 995336 | tf_op jit(solution)/shard_map/ppermute | solution.py:609
  391.0 22.3 %collective-permute-start.54 = (bf16[288,1152]{1,0:T(8,128)(2,1)}, bf16[288,1152]{1,0:T(8,128)(2,1)}, u32[]{:S(2)}, u32[]{:S(2)}) collective-permute-start(bf16[288,1152]{1,0:T(8,128)(2,1)} %get-tuple-element.363), channel_id=1, source_target_pairs={{0,8},{8,0},{1,9},{9,1},{2,10},{10,2},{3,11},{11,3},{4,12},{12,4},... | collective-permute-start | bytes 1990664 | tf_op jit(solution)/shard_map/ppermute | solution.py:609
  391.3 22.0 %collective-permute-start.55 = (bf16[2,144,1152]{2,1,0:T(8,128)(2,1)}, bf16[2,144,1152]{2,1,0:T(8,128)(2,1)}, u32[]{:S(2)}, u32[]{:S(2)}) collective-permute-start(bf16[2,144,1152]{2,1,0:T(8,128)(2,1)} %get-tuple-element.365), channel_id=1, source_target_pairs={{0,16},{16,0},{1,17},{17,1},{2,18},{18,2},{3,19},{19,3},{4,20},{20... | collective-permute-start | bytes 1990664 | tf_op jit(solution)/shard_map/ppermute | solution.py:609
  413.3 17.9 %collective-permute-start.57 = (bf16[2,144,1152]{2,1,0:T(8,128)(2,1)}, bf16[2,144,1152]{2,1,0:T(8,128)(2,1)}, u32[]{:S(2)}, u32[]{:S(2)}) collective-permute-start(bf16[2,144,1152]{2,1,0:T(8,128)(2,1)} %get-tuple-element.381), channel_id=1, source_target_pairs={{0,16},{16,0},{1,17},{17,1},{2,18},{18,2},{3,19},{19,3},{4,20},{20... | collective-permute-start | bytes 1990664 | tf_op jit(solution)/shard_map/ppermute | solution.py:609
  413.8 18.2 %collective-permute-start.58 = (bf16[2,144,1152]{2,1,0:T(8,128)(2,1)}, bf16[2,144,1152]{2,1,0:T(8,128)(2,1)}, u32[]{:S(2)}, u32[]{:S(2)}) collective-permute-start(bf16[2,144,1152]{2,1,0:T(8,128)(2,1)} %add_convert_fusion.7), channel_id=1, source_target_pairs={{0,8},{8,0},{1,9},{9,1},{2,10},{10,2},{3,11},{11,3},{4,12},{12,4},... | collective-permute-start | bytes 1990664 | tf_op jit(solution)/shard_map/ppermute | solution.py:609
  415.6 15.7 %collective-permute-start.59 = (f32[16,1152]{1,0:T(8,128)}, f32[16,1152]{1,0:T(8,128)}, u32[]{:S(2)}, u32[]{:S(2)}) collective-permute-start(f32[16,1152]{1,0:T(8,128)} %pad_maximum_fusion.7), channel_id=1, source_target_pairs={{0,1},{1,0},{2,3},{3,2},{4,5},{5,4},{6,7},{7,6},{8,9},{9,8},{10,11... | collective-permute-start | bytes 221192 | tf_op jit(solution)/shard_map/ppermute | solution.py:950
  419.4 24.4 %collective-permute-start.62 = (bf16[2,144,1152]{2,1,0:T(8,128)(2,1)}, bf16[2,144,1152]{2,1,0:T(8,128)(2,1)}, u32[]{:S(2)}, u32[]{:S(2)}) collective-permute-start(bf16[2,144,1152]{2,1,0:T(8,128)(2,1)} %add_convert_fusion.5), channel_id=1, source_target_pairs={{0,8},{8,0},{1,9},{9,1},{2,10},{10,2},{3,11},{11,3},{4,12},{12,4},... | collective-permute-start | bytes 1990664 | tf_op jit(solution)/shard_map/ppermute | solution.py:609
  432.0 15.1 %collective-permute-start.60 = (bf16[288,1152]{1,0:T(8,128)(2,1)}, bf16[288,1152]{1,0:T(8,128)(2,1)S(1)}, u32[]{:S(2)}, u32[]{:S(2)}) collective-permute-start(bf16[288,1152]{1,0:T(8,128)(2,1)} %get-tuple-element.387), channel_id=1, source_target_pairs={{0,16},{16,0},{1,17},{17,1},{2,18},{18,2},{3,19},{19,3},{4,20},{20... | collective-permute-start | bytes 1990664 | tf_op jit(solution)/shard_map/ppermute | solution.py:609
  447.1 28.4 %collective-permute-start.64 = (bf16[288,1152]{1,0:T(8,128)(2,1)S(1)}, bf16[288,1152]{1,0:T(8,128)(2,1)S(1)}, u32[]{:S(2)}, u32[]{:S(2)}) collective-permute-start(bf16[288,1152]{1,0:T(8,128)(2,1)S(1)} %copy-done.70), channel_id=1, source_target_pairs={{0,16},{16,0},{1,17},{17,1},{2,18},{18,2},{3,19},{19,3},{4,20},{20... | collective-permute-start | bytes 1990664 | tf_op jit(solution)/shard_map/ppermute | solution.py:609
  451.7 23.8 %collective-permute-start.67 = (bf16[144,1152]{1,0:T(8,128)(2,1)S(1)}, bf16[144,1152]{1,0:T(8,128)(2,1)S(1)}, u32[]{:S(2)}, u32[]{:S(2)}) collective-permute-start(bf16[144,1152]{1,0:T(8,128)(2,1)S(1)} %get-tuple-element.469), channel_id=1, source_target_pairs={{0,2},{1,3},{2,0},{3,1},{4,6},{5,7},{6,4},{7,5},{8,10},{9,11},{10,... | collective-permute-start | bytes 995336 | tf_op jit(solution)/shard_map/ppermute | solution.py:609
  452.4 23.1 %collective-permute-start.68 = (bf16[144,1152]{1,0:T(8,128)(2,1)S(1)}, bf16[144,1152]{1,0:T(8,128)(2,1)S(1)}, u32[]{:S(2)}, u32[]{:S(2)}) collective-permute-start(bf16[144,1152]{1,0:T(8,128)(2,1)S(1)} %get-tuple-element.468), channel_id=1, source_target_pairs={{0,1},{1,2},{2,3},{3,0},{4,5},{5,6},{6,7},{7,4},{8,9},{9,10},{10,1... | collective-permute-start | bytes 995336 | tf_op jit(solution)/shard_map/ppermute | solution.py:609
  477.2 17.5 %collective-permute-start.71 = (bf16[144,1152]{1,0:T(8,128)(2,1)S(1)}, bf16[144,1152]{1,0:T(8,128)(2,1)}, u32[]{:S(2)}, u32[]{:S(2)}) collective-permute-start(bf16[144,1152]{1,0:T(8,128)(2,1)S(1)} %slice.228), channel_id=1, source_target_pairs={{0,3},{1,0},{2,1},{3,2},{4,7},{5,4},{6,5},{7,6},{8,11},{9,8},{10,9... | collective-permute-start | bytes 995336 | tf_op jit(solution)/shard_map/ppermute | solution.py:609
  480.2 19.8 %collective-permute-start.72 = (bf16[144,1152]{1,0:T(8,128)(2,1)S(1)}, bf16[144,1152]{1,0:T(8,128)(2,1)S(1)}, u32[]{:S(2)}, u32[]{:S(2)}) collective-permute-start(bf16[144,1152]{1,0:T(8,128)(2,1)S(1)} %fusion.4), channel_id=1, source_target_pairs={{0,3},{1,0},{2,1},{3,2},{4,7},{5,4},{6,5},{7,6},{8,11},{9,8},{10,9... | collective-permute-start | bytes 995336 | tf_op jit(solution)/shard_map/ppermute | solution.py:609
  (81 other events, 942.1 us)
Sparse Core Ops, SparseCore 0:
  86.7 98.0 all-gather.1

commit v5 on v4

--- a/solution.py
+++ b/solution.py
@@ -421,7 +421,7 @@
 
 def norm(table, base, extra, gain, bias, seq, mixed=(), wo=()):
     d = base.shape[1]
-    args = [base] + ([extra[None]] if mixed else []) + [gain[None], bias[None], *mixed, *wo]
+    args = [base] + ([extra] if mixed else []) + [gain, bias, *mixed, *wo]
     outs = [jax.ShapeDtypeStruct((PAD, d), BF16), jax.ShapeDtypeStruct((d, PAD), BF16)]
     if mixed:
         outs = [jax.ShapeDtypeStruct((PAD, d), F32)] + outs
@@ -497,7 +497,7 @@
         compiler_params=params(),
         cost_estimate=cost(2 * PAD * d * units, 2 * d * units + 2 * PAD * units),
         name="ff_back",
-    )(table, gu, w, v, gain[None], base)
+    )(table, gu, w, v, gain, base)
 
 
 def attn_back_kernel(seq, groups, *refs):
@@ -516,7 +516,7 @@
 def attn_back(grads, ws, v, gain, base, seq):
     d = v.shape[1]
     row = jax.ShapeDtypeStruct((1, d), F32)
-    args = [*grads, *ws, v, gain[None], base]
+    args = [*grads, *ws, v, gain, base]
     return pl.pallas_call(
         functools.partial(attn_back_kernel, seq, len(grads)),
         in_specs=specs(len(args))[1:],
@@ -543,9 +543,9 @@
                 outs[number * sets + s][0] = low[number * rows : (number + 1) * rows]
 
 
-def ff_grad(lhs, rhs, slots, parts, sets):
+def ff_grad(lhs, blocks, rhs, slots, parts, sets):
     total = len(lhs)
-    height = lhs[0].shape[0]
+    height = lhs[0].shape[0] // total
     rows = height // parts
     cols = rhs[0].shape[1] // slots
     size = slots // sets
@@ -557,7 +557,7 @@
         functools.partial(ff_grad_kernel, total, parts, sets, size, rows),
         grid=(slots,),
         in_specs=[
-            *[whole((height, PAD)) for _ in lhs],
+            *[pl.BlockSpec((height, PAD), lambda n, b=b: (b, 0)) for b in blocks],
             *[pl.BlockSpec((PAD, cols), lambda n: (0, n)) for _ in rhs],
         ],
         out_specs=[
@@ -750,13 +750,15 @@
             for k in zones
         ]
     )[None]
-    normed_a, na_t = norm(turn_attn, base, None, ln1_gain, ln1_bias, seq)
+    gain_one, gain_two, shift_two, out_row = (
+        v[None] for v in (ln1_gain, ln2_gain, ln2_bias, out_bias)
+    )
+    normed_a, na_t = norm(turn_attn, base, None, gain_one, ln1_bias[None], seq)
     gl_t, down_bias_sum = turn(turn_ff, grad_low)
 
     together = lax.optimization_barrier
     spots = ("z", "y", "x", "c")
     if linked:
-        half = d // 2
         down_z, pairs, down_y, pair_far, y_far_down = [down_own], [], [], [], []
 
         px, py, dx0, dz1 = together(
@@ -792,6 +794,9 @@
                 moves.append(swap(cat(s[k - 2][2 * h :], s[k - 1][2 * h :]), "x"))
                 if k == 2:
                     moves.append(swap(na_t))
+                    moves.append(
+                        (bias_rows, shift, ff_table, zone_table, turn_ff, gain_two, shift_two)
+                    )
             else:
                 moves += [swap(y_parts[-1]), swap(x_parts[-1])]
                 if k == 3:
@@ -804,25 +809,27 @@
                 x_parts.append(moves[3])
                 if k == 2:
                     na_far = moves[4]
+                    bias_rows, shift, ff_table, zone_table, turn_ff, gain_two, shift_two = moves[5]
             else:
                 y_far.append(moves[2])
                 x_far.append(moves[3])
                 if k == 3:
                     down_y.append(moves[4])
         up_whole = lax.all_gather(after(up_own, s[-1]), spots, axis=0, tiled=True)
-        y1, x1, sc3, dz2, dz3 = together(
+        y1, x1, sc3, dz2, p0 = together(
             (
                 swap(cat(s[-2][: 2 * h], s[-1][: 2 * h]), "y"),
                 swap(cat(s[-2][2 * h :], s[-1][2 * h :]), "x"),
                 swap(s[-1]),
                 hop(after(down_z[1], s[-1]), "z", nz, 1),
-                hop(after(down_own, s[-1]), "z", nz, -1),
+                swap(after(pairs[0], s[-1])),
             )
         )
         y_parts.append(y1)
         x_parts.append(x1)
         s_far.append(sc3)
-        down_z += [dz2, dz3]
+        down_z.append(dz2)
+        pair_far.append(p0)
         near = [*s, *y_parts, *x_parts]
         y_far.append(swap(y1))
         x_far.append(swap(x1))
@@ -837,22 +844,25 @@
             kept.append(out)
             normed_a = after(normed_a, out)
             if number == 0:
-                dx2, p0, y0 = swap(down_z[2], "x"), swap(pairs[0]), swap(after(down_y[0], s[-1]))
-                normed_a, dx2, far, p0, y0 = together((normed_a, dx2, far, p0, y0))
-                pair_far.append(p0)
-                y_far_down.append(y0)
+                dx2, dz3 = swap(down_z[2], "x"), hop(after(down_own, dz2), "z", nz, -1)
+                y0 = swap(after(down_y[0], dz2))
+                normed_a, dx2, dz3, far, y0 = together((normed_a, dx2, dz3, far, y0))
+                down_z.append(dz3)
                 pairs.append(cat(down_z[2], dx2))
             if number == 1:
                 dx3, dy2 = swap(down_z[3], "x"), swap(pairs[2], "y")
-                p1, y1 = swap(pairs[1]), swap(down_y[1])
+                p1, y1 = swap(after(pairs[1], dx2)), swap(after(down_y[1], dx2))
+                normed_a, dx3 = together((normed_a, dx3))
             if number == 2:
                 normed_a, dx3, dy2, p1, y1 = together((normed_a, dx3, dy2, p1, y1))
                 pair_far.append(p1)
-                y_far_down.append(y1)
+                y_far_down += [y0, y1]
                 pairs.append(cat(down_z[3], dx3))
                 down_y.append(dy2)
                 dy3 = swap(pairs[3], "y")
-                p2, y2, gl_far = swap(pairs[2]), swap(dy2), swap(after(gl_t[half:], out))
+                p2, y2, gl_far = swap(after(pairs[2], out)), swap(dy2), swap(after(gl_t, out))
+        mixed_last, dy3 = together((out[1], dy3))
+        kept[3] = [out[0], mixed_last, *out[2:]]
     else:
         kept = []
         for number, g in enumerate(groups):
@@ -870,18 +880,18 @@
     hidden, normed_b, nb_t = norm(
         turn_ff,
         base,
-        out_bias,
-        ln2_gain,
-        ln2_bias,
+        out_row,
+        gain_two,
+        shift_two,
         seq,
         [out[1] for out in kept],
         [out[4] for out in kept],
     )
     if linked:
-        normed_b, dy3, p2, y2, gl_far = together((normed_b, dy3, p2, y2, gl_far))
+        normed_b, p2, y2, gl_far = together((normed_b, p2, y2, gl_far))
         down_y.append(dy3)
         p3, y3 = swap(pairs[3]), swap(dy3)
-        nb_far = swap(nb_t[half:])
+        nb_far = swap(nb_t)
     active, slope, up_full = ff_up(zone_table, normed_b, shift, [up_whole], up_plan, nz)
     if linked:
         active, p3, y3, nb_far = together((active, p3, y3, nb_far))
@@ -903,7 +913,7 @@
         grad_upper, active_far = together((grad_upper, active_far))
         upper_far = swap(grad_upper)
         down_parts = [
-            p[0] for p in ff_grad([gl_t[:half], gl_far], [active, active_far], nz, 4, 1)
+            p[0] for p in ff_grad([gl_t, gl_far], [0, 1], [active, active_far], nz, 4, 1)
         ]
         down_one, down_two = swap(down_parts[3], "x"), swap(down_parts[1], "x")
         grad_upper_first = after(grad_upper, down_parts)
@@ -915,12 +925,12 @@
             part = lax.psum_scatter(part, spot, scatter_dimension=0, tiled=True)
             return lax.optimization_barrier(part).astype(F32)
 
-        down_sum = spread(ff_grad([gl_t], [active], nz, 1, 1)[0])
-        up_sum = spread(ff_grad([nb_t], [grad_upper], nz, 1, 1)[0])
+        down_sum = spread(ff_grad([gl_t], [0], [active], nz, 1, 1)[0])
+        up_sum = spread(ff_grad([nb_t], [0], [grad_upper], nz, 1, 1)[0])
         grad_upper_first = grad_upper
 
     grad_hidden, ln2_gain_grad, ln2_bias_grad, grad_attn, ga_t, out_bias_sum = ff_back(
-        turn_attn, grad_upper_first, up_full, hidden, ln2_gain, grad_low
+        turn_attn, grad_upper_first, up_full, hidden, gain_two, grad_low
     )
 
     def in_place(rows, places):
@@ -932,16 +942,15 @@
     def fit(x):
         return jnp.pad(x, ((0, 0), (0, wide - x.shape[1])))
 
-    def early_rows():
+    def early_rows(ready):
+        upper = after(upper_sums, ready)
         vectors = [
             out_bias_sum,
             ln2_gain_grad,
             ln2_bias_grad,
             down_bias_sum,
-            in_place(sums, groups),
-            in_place(
-                [upper_sums[:, slot * cols : (slot + 1) * cols] for slot in range(nz)], zones
-            ),
+            in_place([after(v, ready) for v in sums], [after(k, ready) for k in groups]),
+            in_place([upper[:, slot * cols : (slot + 1) * cols] for slot in range(nz)], zones),
         ]
         rows = cat(*[fit(v) for v in vectors])
         return jnp.pad(rows, ((0, -(rows.shape[0] + 2) % 8), (0, 0)))
@@ -969,7 +978,7 @@
         more = attn_grad([na_t, na_far], [ga_t, ga_far], [grads[1], far_grads], 4)
         more_in = [None, None, swap(more[2], "x"), swap(more[3], "x")]
         upper_first, upper_far = together((grad_upper, upper_far, more))[:2]
-        up_parts = ff_grad([nb_t[:half], nb_far], [upper_first, upper_far], nz, 4, 2)
+        up_parts = ff_grad([nb_t, nb_far], [0, 1], [upper_first, upper_far], nz, 4, 2)
         up_parts, down_two, down_other, ga_first = together(
             (up_parts, down_two, down_other, ga_first)
         )
@@ -989,7 +998,7 @@
         ga_first = after(ga_first, down_line, up_one[1])
         down_line = hop(down_line, "z", nz, -1)
         back(0)
-        early = early_rows()
+        early = early_rows(None)
         grads[0], far_grads, up_near[1], down_line, more_in[1], early = together(
             (grads[0], far_grads, up_near[1], down_line, more_in[1], early)
         )
@@ -1002,7 +1011,7 @@
             [grads_first] + [grads[k] for k in range(1, 4)],
             [out[3] for out in kept],
             base,
-            ln1_gain,
+            gain_one,
             grad_hidden,
             seq,
         )
@@ -1061,14 +1070,14 @@
             [grads[k] for k in range(len(groups))],
             [out[3] for out in kept],
             base,
-            ln1_gain,
+            gain_one,
             grad_hidden,
             seq,
         )
 
 
     if not linked:
-        table = total_sum(cat(fit(ln1_gain_grad), fit(ln1_bias_grad), early_rows()), sizes)
+        table = total_sum(cat(fit(ln1_gain_grad), fit(ln1_bias_grad), early_rows(None)), sizes)
     singles = [table[k, :d] for k in range(6)]
     qv = table[6 : 6 + len(groups)]
     qv_grad = jnp.stack([qv[:, :width].reshape(-1), qv[:, 2 * width : 3 * width].reshape(-1)])

time: 514 us -> 522 us (1.016)
    ppermute x68, waiting for transfers between devices: 95.6 us -> 104 us  [hop(): return lax.ppermute(x, axis, [(i, (i + step) % n) for i in range(n)])]
    slice x3 -> x1, local copies, waits for them, and re-layouts: 6.03 us -> 0.79 us  [early_rows(): upper[:, slot * cols:(slot + 1) * cols]]
    unnamed x149 -> x153, local copies, waits for them, and re-layouts: 12.7 us -> 13.6 us
  transfers between devices with their start and end apart: 74 -> 74, of which waited for: 22 -> 24; matrix products, arithmetic and copies ran while one was open for 13% -> 13% of each run, Pallas kernels for 49% -> 48%
where the time goes in v5:
time: 522 us; the launch traced here: 514 us
  Pallas kernels  247 us (47%)
  waiting for transfers between devices  104 us (20%)
  starting transfers between devices  70.8 us (14%)
  other arithmetic  40.7 us (8%)
  local copies, waits for them, and re-layouts  35.7 us (7%)
  between operations  16 us (3%)
    ppermute x68, waiting for transfers between devices, hop(): return lax.ppermute(x, axis, [(i, (i + step) % n) for i in range(n)])  104 us
    ppermute x68, starting transfers between devices, hop(): return lax.ppermute(x, axis, [(i, (i + step) % n) for i in range(n)])  66.2 us
    pallas_call x4, Pallas kernels, attn_bwd(): pl.pallas_call(functools.partial(attn_bwd_kernel, seq), in_specs=specs(5)...  45.2 us
    pallas_call x4, Pallas kernels, attn_fwd(): pl.pallas_call(functools.partial(attn_fwd_kernel, plan, len(pieces), seq)...  43.9 us
    pallas_call x2, Pallas kernels, ff_grad(): pl.pallas_call(functools.partial(ff_grad_kernel, total, parts, sets, size...  28.9 us
    pallas_call x1, Pallas kernels, ff_down(): pl.pallas_call(functools.partial(ff_down_kernel, plan, len(pieces), slots...  28.2 us
    pallas_call x2, Pallas kernels, attn_grad(): pl.pallas_call(functools.partial(attn_grad_kernel, total, parts, len(more...  22.3 us
    pallas_call x1, Pallas kernels, ff_back(): pl.pallas_call(functools.partial(ff_back_kernel, table.shape[0]), grid=(u...  21.2 us
  transfers between devices with their start and end apart: 74, of which 24 were waited for; matrix products, arithmetic and copies ran while one was open for 13% of the time, Pallas kernels for 48%

profile of v5, /device:TPU:0, one launch (start us, length us, event | category | flops | bytes accessed | tf_op | source)
XLA Modules:
  0.0 514.5 jit_solution(9592950370739362180)
XLA Ops:
  9.2 2.9 collective-permute-start.2
  16.6 3.6 collective-permute-done.1
  20.2 3.8 collective-permute-done
  24.2 1.9 collective-permute-start.4
  30.9 3.0 multiply_convert_fusion.x.refs_1_.refs_5_
  34.5 3.3 turn.1
  37.8 2.9 pad.37.refs_1_.refs_8_
  42.5 4.6 norm.2
  49.8 1.9 pad_maximum_fusion
  52.2 1.8 pad_maximum_fusion.4
  60.4 1.7 constant_dynamic-update-slice_fusion.1
  62.1 7.7 %collective-permute-done.11.refs_9_ = bf16[256,1152]{1,0:T(8,128)(2,1)} collective-permute-done((bf16[256,1152]{1,0:T(8,128)(2,1)}, bf16[256,1152]{1,0:T(8,128)(2,1)}, u32[]{:S(2)}, u32[]{:S(2)}) %collective-permute-start.11) | collective-permute-done | bytes 589856 | tf_op jit(solution)/shard_map/ppermute | solution.py:609
  70.9 1.9 constant_dynamic-update-slice_fusion.refs_5_
  77.1 13.2 %collective-permute-done.17.refs_9_ = bf16[288,1152]{1,0:T(8,128)(2,1)} collective-permute-done((bf16[288,1152]{1,0:T(8,128)(2,1)}, bf16[288,1152]{1,0:T(8,128)(2,1)}, u32[]{:S(2)}, u32[]{:S(2)}) %collective-permute-start.17) | collective-permute-done | bytes 663584 | tf_op jit(solution)/shard_map/ppermute | solution.py:609
  90.3 2.5 collective-permute-done.13.refs_6_
  95.9 16.7 %collective-permute-done.21 = bf16[144,1152]{1,0:T(8,128)(2,1)} collective-permute-done((bf16[144,1152]{1,0:T(8,128)(2,1)S(1)}, bf16[144,1152]{1,0:T(8,128)(2,1)}, u32[]{:S(2)}, u32[]{:S(2)}) %collective-permute-start.21) | collective-permute-done | bytes 331808 | tf_op jit(solution)/shard_map/ppermute | solution.py:609
  112.8 2.6 collective-permute-done.18.refs_8_
  117.2 10.9 %attn_fwd.4 = (bf16[768,864]{1,0:T(8,128)(2,1)}, bf16[768,288]{1,0:T(8,128)(2,1)}, f32[8,768]{1,0:T(8,128)}, bf16[1152,1152]{1,0:T(8,128)(2,1)}, bf16[1152,288]{1,0:T(8,128)(2,1)}) custom-call(s32[8]{0:T(128)} %stack.125.refs_0_, bf16[768,1152]{1,0:T(8,128)(2,1)} %get-tuple-element.300.refs_1_, f32[1,864]{1,0:T(1,128)} %broadcast_in_dim.163.refs_2_, ...), custom_call_target="tpu_custom_call" | custom-call | flops 222717536 | bytes 265420 | tf_op jit(solution)/shard_map/attn_fwd/pallas_call | solution.py:129
  129.1 4.6 collective-permute-done.24
  136.7 10.7 %attn_fwd.5 = (bf16[768,864]{1,0:T(8,128)(2,1)}, bf16[768,288]{1,0:T(8,128)(2,1)}, f32[8,768]{1,0:T(8,128)}, bf16[1152,1152]{1,0:T(8,128)(2,1)}, bf16[1152,288]{1,0:T(8,128)(2,1)}) custom-call(s32[8]{0:T(128)} %stack.125.refs_0_, bf16[768,1152]{1,0:T(8,128)(2,1)} %get-tuple-element.300.refs_1_, f32[1,864]{1,0:T(1,128)} %broadcast_in_dim.164.refs_2_, ...), custom_call_target="tpu_custom_call" | custom-call | flops 222717536 | bytes 265420 | tf_op jit(solution)/shard_map/attn_fwd/pallas_call | solution.py:129
  147.5 11.6 %attn_fwd.6 = (bf16[768,864]{1,0:T(8,128)(2,1)}, bf16[768,288]{1,0:T(8,128)(2,1)}, f32[8,768]{1,0:T(8,128)}, bf16[1152,1152]{1,0:T(8,128)(2,1)}, bf16[1152,288]{1,0:T(8,128)(2,1)}) custom-call(s32[8]{0:T(128)} %stack.125.refs_0_, bf16[768,1152]{1,0:T(8,128)(2,1)} %get-tuple-element.300.refs_1_, f32[1,864]{1,0:T(1,128)} %broadcast_in_dim.165.refs_2_, ...), custom_call_target="tpu_custom_call" | custom-call | flops 222717536 | bytes 265420 | tf_op jit(solution)/shard_map/attn_fwd/pallas_call | solution.py:129
  160.5 1.9 collective-permute-start.32
  163.0 10.7 %attn_fwd.7 = (bf16[768,864]{1,0:T(8,128)(2,1)}, bf16[768,288]{1,0:T(8,128)(2,1)}, f32[8,768]{1,0:T(8,128)}, bf16[1152,1152]{1,0:T(8,128)(2,1)}, bf16[1152,288]{1,0:T(8,128)(2,1)}) custom-call(s32[8]{0:T(128)} %stack.125.refs_0_, bf16[768,1152]{1,0:T(8,128)(2,1)} %get-tuple-element.300.refs_1_, f32[1,864]{1,0:T(1,128)} %broadcast_in_dim.166.refs_2_, ...), custom_call_target="tpu_custom_call" | custom-call | flops 222717536 | bytes 265420 | tf_op jit(solution)/shard_map/attn_fwd/pallas_call | solution.py:129
  173.6 12.7 %collective-permute-done.32.refs_11_ = bf16[288,1152]{1,0:T(8,128)(2,1)} collective-permute-done((bf16[288,1152]{1,0:T(8,128)(2,1)S(1)}, bf16[288,1152]{1,0:T(8,128)(2,1)}, u32[]{:S(2)}, u32[]{:S(2)}) %collective-permute-start.32) | collective-permute-done | bytes 663584 | tf_op jit(solution)/shard_map/ppermute | solution.py:609
  186.3 10.4 %norm.3 = (f32[768,1152]{1,0:T(8,128)}, bf16[768,1152]{1,0:T(8,128)(2,1)}, bf16[1152,768]{1,0:T(8,128)(2,1)}) custom-call(s32[8]{0:T(128)} %stack.116.table.refs_0_, bf16[768,1152]{1,0:T(8,128)(2,1)} %pad.37.refs_1_.refs_8_, f32[1,1152]{1,0:T(1,128)} %broadcast_in_dim.170.refs_2_, f32[1,1152]{1,0:T(1,128)} %broadcast_in_dim.168.refs_3_.refs_4_, ...), custom_call_target="tpu_custom_call" | custom-call | flops 707788 | bytes 442368 | tf_op jit(solution)/shard_map/norm/pallas_call | solution.py:428
  197.8 4.2 collective-permute-done.33.refs_14_
  203.5 20.0 %ff_up.1 = (bf16[768,4608]{1,0:T(8,128)(2,1)}, bf16[768,4608]{1,0:T(8,128)(2,1)}, bf16[1152,4608]{1,0:T(8,128)(2,1)}) custom-call(s32[4]{0:T(128)} %pad_add_fusion.refs_0_, bf16[768,1152]{1,0:T(8,128)(2,1)} %get-tuple-element.314.refs_1_, f32[1,4608]{1,0:T(1,128)} %broadcast_in_dim.167.refs_2_, bf16[4608,1152]{1,0:T(8,128)(2,1)} %all-gather.2.cloned.1.call-done.refs_3_), custom_call_target="tpu_custom_call" | custom-call | flops 407686336 | bytes 1769472 | tf_op jit(solution)/shard_map/ff_up/pallas_call | solution.py:268
  225.2 28.2 %ff_down.1 = (f32[768,1152]{1,0:T(8,128)}, bf16[768,4608]{1,0:T(8,128)(2,1)}, f32[1,4608]{1,0:T(1,128)}) custom-call(s32[8]{0:T(128)} %stack.134.refs_0_, bf16[768,1152]{1,0:T(8,128)(2,1)} %multiply_convert_fusion.x.refs_1_.refs_5_, bf16[768,4608]{1,0:T(8,128)(2,1)} %get-tuple-element.320.refs_2_, bf16[768,4608]{1,0:T(8,128)(2,1)} %get-tuple-element.321.refs_3_, ...), custom_call_target="tpu_custom_call" | custom-call | flops 815372672 | bytes 1592524 | tf_op jit(solution)/shard_map/ff_down/pallas_call | solution.py:337
  255.1 14.1 %ff_grad.2 = (bf16[4,144,1152]{2,1,0:T(8,128)(2,1)}, bf16[4,144,1152]{2,1,0:T(8,128)(2,1)}, bf16[4,144,1152]{2,1,0:T(8,128)(2,1)}, bf16[4,144,1152]{2,1,0:T(8,128)(2,1)}) custom-call(bf16[1152,768]{1,0:T(8,128)(2,1)} %get-tuple-element.313.refs_0_, bf16[1152,768]{1,0:T(8,128)(2,1)} %collective-permute-done.35.refs_1_, ...), custom_call_target="tpu_custom_call" | custom-call | flops 521838526464 | bytes 1245708288 | tf_op jit(solution)/shard_map/ff_grad/pallas_call | solution.py:556
  271.2 21.2 %ff_back.1 = (f32[768,1152]{1,0:T(8,128)}, f32[1,1152]{1,0:T(1,128)}, f32[1,1152]{1,0:T(1,128)}, bf16[768,1152]{1,0:T(8,128)(2,1)}, bf16[1152,768]{1,0:T(8,128)(2,1)}, /*index=5*/f32[1,1152]{1,0:T(1,128)}) custom-call(s32[8]{0:T(128)} %stack.125.refs_0_, bf16[768,4608]{1,0:T(8,128)(2,1)} %get-tuple-element.360.refs_1_.refs_2_, ...), custom_call_target="tpu_custom_call" | custom-call | flops 521838526464 | bytes 1132462080 | tf_op jit(solution)/shard_map/ff_back/pallas_call | solution.py:485
  292.5 11.1 %attn_bwd.4 = (bf16[768,1152]{1,0:T(8,128)(2,1)}, f32[1,864]{1,0:T(1,128)}) custom-call(bf16[768,864]{1,0:T(8,128)(2,1)} %get-tuple-element.345.proj, bf16[768,288]{1,0:T(8,128)(2,1)} %get-tuple-element.304.refs_8_.mixed, f32[8,768]{1,0:T(8,128)} %get-tuple-element.346.lse, bf16[768,1152]{1,0:T(8,128)(2,1)} %get-tuple-element.380.ga, ...), custom_call_target="tpu_custom_call" | custom-call | flops 419161964544 | bytes 495452160 | tf_op jit(solution)/shard_map/attn_bwd/pallas_call | solution.py:192
  304.1 11.6 %attn_bwd.5 = (bf16[768,1152]{1,0:T(8,128)(2,1)}, f32[1,864]{1,0:T(1,128)}) custom-call(bf16[768,864]{1,0:T(8,128)(2,1)} %get-tuple-element.273.proj, bf16[768,288]{1,0:T(8,128)(2,1)} %get-tuple-element.272.refs_6_.mixed, f32[8,768]{1,0:T(8,128)} %get-tuple-element.274.lse, bf16[768,1152]{1,0:T(8,128)(2,1)} %get-tuple-element.380.ga, ...), custom_call_target="tpu_custom_call" | custom-call | flops 419161964544 | bytes 495452160 | tf_op jit(solution)/shard_map/attn_bwd/pallas_call | solution.py:192
  315.7 2.7 add_convert_fusion.1
  320.4 10.7 %attn_grad.2 = (bf16[288,1152]{1,0:T(8,128)(2,1)}, bf16[288,1152]{1,0:T(8,128)(2,1)}, bf16[288,1152]{1,0:T(8,128)(2,1)}, bf16[288,1152]{1,0:T(8,128)(2,1)}) custom-call(bf16[1152,768]{1,0:T(8,128)(2,1)} %get-tuple-element.405.refs_0_, bf16[1152,768]{1,0:T(8,128)(2,1)} %collective-permute-done.12.refs_1_, bf16[1152,768]{1,0:T(8,128)(2,1)} %get-tuple-element.342.refs_2_, ...), custom_call_target="tpu_custom_call" | custom-call | flops 260919263232 | bytes 566231040 | tf_op jit(solution)/shard_map/attn_grad/pallas_call | solution.py:597
  331.2 1.9 collective-permute-start.48
  333.1 14.8 %ff_grad.3 = (bf16[2,144,1152]{2,1,0:T(8,128)(2,1)}, bf16[2,144,1152]{2,1,0:T(8,128)(2,1)}, bf16[2,144,1152]{2,1,0:T(8,128)(2,1)}, bf16[2,144,1152]{2,1,0:T(8,12...) custom-call(bf16[1152,768]{1,0:T(8,128)(2,1)} %get-tuple-element.319, ...), custom_call_target="tpu_custom_call" | custom-call | flops 521838526464 | bytes 1245708288 | tf_op jit(solution)/shard_map/ff_grad/pallas_call | solution.py:556
  347.9 2.0 collective-permute-done.45
  349.9 2.2 add_convert_fusion
  355.1 11.3 %attn_bwd.6 = (bf16[768,1152]{1,0:T(8,128)(2,1)}, f32[1,864]{1,0:T(1,128)}) custom-call(bf16[768,864]{1,0:T(8,128)(2,1)} %get-tuple-element.290.proj, bf16[768,288]{1,0:T(8,128)(2,1)} %get-tuple-element.289.refs_7_.mixed, f32[8,768]{1,0:T(8,128)} %get-tuple-element.291.lse, bf16[768,1152]{1,0:T(8,128)(2,1)} %get-tuple-element.380.ga, ...), custom_call_target="tpu_custom_call" | custom-call | flops 419161964544 | bytes 495452160 | tf_op jit(solution)/shard_map/attn_bwd/pallas_call | solution.py:192
  367.7 2.9 collective-permute-done.49
  370.6 1.9 fusion.7
  373.2 2.1 add_convert_fusion.7
  377.4 11.2 %attn_bwd.7 = (bf16[768,1152]{1,0:T(8,128)(2,1)}, f32[1,864]{1,0:T(1,128)}) custom-call(bf16[768,864]{1,0:T(8,128)(2,1)} %get-tuple-element.255.proj, bf16[768,288]{1,0:T(8,128)(2,1)} %get-tuple-element.254.refs_5_.mixed, f32[8,768]{1,0:T(8,128)} %get-tuple-element.256.lse, bf16[768,1152]{1,0:T(8,128)(2,1)} %get-tuple-element.380.ga, ...), custom_call_target="tpu_custom_call" | custom-call | flops 419161964544 | bytes 495452160 | tf_op jit(solution)/shard_map/attn_bwd/pallas_call | solution.py:192
  390.2 4.2 collective-permute-done.51
  394.4 1.9 fusion.6
  397.8 1.9 collective-permute-start.54
  399.6 19.1 %attn_back.1 = (f32[729,1152]{1,0:T(8,128)}, f32[1,1152]{1,0:T(1,128)}, f32[1,1152]{1,0:T(1,128)}) custom-call(bf16[768,1152]{1,0:T(8,128)(2,1)} %get-tuple-element.401.refs_0_.refs_4_, bf16[768,1152]{1,0:T(8,128)(2,1)} %get-tuple-element.352.refs_4_.refs_1_, bf16[768,1152]{1,0:T(8,128)(2,1)} %get-tuple-element.382.refs_2_, ...), custom_call_target="tpu_custom_call" | custom-call | flops 391378894848 | bytes 1019215872 | tf_op jit(solution)/shard_map/attn_back/pallas_call | solution.py:520
  423.2 2.1 add_convert_fusion.5
  425.9 11.6 %attn_grad.3 = (bf16[288,1152]{1,0:T(8,128)(2,1)}, bf16[288,1152]{1,0:T(8,128)(2,1)}, bf16[288,1152]{1,0:T(8,128)(2,1)}, bf16[288,1152]{1,0:T(8,128)(2,1)}) custom-call(bf16[1152,768]{1,0:T(8,128)(2,1)} %get-tuple-element.405.refs_0_, bf16[1152,768]{1,0:T(8,128)(2,1)} %collective-permute-done.12.refs_1_, bf16[1152,768]{1,0:T(8,128)(2,1)} %get-tuple-element.342.refs_2_, ...), custom_call_target="tpu_custom_call" | custom-call | flops 260919263232 | bytes 566231040 | tf_op jit(solution)/shard_map/attn_grad/pallas_call | solution.py:597
  439.4 2.8 collective-permute-start.63
  443.6 1.7 add_convert_fusion.6
  446.8 1.9 fusion.3
  448.7 1.7 collective-permute-done.62
  450.4 2.0 collective-permute-done.61
  452.5 3.2 collective-permute-done.60
  456.4 1.7 collective-permute-start.68
  458.1 2.2 collective-permute-start.65
  462.4 1.6 fusion.2
  464.1 1.7 add_convert_fusion.2
  465.9 5.2 %copy.33 = f32[1,729,1152]{2,0,1:T(1,128)} copy(f32[1,729,1152]{2,1,0:T(8,128)S(1)} %bitcast.72) | data formatting | bytes 6718464
  471.0 5.3 %collective-permute-done.67 = bf16[144,1152]{1,0:T(8,128)(2,1)S(1)} collective-permute-done((bf16[144,1152]{1,0:T(8,128)(2,1)S(1)}, bf16[144,1152]{1,0:T(8,128)(2,1)S(1)}, u32[]{:S(2)}, u32[]{:S(2)}) %collective-permute-start.67) | collective-permute-done | bytes 331808 | tf_op jit(solution)/shard_map/ppermute | solution.py:609
  477.3 3.9 collective-permute-start.72
  481.8 12.2 %collective-permute-start.71 = (bf16[144,1152]{1,0:T(8,128)(2,1)S(1)}, bf16[144,1152]{1,0:T(8,128)(2,1)S(1)}, u32[]{:S(2)}, u32[]{:S(2)}) collective-permute-start(bf16[144,1152]{1,0:T(8,128)(2,1)S(1)} %slice.212), channel_id=1, source_target_pairs={{0,3},{1,0},{2,1},{3,2},{4,7},{5,4},{6,5},{7,6},{8,11},{9,8},{10,9... | collective-permute-start | bytes 995336 | tf_op jit(solution)/shard_map/ppermute | solution.py:609
  496.3 6.9 %collective-permute-done.71 = bf16[144,1152]{1,0:T(8,128)(2,1)S(1)} collective-permute-done((bf16[144,1152]{1,0:T(8,128)(2,1)S(1)}, bf16[144,1152]{1,0:T(8,128)(2,1)S(1)}, u32[]{:S(2)}, u32[]{:S(2)}) %collective-permute-start.71) | collective-permute-done | bytes 331808 | tf_op jit(solution)/shard_map/ppermute | solution.py:609
  (352 shorter events, 79.8 us)
Async XLA Ops:
  7.2 196.4 %all-gather.2.cloned.1.call-start = ((), (), s32[]{:S(2)}) async-start(), calls=%async_computation | async-start | bytes 10948608 | tf_op jit(solution)/shard_map/all_gather | solution.py:818
  9.2 14.9 %collective-permute-start.2 = (bf16[144,1152]{1,0:T(8,128)(2,1)}, bf16[144,1152]{1,0:T(8,128)(2,1)S(1)}, u32[]{:S(2)}, u32[]{:S(2)}) collective-permute-start(bf16[144,1152]{1,0:T(8,128)(2,1)} %pad.35), channel_id=1, source_target_pairs={{0,8},{8,0},{1,9},{9,1},{2,10},{10,2},{3,11},{11,3},{4,12},{12,4},... | collective-permute-start | bytes 995336 | tf_op jit(solution)/shard_map/ppermute | solution.py:609
  24.2 23.0 %collective-permute-start.4 = (bf16[288,1152]{1,0:T(8,128)(2,1)S(1)}, bf16[288,1152]{1,0:T(8,128)(2,1)S(1)}, u32[]{:S(2)}, u32[]{:S(2)}) collective-permute-start(bf16[288,1152]{1,0:T(8,128)(2,1)S(1)} %pad_maximum_fusion.2.refs_3_), channel_id=1, source_target_pairs={{0,1},{1,2},{2,3},{3,0},{4,5},{5,6},{6,7},{7,4},{8,9},{9,10},{10,1... | collective-permute-start | bytes 1990664 | tf_op jit(solution)/shard_map/ppermute | solution.py:609
  26.1 21.1 %collective-permute-start.7 = (bf16[288,1152]{1,0:T(8,128)(2,1)S(1)}, bf16[288,1152]{1,0:T(8,128)(2,1)S(1)}, u32[]{:S(2)}, u32[]{:S(2)}) collective-permute-start(bf16[288,1152]{1,0:T(8,128)(2,1)S(1)} %pad_maximum_fusion.2.refs_3_), channel_id=1, source_target_pairs={{0,4},{4,0},{1,5},{5,1},{2,6},{6,2},{3,7},{7,3},{8,12},{12,8},{9,1... | collective-permute-start | bytes 1990664 | tf_op jit(solution)/shard_map/ppermute | solution.py:609
  27.1 20.1 %collective-permute-start.5 = (bf16[288,1152]{1,0:T(8,128)(2,1)S(1)}, bf16[288,1152]{1,0:T(8,128)(2,1)}, u32[]{:S(2)}, u32[]{:S(2)}) collective-permute-start(bf16[288,1152]{1,0:T(8,128)(2,1)S(1)} %pad_maximum_fusion.3.refs_4_), channel_id=1, source_target_pairs={{0,16},{16,0},{1,17},{17,1},{2,18},{18,2},{3,19},{19,3},{4,20},{20... | collective-permute-start | bytes 1990664 | tf_op jit(solution)/shard_map/ppermute | solution.py:609
  28.7 18.4 %collective-permute-start.6 = (bf16[144,1152]{1,0:T(8,128)(2,1)S(1)}, bf16[144,1152]{1,0:T(8,128)(2,1)S(1)}, u32[]{:S(2)}, u32[]{:S(2)}) collective-permute-start(bf16[144,1152]{1,0:T(8,128)(2,1)S(1)} %collective-permute-done.3), channel_id=1, source_target_pairs={{0,8},{8,0},{1,9},{9,1},{2,10},{10,2},{3,11},{11,3},{4,12},{12,4},... | collective-permute-start | bytes 995336 | tf_op jit(solution)/shard_map/ppermute | solution.py:609
  47.2 23.6 %collective-permute-start.12 = (bf16[1152,768]{1,0:T(8,128)(2,1)}, bf16[1152,768]{1,0:T(8,128)(2,1)}, u32[]{:S(2)}, u32[]{:S(2)}) collective-permute-start(bf16[1152,768]{1,0:T(8,128)(2,1)} %get-tuple-element.405.refs_0_), channel_id=1, source_target_pairs={{0,4},{4,0},{1,5},{5,1},{2,6},{6,2},{3,7},{7,3},{8,12},{12,8},{9,1... | collective-permute-start | bytes 5308424 | tf_op jit(solution)/shard_map/ppermute | solution.py:609
  48.2 21.7 %collective-permute-start.8 = (bf16[288,1152]{1,0:T(8,128)(2,1)S(1)}, bf16[288,1152]{1,0:T(8,128)(2,1)S(1)}, u32[]{:S(2)}, u32[]{:S(2)}) collective-permute-start(bf16[288,1152]{1,0:T(8,128)(2,1)S(1)} %collective-permute-done.4.refs_4_), channel_id=1, source_target_pairs={{0,1},{1,2},{2,3},{3,0},{4,5},{5,6},{6,7},{7,4},{8,9},{9,10},{10,1... | collective-permute-start | bytes 1990664 | tf_op jit(solution)/shard_map/ppermute | solution.py:609
  49.8 20.1 %collective-permute-start.9 = (bf16[288,1152]{1,0:T(8,128)(2,1)S(1)}, bf16[288,1152]{1,0:T(8,128)(2,1)S(1)}, u32[]{:S(2)}, u32[]{:S(2)}) collective-permute-start(bf16[288,1152]{1,0:T(8,128)(2,1)S(1)} %collective-permute-done.4.refs_4_), channel_id=1, source_target_pairs={{0,4},{4,0},{1,5},{5,1},{2,6},{6,2},{3,7},{7,3},{8,12},{12,8},{9,1... | collective-permute-start | bytes 1990664 | tf_op jit(solution)/shard_map/ppermute | solution.py:609
  51.7 19.1 %collective-permute-start.10 = (bf16[320,1152]{1,0:T(8,128)(2,1)}, bf16[320,1152]{1,0:T(8,128)(2,1)S(1)}, u32[]{:S(2)}, u32[]{:S(2)}) collective-permute-start(bf16[320,1152]{1,0:T(8,128)(2,1)} %pad_maximum_fusion), channel_id=1, source_target_pairs={{0,16},{16,0},{1,17},{17,1},{2,18},{18,2},{3,19},{19,3},{4,20},{20... | collective-permute-start | bytes 2211848 | tf_op jit(solution)/shard_map/ppermute | solution.py:609
  54.1 15.8 %collective-permute-start.11 = (bf16[256,1152]{1,0:T(8,128)(2,1)}, bf16[256,1152]{1,0:T(8,128)(2,1)}, u32[]{:S(2)}, u32[]{:S(2)}) collective-permute-start(bf16[256,1152]{1,0:T(8,128)(2,1)} %pad_maximum_fusion.4), channel_id=1, source_target_pairs={{0,8},{8,0},{1,9},{9,1},{2,10},{10,2},{3,11},{11,3},{4,12},{12,4},... | collective-permute-start | bytes 1769480 | tf_op jit(solution)/shard_map/ppermute | solution.py:609
  70.9 22.0 %collective-permute-start.15 = (bf16[320,1152]{1,0:T(8,128)(2,1)S(1)}, bf16[320,1152]{1,0:T(8,128)(2,1)S(1)}, u32[]{:S(2)}, u32[]{:S(2)}) collective-permute-start(bf16[320,1152]{1,0:T(8,128)(2,1)S(1)} %collective-permute-done.10.refs_7_), channel_id=1, source_target_pairs={{0,4},{4,0},{1,5},{5,1},{2,6},{6,2},{3,7},{7,3},{8,12},{12,8},{9,1... | collective-permute-start | bytes 2211848 | tf_op jit(solution)/shard_map/ppermute | solution.py:609
  72.9 17.4 %collective-permute-start.17 = (bf16[288,1152]{1,0:T(8,128)(2,1)}, bf16[288,1152]{1,0:T(8,128)(2,1)}, u32[]{:S(2)}, u32[]{:S(2)}) collective-permute-start(bf16[288,1152]{1,0:T(8,128)(2,1)} %constant_dynamic-update-slice_fusion.refs_5_), channel_id=1, source_target_pairs={{0,16},{16,0},{1,17},{17,1},{2,18},{18,2},{3,19},{19,3},{4,20},{20... | collective-permute-start | bytes 1990664 | tf_op jit(solution)/shard_map/ppermute | solution.py:609
  74.2 18.6 %collective-permute-start.13 = (bf16[288,1152]{1,0:T(8,128)(2,1)S(1)}, bf16[288,1152]{1,0:T(8,128)(2,1)S(1)}, u32[]{:S(2)}, u32[]{:S(2)}) collective-permute-start(bf16[288,1152]{1,0:T(8,128)(2,1)S(1)} %collective-permute-done.8.refs_5_), channel_id=1, source_target_pairs={{0,1},{1,2},{2,3},{3,0},{4,5},{5,6},{6,7},{7,4},{8,9},{9,10},{10,1... | collective-permute-start | bytes 1990664 | tf_op jit(solution)/shard_map/ppermute | solution.py:609
  75.8 17.0 %collective-permute-start.14 = (bf16[288,1152]{1,0:T(8,128)(2,1)S(1)}, bf16[288,1152]{1,0:T(8,128)(2,1)}, u32[]{:S(2)}, u32[]{:S(2)}) collective-permute-start(bf16[288,1152]{1,0:T(8,128)(2,1)S(1)} %collective-permute-done.8.refs_5_), channel_id=1, source_target_pairs={{0,4},{4,0},{1,5},{5,1},{2,6},{6,2},{3,7},{7,3},{8,12},{12,8},{9,1... | collective-permute-start | bytes 1990664 | tf_op jit(solution)/shard_map/ppermute | solution.py:609
  75.8 14.5 %collective-permute-start.16 = (bf16[256,1152]{1,0:T(8,128)(2,1)}, bf16[256,1152]{1,0:T(8,128)(2,1)}, u32[]{:S(2)}, u32[]{:S(2)}) collective-permute-start(bf16[256,1152]{1,0:T(8,128)(2,1)} %collective-permute-done.11.refs_9_), channel_id=1, source_target_pairs={{0,4},{4,0},{1,5},{5,1},{2,6},{6,2},{3,7},{7,3},{8,12},{12,8},{9,1... | collective-permute-start | bytes 1769480 | tf_op jit(solution)/shard_map/ppermute | solution.py:609
  93.9 18.8 %collective-permute-start.20 = (bf16[288,1152]{1,0:T(8,128)(2,1)S(1)}, bf16[288,1152]{1,0:T(8,128)(2,1)S(1)}, u32[]{:S(2)}, u32[]{:S(2)}) collective-permute-start(bf16[288,1152]{1,0:T(8,128)(2,1)S(1)} %collective-permute-done.13.refs_6_), channel_id=1, source_target_pairs={{0,4},{4,0},{1,5},{5,1},{2,6},{6,2},{3,7},{7,3},{8,12},{12,8},{9,1... | collective-permute-start | bytes 1990664 | tf_op jit(solution)/shard_map/ppermute | solution.py:609
  93.9 18.8 %collective-permute-start.22 = (bf16[288,1152]{1,0:T(8,128)(2,1)S(1)}, bf16[288,1152]{1,0:T(8,128)(2,1)S(1)}, u32[]{:S(2)}, u32[]{:S(2)}) collective-permute-start(bf16[288,1152]{1,0:T(8,128)(2,1)S(1)} %pad_maximum_fusion.3.refs_4_), channel_id=1, source_target_pairs={{0,4},{4,0},{1,5},{5,1},{2,6},{6,2},{3,7},{7,3},{8,12},{12,8},{9,1... | collective-permute-start | bytes 1990664 | tf_op jit(solution)/shard_map/ppermute | solution.py:609
  94.5 20.9 %collective-permute-start.18 = (bf16[320,1152]{1,0:T(8,128)(2,1)S(1)}, bf16[320,1152]{1,0:T(8,128)(2,1)S(1)}, u32[]{:S(2)}, u32[]{:S(2)}) collective-permute-start(bf16[320,1152]{1,0:T(8,128)(2,1)S(1)} %pad_maximum_fusion.1), channel_id=1, source_target_pairs={{0,16},{16,0},{1,17},{17,1},{2,18},{18,2},{3,19},{19,3},{4,20},{20... | collective-permute-start | bytes 2211848 | tf_op jit(solution)/shard_map/ppermute | solution.py:609
  95.3 17.5 %collective-permute-start.19 = (bf16[256,1152]{1,0:T(8,128)(2,1)S(1)}, bf16[256,1152]{1,0:T(8,128)(2,1)S(1)}, u32[]{:S(2)}, u32[]{:S(2)}) collective-permute-start(bf16[256,1152]{1,0:T(8,128)(2,1)S(1)} %pad_maximum_fusion.5), channel_id=1, source_target_pairs={{0,8},{8,0},{1,9},{9,1},{2,10},{10,2},{3,11},{11,3},{4,12},{12,4},... | collective-permute-start | bytes 1769480 | tf_op jit(solution)/shard_map/ppermute | solution.py:609
  95.9 16.7 %collective-permute-start.21 = (bf16[144,1152]{1,0:T(8,128)(2,1)S(1)}, bf16[144,1152]{1,0:T(8,128)(2,1)}, u32[]{:S(2)}, u32[]{:S(2)}) collective-permute-start(bf16[144,1152]{1,0:T(8,128)(2,1)S(1)} %copy-done.43), channel_id=1, source_target_pairs={{0,1},{1,2},{2,3},{3,0},{4,5},{5,6},{6,7},{7,4},{8,9},{9,10},{10,1... | collective-permute-start | bytes 995336 | tf_op jit(solution)/shard_map/ppermute | solution.py:609
  115.4 19.0 %collective-permute-start.25 = (bf16[320,1152]{1,0:T(8,128)(2,1)S(1)}, bf16[320,1152]{1,0:T(8,128)(2,1)S(1)}, u32[]{:S(2)}, u32[]{:S(2)}) collective-permute-start(bf16[320,1152]{1,0:T(8,128)(2,1)S(1)} %collective-permute-done.18.refs_8_), channel_id=1, source_target_pairs={{0,4},{4,0},{1,5},{5,1},{2,6},{6,2},{3,7},{7,3},{8,12},{12,8},{9,1... | collective-permute-start | bytes 2211848 | tf_op jit(solution)/shard_map/ppermute | solution.py:609
  115.4 18.3 %collective-permute-start.27 = (bf16[288,1152]{1,0:T(8,128)(2,1)}, bf16[288,1152]{1,0:T(8,128)(2,1)}, u32[]{:S(2)}, u32[]{:S(2)}) collective-permute-start(bf16[288,1152]{1,0:T(8,128)(2,1)} %collective-permute-done.5.refs_8_), channel_id=1, source_target_pairs={{0,4},{4,0},{1,5},{5,1},{2,6},{6,2},{3,7},{7,3},{8,12},{12,8},{9,1... | collective-permute-start | bytes 1990664 | tf_op jit(solution)/shard_map/ppermute | solution.py:609
  115.9 17.8 %collective-permute-start.26 = (bf16[256,1152]{1,0:T(8,128)(2,1)S(1)}, bf16[256,1152]{1,0:T(8,128)(2,1)S(1)}, u32[]{:S(2)}, u32[]{:S(2)}) collective-permute-start(bf16[256,1152]{1,0:T(8,128)(2,1)S(1)} %collective-permute-done.19.refs_10_), channel_id=1, source_target_pairs={{0,4},{4,0},{1,5},{5,1},{2,6},{6,2},{3,7},{7,3},{8,12},{12,8},{9,1... | collective-permute-start | bytes 1769480 | tf_op jit(solution)/shard_map/ppermute | solution.py:609
  116.0 17.7 %collective-permute-start.24 = (bf16[144,1152]{1,0:T(8,128)(2,1)}, bf16[144,1152]{1,0:T(8,128)(2,1)S(1)}, u32[]{:S(2)}, u32[]{:S(2)}) collective-permute-start(bf16[144,1152]{1,0:T(8,128)(2,1)} %pad.35), channel_id=1, source_target_pairs={{0,3},{1,0},{2,1},{3,2},{4,7},{5,4},{6,5},{7,6},{8,11},{9,8},{10,9... | collective-permute-start | bytes 995336 | tf_op jit(solution)/shard_map/ppermute | solution.py:609
  116.6 17.0 %collective-permute-start.23 = (bf16[144,1152]{1,0:T(8,128)(2,1)}, bf16[144,1152]{1,0:T(8,128)(2,1)}, u32[]{:S(2)}, u32[]{:S(2)}) collective-permute-start(bf16[144,1152]{1,0:T(8,128)(2,1)} %collective-permute-done.21), channel_id=1, source_target_pairs={{0,8},{8,0},{1,9},{9,1},{2,10},{10,2},{3,11},{11,3},{4,12},{12,4},... | collective-permute-start | bytes 995336 | tf_op jit(solution)/shard_map/ppermute | solution.py:609
  134.4 24.7 %collective-permute-start.31 = (bf16[288,1152]{1,0:T(8,128)(2,1)}, bf16[288,1152]{1,0:T(8,128)(2,1)S(1)}, u32[]{:S(2)}, u32[]{:S(2)}) collective-permute-start(bf16[288,1152]{1,0:T(8,128)(2,1)} %collective-permute-done.17.refs_9_), channel_id=1, source_target_pairs={{0,4},{4,0},{1,5},{5,1},{2,6},{6,2},{3,7},{7,3},{8,12},{12,8},{9,1... | collective-permute-start | bytes 1990664 | tf_op jit(solution)/shard_map/ppermute | solution.py:609
  135.7 23.5 %collective-permute-start.30 = (bf16[288,1152]{1,0:T(8,128)(2,1)}, bf16[288,1152]{1,0:T(8,128)(2,1)S(1)}, u32[]{:S(2)}, u32[]{:S(2)}) collective-permute-start(bf16[288,1152]{1,0:T(8,128)(2,1)} %constant_dynamic-update-slice_fusion.refs_5_), channel_id=1, source_target_pairs={{0,4},{4,0},{1,5},{5,1},{2,6},{6,2},{3,7},{7,3},{8,12},{12,8},{9,1... | collective-permute-start | bytes 1990664 | tf_op jit(solution)/shard_map/ppermute | solution.py:609
  136.0 23.2 %collective-permute-start.29 = (bf16[288,1152]{1,0:T(8,128)(2,1)S(1)}, bf16[288,1152]{1,0:T(8,128)(2,1)}, u32[]{:S(2)}, u32[]{:S(2)}) collective-permute-start(bf16[288,1152]{1,0:T(8,128)(2,1)S(1)} %constant_dynamic-update-slice_fusion.2.refs_6_), channel_id=1, source_target_pairs={{0,16},{16,0},{1,17},{17,1},{2,18},{18,2},{3,19},{19,3},{4,20},{20... | collective-permute-start | bytes 1990664 | tf_op jit(solution)/shard_map/ppermute | solution.py:609
  160.5 25.9 %collective-permute-start.32 = (bf16[288,1152]{1,0:T(8,128)(2,1)S(1)}, bf16[288,1152]{1,0:T(8,128)(2,1)}, u32[]{:S(2)}, u32[]{:S(2)}) collective-permute-start(bf16[288,1152]{1,0:T(8,128)(2,1)S(1)} %constant_dynamic-update-slice_fusion.4.refs_7_), channel_id=1, source_target_pairs={{0,16},{16,0},{1,17},{17,1},{2,18},{18,2},{3,19},{19,3},{4,20},{20... | collective-permute-start | bytes 1990664 | tf_op jit(solution)/shard_map/ppermute | solution.py:609
  162.3 41.2 %collective-permute-start.35 = (bf16[1152,768]{1,0:T(8,128)(2,1)}, bf16[1152,768]{1,0:T(8,128)(2,1)}, u32[]{:S(2)}, u32[]{:S(2)}) collective-permute-start(bf16[1152,768]{1,0:T(8,128)(2,1)} %get-tuple-element.313.refs_0_), channel_id=1, source_target_pairs={{0,4},{4,0},{1,5},{5,1},{2,6},{6,2},{3,7},{7,3},{8,12},{12,8},{9,1... | collective-permute-start | bytes 5308424 | tf_op jit(solution)/shard_map/ppermute | solution.py:609
  196.8 26.8 %collective-permute-start.38 = (bf16[1152,768]{1,0:T(8,128)(2,1)}, bf16[1152,768]{1,0:T(8,128)(2,1)}, u32[]{:S(2)}, u32[]{:S(2)}) collective-permute-start(bf16[1152,768]{1,0:T(8,128)(2,1)} %get-tuple-element.319.refs_0_), channel_id=1, source_target_pairs={{0,4},{4,0},{1,5},{5,1},{2,6},{6,2},{3,7},{7,3},{8,12},{12,8},{9,1... | collective-permute-start | bytes 5308424 | tf_op jit(solution)/shard_map/ppermute | solution.py:609
  197.4 26.2 %collective-permute-start.36 = (bf16[288,1152]{1,0:T(8,128)(2,1)S(1)}, bf16[288,1152]{1,0:T(8,128)(2,1)S(1)}, u32[]{:S(2)}, u32[]{:S(2)}) collective-permute-start(bf16[288,1152]{1,0:T(8,128)(2,1)S(1)} %constant_dynamic-update-slice_fusion.4.refs_7_), channel_id=1, source_target_pairs={{0,4},{4,0},{1,5},{5,1},{2,6},{6,2},{3,7},{7,3},{8,12},{12,8},{9,1... | collective-permute-start | bytes 1990664 | tf_op jit(solution)/shard_map/ppermute | solution.py:609
  202.0 21.6 %collective-permute-start.37 = (bf16[288,1152]{1,0:T(8,128)(2,1)}, bf16[288,1152]{1,0:T(8,128)(2,1)S(1)}, u32[]{:S(2)}, u32[]{:S(2)}) collective-permute-start(bf16[288,1152]{1,0:T(8,128)(2,1)} %collective-permute-done.32.refs_11_), channel_id=1, source_target_pairs={{0,4},{4,0},{1,5},{5,1},{2,6},{6,2},{3,7},{7,3},{8,12},{12,8},{9,1... | collective-permute-start | bytes 1990664 | tf_op jit(solution)/shard_map/ppermute | solution.py:609
  223.6 31.3 %collective-permute-start.39 = (bf16[768,4608]{1,0:T(8,128)(2,1)}, bf16[768,4608]{1,0:T(8,128)(2,1)}, u32[]{:S(2)}, u32[]{:S(2)}) collective-permute-start(bf16[768,4608]{1,0:T(8,128)(2,1)} %get-tuple-element.320.refs_2_), channel_id=1, source_target_pairs={{0,4},{4,0},{1,5},{5,1},{2,6},{6,2},{3,7},{7,3},{8,12},{12,8},{9,1... | collective-permute-start | bytes 21233672 | tf_op jit(solution)/shard_map/ppermute | solution.py:609
  254.9 37.6 %collective-permute-start.40 = (bf16[768,4608]{1,0:T(8,128)(2,1)}, bf16[768,4608]{1,0:T(8,128)(2,1)}, u32[]{:S(2)}, u32[]{:S(2)}) collective-permute-start(bf16[768,4608]{1,0:T(8,128)(2,1)} %get-tuple-element.360.refs_1_.refs_2_), channel_id=1, source_target_pairs={{0,4},{4,0},{1,5},{5,1},{2,6},{6,2},{3,7},{7,3},{8,12},{12,8},{9,1... | collective-permute-start | bytes 21233672 | tf_op jit(solution)/shard_map/ppermute | solution.py:609
  269.2 34.9 %collective-permute-start.41 = (bf16[4,144,1152]{2,1,0:T(8,128)(2,1)}, bf16[4,144,1152]{2,1,0:T(8,128)(2,1)}, u32[]{:S(2)}, u32[]{:S(2)}) collective-permute-start(bf16[4,144,1152]{2,1,0:T(8,128)(2,1)} %get-tuple-element.339), channel_id=1, source_target_pairs={{0,8},{8,0},{1,9},{9,1},{2,10},{10,2},{3,11},{11,3},{4,12},{12,4},... | collective-permute-start | bytes 3981320 | tf_op jit(solution)/shard_map/ppermute | solution.py:609
  269.7 78.2 %collective-permute-start.44 = (bf16[4,144,1152]{2,1,0:T(8,128)(2,1)}, bf16[4,144,1152]{2,1,0:T(8,128)(2,1)}, u32[]{:S(2)}, u32[]{:S(2)}) collective-permute-start(bf16[4,144,1152]{2,1,0:T(8,128)(2,1)} %get-tuple-element.337), channel_id=1, source_target_pairs={{0,8},{8,0},{1,9},{9,1},{2,10},{10,2},{3,11},{11,3},{4,12},{12,4},... | collective-permute-start | bytes 3981320 | tf_op jit(solution)/shard_map/ppermute | solution.py:609
  292.4 28.0 %collective-permute-start.43 = (bf16[1152,768]{1,0:T(8,128)(2,1)}, bf16[1152,768]{1,0:T(8,128)(2,1)}, u32[]{:S(2)}, u32[]{:S(2)}) collective-permute-start(bf16[1152,768]{1,0:T(8,128)(2,1)} %get-tuple-element.342.refs_2_), channel_id=1, source_target_pairs={{0,4},{4,0},{1,5},{5,1},{2,6},{6,2},{3,7},{7,3},{8,12},{12,8},{9,1... | collective-permute-start | bytes 5308424 | tf_op jit(solution)/shard_map/ppermute | solution.py:609
  303.6 16.8 %collective-permute-start.42 = (bf16[768,1152]{1,0:T(8,128)(2,1)}, bf16[768,1152]{1,0:T(8,128)(2,1)}, u32[]{:S(2)}, u32[]{:S(2)}) collective-permute-start(bf16[768,1152]{1,0:T(8,128)(2,1)} %get-tuple-element.347.refs_3_), channel_id=1, source_target_pairs={{0,4},{4,0},{1,5},{5,1},{2,6},{6,2},{3,7},{7,3},{8,12},{12,8},{9,1... | collective-permute-start | bytes 5308424 | tf_op jit(solution)/shard_map/ppermute | solution.py:609
  318.5 31.4 %collective-permute-start.45 = (bf16[4,144,1152]{2,1,0:T(8,128)(2,1)}, bf16[4,144,1152]{2,1,0:T(8,128)(2,1)}, u32[]{:S(2)}, u32[]{:S(2)}) collective-permute-start(bf16[4,144,1152]{2,1,0:T(8,128)(2,1)} %add_convert_fusion.1), channel_id=1, source_target_pairs={{0,16},{16,0},{1,17},{17,1},{2,18},{18,2},{3,19},{19,3},{4,20},{20... | collective-permute-start | bytes 3981320 | tf_op jit(solution)/shard_map/ppermute | solution.py:609
  331.1 39.5 %collective-permute-start.47 = (bf16[288,1152]{1,0:T(8,128)(2,1)}, bf16[288,1152]{1,0:T(8,128)(2,1)}, u32[]{:S(2)}, u32[]{:S(2)}) collective-permute-start(bf16[288,1152]{1,0:T(8,128)(2,1)} %get-tuple-element.358), channel_id=1, source_target_pairs={{0,8},{8,0},{1,9},{9,1},{2,10},{10,2},{3,11},{11,3},{4,12},{12,4},... | collective-permute-start | bytes 1990664 | tf_op jit(solution)/shard_map/ppermute | solution.py:609
  331.2 39.4 %collective-permute-start.48 = (bf16[288,1152]{1,0:T(8,128)(2,1)}, bf16[288,1152]{1,0:T(8,128)(2,1)}, u32[]{:S(2)}, u32[]{:S(2)}) collective-permute-start(bf16[288,1152]{1,0:T(8,128)(2,1)} %get-tuple-element.359), channel_id=1, source_target_pairs={{0,8},{8,0},{1,9},{9,1},{2,10},{10,2},{3,11},{11,3},{4,12},{12,4},... | collective-permute-start | bytes 1990664 | tf_op jit(solution)/shard_map/ppermute | solution.py:609
  354.1 13.6 %collective-permute-start.46 = (bf16[144,1152]{1,0:T(8,128)(2,1)}, bf16[144,1152]{1,0:T(8,128)(2,1)}, u32[]{:S(2)}, u32[]{:S(2)}) collective-permute-start(bf16[144,1152]{1,0:T(8,128)(2,1)} %get-tuple-element.497), channel_id=1, source_target_pairs={{0,3},{1,0},{2,1},{3,2},{4,7},{5,4},{6,5},{7,6},{8,11},{9,8},{10,9... | collective-permute-start | bytes 995336 | tf_op jit(solution)/shard_map/ppermute | solution.py:609
  354.4 16.2 %collective-permute-start.49 = (bf16[2,144,1152]{2,1,0:T(8,128)(2,1)}, bf16[2,144,1152]{2,1,0:T(8,128)(2,1)}, u32[]{:S(2)}, u32[]{:S(2)}) collective-permute-start(bf16[2,144,1152]{2,1,0:T(8,128)(2,1)} %get-tuple-element.375), channel_id=1, source_target_pairs={{0,16},{16,0},{1,17},{17,1},{2,18},{18,2},{3,19},{19,3},{4,20},{20... | collective-permute-start | bytes 1990664 | tf_op jit(solution)/shard_map/ppermute | solution.py:609
  372.5 17.7 %collective-permute-start.52 = (bf16[144,1152]{1,0:T(8,128)(2,1)}, bf16[144,1152]{1,0:T(8,128)(2,1)}, u32[]{:S(2)}, u32[]{:S(2)}) collective-permute-start(bf16[144,1152]{1,0:T(8,128)(2,1)} %fusion.7), channel_id=1, source_target_pairs={{0,3},{1,0},{2,1},{3,2},{4,7},{5,4},{6,5},{7,6},{8,11},{9,8},{10,9... | collective-permute-start | bytes 995336 | tf_op jit(solution)/shard_map/ppermute | solution.py:609
  375.3 14.9 %collective-permute-start.53 = (bf16[288,1152]{1,0:T(8,128)(2,1)}, bf16[288,1152]{1,0:T(8,128)(2,1)}, u32[]{:S(2)}, u32[]{:S(2)}) collective-permute-start(bf16[288,1152]{1,0:T(8,128)(2,1)} %get-tuple-element.386), channel_id=1, source_target_pairs={{0,8},{8,0},{1,9},{9,1},{2,10},{10,2},{3,11},{11,3},{4,12},{12,4},... | collective-permute-start | bytes 1990664 | tf_op jit(solution)/shard_map/ppermute | solution.py:609
  376.7 17.6 %collective-permute-start.50 = (bf16[768,1152]{1,0:T(8,128)(2,1)}, bf16[768,1152]{1,0:T(8,128)(2,1)}, u32[]{:S(2)}, u32[]{:S(2)}) collective-permute-start(bf16[768,1152]{1,0:T(8,128)(2,1)} %get-tuple-element.382.refs_2_), channel_id=1, source_target_pairs={{0,4},{4,0},{1,5},{5,1},{2,6},{6,2},{3,7},{7,3},{8,12},{12,8},{9,1... | collective-permute-start | bytes 5308424 | tf_op jit(solution)/shard_map/ppermute | solution.py:609
  376.7 17.6 %collective-permute-start.51 = (bf16[2,144,1152]{2,1,0:T(8,128)(2,1)}, bf16[2,144,1152]{2,1,0:T(8,128)(2,1)}, u32[]{:S(2)}, u32[]{:S(2)}) collective-permute-start(bf16[2,144,1152]{2,1,0:T(8,128)(2,1)} %get-tuple-element.384), channel_id=1, source_target_pairs={{0,16},{16,0},{1,17},{17,1},{2,18},{18,2},{3,19},{19,3},{4,20},{20... | collective-permute-start | bytes 1990664 | tf_op jit(solution)/shard_map/ppermute | solution.py:609
  396.3 23.8 %collective-permute-start.56 = (bf16[144,1152]{1,0:T(8,128)(2,1)}, bf16[144,1152]{1,0:T(8,128)(2,1)}, u32[]{:S(2)}, u32[]{:S(2)}) collective-permute-start(bf16[144,1152]{1,0:T(8,128)(2,1)} %fusion.6), channel_id=1, source_target_pairs={{0,3},{1,0},{2,1},{3,2},{4,7},{5,4},{6,5},{7,6},{8,11},{9,8},{10,9... | collective-permute-start | bytes 995336 | tf_op jit(solution)/shard_map/ppermute | solution.py:609
  397.4 22.7 %collective-permute-start.55 = (bf16[2,144,1152]{2,1,0:T(8,128)(2,1)}, bf16[2,144,1152]{2,1,0:T(8,128)(2,1)}, u32[]{:S(2)}, u32[]{:S(2)}) collective-permute-start(bf16[2,144,1152]{2,1,0:T(8,128)(2,1)} %get-tuple-element.399), channel_id=1, source_target_pairs={{0,16},{16,0},{1,17},{17,1},{2,18},{18,2},{3,19},{19,3},{4,20},{20... | collective-permute-start | bytes 1990664 | tf_op jit(solution)/shard_map/ppermute | solution.py:609
  397.8 22.3 %collective-permute-start.54 = (bf16[288,1152]{1,0:T(8,128)(2,1)}, bf16[288,1152]{1,0:T(8,128)(2,1)}, u32[]{:S(2)}, u32[]{:S(2)}) collective-permute-start(bf16[288,1152]{1,0:T(8,128)(2,1)} %get-tuple-element.397), channel_id=1, source_target_pairs={{0,8},{8,0},{1,9},{9,1},{2,10},{10,2},{3,11},{11,3},{4,12},{12,4},... | collective-permute-start | bytes 1990664 | tf_op jit(solution)/shard_map/ppermute | solution.py:609
  420.1 17.5 %collective-permute-start.59 = (f32[16,1152]{1,0:T(8,128)}, f32[16,1152]{1,0:T(8,128)}, u32[]{:S(2)}, u32[]{:S(2)}) collective-permute-start(f32[16,1152]{1,0:T(8,128)} %pad_maximum_fusion.7), channel_id=1, source_target_pairs={{0,1},{1,0},{2,3},{3,2},{4,5},{5,4},{6,7},{7,6},{8,9},{9,8},{10,11... | collective-permute-start | bytes 221192 | tf_op jit(solution)/shard_map/ppermute | solution.py:959
  420.3 18.2 %collective-permute-start.58 = (bf16[2,144,1152]{2,1,0:T(8,128)(2,1)}, bf16[2,144,1152]{2,1,0:T(8,128)(2,1)}, u32[]{:S(2)}, u32[]{:S(2)}) collective-permute-start(bf16[2,144,1152]{2,1,0:T(8,128)(2,1)} %add_convert_fusion.7), channel_id=1, source_target_pairs={{0,8},{8,0},{1,9},{9,1},{2,10},{10,2},{3,11},{11,3},{4,12},{12,4},... | collective-permute-start | bytes 1990664 | tf_op jit(solution)/shard_map/ppermute | solution.py:609
  421.8 16.7 %collective-permute-start.57 = (bf16[2,144,1152]{2,1,0:T(8,128)(2,1)}, bf16[2,144,1152]{2,1,0:T(8,128)(2,1)}, u32[]{:S(2)}, u32[]{:S(2)}) collective-permute-start(bf16[2,144,1152]{2,1,0:T(8,128)(2,1)} %get-tuple-element.415), channel_id=1, source_target_pairs={{0,16},{16,0},{1,17},{17,1},{2,18},{18,2},{3,19},{19,3},{4,20},{20... | collective-permute-start | bytes 1990664 | tf_op jit(solution)/shard_map/ppermute | solution.py:609
  425.3 25.1 %collective-permute-start.62 = (bf16[2,144,1152]{2,1,0:T(8,128)(2,1)}, bf16[2,144,1152]{2,1,0:T(8,128)(2,1)}, u32[]{:S(2)}, u32[]{:S(2)}) collective-permute-start(bf16[2,144,1152]{2,1,0:T(8,128)(2,1)} %add_convert_fusion.5), channel_id=1, source_target_pairs={{0,8},{8,0},{1,9},{9,1},{2,10},{10,2},{3,11},{11,3},{4,12},{12,4},... | collective-permute-start | bytes 1990664 | tf_op jit(solution)/shard_map/ppermute | solution.py:609
  442.2 13.5 %collective-permute-start.60 = (bf16[288,1152]{1,0:T(8,128)(2,1)}, bf16[288,1152]{1,0:T(8,128)(2,1)S(1)}, u32[]{:S(2)}, u32[]{:S(2)}) collective-permute-start(bf16[288,1152]{1,0:T(8,128)(2,1)} %get-tuple-element.421), channel_id=1, source_target_pairs={{0,16},{16,0},{1,17},{17,1},{2,18},{18,2},{3,19},{19,3},{4,20},{20... | collective-permute-start | bytes 1990664 | tf_op jit(solution)/shard_map/ppermute | solution.py:609
  455.9 20.4 %collective-permute-start.67 = (bf16[144,1152]{1,0:T(8,128)(2,1)S(1)}, bf16[144,1152]{1,0:T(8,128)(2,1)S(1)}, u32[]{:S(2)}, u32[]{:S(2)}) collective-permute-start(bf16[144,1152]{1,0:T(8,128)(2,1)S(1)} %get-tuple-element.499), channel_id=1, source_target_pairs={{0,2},{1,3},{2,0},{3,1},{4,6},{5,7},{6,4},{7,5},{8,10},{9,11},{10,... | collective-permute-start | bytes 995336 | tf_op jit(solution)/shard_map/ppermute | solution.py:609
  456.4 20.0 %collective-permute-start.68 = (bf16[144,1152]{1,0:T(8,128)(2,1)S(1)}, bf16[144,1152]{1,0:T(8,128)(2,1)S(1)}, u32[]{:S(2)}, u32[]{:S(2)}) collective-permute-start(bf16[144,1152]{1,0:T(8,128)(2,1)S(1)} %get-tuple-element.498), channel_id=1, source_target_pairs={{0,1},{1,2},{2,3},{3,0},{4,5},{5,6},{6,7},{7,4},{8,9},{9,10},{10,1... | collective-permute-start | bytes 995336 | tf_op jit(solution)/shard_map/ppermute | solution.py:609
  458.1 19.0 %collective-permute-start.65 = (bf16[144,1152]{1,0:T(8,128)(2,1)S(1)}, bf16[144,1152]{1,0:T(8,128)(2,1)S(1)}, u32[]{:S(2)}, u32[]{:S(2)}) collective-permute-start(bf16[144,1152]{1,0:T(8,128)(2,1)S(1)} %fusion.5), channel_id=1, source_target_pairs={{0,3},{1,0},{2,1},{3,2},{4,7},{5,4},{6,5},{7,6},{8,11},{9,8},{10,9... | collective-permute-start | bytes 995336 | tf_op jit(solution)/shard_map/ppermute | solution.py:609
  460.3 16.7 %collective-permute-start.64 = (bf16[288,1152]{1,0:T(8,128)(2,1)S(1)}, bf16[288,1152]{1,0:T(8,128)(2,1)S(1)}, u32[]{:S(2)}, u32[]{:S(2)}) collective-permute-start(bf16[288,1152]{1,0:T(8,128)(2,1)S(1)} %copy-done.72), channel_id=1, source_target_pairs={{0,16},{16,0},{1,17},{17,1},{2,18},{18,2},{3,19},{19,3},{4,20},{20... | collective-permute-start | bytes 1990664 | tf_op jit(solution)/shard_map/ppermute | solution.py:609
  477.3 29.2 %collective-permute-start.72 = (bf16[144,1152]{1,0:T(8,128)(2,1)S(1)}, bf16[144,1152]{1,0:T(8,128)(2,1)S(1)}, u32[]{:S(2)}, u32[]{:S(2)}) collective-permute-start(bf16[144,1152]{1,0:T(8,128)(2,1)S(1)} %fusion.4), channel_id=1, source_target_pairs={{0,3},{1,0},{2,1},{3,2},{4,7},{5,4},{6,5},{7,6},{8,11},{9,8},{10,9... | collective-permute-start | bytes 995336 | tf_op jit(solution)/shard_map/ppermute | solution.py:609
  481.5 12.5 %collective-permute-start.70 = (f32[16,1152]{1,0:T(8,128)S(1)}, f32[16,1152]{1,0:T(8,128)S(1)}, u32[]{:S(2)}, u32[]{:S(2)}) collective-permute-start(f32[16,1152]{1,0:T(8,128)S(1)} %add.375), channel_id=1, source_target_pairs={{0,4},{4,0},{1,5},{5,1},{2,6},{6,2},{3,7},{7,3},{8,12},{12,8},{9,1... | collective-permute-start | bytes 221192 | tf_op jit(solution)/shard_map/ppermute | solution.py:959
  481.8 21.4 %collective-permute-start.71 = (bf16[144,1152]{1,0:T(8,128)(2,1)S(1)}, bf16[144,1152]{1,0:T(8,128)(2,1)S(1)}, u32[]{:S(2)}, u32[]{:S(2)}) collective-permute-start(bf16[144,1152]{1,0:T(8,128)(2,1)S(1)} %slice.212), channel_id=1, source_target_pairs={{0,3},{1,0},{2,1},{3,2},{4,7},{5,4},{6,5},{7,6},{8,11},{9,8},{10,9... | collective-permute-start | bytes 995336 | tf_op jit(solution)/shard_map/ppermute | solution.py:609
  (83 other events, 903.8 us)
Sparse Core Ops, SparseCore 0:
  93.0 102.0 all-gather.1

commit v6 on v5

--- a/solution.py
+++ b/solution.py
@@ -859,9 +859,12 @@
                 y_far_down += [y0, y1]
                 pairs.append(cat(down_z[3], dx3))
                 down_y.append(dy2)
-                dy3 = swap(pairs[3], "y")
+                near_three = swap(after(down_z[3], out), "y")
                 p2, y2, gl_far = swap(after(pairs[2], out)), swap(dy2), swap(after(gl_t, out))
-        mixed_last, dy3 = together((out[1], dy3))
+        mixed_last, near_three, far_three, p2, y2 = together(
+            (out[1], near_three, swap(dx3, "y"), p2, y2)
+        )
+        dy3 = cat(near_three, far_three)
         kept[3] = [out[0], mixed_last, *out[2:]]
     else:
         kept = []
@@ -888,7 +891,7 @@
         [out[4] for out in kept],
     )
     if linked:
-        normed_b, p2, y2, gl_far = together((normed_b, p2, y2, gl_far))
+        normed_b, gl_far = together((normed_b, gl_far))
         down_y.append(dy3)
         p3, y3 = swap(pairs[3]), swap(dy3)
         nb_far = swap(nb_t)

time: 522 us -> 517 us (level)
    ppermute x5, waiting for transfers between devices: 0.24 us -> 5.75 us  [fold(): lax.ppermute(value, axis, [(i, i ^ step) for i in range(sizes[axis])])]
    ppermute x68 -> x69, waiting for transfers between devices: 104 us -> 100 us  [hop(): return lax.ppermute(x, axis, [(i, (i + step) % n) for i in range(n)])]
    ppermute x68 -> x69, starting transfers between devices: 66.2 us -> 63.7 us  [hop(): return lax.ppermute(x, axis, [(i, (i + step) % n) for i in range(n)])]
    unnamed x153 -> x154, local copies, waits for them, and re-layouts: 13.6 us -> 13.6 us
  transfers between devices with their start and end apart: 74 -> 75, of which waited for: 24 -> 25; matrix products, arithmetic and copies ran while one was open for 13% -> 13% of each run, Pallas kernels for 48% -> 48%
where the time goes in v6:
time: 517 us; the launch traced here: 512 us
  Pallas kernels  246 us (48%)
  waiting for transfers between devices  106 us (21%)
  starting transfers between devices  66.2 us (13%)
  other arithmetic  40.4 us (8%)
  local copies, waits for them, and re-layouts  36.3 us (7%)
  between operations  16.1 us (3%)
    ppermute x69, waiting for transfers between devices, hop(): return lax.ppermute(x, axis, [(i, (i + step) % n) for i in range(n)])  100 us
    ppermute x69, starting transfers between devices, hop(): return lax.ppermute(x, axis, [(i, (i + step) % n) for i in range(n)])  63.7 us
    pallas_call x4, Pallas kernels, attn_bwd(): pl.pallas_call(functools.partial(attn_bwd_kernel, seq), in_specs=specs(5)...  45.2 us
    pallas_call x4, Pallas kernels, attn_fwd(): pl.pallas_call(functools.partial(attn_fwd_kernel, plan, len(pieces), seq)...  43 us
    pallas_call x2, Pallas kernels, ff_grad(): pl.pallas_call(functools.partial(ff_grad_kernel, total, parts, sets, size...  28.8 us
    pallas_call x1, Pallas kernels, ff_down(): pl.pallas_call(functools.partial(ff_down_kernel, plan, len(pieces), slots...  28.2 us
    pallas_call x2, Pallas kernels, attn_grad(): pl.pallas_call(functools.partial(attn_grad_kernel, total, parts, len(more...  22.3 us
    pallas_call x1, Pallas kernels, ff_back(): pl.pallas_call(functools.partial(ff_back_kernel, table.shape[0]), grid=(u...  21.3 us
  transfers between devices with their start and end apart: 75, of which 25 were waited for; matrix products, arithmetic and copies ran while one was open for 13% of the time, Pallas kernels for 48%

profile of v6, /device:TPU:0, one launch (start us, length us, event | category | flops | bytes accessed | tf_op | source)
XLA Modules:
  0.0 511.6 jit_solution(8030438066904398284)
XLA Ops:
  9.2 2.9 collective-permute-start.2
  16.6 3.6 collective-permute-done.1
  20.2 3.8 collective-permute-done
  24.2 1.9 collective-permute-start.4
  30.9 3.0 multiply_convert_fusion.x.refs_1_.refs_5_
  34.5 3.3 turn.1
  37.8 2.9 pad.37.refs_1_.refs_8_
  42.5 4.6 norm.2
  49.8 1.9 pad_maximum_fusion
  52.3 1.8 pad_maximum_fusion.4
  60.2 1.7 constant_dynamic-update-slice_fusion.1
  62.0 7.9 %collective-permute-done.11.refs_9_ = bf16[256,1152]{1,0:T(8,128)(2,1)} collective-permute-done((bf16[256,1152]{1,0:T(8,128)(2,1)}, bf16[256,1152]{1,0:T(8,128)(2,1)}, u32[]{:S(2)}, u32[]{:S(2)}) %collective-permute-start.11) | collective-permute-done | bytes 589856 | tf_op jit(solution)/shard_map/ppermute | solution.py:609
  71.0 1.9 constant_dynamic-update-slice_fusion.refs_5_
  77.2 13.1 %collective-permute-done.17.refs_9_ = bf16[288,1152]{1,0:T(8,128)(2,1)} collective-permute-done((bf16[288,1152]{1,0:T(8,128)(2,1)}, bf16[288,1152]{1,0:T(8,128)(2,1)}, u32[]{:S(2)}, u32[]{:S(2)}) %collective-permute-start.17) | collective-permute-done | bytes 663584 | tf_op jit(solution)/shard_map/ppermute | solution.py:609
  90.3 2.5 collective-permute-done.13.refs_6_
  95.6 16.7 %collective-permute-done.21 = bf16[144,1152]{1,0:T(8,128)(2,1)} collective-permute-done((bf16[144,1152]{1,0:T(8,128)(2,1)S(1)}, bf16[144,1152]{1,0:T(8,128)(2,1)}, u32[]{:S(2)}, u32[]{:S(2)}) %collective-permute-start.21) | collective-permute-done | bytes 331808 | tf_op jit(solution)/shard_map/ppermute | solution.py:609
  113.0 2.3 collective-permute-done.18.refs_8_
  117.1 10.7 %attn_fwd.4 = (bf16[768,864]{1,0:T(8,128)(2,1)}, bf16[768,288]{1,0:T(8,128)(2,1)}, f32[8,768]{1,0:T(8,128)}, bf16[1152,1152]{1,0:T(8,128)(2,1)}, bf16[1152,288]{1,0:T(8,128)(2,1)}) custom-call(s32[8]{0:T(128)} %stack.125.refs_0_, bf16[768,1152]{1,0:T(8,128)(2,1)} %get-tuple-element.302.refs_1_, f32[1,864]{1,0:T(1,128)} %broadcast_in_dim.163.refs_2_, ...), custom_call_target="tpu_custom_call" | custom-call | flops 222717536 | bytes 265420 | tf_op jit(solution)/shard_map/attn_fwd/pallas_call | solution.py:129
  128.8 1.8 collective-permute-done.23
  130.7 5.6 %collective-permute-done.24 = bf16[144,1152]{1,0:T(8,128)(2,1)S(1)} collective-permute-done((bf16[144,1152]{1,0:T(8,128)(2,1)}, bf16[144,1152]{1,0:T(8,128)(2,1)S(1)}, u32[]{:S(2)}, u32[]{:S(2)}) %collective-permute-start.24) | collective-permute-done | bytes 331808 | tf_op jit(solution)/shard_map/ppermute | solution.py:609
  138.3 3.1 collective-permute-start.28
  141.3 10.6 %attn_fwd.5 = (bf16[768,864]{1,0:T(8,128)(2,1)}, bf16[768,288]{1,0:T(8,128)(2,1)}, f32[8,768]{1,0:T(8,128)}, bf16[1152,1152]{1,0:T(8,128)(2,1)}, bf16[1152,288]{1,0:T(8,128)(2,1)}) custom-call(s32[8]{0:T(128)} %stack.125.refs_0_, bf16[768,1152]{1,0:T(8,128)(2,1)} %get-tuple-element.302.refs_1_, f32[1,864]{1,0:T(1,128)} %broadcast_in_dim.164.refs_2_, ...), custom_call_target="tpu_custom_call" | custom-call | flops 222717536 | bytes 265420 | tf_op jit(solution)/shard_map/attn_fwd/pallas_call | solution.py:129
  152.0 11.1 %attn_fwd.6 = (bf16[768,864]{1,0:T(8,128)(2,1)}, bf16[768,288]{1,0:T(8,128)(2,1)}, f32[8,768]{1,0:T(8,128)}, bf16[1152,1152]{1,0:T(8,128)(2,1)}, bf16[1152,288]{1,0:T(8,128)(2,1)}) custom-call(s32[8]{0:T(128)} %stack.125.refs_0_, bf16[768,1152]{1,0:T(8,128)(2,1)} %get-tuple-element.302.refs_1_, f32[1,864]{1,0:T(1,128)} %broadcast_in_dim.165.refs_2_, ...), custom_call_target="tpu_custom_call" | custom-call | flops 222717536 | bytes 265420 | tf_op jit(solution)/shard_map/attn_fwd/pallas_call | solution.py:129
  163.8 2.0 collective-permute-start.32
  166.4 10.6 %attn_fwd.7 = (bf16[768,864]{1,0:T(8,128)(2,1)}, bf16[768,288]{1,0:T(8,128)(2,1)}, f32[8,768]{1,0:T(8,128)}, bf16[1152,1152]{1,0:T(8,128)(2,1)}, bf16[1152,288]{1,0:T(8,128)(2,1)}) custom-call(s32[8]{0:T(128)} %stack.125.refs_0_, bf16[768,1152]{1,0:T(8,128)(2,1)} %get-tuple-element.302.refs_1_, f32[1,864]{1,0:T(1,128)} %broadcast_in_dim.166.refs_2_, ...), custom_call_target="tpu_custom_call" | custom-call | flops 222717536 | bytes 265420 | tf_op jit(solution)/shard_map/attn_fwd/pallas_call | solution.py:129
  177.3 6.9 %collective-permute-done.33 = bf16[144,1152]{1,0:T(8,128)(2,1)} collective-permute-done((bf16[144,1152]{1,0:T(8,128)(2,1)}, bf16[144,1152]{1,0:T(8,128)(2,1)}, u32[]{:S(2)}, u32[]{:S(2)}) %collective-permute-start.33) | collective-permute-done | bytes 331808 | tf_op jit(solution)/shard_map/ppermute | solution.py:609
  184.2 10.9 %norm.3 = (f32[768,1152]{1,0:T(8,128)}, bf16[768,1152]{1,0:T(8,128)(2,1)}, bf16[1152,768]{1,0:T(8,128)(2,1)}) custom-call(s32[8]{0:T(128)} %stack.116.table.refs_0_, bf16[768,1152]{1,0:T(8,128)(2,1)} %pad.37.refs_1_.refs_8_, f32[1,1152]{1,0:T(1,128)} %broadcast_in_dim.170.refs_2_, f32[1,1152]{1,0:T(1,128)} %broadcast_in_dim.168.refs_3_.refs_4_, ...), custom_call_target="tpu_custom_call" | custom-call | flops 707788 | bytes 442368 | tf_op jit(solution)/shard_map/norm/pallas_call | solution.py:428
  199.1 19.7 %ff_up.1 = (bf16[768,4608]{1,0:T(8,128)(2,1)}, bf16[768,4608]{1,0:T(8,128)(2,1)}, bf16[1152,4608]{1,0:T(8,128)(2,1)}) custom-call(s32[4]{0:T(128)} %pad_add_fusion.refs_0_, bf16[768,1152]{1,0:T(8,128)(2,1)} %get-tuple-element.317.refs_1_, f32[1,4608]{1,0:T(1,128)} %broadcast_in_dim.167.refs_2_, bf16[4608,1152]{1,0:T(8,128)(2,1)} %all-gather.2.cloned.1.call-done.refs_3_), custom_call_target="tpu_custom_call" | custom-call | flops 407686336 | bytes 1769472 | tf_op jit(solution)/shard_map/ff_up/pallas_call | solution.py:268
  220.5 28.2 %ff_down.1 = (f32[768,1152]{1,0:T(8,128)}, bf16[768,4608]{1,0:T(8,128)(2,1)}, f32[1,4608]{1,0:T(1,128)}) custom-call(s32[8]{0:T(128)} %stack.134.refs_0_, bf16[768,1152]{1,0:T(8,128)(2,1)} %multiply_convert_fusion.x.refs_1_.refs_5_, bf16[768,4608]{1,0:T(8,128)(2,1)} %get-tuple-element.324.refs_2_, bf16[768,4608]{1,0:T(8,128)(2,1)} %get-tuple-element.325.refs_3_, ...), custom_call_target="tpu_custom_call" | custom-call | flops 815372672 | bytes 1592524 | tf_op jit(solution)/shard_map/ff_down/pallas_call | solution.py:337
  250.5 14.1 %ff_grad.2 = (bf16[4,144,1152]{2,1,0:T(8,128)(2,1)}, bf16[4,144,1152]{2,1,0:T(8,128)(2,1)}, bf16[4,144,1152]{2,1,0:T(8,128)(2,1)}, bf16[4,144,1152]{2,1,0:T(8,128)(2,1)}) custom-call(bf16[1152,768]{1,0:T(8,128)(2,1)} %get-tuple-element.316.refs_0_, bf16[1152,768]{1,0:T(8,128)(2,1)} %collective-permute-done.36.refs_1_, ...), custom_call_target="tpu_custom_call" | custom-call | flops 521838526464 | bytes 1245708288 | tf_op jit(solution)/shard_map/ff_grad/pallas_call | solution.py:556
  264.6 1.7 collective-permute-start.42
  266.6 21.3 %ff_back.1 = (f32[768,1152]{1,0:T(8,128)}, f32[1,1152]{1,0:T(1,128)}, f32[1,1152]{1,0:T(1,128)}, bf16[768,1152]{1,0:T(8,128)(2,1)}, bf16[1152,768]{1,0:T(8,128)(2,1)}, /*index=5*/f32[1,1152]{1,0:T(1,128)}) custom-call(s32[8]{0:T(128)} %stack.125.refs_0_, bf16[768,4608]{1,0:T(8,128)(2,1)} %get-tuple-element.364.refs_1_.refs_2_, ...), custom_call_target="tpu_custom_call" | custom-call | flops 521838526464 | bytes 1132462080 | tf_op jit(solution)/shard_map/ff_back/pallas_call | solution.py:485
  288.0 11.1 %attn_bwd.4 = (bf16[768,1152]{1,0:T(8,128)(2,1)}, f32[1,864]{1,0:T(1,128)}) custom-call(bf16[768,864]{1,0:T(8,128)(2,1)} %get-tuple-element.349.proj, bf16[768,288]{1,0:T(8,128)(2,1)} %get-tuple-element.309.refs_8_.mixed, f32[8,768]{1,0:T(8,128)} %get-tuple-element.350.lse, bf16[768,1152]{1,0:T(8,128)(2,1)} %get-tuple-element.384.ga, ...), custom_call_target="tpu_custom_call" | custom-call | flops 419161964544 | bytes 495452160 | tf_op jit(solution)/shard_map/attn_bwd/pallas_call | solution.py:192
  299.6 11.7 %attn_bwd.5 = (bf16[768,1152]{1,0:T(8,128)(2,1)}, f32[1,864]{1,0:T(1,128)}) custom-call(bf16[768,864]{1,0:T(8,128)(2,1)} %get-tuple-element.275.proj, bf16[768,288]{1,0:T(8,128)(2,1)} %get-tuple-element.274.refs_6_.mixed, f32[8,768]{1,0:T(8,128)} %get-tuple-element.276.lse, bf16[768,1152]{1,0:T(8,128)(2,1)} %get-tuple-element.384.ga, ...), custom_call_target="tpu_custom_call" | custom-call | flops 419161964544 | bytes 495452160 | tf_op jit(solution)/shard_map/attn_bwd/pallas_call | solution.py:192
  311.3 2.7 add_convert_fusion.1
  315.5 10.7 %attn_grad.2 = (bf16[288,1152]{1,0:T(8,128)(2,1)}, bf16[288,1152]{1,0:T(8,128)(2,1)}, bf16[288,1152]{1,0:T(8,128)(2,1)}, bf16[288,1152]{1,0:T(8,128)(2,1)}) custom-call(bf16[1152,768]{1,0:T(8,128)(2,1)} %get-tuple-element.409.refs_0_, bf16[1152,768]{1,0:T(8,128)(2,1)} %collective-permute-done.12.refs_1_, bf16[1152,768]{1,0:T(8,128)(2,1)} %get-tuple-element.346.refs_2_, ...), custom_call_target="tpu_custom_call" | custom-call | flops 260919263232 | bytes 566231040 | tf_op jit(solution)/shard_map/attn_grad/pallas_call | solution.py:597
  328.2 14.7 %ff_grad.3 = (bf16[2,144,1152]{2,1,0:T(8,128)(2,1)}, bf16[2,144,1152]{2,1,0:T(8,128)(2,1)}, bf16[2,144,1152]{2,1,0:T(8,128)(2,1)}, bf16[2,144,1152]{2,1,0:T(8,12...) custom-call(bf16[1152,768]{1,0:T(8,128)(2,1)} %get-tuple-element.323, ...), custom_call_target="tpu_custom_call" | custom-call | flops 521838526464 | bytes 1245708288 | tf_op jit(solution)/shard_map/ff_grad/pallas_call | solution.py:556
  343.0 2.4 collective-permute-done.46
  345.4 2.2 add_convert_fusion
  351.1 11.3 %attn_bwd.6 = (bf16[768,1152]{1,0:T(8,128)(2,1)}, f32[1,864]{1,0:T(1,128)}) custom-call(bf16[768,864]{1,0:T(8,128)(2,1)} %get-tuple-element.292.proj, bf16[768,288]{1,0:T(8,128)(2,1)} %get-tuple-element.291.refs_7_.mixed, f32[8,768]{1,0:T(8,128)} %get-tuple-element.293.lse, bf16[768,1152]{1,0:T(8,128)(2,1)} %get-tuple-element.384.ga, ...), custom_call_target="tpu_custom_call" | custom-call | flops 419161964544 | bytes 495452160 | tf_op jit(solution)/shard_map/attn_bwd/pallas_call | solution.py:192
  363.7 3.2 collective-permute-done.50
  366.9 1.9 fusion.7
  369.3 2.1 add_convert_fusion.7
  371.9 1.7 collective-permute-start.54
  373.7 11.2 %attn_bwd.7 = (bf16[768,1152]{1,0:T(8,128)(2,1)}, f32[1,864]{1,0:T(1,128)}) custom-call(bf16[768,864]{1,0:T(8,128)(2,1)} %get-tuple-element.257.proj, bf16[768,288]{1,0:T(8,128)(2,1)} %get-tuple-element.256.refs_5_.mixed, f32[8,768]{1,0:T(8,128)} %get-tuple-element.258.lse, bf16[768,1152]{1,0:T(8,128)(2,1)} %get-tuple-element.384.ga, ...), custom_call_target="tpu_custom_call" | custom-call | flops 419161964544 | bytes 495452160 | tf_op jit(solution)/shard_map/attn_bwd/pallas_call | solution.py:192
  386.5 2.5 collective-permute-done.52
  389.2 1.9 fusion.6
  395.1 19.0 %attn_back.1 = (f32[729,1152]{1,0:T(8,128)}, f32[1,1152]{1,0:T(1,128)}, f32[1,1152]{1,0:T(1,128)}) custom-call(bf16[768,1152]{1,0:T(8,128)(2,1)} %get-tuple-element.405.refs_0_.refs_4_, bf16[768,1152]{1,0:T(8,128)(2,1)} %get-tuple-element.356.refs_4_.refs_1_, bf16[768,1152]{1,0:T(8,128)(2,1)} %get-tuple-element.386.refs_2_, ...), custom_call_target="tpu_custom_call" | custom-call | flops 391378894848 | bytes 1019215872 | tf_op jit(solution)/shard_map/attn_back/pallas_call | solution.py:520
  418.1 2.1 add_convert_fusion.5
  420.2 1.7 collective-permute-start.63
  421.9 11.6 %attn_grad.3 = (bf16[288,1152]{1,0:T(8,128)(2,1)}, bf16[288,1152]{1,0:T(8,128)(2,1)}, bf16[288,1152]{1,0:T(8,128)(2,1)}, bf16[288,1152]{1,0:T(8,128)(2,1)}) custom-call(bf16[1152,768]{1,0:T(8,128)(2,1)} %get-tuple-element.409.refs_0_, bf16[1152,768]{1,0:T(8,128)(2,1)} %collective-permute-done.12.refs_1_, bf16[1152,768]{1,0:T(8,128)(2,1)} %get-tuple-element.346.refs_2_, ...), custom_call_target="tpu_custom_call" | custom-call | flops 260919263232 | bytes 566231040 | tf_op jit(solution)/shard_map/attn_grad/pallas_call | solution.py:597
  435.7 1.7 add_convert_fusion.6
  437.5 3.3 collective-permute-start.62
  441.8 1.9 fusion.3
  443.7 2.1 collective-permute-done.63
  445.8 2.0 collective-permute-done.64
  454.1 1.9 collective-permute-start.69
  456.0 1.6 fusion.2
  459.3 5.2 %copy.33 = f32[1,729,1152]{2,0,1:T(1,128)} copy(f32[1,729,1152]{2,1,0:T(8,128)S(1)} %bitcast.72) | data formatting | bytes 6718464
  464.5 15.5 %collective-permute-done.68 = bf16[144,1152]{1,0:T(8,128)(2,1)S(1)} collective-permute-done((bf16[144,1152]{1,0:T(8,128)(2,1)S(1)}, bf16[144,1152]{1,0:T(8,128)(2,1)S(1)}, u32[]{:S(2)}, u32[]{:S(2)}) %collective-permute-start.68) | collective-permute-done | bytes 331808 | tf_op jit(solution)/shard_map/ppermute | solution.py:609
  480.7 3.7 collective-permute-done.70
  484.6 7.6 %collective-permute-start.73 = (bf16[144,1152]{1,0:T(8,128)(2,1)S(1)}, bf16[144,1152]{1,0:T(8,128)(2,1)S(1)}, u32[]{:S(2)}, u32[]{:S(2)}) collective-permute-start(bf16[144,1152]{1,0:T(8,128)(2,1)S(1)} %fusion.4), channel_id=1, source_target_pairs={{0,3},{1,0},{2,1},{3,2},{4,7},{5,4},{6,5},{7,6},{8,11},{9,8},{10,9... | collective-permute-start | bytes 995336 | tf_op jit(solution)/shard_map/ppermute | solution.py:609
  494.5 2.8 collective-permute-done.72
  500.7 2.9 collective-permute-done.73
  (356 shorter events, 83.0 us)
Async XLA Ops:
  7.2 191.9 %all-gather.2.cloned.1.call-start = ((), (), s32[]{:S(2)}) async-start(), calls=%async_computation | async-start | bytes 10948608 | tf_op jit(solution)/shard_map/all_gather | solution.py:818
  9.2 14.9 %collective-permute-start.2 = (bf16[144,1152]{1,0:T(8,128)(2,1)}, bf16[144,1152]{1,0:T(8,128)(2,1)S(1)}, u32[]{:S(2)}, u32[]{:S(2)}) collective-permute-start(bf16[144,1152]{1,0:T(8,128)(2,1)} %pad.35), channel_id=1, source_target_pairs={{0,8},{8,0},{1,9},{9,1},{2,10},{10,2},{3,11},{11,3},{4,12},{12,4},... | collective-permute-start | bytes 995336 | tf_op jit(solution)/shard_map/ppermute | solution.py:609
  24.2 23.0 %collective-permute-start.4 = (bf16[288,1152]{1,0:T(8,128)(2,1)S(1)}, bf16[288,1152]{1,0:T(8,128)(2,1)S(1)}, u32[]{:S(2)}, u32[]{:S(2)}) collective-permute-start(bf16[288,1152]{1,0:T(8,128)(2,1)S(1)} %pad_maximum_fusion.2.refs_3_), channel_id=1, source_target_pairs={{0,1},{1,2},{2,3},{3,0},{4,5},{5,6},{6,7},{7,4},{8,9},{9,10},{10,1... | collective-permute-start | bytes 1990664 | tf_op jit(solution)/shard_map/ppermute | solution.py:609
  27.1 20.0 %collective-permute-start.5 = (bf16[288,1152]{1,0:T(8,128)(2,1)S(1)}, bf16[288,1152]{1,0:T(8,128)(2,1)}, u32[]{:S(2)}, u32[]{:S(2)}) collective-permute-start(bf16[288,1152]{1,0:T(8,128)(2,1)S(1)} %pad_maximum_fusion.3.refs_4_), channel_id=1, source_target_pairs={{0,16},{16,0},{1,17},{17,1},{2,18},{18,2},{3,19},{19,3},{4,20},{20... | collective-permute-start | bytes 1990664 | tf_op jit(solution)/shard_map/ppermute | solution.py:609
  28.7 18.5 %collective-permute-start.7 = (bf16[288,1152]{1,0:T(8,128)(2,1)S(1)}, bf16[288,1152]{1,0:T(8,128)(2,1)S(1)}, u32[]{:S(2)}, u32[]{:S(2)}) collective-permute-start(bf16[288,1152]{1,0:T(8,128)(2,1)S(1)} %pad_maximum_fusion.2.refs_3_), channel_id=1, source_target_pairs={{0,4},{4,0},{1,5},{5,1},{2,6},{6,2},{3,7},{7,3},{8,12},{12,8},{9,1... | collective-permute-start | bytes 1990664 | tf_op jit(solution)/shard_map/ppermute | solution.py:609
  28.7 18.4 %collective-permute-start.6 = (bf16[144,1152]{1,0:T(8,128)(2,1)S(1)}, bf16[144,1152]{1,0:T(8,128)(2,1)S(1)}, u32[]{:S(2)}, u32[]{:S(2)}) collective-permute-start(bf16[144,1152]{1,0:T(8,128)(2,1)S(1)} %collective-permute-done.3), channel_id=1, source_target_pairs={{0,8},{8,0},{1,9},{9,1},{2,10},{10,2},{3,11},{11,3},{4,12},{12,4},... | collective-permute-start | bytes 995336 | tf_op jit(solution)/shard_map/ppermute | solution.py:609
  47.2 23.7 %collective-permute-start.12 = (bf16[1152,768]{1,0:T(8,128)(2,1)}, bf16[1152,768]{1,0:T(8,128)(2,1)}, u32[]{:S(2)}, u32[]{:S(2)}) collective-permute-start(bf16[1152,768]{1,0:T(8,128)(2,1)} %get-tuple-element.409.refs_0_), channel_id=1, source_target_pairs={{0,4},{4,0},{1,5},{5,1},{2,6},{6,2},{3,7},{7,3},{8,12},{12,8},{9,1... | collective-permute-start | bytes 5308424 | tf_op jit(solution)/shard_map/ppermute | solution.py:609
  48.1 21.8 %collective-permute-start.8 = (bf16[288,1152]{1,0:T(8,128)(2,1)S(1)}, bf16[288,1152]{1,0:T(8,128)(2,1)S(1)}, u32[]{:S(2)}, u32[]{:S(2)}) collective-permute-start(bf16[288,1152]{1,0:T(8,128)(2,1)S(1)} %collective-permute-done.4.refs_4_), channel_id=1, source_target_pairs={{0,1},{1,2},{2,3},{3,0},{4,5},{5,6},{6,7},{7,4},{8,9},{9,10},{10,1... | collective-permute-start | bytes 1990664 | tf_op jit(solution)/shard_map/ppermute | solution.py:609
  49.7 20.2 %collective-permute-start.9 = (bf16[288,1152]{1,0:T(8,128)(2,1)S(1)}, bf16[288,1152]{1,0:T(8,128)(2,1)S(1)}, u32[]{:S(2)}, u32[]{:S(2)}) collective-permute-start(bf16[288,1152]{1,0:T(8,128)(2,1)S(1)} %collective-permute-done.4.refs_4_), channel_id=1, source_target_pairs={{0,4},{4,0},{1,5},{5,1},{2,6},{6,2},{3,7},{7,3},{8,12},{12,8},{9,1... | collective-permute-start | bytes 1990664 | tf_op jit(solution)/shard_map/ppermute | solution.py:609
  51.8 19.1 %collective-permute-start.10 = (bf16[320,1152]{1,0:T(8,128)(2,1)}, bf16[320,1152]{1,0:T(8,128)(2,1)S(1)}, u32[]{:S(2)}, u32[]{:S(2)}) collective-permute-start(bf16[320,1152]{1,0:T(8,128)(2,1)} %pad_maximum_fusion), channel_id=1, source_target_pairs={{0,16},{16,0},{1,17},{17,1},{2,18},{18,2},{3,19},{19,3},{4,20},{20... | collective-permute-start | bytes 2211848 | tf_op jit(solution)/shard_map/ppermute | solution.py:609
  54.1 15.8 %collective-permute-start.11 = (bf16[256,1152]{1,0:T(8,128)(2,1)}, bf16[256,1152]{1,0:T(8,128)(2,1)}, u32[]{:S(2)}, u32[]{:S(2)}) collective-permute-start(bf16[256,1152]{1,0:T(8,128)(2,1)} %pad_maximum_fusion.4), channel_id=1, source_target_pairs={{0,8},{8,0},{1,9},{9,1},{2,10},{10,2},{3,11},{11,3},{4,12},{12,4},... | collective-permute-start | bytes 1769480 | tf_op jit(solution)/shard_map/ppermute | solution.py:609
  70.9 22.0 %collective-permute-start.15 = (bf16[320,1152]{1,0:T(8,128)(2,1)S(1)}, bf16[320,1152]{1,0:T(8,128)(2,1)S(1)}, u32[]{:S(2)}, u32[]{:S(2)}) collective-permute-start(bf16[320,1152]{1,0:T(8,128)(2,1)S(1)} %collective-permute-done.10.refs_7_), channel_id=1, source_target_pairs={{0,4},{4,0},{1,5},{5,1},{2,6},{6,2},{3,7},{7,3},{8,12},{12,8},{9,1... | collective-permute-start | bytes 2211848 | tf_op jit(solution)/shard_map/ppermute | solution.py:609
  72.9 17.4 %collective-permute-start.17 = (bf16[288,1152]{1,0:T(8,128)(2,1)}, bf16[288,1152]{1,0:T(8,128)(2,1)}, u32[]{:S(2)}, u32[]{:S(2)}) collective-permute-start(bf16[288,1152]{1,0:T(8,128)(2,1)} %constant_dynamic-update-slice_fusion.refs_5_), channel_id=1, source_target_pairs={{0,16},{16,0},{1,17},{17,1},{2,18},{18,2},{3,19},{19,3},{4,20},{20... | collective-permute-start | bytes 1990664 | tf_op jit(solution)/shard_map/ppermute | solution.py:609
  74.3 18.6 %collective-permute-start.13 = (bf16[288,1152]{1,0:T(8,128)(2,1)S(1)}, bf16[288,1152]{1,0:T(8,128)(2,1)S(1)}, u32[]{:S(2)}, u32[]{:S(2)}) collective-permute-start(bf16[288,1152]{1,0:T(8,128)(2,1)S(1)} %collective-permute-done.8.refs_5_), channel_id=1, source_target_pairs={{0,1},{1,2},{2,3},{3,0},{4,5},{5,6},{6,7},{7,4},{8,9},{9,10},{10,1... | collective-permute-start | bytes 1990664 | tf_op jit(solution)/shard_map/ppermute | solution.py:609
  75.8 17.0 %collective-permute-start.14 = (bf16[288,1152]{1,0:T(8,128)(2,1)S(1)}, bf16[288,1152]{1,0:T(8,128)(2,1)}, u32[]{:S(2)}, u32[]{:S(2)}) collective-permute-start(bf16[288,1152]{1,0:T(8,128)(2,1)S(1)} %collective-permute-done.8.refs_5_), channel_id=1, source_target_pairs={{0,4},{4,0},{1,5},{5,1},{2,6},{6,2},{3,7},{7,3},{8,12},{12,8},{9,1... | collective-permute-start | bytes 1990664 | tf_op jit(solution)/shard_map/ppermute | solution.py:609
  75.8 14.5 %collective-permute-start.16 = (bf16[256,1152]{1,0:T(8,128)(2,1)}, bf16[256,1152]{1,0:T(8,128)(2,1)}, u32[]{:S(2)}, u32[]{:S(2)}) collective-permute-start(bf16[256,1152]{1,0:T(8,128)(2,1)} %collective-permute-done.11.refs_9_), channel_id=1, source_target_pairs={{0,4},{4,0},{1,5},{5,1},{2,6},{6,2},{3,7},{7,3},{8,12},{12,8},{9,1... | collective-permute-start | bytes 1769480 | tf_op jit(solution)/shard_map/ppermute | solution.py:609
  93.9 19.0 %collective-permute-start.20 = (bf16[288,1152]{1,0:T(8,128)(2,1)S(1)}, bf16[288,1152]{1,0:T(8,128)(2,1)S(1)}, u32[]{:S(2)}, u32[]{:S(2)}) collective-permute-start(bf16[288,1152]{1,0:T(8,128)(2,1)S(1)} %collective-permute-done.13.refs_6_), channel_id=1, source_target_pairs={{0,4},{4,0},{1,5},{5,1},{2,6},{6,2},{3,7},{7,3},{8,12},{12,8},{9,1... | collective-permute-start | bytes 1990664 | tf_op jit(solution)/shard_map/ppermute | solution.py:609
  94.0 21.3 %collective-permute-start.18 = (bf16[320,1152]{1,0:T(8,128)(2,1)S(1)}, bf16[320,1152]{1,0:T(8,128)(2,1)S(1)}, u32[]{:S(2)}, u32[]{:S(2)}) collective-permute-start(bf16[320,1152]{1,0:T(8,128)(2,1)S(1)} %pad_maximum_fusion.1), channel_id=1, source_target_pairs={{0,16},{16,0},{1,17},{17,1},{2,18},{18,2},{3,19},{19,3},{4,20},{20... | collective-permute-start | bytes 2211848 | tf_op jit(solution)/shard_map/ppermute | solution.py:609
  94.8 18.2 %collective-permute-start.22 = (bf16[288,1152]{1,0:T(8,128)(2,1)S(1)}, bf16[288,1152]{1,0:T(8,128)(2,1)S(1)}, u32[]{:S(2)}, u32[]{:S(2)}) collective-permute-start(bf16[288,1152]{1,0:T(8,128)(2,1)S(1)} %pad_maximum_fusion.3.refs_4_), channel_id=1, source_target_pairs={{0,4},{4,0},{1,5},{5,1},{2,6},{6,2},{3,7},{7,3},{8,12},{12,8},{9,1... | collective-permute-start | bytes 1990664 | tf_op jit(solution)/shard_map/ppermute | solution.py:609
  95.0 17.9 %collective-permute-start.19 = (bf16[256,1152]{1,0:T(8,128)(2,1)S(1)}, bf16[256,1152]{1,0:T(8,128)(2,1)S(1)}, u32[]{:S(2)}, u32[]{:S(2)}) collective-permute-start(bf16[256,1152]{1,0:T(8,128)(2,1)S(1)} %pad_maximum_fusion.5), channel_id=1, source_target_pairs={{0,8},{8,0},{1,9},{9,1},{2,10},{10,2},{3,11},{11,3},{4,12},{12,4},... | collective-permute-start | bytes 1769480 | tf_op jit(solution)/shard_map/ppermute | solution.py:609
  95.6 16.7 %collective-permute-start.21 = (bf16[144,1152]{1,0:T(8,128)(2,1)S(1)}, bf16[144,1152]{1,0:T(8,128)(2,1)}, u32[]{:S(2)}, u32[]{:S(2)}) collective-permute-start(bf16[144,1152]{1,0:T(8,128)(2,1)S(1)} %copy-done.44), channel_id=1, source_target_pairs={{0,1},{1,2},{2,3},{3,0},{4,5},{5,6},{6,7},{7,4},{8,9},{9,10},{10,1... | collective-permute-start | bytes 995336 | tf_op jit(solution)/shard_map/ppermute | solution.py:609
  115.3 20.9 %collective-permute-start.25 = (bf16[320,1152]{1,0:T(8,128)(2,1)S(1)}, bf16[320,1152]{1,0:T(8,128)(2,1)S(1)}, u32[]{:S(2)}, u32[]{:S(2)}) collective-permute-start(bf16[320,1152]{1,0:T(8,128)(2,1)S(1)} %collective-permute-done.18.refs_8_), channel_id=1, source_target_pairs={{0,4},{4,0},{1,5},{5,1},{2,6},{6,2},{3,7},{7,3},{8,12},{12,8},{9,1... | collective-permute-start | bytes 2211848 | tf_op jit(solution)/shard_map/ppermute | solution.py:609
  115.4 20.9 %collective-permute-start.27 = (bf16[288,1152]{1,0:T(8,128)(2,1)}, bf16[288,1152]{1,0:T(8,128)(2,1)}, u32[]{:S(2)}, u32[]{:S(2)}) collective-permute-start(bf16[288,1152]{1,0:T(8,128)(2,1)} %collective-permute-done.5.refs_8_), channel_id=1, source_target_pairs={{0,4},{4,0},{1,5},{5,1},{2,6},{6,2},{3,7},{7,3},{8,12},{12,8},{9,1... | collective-permute-start | bytes 1990664 | tf_op jit(solution)/shard_map/ppermute | solution.py:609
  115.9 20.4 %collective-permute-start.26 = (bf16[256,1152]{1,0:T(8,128)(2,1)S(1)}, bf16[256,1152]{1,0:T(8,128)(2,1)S(1)}, u32[]{:S(2)}, u32[]{:S(2)}) collective-permute-start(bf16[256,1152]{1,0:T(8,128)(2,1)S(1)} %collective-permute-done.19.refs_10_), channel_id=1, source_target_pairs={{0,4},{4,0},{1,5},{5,1},{2,6},{6,2},{3,7},{7,3},{8,12},{12,8},{9,1... | collective-permute-start | bytes 1769480 | tf_op jit(solution)/shard_map/ppermute | solution.py:609
  115.9 14.7 %collective-permute-start.23 = (bf16[144,1152]{1,0:T(8,128)(2,1)}, bf16[144,1152]{1,0:T(8,128)(2,1)}, u32[]{:S(2)}, u32[]{:S(2)}) collective-permute-start(bf16[144,1152]{1,0:T(8,128)(2,1)} %collective-permute-done.21), channel_id=1, source_target_pairs={{0,8},{8,0},{1,9},{9,1},{2,10},{10,2},{3,11},{11,3},{4,12},{12,4},... | collective-permute-start | bytes 995336 | tf_op jit(solution)/shard_map/ppermute | solution.py:609
  116.5 19.8 %collective-permute-start.24 = (bf16[144,1152]{1,0:T(8,128)(2,1)}, bf16[144,1152]{1,0:T(8,128)(2,1)S(1)}, u32[]{:S(2)}, u32[]{:S(2)}) collective-permute-start(bf16[144,1152]{1,0:T(8,128)(2,1)} %pad.35), channel_id=1, source_target_pairs={{0,3},{1,0},{2,1},{3,2},{4,7},{5,4},{6,5},{7,6},{8,11},{9,8},{10,9... | collective-permute-start | bytes 995336 | tf_op jit(solution)/shard_map/ppermute | solution.py:609
  137.5 25.7 %collective-permute-start.29 = (bf16[288,1152]{1,0:T(8,128)(2,1)S(1)}, bf16[288,1152]{1,0:T(8,128)(2,1)S(1)}, u32[]{:S(2)}, u32[]{:S(2)}) collective-permute-start(bf16[288,1152]{1,0:T(8,128)(2,1)S(1)} %constant_dynamic-update-slice_fusion.2.refs_6_), channel_id=1, source_target_pairs={{0,16},{16,0},{1,17},{17,1},{2,18},{18,2},{3,19},{19,3},{4,20},{20... | collective-permute-start | bytes 1990664 | tf_op jit(solution)/shard_map/ppermute | solution.py:609
  137.8 25.4 %collective-permute-start.30 = (bf16[288,1152]{1,0:T(8,128)(2,1)}, bf16[288,1152]{1,0:T(8,128)(2,1)S(1)}, u32[]{:S(2)}, u32[]{:S(2)}) collective-permute-start(bf16[288,1152]{1,0:T(8,128)(2,1)} %constant_dynamic-update-slice_fusion.refs_5_), channel_id=1, source_target_pairs={{0,4},{4,0},{1,5},{5,1},{2,6},{6,2},{3,7},{7,3},{8,12},{12,8},{9,1... | collective-permute-start | bytes 1990664 | tf_op jit(solution)/shard_map/ppermute | solution.py:609
  137.8 25.5 %collective-permute-start.31 = (bf16[288,1152]{1,0:T(8,128)(2,1)}, bf16[288,1152]{1,0:T(8,128)(2,1)}, u32[]{:S(2)}, u32[]{:S(2)}) collective-permute-start(bf16[288,1152]{1,0:T(8,128)(2,1)} %collective-permute-done.17.refs_9_), channel_id=1, source_target_pairs={{0,4},{4,0},{1,5},{5,1},{2,6},{6,2},{3,7},{7,3},{8,12},{12,8},{9,1... | collective-permute-start | bytes 1990664 | tf_op jit(solution)/shard_map/ppermute | solution.py:609
  163.1 21.1 %collective-permute-start.34 = (bf16[288,1152]{1,0:T(8,128)(2,1)S(1)}, bf16[288,1152]{1,0:T(8,128)(2,1)S(1)}, u32[]{:S(2)}, u32[]{:S(2)}) collective-permute-start(bf16[288,1152]{1,0:T(8,128)(2,1)S(1)} %constant_dynamic-update-slice_fusion.2.refs_6_), channel_id=1, source_target_pairs={{0,4},{4,0},{1,5},{5,1},{2,6},{6,2},{3,7},{7,3},{8,12},{12,8},{9,1... | collective-permute-start | bytes 1990664 | tf_op jit(solution)/shard_map/ppermute | solution.py:609
  163.3 21.0 %collective-permute-start.35 = (bf16[288,1152]{1,0:T(8,128)(2,1)S(1)}, bf16[288,1152]{1,0:T(8,128)(2,1)S(1)}, u32[]{:S(2)}, u32[]{:S(2)}) collective-permute-start(bf16[288,1152]{1,0:T(8,128)(2,1)S(1)} %collective-permute-done.29.refs_10_), channel_id=1, source_target_pairs={{0,4},{4,0},{1,5},{5,1},{2,6},{6,2},{3,7},{7,3},{8,12},{12,8},{9,1... | collective-permute-start | bytes 1990664 | tf_op jit(solution)/shard_map/ppermute | solution.py:609
  165.8 18.4 %collective-permute-start.33 = (bf16[144,1152]{1,0:T(8,128)(2,1)}, bf16[144,1152]{1,0:T(8,128)(2,1)}, u32[]{:S(2)}, u32[]{:S(2)}) collective-permute-start(bf16[144,1152]{1,0:T(8,128)(2,1)} %collective-permute-done.28), channel_id=1, source_target_pairs={{0,16},{16,0},{1,17},{17,1},{2,18},{18,2},{3,19},{19,3},{4,20},{20... | collective-permute-start | bytes 995336 | tf_op jit(solution)/shard_map/ppermute | solution.py:609
  165.8 33.3 %collective-permute-start.36 = (bf16[1152,768]{1,0:T(8,128)(2,1)}, bf16[1152,768]{1,0:T(8,128)(2,1)}, u32[]{:S(2)}, u32[]{:S(2)}) collective-permute-start(bf16[1152,768]{1,0:T(8,128)(2,1)} %get-tuple-element.316.refs_0_), channel_id=1, source_target_pairs={{0,4},{4,0},{1,5},{5,1},{2,6},{6,2},{3,7},{7,3},{8,12},{12,8},{9,1... | collective-permute-start | bytes 5308424 | tf_op jit(solution)/shard_map/ppermute | solution.py:609
  195.2 23.8 %collective-permute-start.39 = (bf16[1152,768]{1,0:T(8,128)(2,1)}, bf16[1152,768]{1,0:T(8,128)(2,1)}, u32[]{:S(2)}, u32[]{:S(2)}) collective-permute-start(bf16[1152,768]{1,0:T(8,128)(2,1)} %get-tuple-element.323.refs_0_), channel_id=1, source_target_pairs={{0,4},{4,0},{1,5},{5,1},{2,6},{6,2},{3,7},{7,3},{8,12},{12,8},{9,1... | collective-permute-start | bytes 5308424 | tf_op jit(solution)/shard_map/ppermute | solution.py:609
  196.3 22.6 %collective-permute-start.37 = (bf16[288,1152]{1,0:T(8,128)(2,1)S(1)}, bf16[288,1152]{1,0:T(8,128)(2,1)S(1)}, u32[]{:S(2)}, u32[]{:S(2)}) collective-permute-start(bf16[288,1152]{1,0:T(8,128)(2,1)S(1)} %constant_dynamic-update-slice_fusion.4.refs_7_), channel_id=1, source_target_pairs={{0,4},{4,0},{1,5},{5,1},{2,6},{6,2},{3,7},{7,3},{8,12},{12,8},{9,1... | collective-permute-start | bytes 1990664 | tf_op jit(solution)/shard_map/ppermute | solution.py:609
  198.9 20.0 %collective-permute-start.38 = (bf16[288,1152]{1,0:T(8,128)(2,1)S(1)}, bf16[288,1152]{1,0:T(8,128)(2,1)S(1)}, u32[]{:S(2)}, u32[]{:S(2)}) collective-permute-start(bf16[288,1152]{1,0:T(8,128)(2,1)S(1)} %constant_dynamic-update-slice_fusion.6.refs_11_), channel_id=1, source_target_pairs={{0,4},{4,0},{1,5},{5,1},{2,6},{6,2},{3,7},{7,3},{8,12},{12,8},{9,1... | collective-permute-start | bytes 1990664 | tf_op jit(solution)/shard_map/ppermute | solution.py:609
  218.9 31.3 %collective-permute-start.40 = (bf16[768,4608]{1,0:T(8,128)(2,1)}, bf16[768,4608]{1,0:T(8,128)(2,1)}, u32[]{:S(2)}, u32[]{:S(2)}) collective-permute-start(bf16[768,4608]{1,0:T(8,128)(2,1)} %get-tuple-element.324.refs_2_), channel_id=1, source_target_pairs={{0,4},{4,0},{1,5},{5,1},{2,6},{6,2},{3,7},{7,3},{8,12},{12,8},{9,1... | collective-permute-start | bytes 21233672 | tf_op jit(solution)/shard_map/ppermute | solution.py:609
  250.2 37.8 %collective-permute-start.41 = (bf16[768,4608]{1,0:T(8,128)(2,1)}, bf16[768,4608]{1,0:T(8,128)(2,1)}, u32[]{:S(2)}, u32[]{:S(2)}) collective-permute-start(bf16[768,4608]{1,0:T(8,128)(2,1)} %get-tuple-element.364.refs_1_.refs_2_), channel_id=1, source_target_pairs={{0,4},{4,0},{1,5},{5,1},{2,6},{6,2},{3,7},{7,3},{8,12},{12,8},{9,1... | collective-permute-start | bytes 21233672 | tf_op jit(solution)/shard_map/ppermute | solution.py:609
  264.6 35.0 %collective-permute-start.42 = (bf16[4,144,1152]{2,1,0:T(8,128)(2,1)}, bf16[4,144,1152]{2,1,0:T(8,128)(2,1)}, u32[]{:S(2)}, u32[]{:S(2)}) collective-permute-start(bf16[4,144,1152]{2,1,0:T(8,128)(2,1)} %get-tuple-element.343), channel_id=1, source_target_pairs={{0,8},{8,0},{1,9},{9,1},{2,10},{10,2},{3,11},{11,3},{4,12},{12,4},... | collective-permute-start | bytes 3981320 | tf_op jit(solution)/shard_map/ppermute | solution.py:609
  266.3 76.7 %collective-permute-start.45 = (bf16[4,144,1152]{2,1,0:T(8,128)(2,1)}, bf16[4,144,1152]{2,1,0:T(8,128)(2,1)}, u32[]{:S(2)}, u32[]{:S(2)}) collective-permute-start(bf16[4,144,1152]{2,1,0:T(8,128)(2,1)} %get-tuple-element.341), channel_id=1, source_target_pairs={{0,8},{8,0},{1,9},{9,1},{2,10},{10,2},{3,11},{11,3},{4,12},{12,4},... | collective-permute-start | bytes 3981320 | tf_op jit(solution)/shard_map/ppermute | solution.py:609
  287.9 27.6 %collective-permute-start.44 = (bf16[1152,768]{1,0:T(8,128)(2,1)}, bf16[1152,768]{1,0:T(8,128)(2,1)}, u32[]{:S(2)}, u32[]{:S(2)}) collective-permute-start(bf16[1152,768]{1,0:T(8,128)(2,1)} %get-tuple-element.346.refs_2_), channel_id=1, source_target_pairs={{0,4},{4,0},{1,5},{5,1},{2,6},{6,2},{3,7},{7,3},{8,12},{12,8},{9,1... | collective-permute-start | bytes 5308424 | tf_op jit(solution)/shard_map/ppermute | solution.py:609
  299.1 16.4 %collective-permute-start.43 = (bf16[768,1152]{1,0:T(8,128)(2,1)}, bf16[768,1152]{1,0:T(8,128)(2,1)}, u32[]{:S(2)}, u32[]{:S(2)}) collective-permute-start(bf16[768,1152]{1,0:T(8,128)(2,1)} %get-tuple-element.351.refs_3_), channel_id=1, source_target_pairs={{0,4},{4,0},{1,5},{5,1},{2,6},{6,2},{3,7},{7,3},{8,12},{12,8},{9,1... | collective-permute-start | bytes 5308424 | tf_op jit(solution)/shard_map/ppermute | solution.py:609
  314.0 31.4 %collective-permute-start.46 = (bf16[4,144,1152]{2,1,0:T(8,128)(2,1)}, bf16[4,144,1152]{2,1,0:T(8,128)(2,1)}, u32[]{:S(2)}, u32[]{:S(2)}) collective-permute-start(bf16[4,144,1152]{2,1,0:T(8,128)(2,1)} %add_convert_fusion.1), channel_id=1, source_target_pairs={{0,16},{16,0},{1,17},{17,1},{2,18},{18,2},{3,19},{19,3},{4,20},{20... | collective-permute-start | bytes 3981320 | tf_op jit(solution)/shard_map/ppermute | solution.py:609
  326.2 37.5 %collective-permute-start.48 = (bf16[288,1152]{1,0:T(8,128)(2,1)}, bf16[288,1152]{1,0:T(8,128)(2,1)}, u32[]{:S(2)}, u32[]{:S(2)}) collective-permute-start(bf16[288,1152]{1,0:T(8,128)(2,1)} %get-tuple-element.362), channel_id=1, source_target_pairs={{0,8},{8,0},{1,9},{9,1},{2,10},{10,2},{3,11},{11,3},{4,12},{12,4},... | collective-permute-start | bytes 1990664 | tf_op jit(solution)/shard_map/ppermute | solution.py:609
  327.8 35.8 %collective-permute-start.49 = (bf16[288,1152]{1,0:T(8,128)(2,1)}, bf16[288,1152]{1,0:T(8,128)(2,1)}, u32[]{:S(2)}, u32[]{:S(2)}) collective-permute-start(bf16[288,1152]{1,0:T(8,128)(2,1)} %get-tuple-element.363), channel_id=1, source_target_pairs={{0,8},{8,0},{1,9},{9,1},{2,10},{10,2},{3,11},{11,3},{4,12},{12,4},... | collective-permute-start | bytes 1990664 | tf_op jit(solution)/shard_map/ppermute | solution.py:609
  349.6 14.1 %collective-permute-start.47 = (bf16[144,1152]{1,0:T(8,128)(2,1)}, bf16[144,1152]{1,0:T(8,128)(2,1)}, u32[]{:S(2)}, u32[]{:S(2)}) collective-permute-start(bf16[144,1152]{1,0:T(8,128)(2,1)} %get-tuple-element.501), channel_id=1, source_target_pairs={{0,3},{1,0},{2,1},{3,2},{4,7},{5,4},{6,5},{7,6},{8,11},{9,8},{10,9... | collective-permute-start | bytes 995336 | tf_op jit(solution)/shard_map/ppermute | solution.py:609
  350.8 16.0 %collective-permute-start.50 = (bf16[2,144,1152]{2,1,0:T(8,128)(2,1)}, bf16[2,144,1152]{2,1,0:T(8,128)(2,1)}, u32[]{:S(2)}, u32[]{:S(2)}) collective-permute-start(bf16[2,144,1152]{2,1,0:T(8,128)(2,1)} %get-tuple-element.379), channel_id=1, source_target_pairs={{0,16},{16,0},{1,17},{17,1},{2,18},{18,2},{3,19},{19,3},{4,20},{20... | collective-permute-start | bytes 1990664 | tf_op jit(solution)/shard_map/ppermute | solution.py:609
  368.7 17.8 %collective-permute-start.53 = (bf16[144,1152]{1,0:T(8,128)(2,1)}, bf16[144,1152]{1,0:T(8,128)(2,1)}, u32[]{:S(2)}, u32[]{:S(2)}) collective-permute-start(bf16[144,1152]{1,0:T(8,128)(2,1)} %fusion.7), channel_id=1, source_target_pairs={{0,3},{1,0},{2,1},{3,2},{4,7},{5,4},{6,5},{7,6},{8,11},{9,8},{10,9... | collective-permute-start | bytes 995336 | tf_op jit(solution)/shard_map/ppermute | solution.py:609
  371.4 17.8 %collective-permute-start.51 = (bf16[768,1152]{1,0:T(8,128)(2,1)}, bf16[768,1152]{1,0:T(8,128)(2,1)}, u32[]{:S(2)}, u32[]{:S(2)}) collective-permute-start(bf16[768,1152]{1,0:T(8,128)(2,1)} %get-tuple-element.386.refs_2_), channel_id=1, source_target_pairs={{0,4},{4,0},{1,5},{5,1},{2,6},{6,2},{3,7},{7,3},{8,12},{12,8},{9,1... | collective-permute-start | bytes 5308424 | tf_op jit(solution)/shard_map/ppermute | solution.py:609
  371.4 17.6 %collective-permute-start.52 = (bf16[2,144,1152]{2,1,0:T(8,128)(2,1)}, bf16[2,144,1152]{2,1,0:T(8,128)(2,1)}, u32[]{:S(2)}, u32[]{:S(2)}) collective-permute-start(bf16[2,144,1152]{2,1,0:T(8,128)(2,1)} %get-tuple-element.388), channel_id=1, source_target_pairs={{0,16},{16,0},{1,17},{17,1},{2,18},{18,2},{3,19},{19,3},{4,20},{20... | collective-permute-start | bytes 1990664 | tf_op jit(solution)/shard_map/ppermute | solution.py:609
  371.9 17.4 %collective-permute-start.54 = (bf16[288,1152]{1,0:T(8,128)(2,1)}, bf16[288,1152]{1,0:T(8,128)(2,1)}, u32[]{:S(2)}, u32[]{:S(2)}) collective-permute-start(bf16[288,1152]{1,0:T(8,128)(2,1)} %get-tuple-element.390), channel_id=1, source_target_pairs={{0,8},{8,0},{1,9},{9,1},{2,10},{10,2},{3,11},{11,3},{4,12},{12,4},... | collective-permute-start | bytes 1990664 | tf_op jit(solution)/shard_map/ppermute | solution.py:609
  391.1 24.4 %collective-permute-start.57 = (bf16[144,1152]{1,0:T(8,128)(2,1)}, bf16[144,1152]{1,0:T(8,128)(2,1)}, u32[]{:S(2)}, u32[]{:S(2)}) collective-permute-start(bf16[144,1152]{1,0:T(8,128)(2,1)} %fusion.6), channel_id=1, source_target_pairs={{0,3},{1,0},{2,1},{3,2},{4,7},{5,4},{6,5},{7,6},{8,11},{9,8},{10,9... | collective-permute-start | bytes 995336 | tf_op jit(solution)/shard_map/ppermute | solution.py:609
  392.1 23.3 %collective-permute-start.55 = (bf16[288,1152]{1,0:T(8,128)(2,1)}, bf16[288,1152]{1,0:T(8,128)(2,1)}, u32[]{:S(2)}, u32[]{:S(2)}) collective-permute-start(bf16[288,1152]{1,0:T(8,128)(2,1)} %get-tuple-element.401), channel_id=1, source_target_pairs={{0,8},{8,0},{1,9},{9,1},{2,10},{10,2},{3,11},{11,3},{4,12},{12,4},... | collective-permute-start | bytes 1990664 | tf_op jit(solution)/shard_map/ppermute | solution.py:609
  393.6 21.9 %collective-permute-start.56 = (bf16[2,144,1152]{2,1,0:T(8,128)(2,1)}, bf16[2,144,1152]{2,1,0:T(8,128)(2,1)}, u32[]{:S(2)}, u32[]{:S(2)}) collective-permute-start(bf16[2,144,1152]{2,1,0:T(8,128)(2,1)} %get-tuple-element.403), channel_id=1, source_target_pairs={{0,16},{16,0},{1,17},{17,1},{2,18},{18,2},{3,19},{19,3},{4,20},{20... | collective-permute-start | bytes 1990664 | tf_op jit(solution)/shard_map/ppermute | solution.py:609
  415.5 18.0 %collective-permute-start.58 = (bf16[2,144,1152]{2,1,0:T(8,128)(2,1)}, bf16[2,144,1152]{2,1,0:T(8,128)(2,1)}, u32[]{:S(2)}, u32[]{:S(2)}) collective-permute-start(bf16[2,144,1152]{2,1,0:T(8,128)(2,1)} %get-tuple-element.419), channel_id=1, source_target_pairs={{0,16},{16,0},{1,17},{17,1},{2,18},{18,2},{3,19},{19,3},{4,20},{20... | collective-permute-start | bytes 1990664 | tf_op jit(solution)/shard_map/ppermute | solution.py:609
  416.1 18.2 %collective-permute-start.59 = (bf16[2,144,1152]{2,1,0:T(8,128)(2,1)}, bf16[2,144,1152]{2,1,0:T(8,128)(2,1)}, u32[]{:S(2)}, u32[]{:S(2)}) collective-permute-start(bf16[2,144,1152]{2,1,0:T(8,128)(2,1)} %add_convert_fusion.7), channel_id=1, source_target_pairs={{0,8},{8,0},{1,9},{9,1},{2,10},{10,2},{3,11},{11,3},{4,12},{12,4},... | collective-permute-start | bytes 1990664 | tf_op jit(solution)/shard_map/ppermute | solution.py:609
  416.7 16.8 %collective-permute-start.60 = (f32[16,1152]{1,0:T(8,128)}, f32[16,1152]{1,0:T(8,128)}, u32[]{:S(2)}, u32[]{:S(2)}) collective-permute-start(f32[16,1152]{1,0:T(8,128)} %pad_maximum_fusion.7), channel_id=1, source_target_pairs={{0,1},{1,0},{2,3},{3,2},{4,5},{5,4},{6,7},{7,6},{8,9},{9,8},{10,11... | collective-permute-start | bytes 221192 | tf_op jit(solution)/shard_map/ppermute | solution.py:962
  420.2 25.6 %collective-permute-start.63 = (bf16[2,144,1152]{2,1,0:T(8,128)(2,1)}, bf16[2,144,1152]{2,1,0:T(8,128)(2,1)}, u32[]{:S(2)}, u32[]{:S(2)}) collective-permute-start(bf16[2,144,1152]{2,1,0:T(8,128)(2,1)} %add_convert_fusion.5), channel_id=1, source_target_pairs={{0,8},{8,0},{1,9},{9,1},{2,10},{10,2},{3,11},{11,3},{4,12},{12,4},... | collective-permute-start | bytes 1990664 | tf_op jit(solution)/shard_map/ppermute | solution.py:609
  434.3 15.1 %collective-permute-start.61 = (bf16[288,1152]{1,0:T(8,128)(2,1)}, bf16[288,1152]{1,0:T(8,128)(2,1)S(1)}, u32[]{:S(2)}, u32[]{:S(2)}) collective-permute-start(bf16[288,1152]{1,0:T(8,128)(2,1)} %get-tuple-element.425), channel_id=1, source_target_pairs={{0,16},{16,0},{1,17},{17,1},{2,18},{18,2},{3,19},{19,3},{4,20},{20... | collective-permute-start | bytes 1990664 | tf_op jit(solution)/shard_map/ppermute | solution.py:609
  449.4 30.6 %collective-permute-start.65 = (bf16[288,1152]{1,0:T(8,128)(2,1)S(1)}, bf16[288,1152]{1,0:T(8,128)(2,1)S(1)}, u32[]{:S(2)}, u32[]{:S(2)}) collective-permute-start(bf16[288,1152]{1,0:T(8,128)(2,1)S(1)} %copy-done.72), channel_id=1, source_target_pairs={{0,16},{16,0},{1,17},{17,1},{2,18},{18,2},{3,19},{19,3},{4,20},{20... | collective-permute-start | bytes 1990664 | tf_op jit(solution)/shard_map/ppermute | solution.py:609
  453.0 27.0 %collective-permute-start.68 = (bf16[144,1152]{1,0:T(8,128)(2,1)S(1)}, bf16[144,1152]{1,0:T(8,128)(2,1)S(1)}, u32[]{:S(2)}, u32[]{:S(2)}) collective-permute-start(bf16[144,1152]{1,0:T(8,128)(2,1)S(1)} %get-tuple-element.503), channel_id=1, source_target_pairs={{0,2},{1,3},{2,0},{3,1},{4,6},{5,7},{6,4},{7,5},{8,10},{9,11},{10,... | collective-permute-start | bytes 995336 | tf_op jit(solution)/shard_map/ppermute | solution.py:609
  454.1 25.9 %collective-permute-start.69 = (bf16[144,1152]{1,0:T(8,128)(2,1)S(1)}, bf16[144,1152]{1,0:T(8,128)(2,1)S(1)}, u32[]{:S(2)}, u32[]{:S(2)}) collective-permute-start(bf16[144,1152]{1,0:T(8,128)(2,1)S(1)} %get-tuple-element.502), channel_id=1, source_target_pairs={{0,1},{1,2},{2,3},{3,0},{4,5},{5,6},{6,7},{7,4},{8,9},{9,10},{10,1... | collective-permute-start | bytes 995336 | tf_op jit(solution)/shard_map/ppermute | solution.py:609
  480.6 16.7 %collective-permute-start.72 = (bf16[144,1152]{1,0:T(8,128)(2,1)S(1)}, bf16[144,1152]{1,0:T(8,128)(2,1)}, u32[]{:S(2)}, u32[]{:S(2)}) collective-permute-start(bf16[144,1152]{1,0:T(8,128)(2,1)S(1)} %slice.212), channel_id=1, source_target_pairs={{0,3},{1,0},{2,1},{3,2},{4,7},{5,4},{6,5},{7,6},{8,11},{9,8},{10,9... | collective-permute-start | bytes 995336 | tf_op jit(solution)/shard_map/ppermute | solution.py:609
  484.6 19.0 %collective-permute-start.73 = (bf16[144,1152]{1,0:T(8,128)(2,1)S(1)}, bf16[144,1152]{1,0:T(8,128)(2,1)S(1)}, u32[]{:S(2)}, u32[]{:S(2)}) collective-permute-start(bf16[144,1152]{1,0:T(8,128)(2,1)S(1)} %fusion.4), channel_id=1, source_target_pairs={{0,3},{1,0},{2,1},{3,2},{4,7},{5,4},{6,5},{7,6},{8,11},{9,8},{10,9... | collective-permute-start | bytes 995336 | tf_op jit(solution)/shard_map/ppermute | solution.py:609
  (84 other events, 906.7 us)
Sparse Core Ops, SparseCore 0:
  93.0 97.3 all-gather.1
